TPU v7x, 32 devices: a whole 2x2x4 slice. The times are simulated.
32 devices in a mesh: leaf: 4 (over z), row: 4 (over y, core), col: 2 (over x).
Axes of the slice: x: 2, y: 2, z: 4, core: 2. Of those that a mesh axis runs over, the one named last changes fastest.
Arguments:
- child_loads: bfloat16 [8, 128, 6144], P('leaf', None, 'row'), may hold values from -6 to 6
- child_inverse: bfloat16 [8, 6144, 6144], P('leaf', 'row', 'col'), as said below
- child_panel: bfloat16 [8, 6144, 6144], P('leaf', 'row', 'col'), may hold values from -0.0390625 to 0.0390625
- child_map: int32 [8, 6144], P('leaf'), may hold values from 0 to 6144, as said below
- root_loads: bfloat16 [128, 6144], P(None, 'row'), may hold values from -6 to 6
- root_inverse: bfloat16 [6144, 6144], P('row', 'col'), as said below
Outputs:
- child_solution: float32 [8, 128, 6144], P('leaf', None, 'row')
- root_solution: float32 [128, 6144], P(None, 'row')
Inputs may be any that keep to these rules, and one draw needn't show every extreme that they name: `child_map`: entry [k, j] is the root-front row into which update slot j of child front k adds, or 6144 where the slot is padding. Within each aligned block of 128 slots the live slots come first; the first block of every child is full; the live rows of one child are distinct. `child_inverse`: each child's [6144, 6144] block is upper triangular with a positive diagonal. `root_inverse`: upper triangular with a positive diagonal.
All inputs are finite; a program needn't handle non-finite values.
Results may differ from a plain program's by a relative error of at most 0.025.
Values may be sent and summed in bfloat16 or wider, within the bound.
No kernel may reach another device: no remote copies, remote signals or barrier semaphores. Data moves between devices by JAX's collectives and lax.ppermute only.
A program may use at most 128 MiB of HBM per device.

v0:
```python
import jax
import jax.numpy as jnp
from jax import lax
from jax.sharding import PartitionSpec as P


def solve_root(residual, root_inverse):
    forward_terms = jnp.dot(
        residual.astype(jnp.bfloat16), root_inverse, preferred_element_type=jnp.float32
    )
    root_forward = lax.psum(forward_terms.astype(jnp.bfloat16), "row")
    backward_terms = lax.dot_general(
        root_forward, root_inverse, (((1,), (1,)), ((), ())), preferred_element_type=jnp.float32
    )
    return lax.psum(backward_terms.astype(jnp.bfloat16), "col").astype(jnp.float32)


def on_device(child_loads, child_inverse, child_panel, child_map, root_loads, root_inverse):
    forward_terms = jnp.einsum(
        "knr,krc->knc", child_loads, child_inverse, preferred_element_type=jnp.float32
    )
    forward_solved = lax.psum(forward_terms, "row")
    forward_rounded = forward_solved.astype(jnp.bfloat16)
    update_terms = jnp.einsum(
        "knc,kuc->nku", forward_rounded, child_panel, preferred_element_type=jnp.float32
    )
    update_vals = lax.psum(update_terms, "col").astype(jnp.bfloat16)
    all_updates = lax.all_gather(update_vals, "row", axis=2, tiled=True)
    case_count = all_updates.shape[0]
    root_rows = root_loads.shape[1]
    first_row = lax.axis_index("row") * root_rows
    local_map = child_map - first_row
    inside = (local_map >= 0) & (local_map < root_rows)
    target = jnp.where(inside, local_map, root_rows).reshape(-1)
    values = all_updates.reshape(case_count, -1).astype(jnp.float32)
    extended = (
        jnp.zeros((case_count, root_rows + 1), jnp.float32).at[:, target].add(values)[:, :root_rows]
    )
    totals = lax.psum(extended.astype(jnp.bfloat16), "leaf").astype(jnp.float32)
    root_solution = solve_root(root_loads.astype(jnp.float32) - totals, root_inverse)
    root_full = lax.all_gather(root_solution.astype(jnp.bfloat16), "row", axis=1, tiled=True)
    padded_root = jnp.concatenate([root_full, jnp.zeros((case_count, 1), jnp.bfloat16)], axis=1)
    slot_rows = child_panel.shape[1]
    own_map = lax.dynamic_slice_in_dim(child_map, lax.axis_index("row") * slot_rows, slot_rows, 1)
    picked = jnp.take(padded_root, own_map, axis=1)
    back_terms = jnp.einsum("nku,kuc->knc", picked, child_panel, preferred_element_type=jnp.float32)
    back_sum = lax.psum(back_terms.astype(jnp.bfloat16), "row").astype(jnp.float32)
    remainder = (forward_solved - back_sum).astype(jnp.bfloat16)
    child_terms = jnp.einsum(
        "knc,krc->knr", remainder, child_inverse, preferred_element_type=jnp.float32
    )
    child_solution = lax.psum(child_terms.astype(jnp.bfloat16), "col").astype(jnp.float32)
    return (child_solution, root_solution)


def solution(mesh):
    in_specs = (
        P("leaf", None, "row"),
        P("leaf", "row", "col"),
        P("leaf", "row", "col"),
        P("leaf", None),
        P(None, "row"),
        P("row", "col"),
    )
    out_specs = (P("leaf", None, "row"), P(None, "row"))
    return jax.shard_map(
        on_device, mesh=mesh, in_specs=in_specs, out_specs=out_specs, check_vma=False
    )
```

profile of v0, /device:TPU:0, one launch (start us, length us, event | category | flops | bytes accessed | tf_op | source)
XLA Modules:
  0.0 505.7 jit_solution(1724302122919866879)
XLA Ops:
  7.2 0.0 copy-start
  7.2 0.0 all-reduce.9.cloned.1.call-start
  7.2 1.1 copy-done
  8.3 10.6 %fusion.9 = f32[2,128,3072]{2,1,0:T(8,128)} fusion(bf16[2,128,1536]{2,1,0:T(8,128)(2,1)S(1)} %copy-done, bf16[2,1536,3072]{2,1,0:T(8,128)(2,1)} %param.7), kind=kOutput, calls=%fused_computation.24 | convolution fusion | flops 2415919104 | bytes 22806528 | tf_op jit(solution)/shard_map/knr,krc->knc/dot_general | solution.py:19
  18.9 0.0 all-reduce.9.cloned.1.call-update
  19.0 0.0 all-gather.3.cloned.1.call-start
  19.0 71.2 %all-reduce.9.cloned.1.call-done = f32[2,128,3072]{2,1,0:T(8,128)} async-done(((f32[2,128,3072]{2,1,0:T(8,128)}), f32[2,128,3072]{2,1,0:T(8,128)}) %all-reduce.9.cloned.1.call-update) | async-done | bytes 3145744 | tf_op jit(solution)/shard_map/psum | solution.py:22
  90.2 11.1 %convolution_bitcast_fusion = f32[128,2,1536]{2,0,1:T(8,128)S(1)} fusion(bf16[2,1536,3072]{2,1,0:T(8,128)(2,1)} %param.8, f32[2,128,3072]{2,1,0:T(8,128)} %all-reduce.9.cloned.1.call-done), kind=kOutput, calls=%fused_computation.5 | convolution fusion | flops 2416705536 | bytes 23592960 | tf_op jit(solution)/shard_map/knc,kuc->nku/dot_general | solution.py:24
  101.4 0.0 copy-start.4
  101.4 41.1 %all-reduce.20 = bf16[128,2,1536]{2,0,1:T(8,128)(2,1)} all-reduce(f32[128,2,1536]{2,0,1:T(8,128)S(1)} %convolution_bitcast_fusion), channel_id=1, replica_groups=mesh['leaf'=4,'row'=4,'col'=2] {'col'}, use_global_device_ids=true, to_apply=%region_1.0 | all-reduce | flops 393216 | bytes 2359296 | tf_op jit(solution)/shard_map/psum | solution.py:27
  142.5 0.0 all-gather.3.cloned.1.call-update
  142.6 0.0 all-reduce.11.cloned.1.call-start
  142.6 0.0 copy-done.4
  142.7 0.1 copy.14
  142.7 0.1 compare_select_fusion
  142.8 0.0 copy-start.3
  142.8 28.1 %all-gather.3.cloned.1.call-done = bf16[128,2,6144]{2,0,1:T(8,128)(2,1)} async-done(((bf16[128,2,1536]{2,0,1:T(8,128)(2,1)}), bf16[128,2,6144]{2,0,1:T(8,128)(2,1)}) %all-gather.3.cloned.1.call-update) | async-done | bytes 3145744 | tf_op jit(solution)/shard_map/all_gather | solution.py:28
  170.9 5.4 %copy.11 = f32[128,2,6144]{0,2,1:T(8,128)} copy(bf16[128,2,6144]{2,0,1:T(8,128)(2,1)} %all-gather.3.cloned.1.call-done) | data formatting | bytes 9437184 | tf_op jit(solution)/shard_map/convert_element_type | solution.py:35
  176.3 73.8 %scatter_custom_fusion = f32[128,1537]{0,1:T(8,128)S(1)} fusion(s32[12288]{0:T(1024)S(1)} %bitcast.26, f32[12288,128]{1,0:T(8,128)} %bitcast.24, f32[]{:T(128)} %constant.16.clone.1), kind=kCustom, calls=%fused_computation.14 | custom fusion | flops 1572864 | bytes 787456 | tf_op jit(solution)/shard_map/scatter-add | solution.py:37
  250.1 0.8 slice.9
  250.9 0.0 all-reduce.11.cloned.1.call-update
  251.0 0.0 all-reduce.13.cloned.1.call-start
  251.0 0.0 copy-done.3
  251.0 0.2 copy.10
  251.2 37.2 %all-reduce.11.cloned.1.call-done = bf16[128,1536]{0,1:T(8,128)(2,1)} async-done(((bf16[128,1536]{0,1:T(8,128)(2,1)}), bf16[128,1536]{0,1:T(8,128)(2,1)}) %all-reduce.11.cloned.1.call-update) | async-done | bytes 393232 | tf_op jit(solution)/shard_map/psum | solution.py:39
  288.4 6.1 %convolution_convert_fusion.1 = bf16[128,3072]{1,0:T(8,128)(2,1)} fusion(bf16[1536,3072]{1,0:T(8,128)(2,1)} %param.11, bf16[128,1536]{0,1:T(8,128)(2,1)} %all-reduce.11.cloned.1.call-done, bf16[128,1536]{0,1:T(8,128)(2,1)S(1)} %copy.10), kind=kOutput, calls=%fused_computation.3 | convolution fusion | flops 1209139200 | bytes 11010048 | tf_op jit(solution)/shard_map/dot_general | solution.py:8
  294.6 0.0 all-reduce.13.cloned.1.call-update
  294.6 0.0 all-reduce.15.cloned.1.call-start
  294.6 34.3 %all-reduce.13.cloned.1.call-done = bf16[128,3072]{1,0:T(8,128)(2,1)} async-done(((bf16[128,3072]{1,0:T(8,128)(2,1)}), bf16[128,3072]{1,0:T(8,128)(2,1)}) %all-reduce.13.cloned.1.call-update) | async-done | bytes 786448 | tf_op jit(solution)/shard_map/psum | solution.py:11
  329.0 7.9 %convolution_convert_fusion.3 = bf16[128,1536]{1,0:T(8,128)(2,1)} fusion(bf16[128,3072]{1,0:T(8,128)(2,1)} %all-reduce.13.cloned.1.call-done, bf16[1536,3072]{1,0:T(8,128)(2,1)} %param.11), kind=kOutput, calls=%fused_computation.7 | convolution fusion | flops 1208156160 | bytes 10616832 | tf_op jit(solution)/shard_map/dot_general | solution.py:12
  336.9 0.0 all-reduce.15.cloned.1.call-update
  336.9 0.2 all-gather.5.cloned.1.call-start
  337.2 25.7 %all-reduce.15.cloned.1.call-done = bf16[128,1536]{1,0:T(8,128)(2,1)} async-done(((bf16[128,1536]{1,0:T(8,128)(2,1)}), bf16[128,1536]{1,0:T(8,128)(2,1)}) %all-reduce.15.cloned.1.call-update) | async-done | bytes 393232 | tf_op jit(solution)/shard_map/psum | solution.py:15
  362.9 0.0 all-gather.5.cloned.1.call-update
  362.9 0.0 all-reduce.17.cloned.1.call-start
  363.0 21.0 %all-gather.5.cloned.1.call-done = bf16[128,6144]{1,0:T(8,128)(2,1)} async-done(((bf16[128,1536]{1,0:T(8,128)(2,1)}), bf16[128,6144]{1,0:T(8,128)(2,1)}) %all-gather.5.cloned.1.call-update) | async-done | bytes 1572880 | tf_op jit(solution)/shard_map/all_gather | solution.py:41
  384.0 2.6 copy.13
  386.5 1.5 concatenate.3.clone
  388.1 9.2 %gather_fusion = bf16[3072,128]{1,0:T(8,128)(2,1)S(1)} fusion(bf16[128,6145]{0,1:T(8,128)(2,1)S(1)} %concatenate.3.clone, s32[3072]{0:T(1024)S(1)} %broadcast_clamp_fusion), kind=kCustom, calls=%fused_computation | custom fusion | bytes 1585152 | tf_op jit(solution)/shard_map/jit(_take)/gather | solution.py:45
  397.2 9.1 %convolution_convert_fusion = bf16[2,128,3072]{2,1,0:T(8,128)(2,1)} fusion(bf16[2,1536,3072]{2,1,0:T(8,128)(2,1)} %param.8, bf16[2,1536,128]{2,1,0:T(8,128)(2,1)S(1)} %bitcast.23, pred[2,1536]{1,0:T(4,128)(4,1)S(1)} %get-tuple-element.2), kind=kOutput, calls=%fused_computation.2 | convolution fusion | flops 2417098752 | bytes 21236736 | tf_op jit(solution)/shard_map/nku,kuc->knc/dot_general | solution.py:46
  406.3 0.0 all-reduce.17.cloned.1.call-update
  406.3 0.0 all-reduce.19.cloned.1.call-start
  406.4 42.9 %all-reduce.17.cloned.1.call-done = bf16[2,128,3072]{2,1,0:T(8,128)(2,1)} async-done(((bf16[2,128,3072]{2,1,0:T(8,128)(2,1)}), bf16[2,128,3072]{2,1,0:T(8,128)(2,1)}) %all-reduce.17.cloned.1.call-update) | async-done | bytes 1572880 | tf_op jit(solution)/shard_map/psum | solution.py:47
  449.3 12.4 %convolution_convert_fusion.2 = bf16[2,128,1536]{2,1,0:T(8,128)(2,1)} fusion(bf16[2,1536,3072]{2,1,0:T(8,128)(2,1)} %param.7, f32[2,128,3072]{2,1,0:T(8,128)} %all-reduce.9.cloned.1.call-done, bf16[2,128,3072]{2,1,0:T(8,128)(2,1)} %all-reduce.17.cloned.1.call-done), kind=kOutput, calls=%fused_computation.6 | convolution fusion | flops 2418671616 | bytes 24379392 | tf_op jit(solution)/shard_map/knc,krc->knr/dot_general | solution.py:49
  461.8 0.0 all-reduce.19.cloned.1.call-update
  461.8 1.0 convert_element_type.61
  462.8 33.6 %all-reduce.19.cloned.1.call-done = bf16[2,128,1536]{2,1,0:T(8,128)(2,1)} async-done(((bf16[2,128,1536]{2,1,0:T(8,128)(2,1)}), bf16[2,128,1536]{2,1,0:T(8,128)(2,1)}) %all-reduce.19.cloned.1.call-update) | async-done | bytes 786448 | tf_op jit(solution)/shard_map/psum | solution.py:52
  496.4 2.5 convert_element_type.60
  (8 shorter events, 0.1 us)
Async XLA Ops:
  7.2 1.1 copy-start
  7.2 83.1 %all-reduce.9.cloned.1.call-start = ((), (), s32[]{:S(2)}) async-start(), calls=%async_computation | async-start | bytes 6291456 | tf_op jit(solution)/shard_map/psum | solution.py:22
  19.0 152.0 %all-gather.3.cloned.1.call-start = ((), (), s32[]{:S(2)}) async-start(), calls=%async_computation.1 | async-start | bytes 3932160 | tf_op jit(solution)/shard_map/all_gather | solution.py:28
  101.4 41.2 %copy-start.4 = (s32[2,6144]{1,0:T(2,128)S(1)}, s32[2,6144]{1,0:T(2,128)}, u32[]{:S(2)}) copy-start(s32[2,6144]{1,0:T(2,128)} %param.9) | copy-start | bytes 147460
  142.6 145.9 %all-reduce.11.cloned.1.call-start = ((), (), s32[]{:S(2)}) async-start(), calls=%async_computation.2 | async-start | bytes 786432 | tf_op jit(solution)/shard_map/psum | solution.py:39
  142.8 108.2 %copy-start.3 = (bf16[128,1536]{1,0:T(8,128)(2,1)S(1)}, bf16[128,1536]{1,0:T(8,128)(2,1)}, u32[]{:S(2)}) copy-start(bf16[128,1536]{1,0:T(8,128)(2,1)} %param.10) | copy-start | bytes 1179652
  251.0 78.0 %all-reduce.13.cloned.1.call-start = ((), (), s32[]{:S(2)}) async-start(), calls=%async_computation.3 | async-start | bytes 1572864 | tf_op jit(solution)/shard_map/psum | solution.py:11
  294.6 68.3 %all-reduce.15.cloned.1.call-start = ((), (), s32[]{:S(2)}) async-start(), calls=%async_computation.4 | async-start | bytes 786432 | tf_op jit(solution)/shard_map/psum | solution.py:15
  336.9 47.0 %all-gather.5.cloned.1.call-start = ((), (), s32[]{:S(2)}) async-start(), calls=%async_computation.5 | async-start | bytes 1966080 | tf_op jit(solution)/shard_map/all_gather | solution.py:41
  362.9 86.5 %all-reduce.17.cloned.1.call-start = ((), (), s32[]{:S(2)}) async-start(), calls=%async_computation.6 | async-start | bytes 3145728 | tf_op jit(solution)/shard_map/psum | solution.py:47
  406.3 55.5 %copy-start.2 = (bf16[128,1536]{1,0:T(8,128)(2,1)S(1)}, bf16[128,1536]{1,0:T(8,128)(2,1)}, u32[]{:S(2)}) copy-start(bf16[128,1536]{1,0:T(8,128)(2,1)} %all-reduce.15.cloned.1.call-done) | copy-start | bytes 1179652
  406.3 90.0 %all-reduce.19.cloned.1.call-start = ((), (), s32[]{:S(2)}) async-start(), calls=%async_computation.7 | async-start | bytes 1572864 | tf_op jit(solution)/shard_map/psum | solution.py:52
  449.3 49.5 %copy-start.1 = (bf16[2,128,1536]{2,1,0:T(8,128)(2,1)S(1)}, bf16[2,128,1536]{2,1,0:T(8,128)(2,1)}, u32[]{:S(2)}) copy-start(bf16[2,128,1536]{2,1,0:T(8,128)(2,1)} %param.6) | copy-start | bytes 2359300
Sparse Core Ops, SparseCore 0:
  19.1 71.1 all-reduce.8
  142.7 28.1 all-gather.2
  251.1 37.3 all-reduce.10
  294.7 34.2 all-reduce.12
  337.0 25.7 all-reduce.14
  364.3 19.6 all-gather.4
  406.5 42.8 all-reduce.16
  461.9 34.3 all-reduce.18
where the time goes:
time: 506 us
  waiting for transfers between devices  294 us (58%)
  other arithmetic  77.4 us (15%)
  matrix products  57.4 us (11%)
  blocking collectives  41.1 us (8%)
  local copies, waits for them, and re-layouts  20.8 us (4%)
  between operations  14.3 us (3%)
    scatter-add x1, other arithmetic, on_device(): jnp.zeros((case_count, root_rows + 1), jnp.float32).at[:, target]  73.8 us
    psum x1, waiting for transfers between devices, on_device(): forward_solved = lax.psum(forward_terms, 'row')  71.2 us
    psum x1, waiting for transfers between devices, on_device(): lax.psum(back_terms.astype(jnp.bfloat16), 'row').astype(jnp.float32)  42.9 us
    psum x1, blocking collectives, on_device(): update_vals = lax.psum(update_terms, 'col').astype(jnp.bfloat16)  41.1 us
    psum x1, waiting for transfers between devices, on_device(): totals = lax.psum(extended.astype(jnp.bfloat16), 'leaf').astype(jnp.float32)  37.2 us
    psum x1, waiting for transfers between devices, solve_root(): root_forward = lax.psum(forward_terms.astype(jnp.bfloat16), 'row')  34.3 us
    psum x1, waiting for transfers between devices, on_device(): lax.psum(child_terms.astype(jnp.bfloat16), 'col').astype(jnp.float32)  33.6 us
    all_gather x1, waiting for transfers between devices, on_device(): all_updates = lax.all_gather(update_vals, 'row', axis=2, tiled=True)  28.1 us
  transfers between devices with their start and end apart: 8, of which 8 were waited for; matrix products, arithmetic and copies ran while one was open for 0% of the time, Pallas kernels for 0%

commit v1 on v0

v1 whole, which is shorter than its diff:
```python
import functools

import jax
import jax.numpy as jnp
from jax import lax
from jax.experimental import pallas as pl
from jax.experimental.pallas import tpu as pltpu
from jax.sharding import PartitionSpec as P

BF16 = jnp.bfloat16
F32 = jnp.float32
NN = (((1,), (0,)), ((), ()))
NT = (((1,), (1,)), ((), ()))


def tile_of(extent, *sizes):
    for size in sizes:
        if extent % size == 0:
            return size
    return extent


def params():
    return pltpu.CompilerParams(vmem_limit_bytes=40 * 1024 * 1024)


def cost(flops, nbytes):
    return pl.CostEstimate(flops=flops, bytes_accessed=nbytes, transcendentals=0)


def nn_kernel(half_ref, x_ref, w_ref, o_ref):
    o_ref[...] = lax.dot_general(
        x_ref[...], w_ref[0], NN, preferred_element_type=F32
    ).astype(o_ref.dtype)


def nn_half(x, w, child, half, dtype):
    m, k = x.shape
    n_half = w.shape[2] // 2
    bn = tile_of(n_half, 512, 384, 256, 128)
    steps = n_half // bn
    return pl.pallas_call(
        nn_kernel,
        grid_spec=pltpu.PrefetchScalarGridSpec(
            num_scalar_prefetch=1,
            grid=(steps,),
            in_specs=[
                pl.BlockSpec((m, k), lambda i, h: (0, 0)),
                pl.BlockSpec((1, k, bn), lambda i, h: (child, 0, h[0] * steps + i)),
            ],
            out_specs=pl.BlockSpec((m, bn), lambda i, h: (0, i)),
        ),
        out_shape=jax.ShapeDtypeStruct((m, n_half), dtype),
        compiler_params=params(),
        cost_estimate=cost(2 * m * k * n_half, 2 * k * n_half),
    )(half, x, w)


def nt_kernel(half_ref, a_ref, b_ref, wa_ref, wb_ref, o_ref):
    total = lax.dot_general(a_ref[...], wa_ref[0], NT, preferred_element_type=F32)
    total += lax.dot_general(b_ref[...], wb_ref[0], NT, preferred_element_type=F32)
    o_ref[...] = total.astype(o_ref.dtype)


def nt(mine, other, w, child, half, dtype):
    m, k_half = mine.shape
    u = w.shape[1]
    bu = tile_of(u, 256, 128)
    return pl.pallas_call(
        nt_kernel,
        grid_spec=pltpu.PrefetchScalarGridSpec(
            num_scalar_prefetch=1,
            grid=(u // bu,),
            in_specs=[
                pl.BlockSpec((m, k_half), lambda i, h: (0, 0)),
                pl.BlockSpec((m, k_half), lambda i, h: (0, 0)),
                pl.BlockSpec((1, bu, k_half), lambda i, h: (child, i, h[0])),
                pl.BlockSpec((1, bu, k_half), lambda i, h: (child, i, 1 - h[0])),
            ],
            out_specs=pl.BlockSpec((m, bu), lambda i, h: (0, i)),
        ),
        out_shape=jax.ShapeDtypeStruct((m, u), dtype),
        compiler_params=params(),
        cost_estimate=cost(4 * m * k_half * u, 4 * k_half * u),
    )(half, mine, other, w, w)


def one_hot(rows, first_row, slot_map):
    local = (slot_map - first_row).astype(jnp.int16)
    row_ids = lax.broadcasted_iota(jnp.int16, (rows, slot_map.shape[1]), 0)
    return jnp.where(row_ids == local, BF16(1), BF16(0))


def scatter_kernel(block_rows, tile, odd, *refs):
    row_ref, map_ref, upd_ref, *rest = refs
    o_ref = rest[-1]
    j, t = pl.program_id(0), pl.program_id(1)
    dest = lax.bitwise_xor(row_ref[0], 2 * j + odd)
    hot = one_hot(tile, dest * block_rows + t * tile, map_ref[...])
    total = lax.dot_general(upd_ref[...], hot, NT, preferred_element_type=F32)
    if len(rest) == 2:
        total += rest[0][0].astype(F32)
    o_ref[0] = total.astype(o_ref.dtype)


def scatter(upd, slot_map, row, rows_count, block_rows, odd, before):
    m, u = upd.shape
    tile = tile_of(block_rows, 256, 128)
    count = rows_count // 2
    in_specs = [
        pl.BlockSpec((1, u), lambda j, t, r: (0, 0)),
        pl.BlockSpec((m, u), lambda j, t, r: (0, 0)),
    ]
    block = pl.BlockSpec((1, m, tile), lambda j, t, r: (j, 0, t))
    args = [slot_map, upd]
    if before is not None:
        in_specs.append(block)
        args.append(before)
    return pl.pallas_call(
        functools.partial(scatter_kernel, block_rows, tile, odd),
        grid_spec=pltpu.PrefetchScalarGridSpec(
            num_scalar_prefetch=1,
            grid=(count, block_rows // tile),
            in_specs=in_specs,
            out_specs=block,
        ),
        out_shape=jax.ShapeDtypeStruct((count, m, block_rows), BF16),
        compiler_params=params(),
        cost_estimate=cost(2 * m * u * count * block_rows, 4 * m * count * block_rows),
    )(row, *args)


def gather_kernel(block_rows, tile, rows_at, *refs):
    row_ref, map_ref, root_ref, *rest = refs
    o_ref = rest[-1]
    slot_map = map_ref[0]
    total = None
    for at, (array, which) in enumerate(rows_at):
        first = lax.bitwise_xor(row_ref[0], which) * block_rows
        for start in range(0, block_rows, tile):
            hot = one_hot(tile, first + start, slot_map)
            term = lax.dot_general(
                root_ref[at, :, start : start + tile], hot, NN, preferred_element_type=F32
            )
            total = term if total is None else total + term
    if len(rest) == 2:
        total += rest[0][...].astype(F32)
    o_ref[...] = total.astype(o_ref.dtype)


def gather(root, which, slot_map, row, before):
    blocks, m, block_rows = root.shape
    u = slot_map.shape[2]
    tile = tile_of(block_rows, 512, 384, 256, 128)
    bu = tile_of(u, 512, 384, 256, 128)
    in_specs = [
        pl.BlockSpec((1, 1, bu), lambda i, r: (0, 0, i)),
        pl.BlockSpec((blocks, m, block_rows), lambda i, r: (0, 0, 0)),
    ]
    out_block = pl.BlockSpec((m, bu), lambda i, r: (0, i))
    args = [slot_map, root]
    if before is not None:
        in_specs.append(out_block)
        args.append(before)
    return pl.pallas_call(
        functools.partial(
            gather_kernel, block_rows, tile, [(0, x) for x in which]
        ),
        grid_spec=pltpu.PrefetchScalarGridSpec(
            num_scalar_prefetch=1, grid=(u // bu,), in_specs=in_specs, out_specs=out_block
        ),
        out_shape=jax.ShapeDtypeStruct((m, u), BF16),
        compiler_params=params(),
        cost_estimate=cost(2 * m * u * blocks * block_rows, 2 * m * blocks * block_rows),
    )(row, *args)


def swap(x, axis, bit, size):
    return lax.ppermute(x, axis, [(i, i ^ bit) for i in range(size)])


def bits(size):
    return [1 << b for b in range(size.bit_length() - 1)]


def on_device(sizes, child_loads, child_inverse, child_panel, child_map, root_loads, root_inverse):
    leafs, rows, cols = sizes
    kids = child_loads.shape[0]
    case_count, root_rows = root_loads.shape
    leaf, row, col = (lax.axis_index(a).astype(jnp.int32) for a in ("leaf", "row", "col"))
    core = lax.bitwise_and(row, 1)
    mine = core[None]
    other = (1 - core)[None]
    row_1 = row[None]
    root_w = root_inverse[None]

    def row_sum(x, w, child):
        sent = nn_half(x, w, child, other, BF16)
        kept = nn_half(x, w, child, mine, F32)
        total = kept + swap(sent, "row", 1, rows).astype(F32)
        for bit in bits(rows)[1:]:
            total = total + swap(total.astype(BF16), "row", bit, rows).astype(F32)
        return total

    def times_transposed(half_cols, w, child):
        rounded = half_cols.astype(BF16)
        return nt(rounded, swap(rounded, "row", 1, rows), w, child, mine, BF16)

    slot_rows = child_panel.shape[1]
    own_map = lax.dynamic_slice_in_dim(child_map, row * slot_rows, slot_rows, 1)
    maps = own_map.reshape(kids, 1, slot_rows)

    forward = [row_sum(child_loads[k], child_inverse, k) for k in range(kids)]
    sent = kept = None
    for k in range(kids):
        upd = times_transposed(forward[k], child_panel, k)
        sent = scatter(upd, maps[k], row_1, rows, root_rows, 1, sent)
        kept = scatter(upd, maps[k], row_1, rows, root_rows, 0, kept)

    total = kept.astype(F32) + swap(sent, "row", 1, rows).astype(F32)
    for bit in bits(rows)[1:]:
        away = total[1::2].astype(BF16)
        total = total[0::2] + swap(away, "row", bit, rows).astype(F32)
    total = total[0]
    chunk = case_count // leafs

    def cases_of(x, j):
        return lax.dynamic_slice_in_dim(x, lax.bitwise_xor(leaf, j) * chunk, chunk, 0)

    narrow = total.astype(BF16)
    mine_cases = cases_of(total, 0)
    for j in range(1, leafs):
        mine_cases = mine_cases + swap(cases_of(narrow, j), "leaf", j, leafs).astype(F32)
    for bit in bits(cols):
        narrow = mine_cases.astype(BF16)
        mine_cases = narrow.astype(F32) + swap(narrow, "col", bit, cols).astype(F32)
    residual = (cases_of(root_loads, 0).astype(F32) - mine_cases).astype(BF16)

    root_forward = row_sum(residual, root_w, 0)
    part = times_transposed(root_forward, root_w, 0)
    for bit in bits(cols):
        part = (part.astype(F32) + swap(part, "col", bit, cols).astype(F32)).astype(BF16)

    pieces = [part] + [swap(part, "leaf", j, leafs) for j in range(1, leafs)]
    own = jnp.zeros((case_count, root_rows), BF16)
    for j in range(leafs):
        own = lax.dynamic_update_slice_in_dim(own, pieces[j], lax.bitwise_xor(leaf, j) * chunk, 0)
    root_solution = own.astype(F32)

    groups = own[None]
    for bit in bits(rows)[1:]:
        groups = jnp.concatenate([groups, swap(groups, "row", bit, rows)])
    near = groups[:1]
    near_other = swap(near, "row", 1, rows)
    far = groups[1:]
    far_other = swap(far, "row", 1, rows)
    near_all = jnp.concatenate([near, near_other])
    far_all = jnp.concatenate([far, far_other])
    near_at = [0, 1]
    far_at = [2 * i for i in range(1, rows // 2)] + [2 * i + 1 for i in range(1, rows // 2)]

    solved = []
    picked = [gather(near_all, near_at, maps[k][None], row_1, None) for k in range(kids)]
    for k in range(kids):
        full = gather(far_all, far_at, maps[k][None], row_1, picked[k])
        back = row_sum(full, child_panel, k)
        rest = forward[k] - back
        out = times_transposed(rest, child_inverse, k)
        for bit in bits(cols):
            out = out.astype(F32) + swap(out.astype(BF16), "col", bit, cols).astype(F32)
            if bit != bits(cols)[-1]:
                out = out.astype(BF16)
        solved.append(out)
    return (jnp.stack(solved), root_solution)


def solution(mesh):
    sizes = tuple(mesh.shape[a] for a in ("leaf", "row", "col"))
    in_specs = (
        P("leaf", None, "row"),
        P("leaf", "row", "col"),
        P("leaf", "row", "col"),
        P("leaf", None),
        P(None, "row"),
        P("row", "col"),
    )
    out_specs = (P("leaf", None, "row"), P(None, "row"))
    return jax.shard_map(
        functools.partial(on_device, sizes),
        mesh=mesh,
        in_specs=in_specs,
        out_specs=out_specs,
        check_vma=False,
    )
```

time: 506 us -> 223 us (0.44)
  waiting for transfers between devices: 294 us -> 87.7 us
  Pallas kernels: 0 us -> 92.6 us
  other arithmetic: 77.4 us -> 7.77 us
  matrix products: 57.4 us -> 0 us
  blocking collectives: 41.1 us -> 0 us
  starting transfers between devices: 0.51 us -> 26.6 us
  local copies, waits for them, and re-layouts: 20.8 us -> 6.68 us
  between operations: 14.3 us -> 1.17 us
    psum x6 -> x0, waiting for transfers between devices: 245 us -> none  [the longest x1 71.2 us: on_device(): forward_solved = lax.psum(forward_terms, 'row')]
    pallas_call x0 -> x23, Pallas kernels: none -> 92.6 us  [the longest x5 32.4 us: nt(): pl.pallas_call(nt_kernel, grid_spec=pltpu.PrefetchScalarGridSpec(num_scal...]
    ppermute x0 -> x30, waiting for transfers between devices: none -> 87.7 us  [swap(): return lax.ppermute(x, axis, [(i, i ^ bit) for i in range(size)])]
    scatter-add x1 -> x0, other arithmetic: 73.8 us -> none  [on_device(): jnp.zeros((case_count, root_rows + 1), jnp.float32).at[:, target]]
    dot_general x6 -> x0, matrix products: 57.4 us -> none  [the longest x1 12.4 us: on_device(): jnp.einsum('knc,krc->knr', remainder, child_inverse, preferred_element_ty...]
    all_gather x2 -> x0, waiting for transfers between devices: 49.1 us -> none  [the longest x1 28.1 us: on_device(): all_updates = lax.all_gather(update_vals, 'row', axis=2, tiled=True)]
    psum x1 -> x0, blocking collectives: 41.1 us -> none  [on_device(): update_vals = lax.psum(update_terms, 'col').astype(jnp.bfloat16)]
    ppermute x0 -> x30, starting transfers between devices: none -> 26.6 us  [swap(): return lax.ppermute(x, axis, [(i, i ^ bit) for i in range(size)])]
  transfers between devices with their start and end apart: 8 -> 30, of which waited for: 8 -> 17; matrix products, arithmetic and copies ran while one was open for 0% -> 1% of each run, Pallas kernels for 0% -> 29%
where the time goes in v1:
time: 223 us; the launch traced here: 222 us
  Pallas kernels  92.6 us (42%)
  waiting for transfers between devices  87.7 us (39%)
  starting transfers between devices  26.6 us (12%)
  other arithmetic  7.77 us (3%)
  local copies, waits for them, and re-layouts  6.68 us (3%)
    ppermute x30, waiting for transfers between devices, swap(): return lax.ppermute(x, axis, [(i, i ^ bit) for i in range(size)])  87.7 us
    pallas_call x5, Pallas kernels, nt(): pl.pallas_call(nt_kernel, grid_spec=pltpu.PrefetchScalarGridSpec(num_scal...  32.4 us
    pallas_call x10, Pallas kernels, nn_half(): pl.pallas_call(nn_kernel, grid_spec=pltpu.PrefetchScalarGridSpec(num_scal...  32.2 us
    ppermute x30, starting transfers between devices, swap(): return lax.ppermute(x, axis, [(i, i ^ bit) for i in range(size)])  26.6 us
    pallas_call x4, Pallas kernels, scatter(): pl.pallas_call(functools.partial(scatter_kernel, block_rows, tile, odd),...  20.5 us
    pallas_call x4, Pallas kernels, gather(): pl.pallas_call(functools.partial(gather_kernel, block_rows, tile, [(0, x)...  7.45 us
  transfers between devices with their start and end apart: 30, of which 17 were waited for; matrix products, arithmetic and copies ran while one was open for 1% of the time, Pallas kernels for 29%

profile of v1, /device:TPU:0, one launch (start us, length us, event | category | flops | bytes accessed | tf_op | source)
XLA Modules:
  0.0 222.5 jit_solution(9533488991776991467)
XLA Ops:
  1.8 3.7 %shard_map.78 = bf16[128,1536]{1,0:T(8,128)(2,1)S(1)} custom-call(s32[1]{0:T(128)} %bitcast.2.half_ref, bf16[128,1536]{1,0:T(8,128)(2,1)S(1)} %get-tuple-element.6.x_ref, bf16[2,1536,3072]{2,1,0:T(8,128)(2,1)} %wb_ref.7), custom_call_target="tpu_custom_call" | custom-call | flops 603979776 | bytes 4718592 | tf_op jit(solution)/shard_map/pallas_call | solution.py:42
  6.0 3.6 %shard_map.80 = bf16[128,1536]{1,0:T(8,128)(2,1)S(1)} custom-call(s32[1]{0:T(128)} %bitcast.2.half_ref, bf16[128,1536]{1,0:T(8,128)(2,1)S(1)} %get-tuple-element.7.x_ref, bf16[2,1536,3072]{2,1,0:T(8,128)(2,1)} %wb_ref.7), custom_call_target="tpu_custom_call" | custom-call | flops 603979776 | bytes 4718592 | tf_op jit(solution)/shard_map/pallas_call | solution.py:42
  9.8 3.6 %shard_map.77 = f32[128,1536]{1,0:T(8,128)S(1)} custom-call(s32[1]{0:T(128)} %bitcast.half_ref, bf16[128,1536]{1,0:T(8,128)(2,1)S(1)} %get-tuple-element.6.x_ref, bf16[2,1536,3072]{2,1,0:T(8,128)(2,1)} %wb_ref.7), custom_call_target="tpu_custom_call" | custom-call | flops 603979776 | bytes 4718592 | tf_op jit(solution)/shard_map/pallas_call | solution.py:42
  13.4 3.7 %shard_map.79 = f32[128,1536]{1,0:T(8,128)S(1)} custom-call(s32[1]{0:T(128)} %bitcast.half_ref, bf16[128,1536]{1,0:T(8,128)(2,1)S(1)} %get-tuple-element.7.x_ref, bf16[2,1536,3072]{2,1,0:T(8,128)(2,1)} %wb_ref.7), custom_call_target="tpu_custom_call" | custom-call | flops 603979776 | bytes 4718592 | tf_op jit(solution)/shard_map/pallas_call | solution.py:42
  17.2 3.0 %collective-permute-start.1 = (bf16[128,1536]{1,0:T(8,128)(2,1)S(1)}, bf16[128,1536]{1,0:T(8,128)(2,1)S(1)}, u32[]{:S(2)}, u32[]{:S(2)}) collective-permute-start(bf16[128,1536]{1,0:T(8,128)(2,1)S(1)} %fusion), channel_id=1, source_target_pairs={{0,4},{2,6},{4,0},{6,2},{1,5},{3,7},{5,1},{7,3},{8,12},{10,14},{12... | collective-permute-start | bytes 1179656 | tf_op jit(solution)/shard_map/ppermute | solution.py:179
  20.4 9.7 %collective-permute-done.1 = bf16[128,1536]{1,0:T(8,128)(2,1)S(1)} collective-permute-done((bf16[128,1536]{1,0:T(8,128)(2,1)S(1)}, bf16[128,1536]{1,0:T(8,128)(2,1)S(1)}, u32[]{:S(2)}, u32[]{:S(2)}) %collective-permute-start.1) | collective-permute-done | bytes 393248 | tf_op jit(solution)/shard_map/ppermute | solution.py:179
  30.3 7.6 %collective-permute-done.3 = bf16[128,1536]{1,0:T(8,128)(2,1)S(1)} collective-permute-done((bf16[128,1536]{1,0:T(8,128)(2,1)S(1)}, bf16[128,1536]{1,0:T(8,128)(2,1)S(1)}, u32[]{:S(2)}, u32[]{:S(2)}) %collective-permute-start.3) | collective-permute-done | bytes 393248 | tf_op jit(solution)/shard_map/ppermute | solution.py:179
  39.0 7.0 %shard_map.82.refs_2_ = bf16[128,1536]{1,0:T(8,128)(2,1)S(1)} custom-call(s32[1]{0:T(128)} %bitcast.half_ref, bf16[128,1536]{1,0:T(8,128)(2,1)S(1)} %fusion.4.a_ref, bf16[128,1536]{1,0:T(8,128)(2,1)S(1)} %collective-permute-done.5.b_ref, bf16[2,1536,3072]{2,1,0:T(8,128)(2,1)} %w_ref.15, bf16[2,1536,3072]{2,1,0:T(8,128)(2,1)} %w_ref.15), custom_call_target="tpu_custom_call" | custom-call | flops 1207959552 | bytes 9437184 | tf_op jit(solution)/shard_map/pallas_call | solution.py:69
  46.1 5.1 %shard_map.85.refs_3_ = bf16[2,128,1536]{2,1,0:T(8,128)(2,1)S(1)} custom-call(s32[1]{0:T(128)} %bitcast.3.refs_0_, s32[1,1536]{1,0:T(1,128)S(1)} %get-tuple-element.11.refs_1_, bf16[128,1536]{1,0:T(8,128)(2,1)S(1)} %shard_map.82.refs_2_), custom_call_target="tpu_custom_call" | custom-call | flops 1207959552 | bytes 1572864 | tf_op jit(solution)/shard_map/pallas_call | solution.py:119
  51.2 7.0 %shard_map.81.refs_2_ = bf16[128,1536]{1,0:T(8,128)(2,1)S(1)} custom-call(s32[1]{0:T(128)} %bitcast.half_ref, bf16[128,1536]{1,0:T(8,128)(2,1)S(1)} %fusion.5.a_ref, bf16[128,1536]{1,0:T(8,128)(2,1)S(1)} %collective-permute-done.4.b_ref, bf16[2,1536,3072]{2,1,0:T(8,128)(2,1)} %w_ref.15, bf16[2,1536,3072]{2,1,0:T(8,128)(2,1)} %w_ref.15), custom_call_target="tpu_custom_call" | custom-call | flops 1207959552 | bytes 9437184 | tf_op jit(solution)/shard_map/pallas_call | solution.py:69
  58.2 5.2 %shard_map.86 = bf16[2,128,1536]{2,1,0:T(8,128)(2,1)S(1)} custom-call(s32[1]{0:T(128)} %bitcast.3.refs_0_, s32[1,1536]{1,0:T(1,128)S(1)} %get-tuple-element.12.refs_1_, bf16[128,1536]{1,0:T(8,128)(2,1)S(1)} %shard_map.81.refs_2_, bf16[2,128,1536]{2,1,0:T(8,128)(2,1)S(1)} %shard_map.85.refs_3_), custom_call_target="tpu_custom_call" | custom-call | flops 1207959552 | bytes 1572864 | tf_op jit(solution)/shard_map/pallas_call | solution.py:119
  64.0 5.1 %shard_map.83.refs_3_ = bf16[2,128,1536]{2,1,0:T(8,128)(2,1)S(1)} custom-call(s32[1]{0:T(128)} %bitcast.3.refs_0_, s32[1,1536]{1,0:T(1,128)S(1)} %get-tuple-element.11.refs_1_, bf16[128,1536]{1,0:T(8,128)(2,1)S(1)} %shard_map.82.refs_2_), custom_call_target="tpu_custom_call" | custom-call | flops 1207959552 | bytes 1572864 | tf_op jit(solution)/shard_map/pallas_call | solution.py:119
  69.1 5.2 %shard_map.84 = bf16[2,128,1536]{2,1,0:T(8,128)(2,1)S(1)} custom-call(s32[1]{0:T(128)} %bitcast.3.refs_0_, s32[1,1536]{1,0:T(1,128)S(1)} %get-tuple-element.12.refs_1_, bf16[128,1536]{1,0:T(8,128)(2,1)S(1)} %shard_map.81.refs_2_, bf16[2,128,1536]{2,1,0:T(8,128)(2,1)S(1)} %shard_map.83.refs_3_), custom_call_target="tpu_custom_call" | custom-call | flops 1207959552 | bytes 1572864 | tf_op jit(solution)/shard_map/pallas_call | solution.py:119
  75.3 1.7 collective-permute-start.7
  77.1 9.6 %collective-permute-done.7 = bf16[1,128,1536]{2,1,0:T(8,128)(2,1)} collective-permute-done((bf16[1,128,1536]{2,1,0:T(8,128)(2,1)}, bf16[1,128,1536]{2,1,0:T(8,128)(2,1)}, u32[]{:S(2)}, u32[]{:S(2)}) %collective-permute-start.7) | collective-permute-done | bytes 393248 | tf_op jit(solution)/shard_map/ppermute | solution.py:179
  86.7 2.0 fusion.10
  88.7 1.9 collective-permute-start.8
  90.6 2.5 %collective-permute-start.10 = (bf16[32,1536]{1,0:T(8,128)(2,1)S(1)}, bf16[32,1536]{1,0:T(8,128)(2,1)S(1)}, u32[]{:S(2)}, u32[]{:S(2)}) collective-permute-start(bf16[32,1536]{1,0:T(8,128)(2,1)S(1)} %get-tuple-element.9), channel_id=1, source_target_pairs={{0,24},{8,16},{16,8},{24,0},{1,25},{9,17},{17,9},{25,1},{2,26},{10... | collective-permute-start | bytes 294920 | tf_op jit(solution)/shard_map/ppermute | solution.py:179
  93.5 4.6 %collective-permute-done.10 = bf16[32,1536]{1,0:T(8,128)(2,1)S(1)} collective-permute-done((bf16[32,1536]{1,0:T(8,128)(2,1)S(1)}, bf16[32,1536]{1,0:T(8,128)(2,1)S(1)}, u32[]{:S(2)}, u32[]{:S(2)}) %collective-permute-start.10) | collective-permute-done | bytes 98336 | tf_op jit(solution)/shard_map/ppermute | solution.py:179
  98.1 3.3 %collective-permute-done.9 = bf16[32,1536]{1,0:T(8,128)(2,1)S(1)} collective-permute-done((bf16[32,1536]{1,0:T(8,128)(2,1)S(1)}, bf16[32,1536]{1,0:T(8,128)(2,1)S(1)}, u32[]{:S(2)}, u32[]{:S(2)}) %collective-permute-start.9) | collective-permute-done | bytes 98336 | tf_op jit(solution)/shard_map/ppermute | solution.py:179
  102.3 1.6 collective-permute-start.11
  103.9 3.1 %collective-permute-done.11 = bf16[32,1536]{1,0:T(8,128)(2,1)S(1)} collective-permute-done((bf16[32,1536]{1,0:T(8,128)(2,1)S(1)}, bf16[32,1536]{1,0:T(8,128)(2,1)S(1)}, u32[]{:S(2)}, u32[]{:S(2)}) %collective-permute-start.11) | collective-permute-done | bytes 98336 | tf_op jit(solution)/shard_map/ppermute | solution.py:179
  107.9 3.7 %copy-done = bf16[1536,3072]{1,0:T(8,128)(2,1)S(1)} copy-done((bf16[1536,3072]{1,0:T(8,128)(2,1)S(1)}, bf16[1536,3072]{1,0:T(8,128)(2,1)}, u32[]{:S(2)}) %copy-start) | copy-done | bytes 9437208
  113.2 1.5 shard_map.87
  114.7 1.6 collective-permute-start.13
  116.3 3.7 %collective-permute-done.13 = bf16[32,1536]{1,0:T(8,128)(2,1)S(1)} collective-permute-done((bf16[32,1536]{1,0:T(8,128)(2,1)S(1)}, bf16[32,1536]{1,0:T(8,128)(2,1)S(1)}, u32[]{:S(2)}, u32[]{:S(2)}) %collective-permute-start.13) | collective-permute-done | bytes 98336 | tf_op jit(solution)/shard_map/ppermute | solution.py:179
  121.4 4.2 %shard_map.89 = bf16[32,1536]{1,0:T(8,128)(2,1)S(1)} custom-call(s32[1]{0:T(128)} %bitcast.half_ref, bf16[32,1536]{1,0:T(8,128)(2,1)S(1)} %add_convert_fusion.1.a_ref, bf16[32,1536]{1,0:T(8,128)(2,1)S(1)} %collective-permute-done.14.b_ref, bf16[1,1536,3072]{2,1,0:T(8,128)(2,1)S(1)} %bitcast.33, bf16[1,1536,3072]{2,1,0:T(8,128)(2,1)S(1)} %bitcast.34), custom_call_target="tpu_custom_call" | custom-call | flops 301989888 | bytes 9437184 | tf_op jit(solution)/shard_map/pallas_call | solution.py:69
  125.6 1.6 collective-permute-start.15
  127.2 3.4 %collective-permute-done.15 = bf16[32,1536]{1,0:T(8,128)(2,1)S(1)} collective-permute-done((bf16[32,1536]{1,0:T(8,128)(2,1)S(1)}, bf16[32,1536]{1,0:T(8,128)(2,1)S(1)}, u32[]{:S(2)}, u32[]{:S(2)}) %collective-permute-start.15) | collective-permute-done | bytes 98336 | tf_op jit(solution)/shard_map/ppermute | solution.py:179
  130.7 3.2 %collective-permute-start.17 = (bf16[32,1536]{1,0:T(8,128)(2,1)S(1)}, bf16[32,1536]{1,0:T(8,128)(2,1)S(1)}, u32[]{:S(2)}, u32[]{:S(2)}) collective-permute-start(bf16[32,1536]{1,0:T(8,128)(2,1)S(1)} %get-tuple-element.3), channel_id=1, source_target_pairs={{0,16},{8,24},{16,0},{24,8},{1,17},{9,25},{17,1},{25,9},{2,18},{10... | collective-permute-start | bytes 294920 | tf_op jit(solution)/shard_map/ppermute | solution.py:179
  136.0 5.1 %collective-permute-done.17 = bf16[32,1536]{1,0:T(8,128)(2,1)S(1)} collective-permute-done((bf16[32,1536]{1,0:T(8,128)(2,1)S(1)}, bf16[32,1536]{1,0:T(8,128)(2,1)S(1)}, u32[]{:S(2)}, u32[]{:S(2)}) %collective-permute-start.17) | collective-permute-done | bytes 98336 | tf_op jit(solution)/shard_map/ppermute | solution.py:179
  141.2 1.6 collective-permute-start.19
  142.7 7.1 %collective-permute-done.19 = bf16[1,128,1536]{2,1,0:T(8,128)(2,1)S(1)} collective-permute-done((bf16[1,128,1536]{2,1,0:T(8,128)(2,1)S(1)}, bf16[1,128,1536]{2,1,0:T(8,128)(2,1)S(1)}, u32[]{:S(2)}, u32[]{:S(2)}) %collective-permute-start.19) | collective-permute-done | bytes 393248 | tf_op jit(solution)/shard_map/ppermute | solution.py:179
  149.9 1.9 shard_map.95.refs_3_
  151.8 1.9 shard_map.96.x_ref
  153.7 3.7 %shard_map.98 = bf16[128,1536]{1,0:T(8,128)(2,1)S(1)} custom-call(s32[1]{0:T(128)} %bitcast.2.half_ref, bf16[128,1536]{1,0:T(8,128)(2,1)S(1)} %shard_map.96.x_ref, bf16[2,1536,3072]{2,1,0:T(8,128)(2,1)} %w_ref.15), custom_call_target="tpu_custom_call" | custom-call | flops 603979776 | bytes 4718592 | tf_op jit(solution)/shard_map/pallas_call | solution.py:42
  157.9 1.8 shard_map.90.refs_3_
  159.8 1.9 shard_map.91.x_ref
  161.7 3.7 %shard_map.93 = bf16[128,1536]{1,0:T(8,128)(2,1)S(1)} custom-call(s32[1]{0:T(128)} %bitcast.2.half_ref, bf16[128,1536]{1,0:T(8,128)(2,1)S(1)} %shard_map.91.x_ref, bf16[2,1536,3072]{2,1,0:T(8,128)(2,1)} %w_ref.15), custom_call_target="tpu_custom_call" | custom-call | flops 603979776 | bytes 4718592 | tf_op jit(solution)/shard_map/pallas_call | solution.py:42
  165.4 3.6 %shard_map.97 = f32[128,1536]{1,0:T(8,128)S(1)} custom-call(s32[1]{0:T(128)} %bitcast.half_ref, bf16[128,1536]{1,0:T(8,128)(2,1)S(1)} %shard_map.96.x_ref, bf16[2,1536,3072]{2,1,0:T(8,128)(2,1)} %w_ref.15), custom_call_target="tpu_custom_call" | custom-call | flops 603979776 | bytes 4718592 | tf_op jit(solution)/shard_map/pallas_call | solution.py:42
  169.1 3.7 %shard_map.92 = f32[128,1536]{1,0:T(8,128)S(1)} custom-call(s32[1]{0:T(128)} %bitcast.half_ref, bf16[128,1536]{1,0:T(8,128)(2,1)S(1)} %shard_map.91.x_ref, bf16[2,1536,3072]{2,1,0:T(8,128)(2,1)} %w_ref.15), custom_call_target="tpu_custom_call" | custom-call | flops 603979776 | bytes 4718592 | tf_op jit(solution)/shard_map/pallas_call | solution.py:42
  172.9 1.6 collective-permute-start.27
  175.1 9.7 %collective-permute-done.27 = bf16[128,1536]{1,0:T(8,128)(2,1)S(1)} collective-permute-done((bf16[128,1536]{1,0:T(8,128)(2,1)S(1)}, bf16[128,1536]{1,0:T(8,128)(2,1)S(1)}, u32[]{:S(2)}, u32[]{:S(2)}) %collective-permute-start.27) | collective-permute-done | bytes 393248 | tf_op jit(solution)/shard_map/ppermute | solution.py:179
  185.2 7.6 %collective-permute-done.23 = bf16[128,1536]{1,0:T(8,128)(2,1)S(1)} collective-permute-done((bf16[128,1536]{1,0:T(8,128)(2,1)S(1)}, bf16[128,1536]{1,0:T(8,128)(2,1)S(1)}, u32[]{:S(2)}, u32[]{:S(2)}) %collective-permute-start.23) | collective-permute-done | bytes 393248 | tf_op jit(solution)/shard_map/ppermute | solution.py:179
  193.3 7.0 %shard_map.99 = bf16[128,1536]{1,0:T(8,128)(2,1)S(1)} custom-call(s32[1]{0:T(128)} %bitcast.half_ref, bf16[128,1536]{1,0:T(8,128)(2,1)S(1)} %subtract_convert_fusion.a_ref, bf16[128,1536]{1,0:T(8,128)(2,1)S(1)} %collective-permute-done.28.b_ref, bf16[2,1536,3072]{2,1,0:T(8,128)(2,1)} %wb_ref.7, bf16[2,1536,3072]{2,1,0:T(8,128)(2,1)} %wb_ref.7), custom_call_target="tpu_custom_call" | custom-call | flops 1207959552 | bytes 9437184 | tf_op jit(solution)/shard_map/pallas_call | solution.py:69
  200.3 1.6 collective-permute-start.29
  202.8 7.0 %shard_map.94 = bf16[128,1536]{1,0:T(8,128)(2,1)S(1)} custom-call(s32[1]{0:T(128)} %bitcast.half_ref, bf16[128,1536]{1,0:T(8,128)(2,1)S(1)} %subtract_convert_fusion.1.a_ref, bf16[128,1536]{1,0:T(8,128)(2,1)S(1)} %collective-permute-done.24.b_ref, bf16[2,1536,3072]{2,1,0:T(8,128)(2,1)} %wb_ref.7, bf16[2,1536,3072]{2,1,0:T(8,128)(2,1)} %wb_ref.7), custom_call_target="tpu_custom_call" | custom-call | flops 1207959552 | bytes 9437184 | tf_op jit(solution)/shard_map/pallas_call | solution.py:69
  212.0 9.1 %collective-permute-done.25 = bf16[128,1536]{1,0:T(8,128)(2,1)S(1)} collective-permute-done((bf16[128,1536]{1,0:T(8,128)(2,1)S(1)}, bf16[128,1536]{1,0:T(8,128)(2,1)S(1)}, u32[]{:S(2)}, u32[]{:S(2)}) %collective-permute-start.25) | collective-permute-done | bytes 393248 | tf_op jit(solution)/shard_map/ppermute | solution.py:179
  (86 shorter events, 19.2 us)
Async XLA Ops:
  5.5 11.6 %collective-permute-start = (bf16[128,1536]{1,0:T(8,128)(2,1)S(1)}, bf16[128,1536]{1,0:T(8,128)(2,1)S(1)}, u32[]{:S(2)}, u32[]{:S(2)}) collective-permute-start(bf16[128,1536]{1,0:T(8,128)(2,1)S(1)} %shard_map.78), channel_id=1, source_target_pairs={{0,2},{2,0},{4,6},{6,4},{1,3},{3,1},{5,7},{7,5},{8,10},{10,8},{12,... | collective-permute-start | bytes 1179656 | tf_op jit(solution)/shard_map/ppermute | solution.py:179
  9.6 10.6 %collective-permute-start.2 = (bf16[128,1536]{1,0:T(8,128)(2,1)S(1)}, bf16[128,1536]{1,0:T(8,128)(2,1)S(1)}, u32[]{:S(2)}, u32[]{:S(2)}) collective-permute-start(bf16[128,1536]{1,0:T(8,128)(2,1)S(1)} %shard_map.80), channel_id=1, source_target_pairs={{0,2},{2,0},{4,6},{6,4},{1,3},{3,1},{5,7},{7,5},{8,10},{10,8},{12,... | collective-permute-start | bytes 1179656 | tf_op jit(solution)/shard_map/ppermute | solution.py:179
  17.2 12.9 %collective-permute-start.1 = (bf16[128,1536]{1,0:T(8,128)(2,1)S(1)}, bf16[128,1536]{1,0:T(8,128)(2,1)S(1)}, u32[]{:S(2)}, u32[]{:S(2)}) collective-permute-start(bf16[128,1536]{1,0:T(8,128)(2,1)S(1)} %fusion), channel_id=1, source_target_pairs={{0,4},{2,6},{4,0},{6,2},{1,5},{3,7},{5,1},{7,3},{8,12},{10,14},{12... | collective-permute-start | bytes 1179656 | tf_op jit(solution)/shard_map/ppermute | solution.py:179
  20.2 17.7 %copy-start.1 = (bf16[128,1536]{1,0:T(8,128)(2,1)}, bf16[128,1536]{1,0:T(8,128)(2,1)S(1)}, u32[]{:S(2)}) copy-start(bf16[128,1536]{1,0:T(8,128)(2,1)S(1)} %collective-permute-done.2) | copy-start | bytes 1179652
  20.3 17.7 %collective-permute-start.3 = (bf16[128,1536]{1,0:T(8,128)(2,1)S(1)}, bf16[128,1536]{1,0:T(8,128)(2,1)S(1)}, u32[]{:S(2)}, u32[]{:S(2)}) collective-permute-start(bf16[128,1536]{1,0:T(8,128)(2,1)S(1)} %fusion.1), channel_id=1, source_target_pairs={{0,4},{2,6},{4,0},{6,2},{1,5},{3,7},{5,1},{7,3},{8,12},{10,14},{12... | collective-permute-start | bytes 1179656 | tf_op jit(solution)/shard_map/ppermute | solution.py:179
  30.1 7.9 %copy-start.3 = (bf16[128,1536]{1,0:T(8,128)(2,1)}, bf16[128,1536]{1,0:T(8,128)(2,1)S(1)}, u32[]{:S(2)}) copy-start(bf16[128,1536]{1,0:T(8,128)(2,1)S(1)} %collective-permute-done.1) | copy-start | bytes 1179652
  30.3 8.8 %collective-permute-start.5 = (bf16[128,1536]{1,0:T(8,128)(2,1)S(1)}, bf16[128,1536]{1,0:T(8,128)(2,1)S(1)}, u32[]{:S(2)}, u32[]{:S(2)}) collective-permute-start(bf16[128,1536]{1,0:T(8,128)(2,1)S(1)} %fusion.4.a_ref), channel_id=1, source_target_pairs={{0,2},{2,0},{4,6},{6,4},{1,3},{3,1},{5,7},{7,5},{8,10},{10,8},{12,... | collective-permute-start | bytes 1179656 | tf_op jit(solution)/shard_map/ppermute | solution.py:179
  37.9 8.1 %copy-start.5 = (bf16[128,1536]{1,0:T(8,128)(2,1)}, bf16[128,1536]{1,0:T(8,128)(2,1)S(1)}, u32[]{:S(2)}) copy-start(bf16[128,1536]{1,0:T(8,128)(2,1)S(1)} %collective-permute-done.3) | copy-start | bytes 1179652
  38.1 13.1 %collective-permute-start.4 = (bf16[128,1536]{1,0:T(8,128)(2,1)S(1)}, bf16[128,1536]{1,0:T(8,128)(2,1)S(1)}, u32[]{:S(2)}, u32[]{:S(2)}) collective-permute-start(bf16[128,1536]{1,0:T(8,128)(2,1)S(1)} %fusion.5.a_ref), channel_id=1, source_target_pairs={{0,2},{2,0},{4,6},{6,4},{1,3},{3,1},{5,7},{7,5},{8,10},{10,8},{12,... | collective-permute-start | bytes 1179656 | tf_op jit(solution)/shard_map/ppermute | solution.py:179
  63.5 10.8 %collective-permute-start.6 = (bf16[2,128,1536]{2,1,0:T(8,128)(2,1)S(1)}, bf16[2,128,1536]{2,1,0:T(8,128)(2,1)S(1)}, u32[]{:S(2)}, u32[]{:S(2)}) collective-permute-start(bf16[2,128,1536]{2,1,0:T(8,128)(2,1)S(1)} %shard_map.86), channel_id=1, source_target_pairs={{0,2},{2,0},{4,6},{6,4},{1,3},{3,1},{5,7},{7,5},{8,10},{10,8},{12,... | collective-permute-start | bytes 2359304 | tf_op jit(solution)/shard_map/ppermute | solution.py:179
  75.3 11.4 %collective-permute-start.7 = (bf16[1,128,1536]{2,1,0:T(8,128)(2,1)}, bf16[1,128,1536]{2,1,0:T(8,128)(2,1)}, u32[]{:S(2)}, u32[]{:S(2)}) collective-permute-start(bf16[1,128,1536]{2,1,0:T(8,128)(2,1)} %slice.47), channel_id=1, source_target_pairs={{0,4},{2,6},{4,0},{6,2},{1,5},{3,7},{5,1},{7,3},{8,12},{10,14},{12... | collective-permute-start | bytes 1179656 | tf_op jit(solution)/shard_map/ppermute | solution.py:179
  88.7 4.8 %collective-permute-start.8 = (bf16[32,1536]{1,0:T(8,128)(2,1)S(1)}, bf16[32,1536]{1,0:T(8,128)(2,1)S(1)}, u32[]{:S(2)}, u32[]{:S(2)}) collective-permute-start(bf16[32,1536]{1,0:T(8,128)(2,1)S(1)} %get-tuple-element.8), channel_id=1, source_target_pairs={{0,8},{8,0},{16,24},{24,16},{1,9},{9,1},{17,25},{25,17},{2,10},{10... | collective-permute-start | bytes 294920 | tf_op jit(solution)/shard_map/ppermute | solution.py:179
  90.6 7.5 %collective-permute-start.10 = (bf16[32,1536]{1,0:T(8,128)(2,1)S(1)}, bf16[32,1536]{1,0:T(8,128)(2,1)S(1)}, u32[]{:S(2)}, u32[]{:S(2)}) collective-permute-start(bf16[32,1536]{1,0:T(8,128)(2,1)S(1)} %get-tuple-element.9), channel_id=1, source_target_pairs={{0,24},{8,16},{16,8},{24,0},{1,25},{9,17},{17,9},{25,1},{2,26},{10... | collective-permute-start | bytes 294920 | tf_op jit(solution)/shard_map/ppermute | solution.py:179
  93.0 8.3 %collective-permute-start.9 = (bf16[32,1536]{1,0:T(8,128)(2,1)S(1)}, bf16[32,1536]{1,0:T(8,128)(2,1)S(1)}, u32[]{:S(2)}, u32[]{:S(2)}) collective-permute-start(bf16[32,1536]{1,0:T(8,128)(2,1)S(1)} %get-tuple-element.10), channel_id=1, source_target_pairs={{0,16},{8,24},{16,0},{24,8},{1,17},{9,25},{17,1},{25,9},{2,18},{10... | collective-permute-start | bytes 294920 | tf_op jit(solution)/shard_map/ppermute | solution.py:179
  102.3 4.7 %collective-permute-start.11 = (bf16[32,1536]{1,0:T(8,128)(2,1)S(1)}, bf16[32,1536]{1,0:T(8,128)(2,1)S(1)}, u32[]{:S(2)}, u32[]{:S(2)}) collective-permute-start(bf16[32,1536]{1,0:T(8,128)(2,1)S(1)} %fusion.8), channel_id=1, source_target_pairs={{0,1},{1,0},{2,3},{3,2},{4,5},{5,4},{6,7},{7,6},{8,9},{9,8},{10,11... | collective-permute-start | bytes 294920 | tf_op jit(solution)/shard_map/ppermute | solution.py:179
  107.9 3.7 %copy-start = (bf16[1536,3072]{1,0:T(8,128)(2,1)S(1)}, bf16[1536,3072]{1,0:T(8,128)(2,1)}, u32[]{:S(2)}) copy-start(bf16[1536,3072]{1,0:T(8,128)(2,1)} %param.11) | copy-start | bytes 28311556
  111.6 9.8 %slice-start = ((s8[9437184]{0:T(1024)(128)(4,1)}), s8[4194304]{0:T(1024)(128)(4,1)S(1)}, s32[]{:S(2)}) async-start(s8[9437184]{0:T(1024)(128)(4,1)} %bitcast.31), calls=%async_computation | async-start | bytes 8388608
  111.6 9.8 %slice-start.1 = ((s8[9437184]{0:T(1024)(128)(4,1)}), s8[4194304]{0:T(1024)(128)(4,1)S(1)}, s32[]{:S(2)}) async-start(s8[9437184]{0:T(1024)(128)(4,1)} %bitcast.31), calls=%async_computation.1 | async-start | bytes 8388608
  113.1 8.3 %slice-start.2 = ((s8[9437184]{0:T(1024)(128)(4,1)}), s8[1048576]{0:T(1024)(128)(4,1)S(1)}, s32[]{:S(2)}) async-start(s8[9437184]{0:T(1024)(128)(4,1)} %bitcast.31), calls=%async_computation.2 | async-start | bytes 2097152
  113.1 1.6 collective-permute-start.12
  114.7 5.2 %collective-permute-start.13 = (bf16[32,1536]{1,0:T(8,128)(2,1)S(1)}, bf16[32,1536]{1,0:T(8,128)(2,1)S(1)}, u32[]{:S(2)}, u32[]{:S(2)}) collective-permute-start(bf16[32,1536]{1,0:T(8,128)(2,1)S(1)} %fusion.9), channel_id=1, source_target_pairs={{0,4},{2,6},{4,0},{6,2},{1,5},{3,7},{5,1},{7,3},{8,12},{10,14},{12... | collective-permute-start | bytes 294920 | tf_op jit(solution)/shard_map/ppermute | solution.py:179
  120.0 1.4 collective-permute-start.14
  125.6 4.9 %collective-permute-start.15 = (bf16[32,1536]{1,0:T(8,128)(2,1)S(1)}, bf16[32,1536]{1,0:T(8,128)(2,1)S(1)}, u32[]{:S(2)}, u32[]{:S(2)}) collective-permute-start(bf16[32,1536]{1,0:T(8,128)(2,1)S(1)} %shard_map.89), channel_id=1, source_target_pairs={{0,1},{1,0},{2,3},{3,2},{4,5},{5,4},{6,7},{7,6},{8,9},{9,8},{10,11... | collective-permute-start | bytes 294920 | tf_op jit(solution)/shard_map/ppermute | solution.py:179
  130.6 5.4 %collective-permute-start.16 = (bf16[32,1536]{1,0:T(8,128)(2,1)S(1)}, bf16[32,1536]{1,0:T(8,128)(2,1)S(1)}, u32[]{:S(2)}, u32[]{:S(2)}) collective-permute-start(bf16[32,1536]{1,0:T(8,128)(2,1)S(1)} %get-tuple-element.3), channel_id=1, source_target_pairs={{0,8},{8,0},{16,24},{24,16},{1,9},{9,1},{17,25},{25,17},{2,10},{10... | collective-permute-start | bytes 294920 | tf_op jit(solution)/shard_map/ppermute | solution.py:179
  130.7 10.4 %collective-permute-start.17 = (bf16[32,1536]{1,0:T(8,128)(2,1)S(1)}, bf16[32,1536]{1,0:T(8,128)(2,1)S(1)}, u32[]{:S(2)}, u32[]{:S(2)}) collective-permute-start(bf16[32,1536]{1,0:T(8,128)(2,1)S(1)} %get-tuple-element.3), channel_id=1, source_target_pairs={{0,16},{8,24},{16,0},{24,8},{1,17},{9,25},{17,1},{25,9},{2,18},{10... | collective-permute-start | bytes 294920 | tf_op jit(solution)/shard_map/ppermute | solution.py:179
  133.9 7.3 %collective-permute-start.18 = (bf16[32,1536]{1,0:T(8,128)(2,1)S(1)}, bf16[32,1536]{1,0:T(8,128)(2,1)S(1)}, u32[]{:S(2)}, u32[]{:S(2)}) collective-permute-start(bf16[32,1536]{1,0:T(8,128)(2,1)S(1)} %get-tuple-element.3), channel_id=1, source_target_pairs={{0,24},{8,16},{16,8},{24,0},{1,25},{9,17},{17,9},{25,1},{2,26},{10... | collective-permute-start | bytes 294920 | tf_op jit(solution)/shard_map/ppermute | solution.py:179
  141.2 8.6 %collective-permute-start.19 = (bf16[1,128,1536]{2,1,0:T(8,128)(2,1)S(1)}, bf16[1,128,1536]{2,1,0:T(8,128)(2,1)S(1)}, u32[]{:S(2)}, u32[]{:S(2)}) collective-permute-start(bf16[1,128,1536]{2,1,0:T(8,128)(2,1)S(1)} %bitcast.39), channel_id=1, source_target_pairs={{0,4},{2,6},{4,0},{6,2},{1,5},{3,7},{5,1},{7,3},{8,12},{10,14},{12... | collective-permute-start | bytes 1179656 | tf_op jit(solution)/shard_map/ppermute | solution.py:179
  142.7 7.1 %collective-permute-start.21 = (bf16[1,128,1536]{2,1,0:T(8,128)(2,1)S(1)}, bf16[1,128,1536]{2,1,0:T(8,128)(2,1)S(1)}, u32[]{:S(2)}, u32[]{:S(2)}) collective-permute-start(bf16[1,128,1536]{2,1,0:T(8,128)(2,1)S(1)} %bitcast.40), channel_id=1, source_target_pairs={{0,2},{2,0},{4,6},{6,4},{1,3},{3,1},{5,7},{7,5},{8,10},{10,8},{12,... | collective-permute-start | bytes 1179656 | tf_op jit(solution)/shard_map/ppermute | solution.py:179
  149.8 2.0 collective-permute-start.20
  157.4 15.4 %collective-permute-start.26 = (bf16[128,1536]{1,0:T(8,128)(2,1)S(1)}, bf16[128,1536]{1,0:T(8,128)(2,1)S(1)}, u32[]{:S(2)}, u32[]{:S(2)}) collective-permute-start(bf16[128,1536]{1,0:T(8,128)(2,1)S(1)} %shard_map.98), channel_id=1, source_target_pairs={{0,2},{2,0},{4,6},{6,4},{1,3},{3,1},{5,7},{7,5},{8,10},{10,8},{12,... | collective-permute-start | bytes 1179656 | tf_op jit(solution)/shard_map/ppermute | solution.py:179
  165.3 9.1 %collective-permute-start.22 = (bf16[128,1536]{1,0:T(8,128)(2,1)S(1)}, bf16[128,1536]{1,0:T(8,128)(2,1)S(1)}, u32[]{:S(2)}, u32[]{:S(2)}) collective-permute-start(bf16[128,1536]{1,0:T(8,128)(2,1)S(1)} %shard_map.93), channel_id=1, source_target_pairs={{0,2},{2,0},{4,6},{6,4},{1,3},{3,1},{5,7},{7,5},{8,10},{10,8},{12,... | collective-permute-start | bytes 1179656 | tf_op jit(solution)/shard_map/ppermute | solution.py:179
  172.8 12.1 %copy-start.2 = (bf16[128,1536]{1,0:T(8,128)(2,1)S(1)}, bf16[128,1536]{1,0:T(8,128)(2,1)}, u32[]{:S(2)}) copy-start(bf16[128,1536]{1,0:T(8,128)(2,1)} %copy-done.1) | copy-start | bytes 1179652
  172.8 12.1 %copy-start.6 = (bf16[128,1536]{1,0:T(8,128)(2,1)S(1)}, bf16[128,1536]{1,0:T(8,128)(2,1)}, u32[]{:S(2)}) copy-start(bf16[128,1536]{1,0:T(8,128)(2,1)} %copy-done.5) | copy-start | bytes 1179652
  172.9 12.0 %collective-permute-start.27 = (bf16[128,1536]{1,0:T(8,128)(2,1)S(1)}, bf16[128,1536]{1,0:T(8,128)(2,1)S(1)}, u32[]{:S(2)}, u32[]{:S(2)}) collective-permute-start(bf16[128,1536]{1,0:T(8,128)(2,1)S(1)} %fusion.3), channel_id=1, source_target_pairs={{0,4},{2,6},{4,0},{6,2},{1,5},{3,7},{5,1},{7,3},{8,12},{10,14},{12... | collective-permute-start | bytes 1179656 | tf_op jit(solution)/shard_map/ppermute | solution.py:179
  174.5 18.3 %copy-start.4 = (bf16[128,1536]{1,0:T(8,128)(2,1)S(1)}, bf16[128,1536]{1,0:T(8,128)(2,1)}, u32[]{:S(2)}) copy-start(bf16[128,1536]{1,0:T(8,128)(2,1)} %copy-done.3) | copy-start | bytes 1179652
  174.5 18.3 %collective-permute-start.23 = (bf16[128,1536]{1,0:T(8,128)(2,1)S(1)}, bf16[128,1536]{1,0:T(8,128)(2,1)S(1)}, u32[]{:S(2)}, u32[]{:S(2)}) collective-permute-start(bf16[128,1536]{1,0:T(8,128)(2,1)S(1)} %fusion.2), channel_id=1, source_target_pairs={{0,4},{2,6},{4,0},{6,2},{1,5},{3,7},{5,1},{7,3},{8,12},{10,14},{12... | collective-permute-start | bytes 1179656 | tf_op jit(solution)/shard_map/ppermute | solution.py:179
  185.2 8.1 %collective-permute-start.28 = (bf16[128,1536]{1,0:T(8,128)(2,1)S(1)}, bf16[128,1536]{1,0:T(8,128)(2,1)S(1)}, u32[]{:S(2)}, u32[]{:S(2)}) collective-permute-start(bf16[128,1536]{1,0:T(8,128)(2,1)S(1)} %subtract_convert_fusion.a_ref), channel_id=1, source_target_pairs={{0,2},{2,0},{4,6},{6,4},{1,3},{3,1},{5,7},{7,5},{8,10},{10,8},{12,... | collective-permute-start | bytes 1179656 | tf_op jit(solution)/shard_map/ppermute | solution.py:179
  193.2 9.6 %collective-permute-start.24 = (bf16[128,1536]{1,0:T(8,128)(2,1)S(1)}, bf16[128,1536]{1,0:T(8,128)(2,1)S(1)}, u32[]{:S(2)}, u32[]{:S(2)}) collective-permute-start(bf16[128,1536]{1,0:T(8,128)(2,1)S(1)} %subtract_convert_fusion.1.a_ref), channel_id=1, source_target_pairs={{0,2},{2,0},{4,6},{6,4},{1,3},{3,1},{5,7},{7,5},{8,10},{10,8},{12,... | collective-permute-start | bytes 1179656 | tf_op jit(solution)/shard_map/ppermute | solution.py:179
  200.3 11.6 %collective-permute-start.29 = (bf16[128,1536]{1,0:T(8,128)(2,1)S(1)}, bf16[128,1536]{1,0:T(8,128)(2,1)S(1)}, u32[]{:S(2)}, u32[]{:S(2)}) collective-permute-start(bf16[128,1536]{1,0:T(8,128)(2,1)S(1)} %shard_map.99), channel_id=1, source_target_pairs={{0,1},{1,0},{2,3},{3,2},{4,5},{5,4},{6,7},{7,6},{8,9},{9,8},{10,11... | collective-permute-start | bytes 1179656 | tf_op jit(solution)/shard_map/ppermute | solution.py:179
  209.8 11.3 %collective-permute-start.25 = (bf16[128,1536]{1,0:T(8,128)(2,1)S(1)}, bf16[128,1536]{1,0:T(8,128)(2,1)S(1)}, u32[]{:S(2)}, u32[]{:S(2)}) collective-permute-start(bf16[128,1536]{1,0:T(8,128)(2,1)S(1)} %shard_map.94), channel_id=1, source_target_pairs={{0,1},{1,0},{2,3},{3,2},{4,5},{5,4},{6,7},{7,6},{8,9},{9,8},{10,11... | collective-permute-start | bytes 1179656 | tf_op jit(solution)/shard_map/ppermute | solution.py:179

commit v2 on v1

v2 whole, which is shorter than its diff:
```python
import functools

import jax
import jax.numpy as jnp
from jax import lax
from jax.experimental import pallas as pl
from jax.experimental.pallas import tpu as pltpu
from jax.sharding import PartitionSpec as P

BF16 = jnp.bfloat16
F32 = jnp.float32
I16 = jnp.int16
NN = (((1,), (0,)), ((), ()))
NT = (((1,), (1,)), ((), ()))
LANES = 128
ANY = pl.BlockSpec(memory_space=pl.ANY)


def tile_of(extent, *sizes):
    for size in sizes:
        if extent % size == 0:
            return size
    return extent


def params():
    return pltpu.CompilerParams(vmem_limit_bytes=20 * 1024 * 1024)


def cost(flops, nbytes):
    return pl.CostEstimate(flops=flops // 64, bytes_accessed=nbytes // 64, transcendentals=0)


def in_hbm(w):
    return pltpu.with_memory_space_constraint(w, pltpu.HBM)


def nn_kernel(steps, parts, half_ref, x_ref, w_ref, *rest):
    outs = rest[-len(parts):]
    x = x_ref[0] if len(x_ref.shape) == 3 else x_ref[...]
    product = lax.dot_general(x, w_ref[0], NN, preferred_element_type=F32)
    if len(parts) == 1:
        outs[0][...] = product.astype(outs[0].dtype)
        return
    for at, out in enumerate(outs):

        @pl.when(pl.program_id(0) // steps == at)
        def _(out=out):
            out[...] = product.astype(out.dtype)


def nn(x, w, child, core, parts, after=()):
    m, k = x.shape[-2:]
    n_half = w.shape[2] // 2
    bn = tile_of(n_half, 768, 512, 384, 256, 128)
    steps = n_half // bn
    count = len(parts)

    def w_at(i, h):
        part = i // steps
        which = (parts[0] + part * (parts[-1] - parts[0])) if count == 2 else parts[0]
        return (child, 0, lax.bitwise_xor(h[0], which) * steps + lax.rem(i, steps))

    def out_at(at):
        return lambda i, h: (0, jnp.clip(i - at * steps, 0, steps - 1))

    if x.ndim == 3:
        x_spec = pl.BlockSpec((1, m, k), lambda i, h: (child, 0, 0))
    else:
        x_spec = pl.BlockSpec((m, k), lambda i, h: (0, 0))
    outs = pl.pallas_call(
        functools.partial(nn_kernel, steps, parts),
        grid_spec=pltpu.PrefetchScalarGridSpec(
            num_scalar_prefetch=1,
            grid=(count * steps,),
            in_specs=[x_spec, pl.BlockSpec((1, k, bn), w_at)] + [ANY] * len(after),
            out_specs=[pl.BlockSpec((m, bn), out_at(at)) for at in range(count)],
        ),
        out_shape=[jax.ShapeDtypeStruct((m, n_half), BF16 if p else F32) for p in parts],
        compiler_params=params(),
        cost_estimate=cost(2 * m * k * n_half * count, 2 * k * n_half * count),
    )(core, x, in_hbm(w), *after)
    return outs


def nt_kernel(half_ref, a_ref, b_ref, wa_ref, wb_ref, *rest):
    o_ref = rest[-1]
    total = lax.dot_general(a_ref[...], wa_ref[0], NT, preferred_element_type=F32)
    total += lax.dot_general(b_ref[...], wb_ref[0], NT, preferred_element_type=F32)
    o_ref[...] = total.astype(o_ref.dtype)


def nt(mine, other, w, child, core, chunk=0, chunks=1, after=()):
    m, k_half = mine.shape
    u = w.shape[1] // chunks
    bu = tile_of(u, 512, 384, 256, 128)
    first = chunk * (u // bu)
    return pl.pallas_call(
        nt_kernel,
        grid_spec=pltpu.PrefetchScalarGridSpec(
            num_scalar_prefetch=1,
            grid=(u // bu,),
            in_specs=[
                pl.BlockSpec((m, k_half), lambda i, h: (0, 0)),
                pl.BlockSpec((m, k_half), lambda i, h: (0, 0)),
                pl.BlockSpec((1, bu, k_half), lambda i, h: (child, first + i, h[0])),
                pl.BlockSpec((1, bu, k_half), lambda i, h: (child, first + i, 1 - h[0])),
            ]
            + [ANY] * len(after),
            out_specs=pl.BlockSpec((m, bu), lambda i, h: (0, i)),
        ),
        out_shape=jax.ShapeDtypeStruct((m, u), BF16),
        compiler_params=params(),
        cost_estimate=cost(4 * m * k_half * u, 4 * k_half * u),
    )(core, mine, other, in_hbm(w), in_hbm(w), *after)


def spread_kernel(map_ref, o_ref):
    u = map_ref.shape[2]
    step = tile_of(u, LANES)
    for start in range(0, u, step):
        row = map_ref[0, :, start : start + step]
        o_ref[0, start : start + step, :] = jnp.broadcast_to(row, (LANES, step)).T.astype(I16)


def spread(maps):
    kids, _, u = maps.shape
    return pl.pallas_call(
        spread_kernel,
        grid=(kids,),
        in_specs=[pl.BlockSpec((1, 1, u), lambda k: (k, 0, 0))],
        out_specs=pl.BlockSpec((1, u, LANES), lambda k: (k, 0, 0)),
        out_shape=jax.ShapeDtypeStruct((kids, u, LANES), I16),
        compiler_params=params(),
        cost_estimate=cost(kids * u * LANES, 2 * kids * u * LANES),
    )(maps)


def store_in_order(order_ref, chunk, store, value):
    for i in range(value.shape[0] // chunk):
        store(
            pl.ds(pl.multiple_of(order_ref[i] * chunk, chunk), chunk),
            value[i * chunk : (i + 1) * chunk],
        )


def scatter_kernel(block_rows, tile, odd, chunk, *refs):
    row_ref, order_ref, map_ref, upd_ref, *rest = refs
    o_ref = rest[-1]
    j, t = pl.program_id(0), pl.program_id(1)
    dest = lax.bitwise_xor(row_ref[0], 2 * j + odd)
    first = (dest * block_rows + t * tile).astype(I16)
    local = map_ref[0] - first
    u = local.shape[0]
    sub = tile_of(tile, 256, 128)
    upd = upd_ref[...]
    for start in range(0, tile, sub):
        wide = jnp.concatenate([local] * (sub // LANES), axis=1)
        row_ids = lax.broadcasted_iota(I16, (u, sub), 1) + jnp.int16(start)
        hot = jnp.where(row_ids == wide, BF16(1), BF16(0))
        total = lax.dot_general(upd, hot, NN, preferred_element_type=F32)
        if len(rest) == 2:
            at = slice(start, start + sub)
            before = rest[0]

            def store(ds, value, at=at, before=before):
                o_ref[0, ds, at] = (value + before[0, ds, at].astype(F32)).astype(o_ref.dtype)

        else:
            at = slice(start, start + sub)

            def store(ds, value, at=at):
                o_ref[0, ds, at] = value.astype(o_ref.dtype)

        store_in_order(order_ref, chunk, store, total)


def scatter(upd, spread_maps, child, row, order, rows_count, block_rows, odd, before):
    m, u = upd.shape
    tile = tile_of(block_rows, 768, 512, 384, 256, 128)
    count = rows_count // 2
    chunk = m // order.shape[0]
    block = pl.BlockSpec((1, m, tile), lambda j, t, r, o: (j, 0, t))
    in_specs = [
        pl.BlockSpec((1, u, LANES), lambda j, t, r, o: (child, 0, 0)),
        pl.BlockSpec((m, u), lambda j, t, r, o: (0, 0)),
    ]
    args = [spread_maps, upd]
    if before is not None:
        in_specs.append(block)
        args.append(before)
    return pl.pallas_call(
        functools.partial(scatter_kernel, block_rows, tile, odd, chunk),
        grid_spec=pltpu.PrefetchScalarGridSpec(
            num_scalar_prefetch=2,
            grid=(count, block_rows // tile),
            in_specs=in_specs,
            out_specs=block,
        ),
        out_shape=jax.ShapeDtypeStruct((count, m, block_rows), BF16),
        compiler_params=params(),
        cost_estimate=cost(2 * m * u * count * block_rows, 4 * m * count * block_rows),
    )(row, order, *args)


def gather_kernel(block_rows, tile, which, chunk, *refs):
    row_ref, order_ref, map_ref, *rest = refs
    blocks, o_ref = rest[: len(which)], rest[-1]
    slot_map = map_ref[0]
    total = None
    for block_ref, j in zip(blocks, which):
        first = lax.bitwise_xor(row_ref[0], j) * block_rows
        for start in range(0, block_rows, tile):
            local = (slot_map - (first + start)).astype(I16)
            row_ids = lax.broadcasted_iota(I16, (tile, slot_map.shape[1]), 0)
            hot = jnp.where(row_ids == local, BF16(1), BF16(0))
            term = lax.dot_general(
                block_ref[:, start : start + tile], hot, NN, preferred_element_type=F32
            )
            total = term if total is None else total + term
    before = rest[len(which)] if len(rest) == len(which) + 2 else None

    def store(ds, value):
        if before is not None:
            value = value + before[ds, :].astype(F32)
        o_ref[ds, :] = value.astype(o_ref.dtype)

    store_in_order(order_ref, chunk, store, total)


def gather(blocks, which, maps, child, row, order, before):
    m, block_rows = blocks[0].shape
    u = maps.shape[2]
    tile = tile_of(block_rows, 512, 384, 256, 128)
    bu = tile_of(u, 512, 384, 256, 128)
    chunk = m // order.shape[0]
    in_specs = [pl.BlockSpec((1, 1, bu), lambda i, r, o: (child, 0, i))]
    in_specs += [pl.BlockSpec((m, block_rows), lambda i, r, o: (0, 0))] * len(blocks)
    out_block = pl.BlockSpec((m, bu), lambda i, r, o: (0, i))
    args = [maps, *blocks]
    if before is not None:
        in_specs.append(out_block)
        args.append(before)
    return pl.pallas_call(
        functools.partial(gather_kernel, block_rows, tile, which, chunk),
        grid_spec=pltpu.PrefetchScalarGridSpec(
            num_scalar_prefetch=2, grid=(u // bu,), in_specs=in_specs, out_specs=out_block
        ),
        out_shape=jax.ShapeDtypeStruct((m, u), BF16),
        compiler_params=params(),
        cost_estimate=cost(
            2 * m * u * len(blocks) * block_rows, 2 * m * len(blocks) * block_rows
        ),
    )(row, order, *args)


def reorder_kernel(order_ref, x_ref, o_ref):
    o_ref[...] = x_ref[...].astype(o_ref.dtype)


def reorder(x, order):
    m, n = x.shape
    chunk = m // order.shape[0]
    return pl.pallas_call(
        reorder_kernel,
        grid_spec=pltpu.PrefetchScalarGridSpec(
            num_scalar_prefetch=1,
            grid=(order.shape[0],),
            in_specs=[pl.BlockSpec((chunk, n), lambda i, o: (i, 0))],
            out_specs=pl.BlockSpec((chunk, n), lambda i, o: (o[i], 0)),
        ),
        out_shape=jax.ShapeDtypeStruct((m, n), F32),
        compiler_params=params(),
        cost_estimate=cost(m * n, 6 * m * n),
    )(order, x)


def join_kernel(sign, *refs):
    x_ref, y_ref, *rest = refs
    wide_ref, narrow_ref = rest[-2:]
    total = x_ref[...].astype(F32) + sign * y_ref[...].astype(F32)
    wide_ref[...] = total
    narrow_ref[...] = total.astype(BF16)


def join(x, y, after=()):
    whole = pl.BlockSpec(x.shape, lambda: (0, 0))
    return pl.pallas_call(
        functools.partial(join_kernel, 1),
        in_specs=[whole, whole] + [ANY] * len(after),
        out_specs=[whole, whole],
        out_shape=[jax.ShapeDtypeStruct(x.shape, F32), jax.ShapeDtypeStruct(x.shape, BF16)],
        compiler_params=params(),
        cost_estimate=cost(x.size, 12 * x.size),
    )(x, y, *after)


def swap(x, axis, bit, size):
    return lax.ppermute(x, axis, [(i, i ^ bit) for i in range(size)])


def add(x, y):
    return x.astype(F32) + y.astype(F32)


def bits(size):
    return [1 << b for b in range(size.bit_length() - 1)]


def on_device(sizes, child_loads, child_inverse, child_panel, child_map, root_loads, root_inverse):
    leafs, rows, cols = sizes
    kids = child_loads.shape[0]
    case_count, root_rows = root_loads.shape
    leaf, row, col = (lax.axis_index(a).astype(jnp.int32) for a in ("leaf", "row", "col"))
    core = lax.bitwise_and(row, 1)[None]
    row_1 = row[None]
    root_w = root_inverse[None]
    piece = case_count // (leafs * cols)
    wide = rows == 4 and cols == 2 and piece % 16 == 0 and root_rows % 256 == 0

    def to_row(x, bit):
        return swap(x, "row", bit, rows)

    def to_col(x, bit=1):
        return swap(x, "col", bit, cols)

    def to_leaf(x, j):
        return swap(x, "leaf", j, leafs)

    def row_sum(x, w, child, split, after=()):
        if split:
            (sent,) = nn(x, w, child, core, (1,), after)
            (kept,) = nn(x, w, child, core, (0,), (sent,))
        else:
            sent, kept = nn(x, w, child, core, (1, 0), after)
        return join(kept, to_row(sent, 1))

    def row_end(total, narrow, after=()):
        for bit in bits(rows)[1:]:
            total, narrow = join(total, to_row(narrow, bit), after)
        return total, narrow

    def halves(rounded):
        return rounded, to_row(rounded, 1)

    slot_rows = child_panel.shape[1]
    own_map = lax.dynamic_slice_in_dim(child_map, row * slot_rows, slot_rows, 1)
    maps = own_map.reshape(kids, 1, slot_rows)
    spread_maps = spread(maps)

    if wide:
        ids = jnp.arange(cols * leafs, dtype=jnp.int32)
        order = lax.bitwise_xor(ids, col * leafs + leaf)
    else:
        order = jnp.zeros((1,), jnp.int32)

    begun = []
    after = ()
    for k in range(kids):
        begun.append(row_sum(child_loads, child_inverse, k, k == 0, after))
        after = begun[k][1:]
    forward = []
    sent = kept = None
    for k in range(kids):
        total, rounded = row_end(*begun[k], after if k == 0 else (sent, kept))
        forward.append(total)
        upd = nt(*halves(rounded), child_panel, k, core)
        sent = scatter(upd, spread_maps, k, row_1, order, rows, root_rows, 1, sent)
        kept = scatter(upd, spread_maps, k, row_1, order, rows, root_rows, 0, kept)

    total = add(kept, to_row(sent, 1))
    if wide:
        half, cut = case_count // 2, root_rows // 2
        left = add(total[:, :half, :cut], to_col(total[:, half:, :cut].astype(BF16)))
        right = add(total[0, :, cut:], to_row(total[1, :, cut:].astype(BF16), 2))
        left = add(left[0], to_row(left[1].astype(BF16), 2))
        right = add(right[:half], to_col(right[half:].astype(BF16)))
        total = jnp.concatenate([left, right], axis=1)
        narrow = total.astype(BF16)
        mine_cases = total[:piece]
        for j in range(1, leafs):
            away = narrow[j * piece : (j + 1) * piece]
            mine_cases = add(mine_cases, to_leaf(away, j))
        first_case = (col * leafs + leaf) * piece
        loads = lax.dynamic_slice_in_dim(root_loads, first_case, piece, 0)
        residual = (loads.astype(F32) - mine_cases).astype(BF16)
        residual = jnp.concatenate([residual, to_col(residual)])
    else:
        for bit in bits(rows)[1:]:
            total = add(total[0::2], to_row(total[1::2].astype(BF16), bit))
        total = total[0]
        chunk = case_count // leafs

        def cases_of(x, j):
            return lax.dynamic_slice_in_dim(x, lax.bitwise_xor(leaf, j) * chunk, chunk, 0)

        narrow = total.astype(BF16)
        mine_cases = cases_of(total, 0)
        for j in range(1, leafs):
            mine_cases = add(mine_cases, to_leaf(cases_of(narrow, j), j))
        for bit in bits(cols):
            narrow = mine_cases.astype(BF16)
            mine_cases = add(narrow, to_col(narrow, bit))
        residual = (cases_of(root_loads, 0).astype(F32) - mine_cases).astype(BF16)

    _, root_forward = row_end(*row_sum(residual, root_w, 0, False))
    part = nt(*halves(root_forward), root_w, 0, core)

    picked = [None] * kids
    if wide:
        part = add(part[:piece], to_col(part[piece:])).astype(BF16)
        held = jnp.concatenate([part] + [to_leaf(part, j) for j in range(1, leafs)])
        beside, across = to_col(held), to_row(held, 2)
        near = jnp.concatenate([held, beside])
        near_other = to_row(near, 1)
        cut = held.shape[0] // 2
        far = jnp.concatenate([across, to_col(across[:cut]), to_row(beside[cut:], 2)])
        far_other = to_row(far, 1)
        root_solution = reorder(near, order)
        for k in range(kids):
            picked[k] = gather([near, near_other], [0, 1], maps, k, row_1, order, None)
        last_blocks, last_at = [far, far_other], [2, 3]
    else:
        for bit in bits(cols):
            part = add(part, to_col(part, bit)).astype(BF16)
        own = jnp.zeros((case_count, root_rows), BF16)
        for j in range(leafs):
            got = part if j == 0 else to_leaf(part, j)
            own = lax.dynamic_update_slice_in_dim(
                own, got, lax.bitwise_xor(leaf, j) * (case_count // leafs), 0
            )
        root_solution = own.astype(F32)
        groups = [own]
        for bit in [1, *bits(rows)[1:]]:
            got = to_row(jnp.stack(groups), bit)
            groups += [got[i] for i in range(len(groups))]
        last_blocks, last_at = groups, list(range(rows))

    begun = []
    after = ()
    for k in range(kids):
        full = gather(last_blocks, last_at, maps, k, row_1, order, picked[k])
        begun.append(row_sum(full, child_panel, k, k == 0, after))
        after = begun[k][1:]
    solved = []
    for k in range(kids):
        back, _ = row_end(*begun[k], after)
        pair = halves((forward[k] - back).astype(BF16))
        chunks = 2 if k == kids - 1 and slot_rows % 256 == 0 else 1
        outs = []
        for at in range(chunks):
            out = nt(*pair, child_inverse, k, core, at, chunks)
            after = (out,)
            for bit in bits(cols):
                out = add(out.astype(BF16), to_col(out.astype(BF16), bit))
            outs.append(out)
        solved.append(jnp.concatenate(outs, axis=1) if chunks > 1 else outs[0])
    return (jnp.stack(solved), root_solution)


def solution(mesh):
    sizes = tuple(mesh.shape[a] for a in ("leaf", "row", "col"))
    in_specs = (
        P("leaf", None, "row"),
        P("leaf", "row", "col"),
        P("leaf", "row", "col"),
        P("leaf", None),
        P(None, "row"),
        P("row", "col"),
    )
    out_specs = (P("leaf", None, "row"), P(None, "row"))
    return jax.shard_map(
        functools.partial(on_device, sizes),
        mesh=mesh,
        in_specs=in_specs,
        out_specs=out_specs,
        check_vma=False,
    )
```

time: 223 us -> 197 us (0.88)
  waiting for transfers between devices: 87.7 us -> 70.5 us
  starting transfers between devices: 26.6 us -> 32.8 us
  Pallas kernels: 92.6 us -> 87.2 us
  other arithmetic: 7.77 us -> 3.04 us
  local copies, waits for them, and re-layouts: 6.68 us -> 2.31 us
    ppermute x30 -> x37, waiting for transfers between devices: 87.7 us -> 70.5 us  [swap(): return lax.ppermute(x, axis, [(i, i ^ bit) for i in range(size)])]
    ppermute x30 -> x37, starting transfers between devices: 26.6 us -> 32.8 us  [swap(): return lax.ppermute(x, axis, [(i, i ^ bit) for i in range(size)])]
    pallas_call x18 -> x27, Pallas kernels: 60.2 us -> 56.4 us  [the longest x7 28.1 us: nn(): pl.pallas_call(functools.partial(nn_kernel, steps, parts), grid_spec=pltp...]
    convert_element_type x13 -> x3, other arithmetic: 4.02 us -> 1.01 us  [the longest x1 0.83 us: on_device(): residual = (loads.astype(F32) - mine_cases).astype(BF16)]
    pallas_call x5 -> x6, Pallas kernels: 32.4 us -> 30.8 us  [nt(): pl.pallas_call(nt_kernel, grid_spec=pltpu.PrefetchScalarGridSpec(num_scal...]
  transfers between devices with their start and end apart: 30 -> 37, of which waited for: 17 -> 24; matrix products, arithmetic and copies ran while one was open for 1% -> 0% of each run, Pallas kernels for 29% -> 22%
where the time goes in v2:
time: 197 us
  Pallas kernels  87.2 us (44%)
  waiting for transfers between devices  70.5 us (36%)
  starting transfers between devices  32.8 us (17%)
  other arithmetic  3.04 us (2%)
  local copies, waits for them, and re-layouts  2.31 us (1%)
    ppermute x37, waiting for transfers between devices, swap(): return lax.ppermute(x, axis, [(i, i ^ bit) for i in range(size)])  70.5 us
    ppermute x37, starting transfers between devices, swap(): return lax.ppermute(x, axis, [(i, i ^ bit) for i in range(size)])  32.8 us
    pallas_call x6, Pallas kernels, nt(): pl.pallas_call(nt_kernel, grid_spec=pltpu.PrefetchScalarGridSpec(num_scal...  30.8 us
    pallas_call x7, Pallas kernels, nn(): pl.pallas_call(functools.partial(nn_kernel, steps, parts), grid_spec=pltp...  28.1 us
    pallas_call x4, Pallas kernels, scatter(): pl.pallas_call(functools.partial(scatter_kernel, block_rows, tile, odd, c...  10.8 us
    pallas_call x4, Pallas kernels, gather(): pl.pallas_call(functools.partial(gather_kernel, block_rows, tile, which,...  9.65 us
    pallas_call x10, Pallas kernels, join(): pl.pallas_call(functools.partial(join_kernel, 1), in_specs=[whole, whole]...  4.06 us
  transfers between devices with their start and end apart: 37, of which 24 were waited for; matrix products, arithmetic and copies ran while one was open for 0% of the time, Pallas kernels for 22%

profile of v2, /device:TPU:0, one launch (start us, length us, event | category | flops | bytes accessed | tf_op | source)
XLA Modules:
  0.0 197.0 jit_solution(7609436974481422751)
XLA Ops:
  1.8 2.9 %shard_map.77.rest_0_ = bf16[128,1536]{1,0:T(8,128)(2,1)S(1)} custom-call(s32[1]{0:T(128)} %bitcast.half_ref, bf16[2,128,1536]{2,1,0:T(8,128)(2,1)S(1)} %copy-done.2, bf16[2,1536,3072]{2,1,0:T(8,128)(2,1)} %wb_ref.9), custom_call_target="tpu_custom_call" | custom-call | flops 9437184 | bytes 73728 | tf_op jit(solution)/shard_map/pallas_call | solution.py:71
  5.2 2.9 %shard_map.78.refs_0_ = f32[128,1536]{1,0:T(8,128)S(1)} custom-call(s32[1]{0:T(128)} %bitcast.half_ref, bf16[2,128,1536]{2,1,0:T(8,128)(2,1)S(1)} %copy-done.2, bf16[2,1536,3072]{2,1,0:T(8,128)(2,1)} %wb_ref.9, bf16[128,1536]{1,0:T(8,128)(2,1)S(1)} %shard_map.77.rest_0_), custom_call_target="tpu_custom_call" | custom-call | flops 9437184 | bytes 73728 | tf_op jit(solution)/shard_map/pallas_call | solution.py:71
  9.3 5.4 %shard_map.80 = (bf16[128,1536]{1,0:T(8,128)(2,1)S(1)}, f32[128,1536]{1,0:T(8,128)S(1)}) custom-call(s32[1]{0:T(128)} %bitcast.half_ref, bf16[2,128,1536]{2,1,0:T(8,128)(2,1)S(1)} %copy-done.3, bf16[2,1536,3072]{2,1,0:T(8,128)(2,1)} %wb_ref.9, bf16[128,1536]{1,0:T(8,128)(2,1)S(1)} %get-tuple-element.26.rest_0_), custom_call_target="tpu_custom_call" | custom-call | flops 18874368 | bytes 147456 | tf_op jit(solution)/shard_map/pallas_call | solution.py:71
  14.8 3.0 %collective-permute-start.1 = (bf16[128,1536]{1,0:T(8,128)(2,1)S(1)}, bf16[128,1536]{1,0:T(8,128)(2,1)S(1)}, u32[]{:S(2)}, u32[]{:S(2)}) collective-permute-start(bf16[128,1536]{1,0:T(8,128)(2,1)S(1)} %get-tuple-element.26.rest_0_), channel_id=1, source_target_pairs={{0,4},{2,6},{4,0},{6,2},{1,5},{3,7},{5,1},{7,3},{8,12},{10,14},{12... | collective-permute-start | bytes 1179656 | tf_op jit(solution)/shard_map/ppermute | solution.py:299
  17.9 9.2 %collective-permute-done.1.refs_1_ = bf16[128,1536]{1,0:T(8,128)(2,1)S(1)} collective-permute-done((bf16[128,1536]{1,0:T(8,128)(2,1)S(1)}, bf16[128,1536]{1,0:T(8,128)(2,1)S(1)}, u32[]{:S(2)}, u32[]{:S(2)}) %collective-permute-start.1) | collective-permute-done | bytes 393248 | tf_op jit(solution)/shard_map/ppermute | solution.py:299
  27.3 1.8 collective-permute-start.3
  29.8 6.1 %shard_map.84.refs_3_ = bf16[128,1536]{1,0:T(8,128)(2,1)S(1)} custom-call(s32[1]{0:T(128)} %bitcast.half_ref, bf16[128,1536]{1,0:T(8,128)(2,1)S(1)} %get-tuple-element.32.a_ref, bf16[128,1536]{1,0:T(8,128)(2,1)S(1)} %collective-permute-done.4.b_ref, bf16[2,1536,3072]{2,1,0:T(8,128)(2,1)} %w_ref.11, bf16[2,1536,3072]{2,1,0:T(8,128)(2,1)} %w_ref.11), custom_call_target="tpu_custom_call" | custom-call | flops 18874368 | bytes 147456 | tf_op jit(solution)/shard_map/pallas_call | solution.py:98
  35.9 2.7 %shard_map.86.refs_3_.refs_4_ = bf16[2,128,1536]{2,1,0:T(8,128)(2,1)S(1)} custom-call(s32[1]{0:T(128)} %bitcast.1.refs_0_, s32[8]{0:T(128)S(1)} %iota_xor_fusion.refs_1_.order_ref, s16[2,1536,128]{2,1,0:T(8,128)(2,1)S(1)} %shard_map.83.refs_2_, bf16[128,1536]{1,0:T(8,128)(2,1)S(1)} %shard_map.84.refs_3_), custom_call_target="tpu_custom_call" | custom-call | flops 18874368 | bytes 24576 | tf_op jit(solution)/shard_map/pallas_call | solution.py:192
  38.6 2.7 %shard_map.85.refs_2_.refs_4_ = bf16[2,128,1536]{2,1,0:T(8,128)(2,1)S(1)} custom-call(s32[1]{0:T(128)} %bitcast.1.refs_0_, s32[8]{0:T(128)S(1)} %iota_xor_fusion.refs_1_.order_ref, s16[2,1536,128]{2,1,0:T(8,128)(2,1)S(1)} %shard_map.83.refs_2_, bf16[128,1536]{1,0:T(8,128)(2,1)S(1)} %shard_map.84.refs_3_), custom_call_target="tpu_custom_call" | custom-call | flops 18874368 | bytes 24576 | tf_op jit(solution)/shard_map/pallas_call | solution.py:192
  42.6 1.5 collective-permute-done.5.b_ref
  44.1 6.1 %shard_map.88.refs_3_ = bf16[128,1536]{1,0:T(8,128)(2,1)S(1)} custom-call(s32[1]{0:T(128)} %bitcast.half_ref, bf16[128,1536]{1,0:T(8,128)(2,1)S(1)} %get-tuple-element.33.a_ref, bf16[128,1536]{1,0:T(8,128)(2,1)S(1)} %collective-permute-done.5.b_ref, bf16[2,1536,3072]{2,1,0:T(8,128)(2,1)} %w_ref.11, bf16[2,1536,3072]{2,1,0:T(8,128)(2,1)} %w_ref.11), custom_call_target="tpu_custom_call" | custom-call | flops 18874368 | bytes 147456 | tf_op jit(solution)/shard_map/pallas_call | solution.py:98
  50.2 2.8 %shard_map.90 = bf16[2,128,1536]{2,1,0:T(8,128)(2,1)S(1)} custom-call(s32[1]{0:T(128)} %bitcast.1.refs_0_, s32[8]{0:T(128)S(1)} %iota_xor_fusion.refs_1_.order_ref, s16[2,1536,128]{2,1,0:T(8,128)(2,1)S(1)} %shard_map.83.refs_2_, bf16[128,1536]{1,0:T(8,128)(2,1)S(1)} %shard_map.88.refs_3_, bf16[2,128,1536]{2,1,0:T(8,128)(2,1)S(1)} %shard_map.85.refs_2_.refs_4_), custom_call_target="tpu_custom_call" | custom-call | flops 18874368 | bytes 24576 | tf_op jit(solution)/shard_map/pallas_call | solution.py:192
  53.2 2.8 %shard_map.89 = bf16[2,128,1536]{2,1,0:T(8,128)(2,1)S(1)} custom-call(s32[1]{0:T(128)} %bitcast.1.refs_0_, s32[8]{0:T(128)S(1)} %iota_xor_fusion.refs_1_.order_ref, s16[2,1536,128]{2,1,0:T(8,128)(2,1)S(1)} %shard_map.83.refs_2_, bf16[128,1536]{1,0:T(8,128)(2,1)S(1)} %shard_map.88.refs_3_, bf16[2,128,1536]{2,1,0:T(8,128)(2,1)S(1)} %shard_map.86.refs_3_.refs_4_), custom_call_target="tpu_custom_call" | custom-call | flops 18874368 | bytes 24576 | tf_op jit(solution)/shard_map/pallas_call | solution.py:192
  57.4 1.6 collective-permute-start.7
  58.9 4.6 %collective-permute-done.9 = bf16[128,768]{1,0:T(8,128)(2,1)S(1)} collective-permute-done((bf16[128,768]{1,0:T(8,128)(2,1)S(1)}, bf16[128,768]{1,0:T(8,128)(2,1)S(1)}, u32[]{:S(2)}, u32[]{:S(2)}) %collective-permute-start.9) | collective-permute-done | bytes 196640 | tf_op jit(solution)/shard_map/ppermute | solution.py:299
  63.6 1.6 collective-permute-start.10
  66.3 2.0 %collective-permute-done.10 = bf16[64,768]{1,0:T(8,128)(2,1)S(1)} collective-permute-done((bf16[64,768]{1,0:T(8,128)(2,1)S(1)}, bf16[64,768]{1,0:T(8,128)(2,1)S(1)}, u32[]{:S(2)}, u32[]{:S(2)}) %collective-permute-start.10) | collective-permute-done | bytes 98336 | tf_op jit(solution)/shard_map/ppermute | solution.py:299
  68.3 1.6 collective-permute-done.8
  70.0 1.7 collective-permute-start.11
  71.6 2.6 %collective-permute-start.12 = (bf16[16,1536]{1,0:T(8,128)(2,1)S(1)}, bf16[16,1536]{1,0:T(8,128)(2,1)S(1)}, u32[]{:S(2)}, u32[]{:S(2)}) collective-permute-start(bf16[16,1536]{1,0:T(8,128)(2,1)S(1)} %get-tuple-element.54), channel_id=1, source_target_pairs={{0,16},{8,24},{16,0},{24,8},{1,17},{9,25},{17,1},{25,9},{2,18},{10... | collective-permute-start | bytes 147464 | tf_op jit(solution)/shard_map/ppermute | solution.py:299
  74.4 3.2 %collective-permute-done.12 = bf16[16,1536]{1,0:T(8,128)(2,1)S(1)} collective-permute-done((bf16[16,1536]{1,0:T(8,128)(2,1)S(1)}, bf16[16,1536]{1,0:T(8,128)(2,1)S(1)}, u32[]{:S(2)}, u32[]{:S(2)}) %collective-permute-start.12) | collective-permute-done | bytes 49184 | tf_op jit(solution)/shard_map/ppermute | solution.py:299
  77.7 2.5 %collective-permute-done.13 = bf16[16,1536]{1,0:T(8,128)(2,1)S(1)} collective-permute-done((bf16[16,1536]{1,0:T(8,128)(2,1)S(1)}, bf16[16,1536]{1,0:T(8,128)(2,1)S(1)}, u32[]{:S(2)}, u32[]{:S(2)}) %collective-permute-start.13) | collective-permute-done | bytes 49184 | tf_op jit(solution)/shard_map/ppermute | solution.py:299
  81.7 3.4 %collective-permute-done.14 = bf16[16,1536]{1,0:T(8,128)(2,1)S(1)} collective-permute-done((bf16[16,1536]{1,0:T(8,128)(2,1)S(1)}, bf16[16,1536]{1,0:T(8,128)(2,1)S(1)}, u32[]{:S(2)}, u32[]{:S(2)}) %collective-permute-start.14) | collective-permute-done | bytes 49184 | tf_op jit(solution)/shard_map/ppermute | solution.py:299
  85.2 5.4 %shard_map.91 = (bf16[32,1536]{1,0:T(8,128)(2,1)S(1)}, f32[32,1536]{1,0:T(8,128)S(1)}) custom-call(s32[1]{0:T(128)} %bitcast.half_ref, bf16[32,1536]{1,0:T(8,128)(2,1)S(1)} %pad_maximum_fusion.3.x_ref, bf16[1,1536,3072]{2,1,0:T(8,128)(2,1)} %bitcast.19), custom_call_target="tpu_custom_call" | custom-call | flops 4718592 | bytes 147456 | tf_op jit(solution)/shard_map/pallas_call | solution.py:71
  93.0 3.9 %collective-permute-done.16.refs_1_ = bf16[32,1536]{1,0:T(8,128)(2,1)S(1)} collective-permute-done((bf16[32,1536]{1,0:T(8,128)(2,1)S(1)}, bf16[32,1536]{1,0:T(8,128)(2,1)S(1)}, u32[]{:S(2)}, u32[]{:S(2)}) %collective-permute-start.16) | collective-permute-done | bytes 98336 | tf_op jit(solution)/shard_map/ppermute | solution.py:299
  98.9 5.9 %shard_map.94 = bf16[32,1536]{1,0:T(8,128)(2,1)S(1)} custom-call(s32[1]{0:T(128)} %bitcast.half_ref, bf16[32,1536]{1,0:T(8,128)(2,1)S(1)} %get-tuple-element.38.a_ref, bf16[32,1536]{1,0:T(8,128)(2,1)S(1)} %collective-permute-done.17.b_ref, bf16[1,1536,3072]{2,1,0:T(8,128)(2,1)} %bitcast.20, bf16[1,1536,3072]{2,1,0:T(8,128)(2,1)} %bitcast.21), custom_call_target="tpu_custom_call" | custom-call | flops 4718592 | bytes 147456 | tf_op jit(solution)/shard_map/pallas_call | solution.py:98
  105.5 3.4 %collective-permute-done.18 = bf16[16,1536]{1,0:T(8,128)(2,1)S(1)} collective-permute-done((bf16[16,1536]{1,0:T(8,128)(2,1)S(1)}, bf16[16,1536]{1,0:T(8,128)(2,1)S(1)}, u32[]{:S(2)}, u32[]{:S(2)}) %collective-permute-start.18) | collective-permute-done | bytes 49184 | tf_op jit(solution)/shard_map/ppermute | solution.py:299
  110.1 3.3 %collective-permute-start.21 = (bf16[16,1536]{1,0:T(8,128)(2,1)S(1)}, bf16[16,1536]{1,0:T(8,128)(2,1)S(1)}, u32[]{:S(2)}, u32[]{:S(2)}) collective-permute-start(bf16[16,1536]{1,0:T(8,128)(2,1)S(1)} %get-tuple-element.49), channel_id=1, source_target_pairs={{0,24},{8,16},{16,8},{24,0},{1,25},{9,17},{17,9},{25,1},{2,26},{10... | collective-permute-start | bytes 147464 | tf_op jit(solution)/shard_map/ppermute | solution.py:299
  114.2 1.7 collective-permute-done.21
  117.8 3.9 %collective-permute-done.24 = bf16[64,1536]{1,0:T(8,128)(2,1)S(1)} collective-permute-done((bf16[64,1536]{1,0:T(8,128)(2,1)S(1)}, bf16[64,1536]{1,0:T(8,128)(2,1)S(1)}, u32[]{:S(2)}, u32[]{:S(2)}) %collective-permute-start.24) | collective-permute-done | bytes 196640 | tf_op jit(solution)/shard_map/ppermute | solution.py:299
  122.4 1.4 collective-permute-start.23
  124.9 2.2 %collective-permute-done.23 = bf16[32,1536]{1,0:T(8,128)(2,1)S(1)} collective-permute-done((bf16[32,1536]{1,0:T(8,128)(2,1)S(1)}, bf16[32,1536]{1,0:T(8,128)(2,1)S(1)}, u32[]{:S(2)}, u32[]{:S(2)}) %collective-permute-start.23) | collective-permute-done | bytes 98336 | tf_op jit(solution)/shard_map/ppermute | solution.py:299
  128.6 2.4 %shard_map.95.refs_5_ = bf16[128,1536]{1,0:T(8,128)(2,1)S(1)} custom-call(s32[1]{0:T(128)} %bitcast.1.refs_0_, s32[8]{0:T(128)S(1)} %iota_xor_fusion.refs_1_.order_ref, s32[2,1,1536]{2,1,0:T(1,128)S(1)} %reshape.9.map_ref.refs_2_, bf16[128,1536]{1,0:T(8,128)(2,1)S(1)} %constant_dynamic-update-slice_fusion.3.refs_3_.x_ref, ...), custom_call_target="tpu_custom_call" | custom-call | flops 18874368 | bytes 12288 | tf_op jit(solution)/shard_map/pallas_call | solution.py:244
  131.0 2.4 %shard_map.96.x_ref = bf16[128,1536]{1,0:T(8,128)(2,1)S(1)} custom-call(s32[1]{0:T(128)} %bitcast.1.refs_0_, s32[8]{0:T(128)S(1)} %iota_xor_fusion.refs_1_.order_ref, s32[2,1,1536]{2,1,0:T(1,128)S(1)} %reshape.9.map_ref.refs_2_, bf16[128,1536]{1,0:T(8,128)(2,1)S(1)} %constant_dynamic-update-slice_fusion.refs_3_, ...), custom_call_target="tpu_custom_call" | custom-call | flops 18874368 | bytes 12288 | tf_op jit(solution)/shard_map/pallas_call | solution.py:244
  133.5 2.9 %shard_map.97.rest_0_ = bf16[128,1536]{1,0:T(8,128)(2,1)S(1)} custom-call(s32[1]{0:T(128)} %bitcast.half_ref, bf16[128,1536]{1,0:T(8,128)(2,1)S(1)} %shard_map.96.x_ref, bf16[2,1536,3072]{2,1,0:T(8,128)(2,1)} %w_ref.11), custom_call_target="tpu_custom_call" | custom-call | flops 9437184 | bytes 73728 | tf_op jit(solution)/shard_map/pallas_call | solution.py:71
  137.0 2.4 %shard_map.100.refs_5_ = bf16[128,1536]{1,0:T(8,128)(2,1)S(1)} custom-call(s32[1]{0:T(128)} %bitcast.1.refs_0_, s32[8]{0:T(128)S(1)} %iota_xor_fusion.refs_1_.order_ref, s32[2,1,1536]{2,1,0:T(1,128)S(1)} %reshape.9.map_ref.refs_2_, bf16[128,1536]{1,0:T(8,128)(2,1)S(1)} %constant_dynamic-update-slice_fusion.3.refs_3_.x_ref, ...), custom_call_target="tpu_custom_call" | custom-call | flops 18874368 | bytes 12288 | tf_op jit(solution)/shard_map/pallas_call | solution.py:244
  139.4 2.9 %shard_map.98.refs_0_ = f32[128,1536]{1,0:T(8,128)S(1)} custom-call(s32[1]{0:T(128)} %bitcast.half_ref, bf16[128,1536]{1,0:T(8,128)(2,1)S(1)} %shard_map.96.x_ref, bf16[2,1536,3072]{2,1,0:T(8,128)(2,1)} %w_ref.11, bf16[128,1536]{1,0:T(8,128)(2,1)S(1)} %shard_map.97.rest_0_), custom_call_target="tpu_custom_call" | custom-call | flops 9437184 | bytes 73728 | tf_op jit(solution)/shard_map/pallas_call | solution.py:71
  142.3 2.4 %shard_map.101.x_ref = bf16[128,1536]{1,0:T(8,128)(2,1)S(1)} custom-call(s32[1]{0:T(128)} %bitcast.1.refs_0_, s32[8]{0:T(128)S(1)} %iota_xor_fusion.refs_1_.order_ref, s32[2,1,1536]{2,1,0:T(1,128)S(1)} %reshape.9.map_ref.refs_2_, bf16[128,1536]{1,0:T(8,128)(2,1)S(1)} %constant_dynamic-update-slice_fusion.refs_3_, ...), custom_call_target="tpu_custom_call" | custom-call | flops 18874368 | bytes 12288 | tf_op jit(solution)/shard_map/pallas_call | solution.py:244
  144.9 5.6 %shard_map.102 = (bf16[128,1536]{1,0:T(8,128)(2,1)S(1)}, f32[128,1536]{1,0:T(8,128)S(1)}) custom-call(s32[1]{0:T(128)} %bitcast.half_ref, bf16[128,1536]{1,0:T(8,128)(2,1)S(1)} %shard_map.101.x_ref, bf16[2,1536,3072]{2,1,0:T(8,128)(2,1)} %w_ref.11, bf16[128,1536]{1,0:T(8,128)(2,1)S(1)} %get-tuple-element.40.rest_0_), custom_call_target="tpu_custom_call" | custom-call | flops 18874368 | bytes 147456 | tf_op jit(solution)/shard_map/pallas_call | solution.py:71
  152.4 9.7 %collective-permute-done.29.refs_1_ = bf16[128,1536]{1,0:T(8,128)(2,1)S(1)} collective-permute-done((bf16[128,1536]{1,0:T(8,128)(2,1)S(1)}, bf16[128,1536]{1,0:T(8,128)(2,1)S(1)}, u32[]{:S(2)}, u32[]{:S(2)}) %collective-permute-start.29) | collective-permute-done | bytes 393248 | tf_op jit(solution)/shard_map/ppermute | solution.py:299
  164.8 6.1 %shard_map.105.refs_2_ = bf16[128,1536]{1,0:T(8,128)(2,1)S(1)} custom-call(s32[1]{0:T(128)} %bitcast.half_ref, bf16[128,1536]{1,0:T(8,128)(2,1)S(1)} %subtract_convert_fusion.1.a_ref, bf16[128,1536]{1,0:T(8,128)(2,1)S(1)} %collective-permute-done.31.b_ref, bf16[2,1536,3072]{2,1,0:T(8,128)(2,1)} %wb_ref.9, bf16[2,1536,3072]{2,1,0:T(8,128)(2,1)} %wb_ref.9), custom_call_target="tpu_custom_call" | custom-call | flops 18874368 | bytes 147456 | tf_op jit(solution)/shard_map/pallas_call | solution.py:98
  170.9 3.7 %collective-permute-done.33.refs_1_ = bf16[128,1536]{1,0:T(8,128)(2,1)S(1)} collective-permute-done((bf16[128,1536]{1,0:T(8,128)(2,1)S(1)}, bf16[128,1536]{1,0:T(8,128)(2,1)S(1)}, u32[]{:S(2)}, u32[]{:S(2)}) %collective-permute-start.33) | collective-permute-done | bytes 393248 | tf_op jit(solution)/shard_map/ppermute | solution.py:299
  176.4 3.2 %shard_map.109 = f32[128,1536]{1,0:T(8,128)} custom-call(s32[8]{0:T(128)S(1)} %iota_xor_fusion.refs_1_.order_ref, bf16[128,1536]{1,0:T(8,128)(2,1)S(1)} %constant_dynamic-update-slice_fusion.3.refs_3_.x_ref), custom_call_target="tpu_custom_call" | custom-call | flops 3072 | bytes 18432 | tf_op jit(solution)/shard_map/pallas_call | solution.py:264
  179.5 3.3 %shard_map.107 = bf16[128,768]{1,0:T(8,128)(2,1)S(1)} custom-call(s32[1]{0:T(128)} %bitcast.half_ref, bf16[128,1536]{1,0:T(8,128)(2,1)S(1)} %subtract_convert_fusion.a_ref, bf16[128,1536]{1,0:T(8,128)(2,1)S(1)} %collective-permute-done.34.b_ref, bf16[2,1536,3072]{2,1,0:T(8,128)(2,1)} %wb_ref.9, bf16[2,1536,3072]{2,1,0:T(8,128)(2,1)} %wb_ref.9), custom_call_target="tpu_custom_call" | custom-call | flops 9437184 | bytes 73728 | tf_op jit(solution)/shard_map/pallas_call | solution.py:98
  182.9 1.4 collective-permute-start.35
  184.3 3.3 %shard_map.108 = bf16[128,768]{1,0:T(8,128)(2,1)S(1)} custom-call(s32[1]{0:T(128)} %bitcast.half_ref, bf16[128,1536]{1,0:T(8,128)(2,1)S(1)} %subtract_convert_fusion.a_ref, bf16[128,1536]{1,0:T(8,128)(2,1)S(1)} %collective-permute-done.34.b_ref, bf16[2,1536,3072]{2,1,0:T(8,128)(2,1)} %wb_ref.9, bf16[2,1536,3072]{2,1,0:T(8,128)(2,1)} %wb_ref.9), custom_call_target="tpu_custom_call" | custom-call | flops 9437184 | bytes 73728 | tf_op jit(solution)/shard_map/pallas_call | solution.py:98
  188.5 3.3 %collective-permute-done.35 = bf16[128,768]{1,0:T(8,128)(2,1)S(1)} collective-permute-done((bf16[128,768]{1,0:T(8,128)(2,1)S(1)}, bf16[128,768]{1,0:T(8,128)(2,1)S(1)}, u32[]{:S(2)}, u32[]{:S(2)}) %collective-permute-start.35) | collective-permute-done | bytes 196640 | tf_op jit(solution)/shard_map/ppermute | solution.py:299
  191.9 3.7 %collective-permute-done.36 = bf16[128,768]{1,0:T(8,128)(2,1)S(1)} collective-permute-done((bf16[128,768]{1,0:T(8,128)(2,1)S(1)}, bf16[128,768]{1,0:T(8,128)(2,1)S(1)}, u32[]{:S(2)}, u32[]{:S(2)}) %collective-permute-start.36) | collective-permute-done | bytes 196640 | tf_op jit(solution)/shard_map/ppermute | solution.py:299
  (102 shorter events, 31.3 us)
Async XLA Ops:
  0.6 28.5 %copy-start = (s32[2,6144]{1,0:T(2,128)S(1)}, s32[2,6144]{1,0:T(2,128)}, u32[]{:S(2)}) copy-start(s32[2,6144]{1,0:T(2,128)} %param.9) | copy-start | bytes 147460
  0.7 1.1 copy-start.2
  4.7 3.5 %collective-permute-start = (bf16[128,1536]{1,0:T(8,128)(2,1)S(1)}, bf16[128,1536]{1,0:T(8,128)(2,1)S(1)}, u32[]{:S(2)}, u32[]{:S(2)}) collective-permute-start(bf16[128,1536]{1,0:T(8,128)(2,1)S(1)} %shard_map.77.rest_0_), channel_id=1, source_target_pairs={{0,2},{2,0},{4,6},{6,4},{1,3},{3,1},{5,7},{7,5},{8,10},{10,8},{12,... | collective-permute-start | bytes 1179656 | tf_op jit(solution)/shard_map/ppermute | solution.py:299
  8.2 1.1 copy-start.3
  14.7 3.1 %collective-permute-start.2 = (bf16[128,1536]{1,0:T(8,128)(2,1)S(1)}, bf16[128,1536]{1,0:T(8,128)(2,1)S(1)}, u32[]{:S(2)}, u32[]{:S(2)}) collective-permute-start(bf16[128,1536]{1,0:T(8,128)(2,1)S(1)} %get-tuple-element.28), channel_id=1, source_target_pairs={{0,2},{2,0},{4,6},{6,4},{1,3},{3,1},{5,7},{7,5},{8,10},{10,8},{12,... | collective-permute-start | bytes 1179656 | tf_op jit(solution)/shard_map/ppermute | solution.py:299
  14.8 12.3 %collective-permute-start.1 = (bf16[128,1536]{1,0:T(8,128)(2,1)S(1)}, bf16[128,1536]{1,0:T(8,128)(2,1)S(1)}, u32[]{:S(2)}, u32[]{:S(2)}) collective-permute-start(bf16[128,1536]{1,0:T(8,128)(2,1)S(1)} %get-tuple-element.26.rest_0_), channel_id=1, source_target_pairs={{0,4},{2,6},{4,0},{6,2},{1,5},{3,7},{5,1},{7,3},{8,12},{10,14},{12... | collective-permute-start | bytes 1179656 | tf_op jit(solution)/shard_map/ppermute | solution.py:299
  27.3 2.5 %collective-permute-start.4 = (bf16[128,1536]{1,0:T(8,128)(2,1)S(1)}, bf16[128,1536]{1,0:T(8,128)(2,1)S(1)}, u32[]{:S(2)}, u32[]{:S(2)}) collective-permute-start(bf16[128,1536]{1,0:T(8,128)(2,1)S(1)} %get-tuple-element.32.a_ref), channel_id=1, source_target_pairs={{0,2},{2,0},{4,6},{6,4},{1,3},{3,1},{5,7},{7,5},{8,10},{10,8},{12,... | collective-permute-start | bytes 1179656 | tf_op jit(solution)/shard_map/ppermute | solution.py:299
  27.3 13.9 %collective-permute-start.3 = (bf16[128,1536]{1,0:T(8,128)(2,1)S(1)}, bf16[128,1536]{1,0:T(8,128)(2,1)}, u32[]{:S(2)}, u32[]{:S(2)}) collective-permute-start(bf16[128,1536]{1,0:T(8,128)(2,1)S(1)} %get-tuple-element.29.refs_2_), channel_id=1, source_target_pairs={{0,4},{2,6},{4,0},{6,2},{1,5},{3,7},{5,1},{7,3},{8,12},{10,14},{12... | collective-permute-start | bytes 1179656 | tf_op jit(solution)/shard_map/ppermute | solution.py:299
  42.3 1.8 collective-permute-start.5
  53.0 3.0 %collective-permute-start.6 = (bf16[2,128,1536]{2,1,0:T(8,128)(2,1)S(1)}, bf16[2,128,1536]{2,1,0:T(8,128)(2,1)S(1)}, u32[]{:S(2)}, u32[]{:S(2)}) collective-permute-start(bf16[2,128,1536]{2,1,0:T(8,128)(2,1)S(1)} %shard_map.90), channel_id=1, source_target_pairs={{0,2},{2,0},{4,6},{6,4},{1,3},{3,1},{5,7},{7,5},{8,10},{10,8},{12,... | collective-permute-start | bytes 2359304 | tf_op jit(solution)/shard_map/ppermute | solution.py:299
  56.3 7.2 %collective-permute-start.9 = (bf16[128,768]{1,0:T(8,128)(2,1)S(1)}, bf16[128,768]{1,0:T(8,128)(2,1)S(1)}, u32[]{:S(2)}, u32[]{:S(2)}) collective-permute-start(bf16[128,768]{1,0:T(8,128)(2,1)S(1)} %slice_bitcast_fusion.1), channel_id=1, source_target_pairs={{0,4},{2,6},{4,0},{6,2},{1,5},{3,7},{5,1},{7,3},{8,12},{10,14},{12... | collective-permute-start | bytes 589832 | tf_op jit(solution)/shard_map/ppermute | solution.py:299
  57.4 7.8 %collective-permute-start.7 = (bf16[2,64,768]{2,1,0:T(8,128)(2,1)S(1)}, bf16[2,64,768]{2,1,0:T(8,128)(2,1)S(1)}, u32[]{:S(2)}, u32[]{:S(2)}) collective-permute-start(bf16[2,64,768]{2,1,0:T(8,128)(2,1)S(1)} %slice.69), channel_id=1, source_target_pairs={{0,1},{1,0},{2,3},{3,2},{4,5},{5,4},{6,7},{7,6},{8,9},{9,8},{10,11... | collective-permute-start | bytes 589832 | tf_op jit(solution)/shard_map/ppermute | solution.py:299
  63.6 4.7 %collective-permute-start.10 = (bf16[64,768]{1,0:T(8,128)(2,1)S(1)}, bf16[64,768]{1,0:T(8,128)(2,1)S(1)}, u32[]{:S(2)}, u32[]{:S(2)}) collective-permute-start(bf16[64,768]{1,0:T(8,128)(2,1)S(1)} %slice.115), channel_id=1, source_target_pairs={{0,1},{1,0},{2,3},{3,2},{4,5},{5,4},{6,7},{7,6},{8,9},{9,8},{10,11... | collective-permute-start | bytes 294920 | tf_op jit(solution)/shard_map/ppermute | solution.py:299
  65.2 4.7 %collective-permute-start.8 = (bf16[64,768]{1,0:T(8,128)(2,1)S(1)}, bf16[64,768]{1,0:T(8,128)(2,1)S(1)}, u32[]{:S(2)}, u32[]{:S(2)}) collective-permute-start(bf16[64,768]{1,0:T(8,128)(2,1)S(1)} %fusion.3), channel_id=1, source_target_pairs={{0,4},{2,6},{4,0},{6,2},{1,5},{3,7},{5,1},{7,3},{8,12},{10,14},{12... | collective-permute-start | bytes 294920 | tf_op jit(solution)/shard_map/ppermute | solution.py:299
  70.0 4.5 %collective-permute-start.11 = (bf16[16,1536]{1,0:T(8,128)(2,1)S(1)}, bf16[16,1536]{1,0:T(8,128)(2,1)S(1)}, u32[]{:S(2)}, u32[]{:S(2)}) collective-permute-start(bf16[16,1536]{1,0:T(8,128)(2,1)S(1)} %get-tuple-element.52), channel_id=1, source_target_pairs={{0,8},{8,0},{16,24},{24,16},{1,9},{9,1},{17,25},{25,17},{2,10},{10... | collective-permute-start | bytes 147464 | tf_op jit(solution)/shard_map/ppermute | solution.py:299
  71.6 6.0 %collective-permute-start.12 = (bf16[16,1536]{1,0:T(8,128)(2,1)S(1)}, bf16[16,1536]{1,0:T(8,128)(2,1)S(1)}, u32[]{:S(2)}, u32[]{:S(2)}) collective-permute-start(bf16[16,1536]{1,0:T(8,128)(2,1)S(1)} %get-tuple-element.54), channel_id=1, source_target_pairs={{0,16},{8,24},{16,0},{24,8},{1,17},{9,25},{17,1},{25,9},{2,18},{10... | collective-permute-start | bytes 147464 | tf_op jit(solution)/shard_map/ppermute | solution.py:299
  74.3 5.9 %collective-permute-start.13 = (bf16[16,1536]{1,0:T(8,128)(2,1)S(1)}, bf16[16,1536]{1,0:T(8,128)(2,1)S(1)}, u32[]{:S(2)}, u32[]{:S(2)}) collective-permute-start(bf16[16,1536]{1,0:T(8,128)(2,1)S(1)} %get-tuple-element.53), channel_id=1, source_target_pairs={{0,24},{8,16},{16,8},{24,0},{1,25},{9,17},{17,9},{25,1},{2,26},{10... | collective-permute-start | bytes 147464 | tf_op jit(solution)/shard_map/ppermute | solution.py:299
  81.0 4.2 %collective-permute-start.14 = (bf16[16,1536]{1,0:T(8,128)(2,1)S(1)}, bf16[16,1536]{1,0:T(8,128)(2,1)S(1)}, u32[]{:S(2)}, u32[]{:S(2)}) collective-permute-start(bf16[16,1536]{1,0:T(8,128)(2,1)S(1)} %fusion.9), channel_id=1, source_target_pairs={{0,1},{1,0},{2,3},{3,2},{4,5},{5,4},{6,7},{7,6},{8,9},{9,8},{10,11... | collective-permute-start | bytes 147464 | tf_op jit(solution)/shard_map/ppermute | solution.py:299
  90.5 1.4 collective-permute-start.15
  91.9 4.9 %collective-permute-start.16 = (bf16[32,1536]{1,0:T(8,128)(2,1)S(1)}, bf16[32,1536]{1,0:T(8,128)(2,1)S(1)}, u32[]{:S(2)}, u32[]{:S(2)}) collective-permute-start(bf16[32,1536]{1,0:T(8,128)(2,1)S(1)} %get-tuple-element.37), channel_id=1, source_target_pairs={{0,4},{2,6},{4,0},{6,2},{1,5},{3,7},{5,1},{7,3},{8,12},{10,14},{12... | collective-permute-start | bytes 294920 | tf_op jit(solution)/shard_map/ppermute | solution.py:299
  97.6 1.3 collective-permute-start.17
  104.7 4.2 %collective-permute-start.18 = (bf16[16,1536]{1,0:T(8,128)(2,1)S(1)}, bf16[16,1536]{1,0:T(8,128)(2,1)S(1)}, u32[]{:S(2)}, u32[]{:S(2)}) collective-permute-start(bf16[16,1536]{1,0:T(8,128)(2,1)S(1)} %slice.82), channel_id=1, source_target_pairs={{0,1},{1,0},{2,3},{3,2},{4,5},{5,4},{6,7},{7,6},{8,9},{9,8},{10,11... | collective-permute-start | bytes 147464 | tf_op jit(solution)/shard_map/ppermute | solution.py:299
  108.9 4.5 %collective-permute-start.19 = (bf16[16,1536]{1,0:T(8,128)(2,1)S(1)}, bf16[16,1536]{1,0:T(8,128)(2,1)S(1)}, u32[]{:S(2)}, u32[]{:S(2)}) collective-permute-start(bf16[16,1536]{1,0:T(8,128)(2,1)S(1)} %get-tuple-element.49), channel_id=1, source_target_pairs={{0,8},{8,0},{16,24},{24,16},{1,9},{9,1},{17,25},{25,17},{2,10},{10... | collective-permute-start | bytes 147464 | tf_op jit(solution)/shard_map/ppermute | solution.py:299
  109.0 5.2 %collective-permute-start.20 = (bf16[16,1536]{1,0:T(8,128)(2,1)S(1)}, bf16[16,1536]{1,0:T(8,128)(2,1)S(1)}, u32[]{:S(2)}, u32[]{:S(2)}) collective-permute-start(bf16[16,1536]{1,0:T(8,128)(2,1)S(1)} %get-tuple-element.49), channel_id=1, source_target_pairs={{0,16},{8,24},{16,0},{24,8},{1,17},{9,25},{17,1},{25,9},{2,18},{10... | collective-permute-start | bytes 147464 | tf_op jit(solution)/shard_map/ppermute | solution.py:299
  110.1 5.9 %collective-permute-start.21 = (bf16[16,1536]{1,0:T(8,128)(2,1)S(1)}, bf16[16,1536]{1,0:T(8,128)(2,1)S(1)}, u32[]{:S(2)}, u32[]{:S(2)}) collective-permute-start(bf16[16,1536]{1,0:T(8,128)(2,1)S(1)} %get-tuple-element.49), channel_id=1, source_target_pairs={{0,24},{8,16},{16,8},{24,0},{1,25},{9,17},{17,9},{25,1},{2,26},{10... | collective-permute-start | bytes 147464 | tf_op jit(solution)/shard_map/ppermute | solution.py:299
  116.0 5.7 %collective-permute-start.24 = (bf16[64,1536]{1,0:T(8,128)(2,1)S(1)}, bf16[64,1536]{1,0:T(8,128)(2,1)S(1)}, u32[]{:S(2)}, u32[]{:S(2)}) collective-permute-start(bf16[64,1536]{1,0:T(8,128)(2,1)S(1)} %pad_maximum_fusion.2), channel_id=1, source_target_pairs={{0,1},{1,0},{2,3},{3,2},{4,5},{5,4},{6,7},{7,6},{8,9},{9,8},{10,11... | collective-permute-start | bytes 589832 | tf_op jit(solution)/shard_map/ppermute | solution.py:299
  116.7 5.7 %collective-permute-start.22 = (bf16[64,1536]{1,0:T(8,128)(2,1)S(1)}, bf16[64,1536]{1,0:T(8,128)(2,1)S(1)}, u32[]{:S(2)}, u32[]{:S(2)}) collective-permute-start(bf16[64,1536]{1,0:T(8,128)(2,1)S(1)} %pad_maximum_fusion.2), channel_id=1, source_target_pairs={{0,4},{2,6},{4,0},{6,2},{1,5},{3,7},{5,1},{7,3},{8,12},{10,14},{12... | collective-permute-start | bytes 589832 | tf_op jit(solution)/shard_map/ppermute | solution.py:299
  121.8 6.9 %collective-permute-start.27 = (bf16[128,1536]{1,0:T(8,128)(2,1)S(1)}, bf16[128,1536]{1,0:T(8,128)(2,1)S(1)}, u32[]{:S(2)}, u32[]{:S(2)}) collective-permute-start(bf16[128,1536]{1,0:T(8,128)(2,1)S(1)} %constant_dynamic-update-slice_fusion.3.refs_3_.x_ref), channel_id=1, source_target_pairs={{0,2},{2,0},{4,6},{6,4},{1,3},{3,1},{5,7},{7,5},{8,10},{10,8},{12,... | collective-permute-start | bytes 1179656 | tf_op jit(solution)/shard_map/ppermute | solution.py:299
  122.4 4.7 %collective-permute-start.23 = (bf16[32,1536]{1,0:T(8,128)(2,1)S(1)}, bf16[32,1536]{1,0:T(8,128)(2,1)S(1)}, u32[]{:S(2)}, u32[]{:S(2)}) collective-permute-start(bf16[32,1536]{1,0:T(8,128)(2,1)S(1)} %slice.83), channel_id=1, source_target_pairs={{0,1},{1,0},{2,3},{3,2},{4,5},{5,4},{6,7},{7,6},{8,9},{9,8},{10,11... | collective-permute-start | bytes 294920 | tf_op jit(solution)/shard_map/ppermute | solution.py:299
  123.8 4.7 %collective-permute-start.25 = (bf16[32,1536]{1,0:T(8,128)(2,1)S(1)}, bf16[32,1536]{1,0:T(8,128)(2,1)S(1)}, u32[]{:S(2)}, u32[]{:S(2)}) collective-permute-start(bf16[32,1536]{1,0:T(8,128)(2,1)S(1)} %slice.84), channel_id=1, source_target_pairs={{0,4},{2,6},{4,0},{6,2},{1,5},{3,7},{5,1},{7,3},{8,12},{10,14},{12... | collective-permute-start | bytes 294920 | tf_op jit(solution)/shard_map/ppermute | solution.py:299
  128.5 2.5 %collective-permute-start.26 = (bf16[128,1536]{1,0:T(8,128)(2,1)S(1)}, bf16[128,1536]{1,0:T(8,128)(2,1)S(1)}, u32[]{:S(2)}, u32[]{:S(2)}) collective-permute-start(bf16[128,1536]{1,0:T(8,128)(2,1)S(1)} %constant_dynamic-update-slice_fusion.refs_3_), channel_id=1, source_target_pairs={{0,2},{2,0},{4,6},{6,4},{1,3},{3,1},{5,7},{7,5},{8,10},{10,8},{12,... | collective-permute-start | bytes 1179656 | tf_op jit(solution)/shard_map/ppermute | solution.py:299
  136.4 8.3 %collective-permute-start.28 = (bf16[128,1536]{1,0:T(8,128)(2,1)S(1)}, bf16[128,1536]{1,0:T(8,128)(2,1)S(1)}, u32[]{:S(2)}, u32[]{:S(2)}) collective-permute-start(bf16[128,1536]{1,0:T(8,128)(2,1)S(1)} %shard_map.97.rest_0_), channel_id=1, source_target_pairs={{0,2},{2,0},{4,6},{6,4},{1,3},{3,1},{5,7},{7,5},{8,10},{10,8},{12,... | collective-permute-start | bytes 1179656 | tf_op jit(solution)/shard_map/ppermute | solution.py:299
  150.5 1.8 collective-permute-start.30
  150.6 11.5 %collective-permute-start.29 = (bf16[128,1536]{1,0:T(8,128)(2,1)S(1)}, bf16[128,1536]{1,0:T(8,128)(2,1)S(1)}, u32[]{:S(2)}, u32[]{:S(2)}) collective-permute-start(bf16[128,1536]{1,0:T(8,128)(2,1)S(1)} %get-tuple-element.40.rest_0_), channel_id=1, source_target_pairs={{0,4},{2,6},{4,0},{6,2},{1,5},{3,7},{5,1},{7,3},{8,12},{10,14},{12... | collective-permute-start | bytes 1179656 | tf_op jit(solution)/shard_map/ppermute | solution.py:299
  163.0 1.8 collective-permute-start.31
  163.1 11.5 %collective-permute-start.33 = (bf16[128,1536]{1,0:T(8,128)(2,1)S(1)}, bf16[128,1536]{1,0:T(8,128)(2,1)S(1)}, u32[]{:S(2)}, u32[]{:S(2)}) collective-permute-start(bf16[128,1536]{1,0:T(8,128)(2,1)S(1)} %get-tuple-element.43.refs_2_), channel_id=1, source_target_pairs={{0,4},{2,6},{4,0},{6,2},{1,5},{3,7},{5,1},{7,3},{8,12},{10,14},{12... | collective-permute-start | bytes 1179656 | tf_op jit(solution)/shard_map/ppermute | solution.py:299
  175.6 4.0 %collective-permute-start.34 = (bf16[128,1536]{1,0:T(8,128)(2,1)S(1)}, bf16[128,1536]{1,0:T(8,128)(2,1)S(1)}, u32[]{:S(2)}, u32[]{:S(2)}) collective-permute-start(bf16[128,1536]{1,0:T(8,128)(2,1)S(1)} %subtract_convert_fusion.a_ref), channel_id=1, source_target_pairs={{0,2},{2,0},{4,6},{6,4},{1,3},{3,1},{5,7},{7,5},{8,10},{10,8},{12,... | collective-permute-start | bytes 1179656 | tf_op jit(solution)/shard_map/ppermute | solution.py:299
  175.6 12.8 %collective-permute-start.32 = (bf16[128,1536]{1,0:T(8,128)(2,1)S(1)}, bf16[128,1536]{1,0:T(8,128)(2,1)S(1)}, u32[]{:S(2)}, u32[]{:S(2)}) collective-permute-start(bf16[128,1536]{1,0:T(8,128)(2,1)S(1)} %shard_map.105.refs_2_), channel_id=1, source_target_pairs={{0,1},{1,0},{2,3},{3,2},{4,5},{5,4},{6,7},{7,6},{8,9},{9,8},{10,11... | collective-permute-start | bytes 1179656 | tf_op jit(solution)/shard_map/ppermute | solution.py:299
  182.9 8.9 %collective-permute-start.35 = (bf16[128,768]{1,0:T(8,128)(2,1)S(1)}, bf16[128,768]{1,0:T(8,128)(2,1)S(1)}, u32[]{:S(2)}, u32[]{:S(2)}) collective-permute-start(bf16[128,768]{1,0:T(8,128)(2,1)S(1)} %shard_map.107), channel_id=1, source_target_pairs={{0,1},{1,0},{2,3},{3,2},{4,5},{5,4},{6,7},{7,6},{8,9},{9,8},{10,11... | collective-permute-start | bytes 589832 | tf_op jit(solution)/shard_map/ppermute | solution.py:299
  187.6 7.9 %collective-permute-start.36 = (bf16[128,768]{1,0:T(8,128)(2,1)S(1)}, bf16[128,768]{1,0:T(8,128)(2,1)S(1)}, u32[]{:S(2)}, u32[]{:S(2)}) collective-permute-start(bf16[128,768]{1,0:T(8,128)(2,1)S(1)} %shard_map.108), channel_id=1, source_target_pairs={{0,1},{1,0},{2,3},{3,2},{4,5},{5,4},{6,7},{7,6},{8,9},{9,8},{10,11... | collective-permute-start | bytes 589832 | tf_op jit(solution)/shard_map/ppermute | solution.py:299
  195.6 1.4 copy-start.1

commit v3 on v2

v3 whole, which is shorter than its diff:
```python
import functools

import jax
import jax.numpy as jnp
from jax import lax
from jax.experimental import pallas as pl
from jax.experimental.pallas import tpu as pltpu
from jax.sharding import PartitionSpec as P

BF16 = jnp.bfloat16
F32 = jnp.float32
I16 = jnp.int16
NN = (((1,), (0,)), ((), ()))
NT = (((1,), (1,)), ((), ()))
LANES = 128
ANY = pl.BlockSpec(memory_space=pl.ANY)
WHOLE = pl.BlockSpec(memory_space=pltpu.VMEM)
SCALARS = pl.BlockSpec(memory_space=pltpu.SMEM)


def tile_of(extent, *sizes):
    for size in sizes:
        if extent % size == 0:
            return size
    return extent


def params():
    return pltpu.CompilerParams(vmem_limit_bytes=10 * 1024 * 1024)


def cost(flops, nbytes):
    return pl.CostEstimate(flops=flops // 64, bytes_accessed=nbytes // 64, transcendentals=0)


def in_hbm(w):
    return pltpu.with_memory_space_constraint(w, pltpu.HBM)


def in_vmem(w):
    return pltpu.with_memory_space_constraint(w, pltpu.VMEM)


def preload_kernel(child, w_ref, *rest):
    o_ref, sem = rest[-2:]
    copy = pltpu.make_async_copy(w_ref.at[child], o_ref, sem)
    copy.start()
    copy.wait()


def preload(w, child, after=()):
    return pl.pallas_call(
        functools.partial(preload_kernel, child),
        in_specs=[pl.BlockSpec(memory_space=pltpu.HBM)] + [ANY] * len(after),
        out_specs=WHOLE,
        out_shape=pltpu.VMEM(w.shape[1:], w.dtype),
        scratch_shapes=[pltpu.SemaphoreType.DMA],
        compiler_params=params(),
        cost_estimate=cost(0, w[0].size * 2),
    )(in_hbm(w), *after)


def put_pieces(refs, value):
    rows = value.shape[0] // len(refs)
    for i, ref in enumerate(refs):
        ref[...] = value[i * rows : (i + 1) * rows].astype(ref.dtype)


def take_pieces(refs):
    return refs[0][...] if len(refs) == 1 else jnp.concatenate([r[...] for r in refs], axis=0)


def nn_kernel(half_ref, x_ref, w_ref, *outs):
    x = x_ref[0] if len(x_ref.shape) == 3 else x_ref[...]
    product = lax.dot_general(x, w_ref[0], NN, preferred_element_type=F32)
    put_pieces(outs, product)


def nn(x, w, child, core, part, pieces=1, after=()):
    m, k = x.shape[-2:]
    n_half = w.shape[2] // 2
    bn = tile_of(n_half, 768, 512, 384, 256, 128)
    steps = n_half // bn
    if x.ndim == 3:
        x_spec = pl.BlockSpec((1, m, k), lambda i, h: (child, 0, 0))
        x = in_hbm(x)
    else:
        x_spec = pl.BlockSpec((m, k), lambda i, h: (0, 0))

    def kernel(half_ref, x_ref, w_ref, *rest):
        nn_kernel(half_ref, x_ref, w_ref, *rest[len(after) :])

    return pl.pallas_call(
        kernel,
        grid_spec=pltpu.PrefetchScalarGridSpec(
            num_scalar_prefetch=1,
            grid=(steps,),
            in_specs=[
                x_spec,
                pl.BlockSpec(
                    (1, k, bn), lambda i, h: (child, 0, lax.bitwise_xor(h[0], part) * steps + i)
                ),
            ]
            + [ANY] * len(after),
            out_specs=[pl.BlockSpec((m // pieces, bn), lambda i, h: (0, i))] * pieces,
        ),
        out_shape=[jax.ShapeDtypeStruct((m // pieces, n_half), BF16 if part else F32)] * pieces,
        compiler_params=params(),
        cost_estimate=cost(2 * m * k * n_half, 2 * k * n_half),
    )(core, x, in_hbm(w), *after)


def held_nn(x, w, core, part, pieces=1, after=()):
    m, k = x.shape
    n_half = w.shape[1] // 2
    bn = tile_of(n_half, 512, 384, 256, 128)

    def kernel(half_ref, x_ref, w_ref, *rest):
        outs = rest[len(after) :]
        base = lax.bitwise_xor(half_ref[0], part) * n_half
        x = x_ref[...]
        for start in range(0, n_half, bn):
            cols = pl.ds(pl.multiple_of(base + start, LANES), bn)
            product = lax.dot_general(x, w_ref[:, cols], NN, preferred_element_type=F32)
            for i, out in enumerate(outs):
                rows = m // pieces
                out[:, start : start + bn] = product[i * rows : (i + 1) * rows].astype(out.dtype)

    return pl.pallas_call(
        kernel,
        in_specs=[SCALARS, WHOLE, WHOLE] + [ANY] * len(after),
        out_specs=[WHOLE] * pieces,
        out_shape=[jax.ShapeDtypeStruct((m // pieces, n_half), BF16 if part else F32)] * pieces,
        compiler_params=params(),
        cost_estimate=cost(2 * m * k * n_half, 2 * k * n_half),
    )(core, x, in_vmem(w), *after)


def held_nt(mine, other, w, core, chunk=0, chunks=1, after=()):
    m = sum(x.shape[0] for x in mine)
    k_half = mine[0].shape[1]
    u = w.shape[0] // chunks
    bu = tile_of(u, 512, 384, 256, 128)
    first = chunk * u

    def kernel(half_ref, *refs):
        a = take_pieces(refs[: len(mine)])
        b = take_pieces(refs[len(mine) : len(mine) + len(other)])
        w_ref, o_ref = refs[len(mine) + len(other)], refs[-1]
        low = half_ref[0] == 0
        left, right = jnp.where(low, a, b), jnp.where(low, b, a)
        for start in range(0, u, bu):
            at = slice(first + start, first + start + bu)
            total = lax.dot_general(left, w_ref[at, :k_half], NT, preferred_element_type=F32)
            total += lax.dot_general(right, w_ref[at, k_half:], NT, preferred_element_type=F32)
            o_ref[:, start : start + bu] = total.astype(o_ref.dtype)

    return pl.pallas_call(
        kernel,
        in_specs=[SCALARS] + [WHOLE] * (len(mine) + len(other) + 1) + [ANY] * len(after),
        out_specs=WHOLE,
        out_shape=jax.ShapeDtypeStruct((m, u), BF16),
        compiler_params=params(),
        cost_estimate=cost(4 * m * k_half * u, 4 * k_half * u),
    )(core, *mine, *other, in_vmem(w), *after)


def spread_kernel(map_ref, o_ref):
    u = map_ref.shape[2]
    step = tile_of(u, LANES)
    for start in range(0, u, step):
        row = map_ref[0, :, start : start + step]
        o_ref[0, start : start + step, :] = jnp.broadcast_to(row, (LANES, step)).T.astype(I16)


def spread(maps):
    kids, _, u = maps.shape
    return pl.pallas_call(
        spread_kernel,
        grid=(kids,),
        in_specs=[pl.BlockSpec((1, 1, u), lambda k: (k, 0, 0))],
        out_specs=pl.BlockSpec((1, u, LANES), lambda k: (k, 0, 0)),
        out_shape=jax.ShapeDtypeStruct((kids, u, LANES), I16),
        compiler_params=params(),
        cost_estimate=cost(kids * u * LANES, 2 * kids * u * LANES),
    )(maps)


def store_in_order(order_ref, chunk, store, value):
    for i in range(value.shape[0] // chunk):
        store(
            pl.ds(pl.multiple_of(order_ref[i] * chunk, chunk), chunk),
            value[i * chunk : (i + 1) * chunk],
        )


def scatter_kernel(block_rows, tile, odd, chunk, *refs):
    row_ref, order_ref, map_ref, upd_ref, *rest = refs
    o_ref = rest[-1]
    j, t = pl.program_id(0), pl.program_id(1)
    dest = lax.bitwise_xor(row_ref[0], 2 * j + odd)
    first = (dest * block_rows + t * tile).astype(I16)
    local = map_ref[0] - first
    u = local.shape[0]
    sub = tile_of(tile, 256, 128)
    upd = upd_ref[...]
    for start in range(0, tile, sub):
        wide = jnp.concatenate([local] * (sub // LANES), axis=1)
        row_ids = lax.broadcasted_iota(I16, (u, sub), 1) + jnp.int16(start)
        hot = jnp.where(row_ids == wide, BF16(1), BF16(0))
        total = lax.dot_general(upd, hot, NN, preferred_element_type=F32)
        if len(rest) == 2:
            at = slice(start, start + sub)
            before = rest[0]

            def store(ds, value, at=at, before=before):
                o_ref[0, ds, at] = (value + before[0, ds, at].astype(F32)).astype(o_ref.dtype)

        else:
            at = slice(start, start + sub)

            def store(ds, value, at=at):
                o_ref[0, ds, at] = value.astype(o_ref.dtype)

        store_in_order(order_ref, chunk, store, total)


def scatter(upd, spread_maps, child, row, order, rows_count, block_rows, odd, before):
    m, u = upd.shape
    tile = tile_of(block_rows, 768, 512, 384, 256, 128)
    count = rows_count // 2
    chunk = m // order.shape[0]
    block = pl.BlockSpec((1, m, tile), lambda j, t, r, o: (j, 0, t))
    in_specs = [
        pl.BlockSpec((1, u, LANES), lambda j, t, r, o: (child, 0, 0)),
        pl.BlockSpec((m, u), lambda j, t, r, o: (0, 0)),
    ]
    args = [spread_maps, upd]
    if before is not None:
        in_specs.append(block)
        args.append(before)
    return pl.pallas_call(
        functools.partial(scatter_kernel, block_rows, tile, odd, chunk),
        grid_spec=pltpu.PrefetchScalarGridSpec(
            num_scalar_prefetch=2,
            grid=(count, block_rows // tile),
            in_specs=in_specs,
            out_specs=block,
        ),
        out_shape=jax.ShapeDtypeStruct((count, m, block_rows), BF16),
        compiler_params=params(),
        cost_estimate=cost(2 * m * u * count * block_rows, 4 * m * count * block_rows),
    )(row, order, *args)


def gather_kernel(block_rows, tile, which, counts, chunk, added, row_ref, order_ref, map_ref, *rest):
    o_ref = rest[-1]
    slot_map = map_ref[0]
    total, at = None, 0
    for j, count in zip(which, counts):
        pieces = rest[at : at + count]
        at += count
        first = lax.bitwise_xor(row_ref[0], j) * block_rows
        for start in range(0, block_rows, tile):
            local = (slot_map - (first + start)).astype(I16)
            row_ids = lax.broadcasted_iota(I16, (tile, slot_map.shape[1]), 0)
            hot = jnp.where(row_ids == local, BF16(1), BF16(0))
            block = [p[:, start : start + tile] for p in pieces]
            block = block[0] if count == 1 else jnp.concatenate(block, axis=0)
            term = lax.dot_general(block, hot, NN, preferred_element_type=F32)
            total = term if total is None else total + term

    def store(ds, value):
        if added:
            value = value + rest[at][ds, :].astype(F32)
        o_ref[ds, :] = value.astype(o_ref.dtype)

    store_in_order(order_ref, chunk, store, total)


def gather(blocks, which, maps, child, row, order, before, after=()):
    m = sum(p.shape[0] for p in blocks[0])
    block_rows = blocks[0][0].shape[1]
    u = maps.shape[2]
    tile = tile_of(block_rows, 512, 384, 256, 128)
    bu = tile_of(u, 512, 384, 256, 128)
    chunk = m // order.shape[0]
    counts = [len(b) for b in blocks]
    in_specs = [pl.BlockSpec((1, 1, bu), lambda i, r, o: (child, 0, i))]
    args = [maps]
    for p in (p for b in blocks for p in b):
        in_specs.append(pl.BlockSpec(p.shape, lambda i, r, o: (0, 0)))
        args.append(p)
    out_block = pl.BlockSpec((m, bu), lambda i, r, o: (0, i))
    if before is not None:
        in_specs.append(out_block)
        args.append(before)
    in_specs += [ANY] * len(after)
    return pl.pallas_call(
        functools.partial(
            gather_kernel, block_rows, tile, which, counts, chunk, before is not None
        ),
        grid_spec=pltpu.PrefetchScalarGridSpec(
            num_scalar_prefetch=2, grid=(u // bu,), in_specs=in_specs, out_specs=out_block
        ),
        out_shape=jax.ShapeDtypeStruct((m, u), BF16),
        compiler_params=params(),
        cost_estimate=cost(
            2 * m * u * len(blocks) * block_rows, 2 * m * len(blocks) * block_rows
        ),
    )(row, order, *args, *after)


def finish(held, kids, child, chunk, chunks, terms):
    m, n = terms[0].shape
    place = pl.BlockSpec((1, m, n), lambda i: (child, 0, chunk))
    whole = pl.BlockSpec((m, n), lambda i: (0, 0))

    def kernel(*refs):
        total = refs[0][...].astype(F32)
        for ref in refs[1 : len(terms)]:
            total += ref[...].astype(F32)
        refs[-1][0] = total

    extra = () if held is None else (held,)
    return pl.pallas_call(
        kernel,
        grid=(1,),
        in_specs=[whole] * len(terms) + [ANY] * len(extra),
        out_specs=place,
        out_shape=jax.ShapeDtypeStruct((kids, m, n * chunks), F32),
        input_output_aliases={len(terms): 0} if extra else {},
        compiler_params=params(),
        cost_estimate=cost(m * n, 8 * m * n),
    )(*terms, *extra)


def reorder(pieces, order):
    m, n = sum(p.shape[0] for p in pieces), pieces[0].shape[1]
    chunk = m // order.shape[0]

    def kernel(order_ref, *refs):
        def store(ds, value):
            refs[-1][ds, :] = value

        store_in_order(order_ref, chunk, store, take_pieces(refs[:-1]).astype(F32))

    return pl.pallas_call(
        kernel,
        in_specs=[SCALARS] + [WHOLE] * len(pieces),
        out_specs=WHOLE,
        out_shape=jax.ShapeDtypeStruct((m, n), F32),
        compiler_params=params(),
        cost_estimate=cost(m * n, 6 * m * n),
    )(order, *pieces)


def join(terms, signs, after=(), wide=True, narrow=1):
    m = sum(x.shape[0] for x in terms[0])
    n = terms[0][0].shape[1]
    counts = [len(t) for t in terms]

    def kernel(*refs):
        outs = refs[sum(counts) + len(after) :]
        total, at = None, 0
        for count, sign in zip(counts, signs):
            value = take_pieces(refs[at : at + count]).astype(F32)
            at += count
            value = value if sign > 0 else -value
            total = value if total is None else total + value
        if wide:
            outs[0][...] = total
            outs = outs[1:]
        if narrow:
            put_pieces(outs, total)

    shapes = [jax.ShapeDtypeStruct((m, n), F32)] if wide else []
    shapes += [jax.ShapeDtypeStruct((m // narrow, n), BF16)] * narrow if narrow else []
    outs = pl.pallas_call(
        kernel,
        in_specs=[WHOLE] * sum(counts) + [ANY] * len(after),
        out_specs=[WHOLE] * len(shapes),
        out_shape=shapes,
        compiler_params=params(),
        cost_estimate=cost(m * n, 12 * m * n),
    )(*[x for t in terms for x in t], *after)
    return (outs[0] if wide else None), (outs[1:] if wide else outs)


def swap(x, axis, bit, size):
    return lax.ppermute(x, axis, [(i, i ^ bit) for i in range(size)])


def add(x, y):
    return x.astype(F32) + y.astype(F32)


def bits(size):
    return [1 << b for b in range(size.bit_length() - 1)]


def on_device(sizes, child_loads, child_inverse, child_panel, child_map, root_loads, root_inverse):
    leafs, rows, cols = sizes
    kids = child_loads.shape[0]
    case_count, root_rows = root_loads.shape
    leaf, row, col = (lax.axis_index(a).astype(jnp.int32) for a in ("leaf", "row", "col"))
    core = lax.bitwise_and(row, 1)[None]
    row_1 = row[None]
    root_w = root_inverse[None]
    piece = case_count // (leafs * cols)
    wide = rows == 4 and cols == 2 and piece % 16 == 0 and root_rows % 256 == 0

    def to_row(x, bit):
        return swap(x, "row", bit, rows)

    def to_col(x, bit=1):
        return swap(x, "col", bit, cols)

    def to_leaf(x, j):
        return swap(x, "leaf", j, leafs)

    def pieces_of(k, m=case_count):
        return 4 if k and m % 64 == 0 else 1

    def core_sum(kept, sent):
        total, narrow = join([[kept], [to_row(x, 1) for x in sent]], (1, 1))
        return total, narrow[0]

    def row_end(total, narrow, after=(), base=None, wide=True, pieces=1):
        steps = bits(rows)[1:]
        for at, bit in enumerate(steps):
            last = at == len(steps) - 1
            terms, signs = [[total], [to_row(narrow, bit)]], (1, 1)
            if last and base is not None:
                terms, signs = [[base], *terms], (1, -1, -1)
            total, out = join(
                terms, signs, after, wide or not last, pieces if last else 1
            )
            narrow = out[0]
        return total, out

    def halves(rounded):
        return rounded, [to_row(x, 1) for x in rounded]

    slot_rows = child_panel.shape[1]
    own_map = lax.dynamic_slice_in_dim(child_map, row * slot_rows, slot_rows, 1)
    maps = own_map.reshape(kids, 1, slot_rows)
    spread_maps = spread(maps)

    if wide:
        ids = jnp.arange(cols * leafs, dtype=jnp.int32)
        order = lax.bitwise_xor(ids, col * leafs + leaf)
    else:
        order = jnp.zeros((1,), jnp.int32)

    begun = []
    after = ()
    for k in range(kids):
        sent = nn(child_loads, child_inverse, k, core, 1, pieces_of(k))
        kept = nn(child_loads, child_inverse, k, core, 0, 1, (sent[0], *after))
        begun.append(core_sum(kept[0], sent))
        after = begun[k][1:]
    panels = []
    for k in range(kids):
        panels.append(preload(child_panel, k, after))
        after = (panels[k],)
    forward = []
    sent = kept = None
    for k in range(kids):
        after = after if k == 0 else (sent,)
        total, rounded = row_end(*begun[k], after, pieces=pieces_of(k == 0))
        forward.append(total)
        upd = held_nt(*halves(rounded), panels[k], core)
        sent = scatter(upd, spread_maps, k, row_1, order, rows, root_rows, 1, sent)
        kept = scatter(upd, spread_maps, k, row_1, order, rows, root_rows, 0, kept)

    total = add(kept, to_row(sent, 1))
    if wide:
        half, cut = case_count // 2, root_rows // 2
        left = add(total[:, :half, :cut], to_col(total[:, half:, :cut].astype(BF16)))
        right = add(total[0, :, cut:], to_row(total[1, :, cut:].astype(BF16), 2))
        left = add(left[0], to_row(left[1].astype(BF16), 2))
        right = add(right[:half], to_col(right[half:].astype(BF16)))
        total = jnp.concatenate([left, right], axis=1)
        narrow = total.astype(BF16)
        shares = [narrow[j * piece : (j + 1) * piece] for j in range(1, leafs)]
        root_held = preload(root_w, 0, shares)
        first_case = (col * leafs + leaf) * piece
        loads = lax.dynamic_slice_in_dim(root_loads, first_case, piece, 0)
        terms = [loads, total[:piece]] + [to_leaf(x, j + 1) for j, x in enumerate(shares)]
        _, (residual,) = join([[x] for x in terms], (1,) + (-1,) * leafs, (root_held,), False)
        residual = jnp.concatenate([residual, to_col(residual)])
    else:
        for bit in bits(rows)[1:]:
            total = add(total[0::2], to_row(total[1::2].astype(BF16), bit))
        total = total[0]
        chunk = case_count // leafs

        def cases_of(x, j):
            return lax.dynamic_slice_in_dim(x, lax.bitwise_xor(leaf, j) * chunk, chunk, 0)

        narrow = total.astype(BF16)
        mine_cases = cases_of(total, 0)
        for j in range(1, leafs):
            mine_cases = add(mine_cases, to_leaf(cases_of(narrow, j), j))
        for bit in bits(cols):
            narrow = mine_cases.astype(BF16)
            mine_cases = add(narrow, to_col(narrow, bit))
        residual = (cases_of(root_loads, 0).astype(F32) - mine_cases).astype(BF16)

    if not wide:
        root_held = preload(root_w, 0, (kept,))
    sent = held_nn(residual, root_held, core, 1)
    kept = held_nn(residual, root_held, core, 0, 1, sent)
    begun = core_sum(kept[0], sent)
    panels = [preload(child_panel, 0, begun[1:])]
    _, root_forward = row_end(*begun, (panels[0],), wide=False)
    part = held_nt(*halves(root_forward), root_held, core)
    panels += [preload(child_panel, k, (part,)) for k in range(1, kids)]

    picked = [None] * kids
    if wide:
        _, (part,) = join(
            [[part[:piece]], [to_col(part[piece:])]], (1, 1), tuple(panels[1:]), False
        )
        inverses = [preload(child_inverse, 0, (part,))]
        shares = [part] + [to_leaf(part, j) for j in range(1, leafs)]
        _, (held,) = join([shares], (1,), tuple(inverses), False)
        inverses += [preload(child_inverse, k, (held,)) for k in range(1, kids)]
        beside, across = to_col(held), to_row(held, 2)
        cut = held.shape[0] // 2
        _, near = join([[held, beside]], (1,), tuple(inverses[1:]), False, 4)
        near_other = [to_row(x, 1) for x in near]
        rest = [to_col(across[:cut]), to_row(beside[cut:], 2)]
        for k in range(kids):
            picked[k] = gather([near, near_other], [0, 1], maps, k, row_1, order, None, (across,))
        _, far = join([[across, *rest]], (1,), tuple(picked), False)
        far_other = [to_row(x, 1) for x in far]
        root_solution = reorder(near, order)
        last_blocks, last_at = [far, far_other], [2, 3]
    else:
        inverses = [preload(child_inverse, k, (part,)) for k in range(kids)]
        for bit in bits(cols):
            part = add(part, to_col(part, bit)).astype(BF16)
        own = jnp.zeros((case_count, root_rows), BF16)
        for j in range(leafs):
            got = part if j == 0 else to_leaf(part, j)
            own = lax.dynamic_update_slice_in_dim(
                own, got, lax.bitwise_xor(leaf, j) * (case_count // leafs), 0
            )
        root_solution = own.astype(F32)
        groups = [own]
        for bit in [1, *bits(rows)[1:]]:
            got = to_row(jnp.stack(groups), bit)
            groups += [got[i] for i in range(len(groups))]
        last_blocks, last_at = [[g] for g in groups], list(range(rows))

    begun = []
    after = ()
    for k in range(kids):
        full = gather(last_blocks, last_at, maps, k, row_1, order, picked[k], after)
        sent = held_nn(full, panels[k], core, 1, pieces_of(k))
        kept = held_nn(full, panels[k], core, 0, 1, sent[:1])
        begun.append(core_sum(kept[0], sent))
        after = begun[k][1:]
    solved = None
    chunks = 2 if slot_rows % 256 == 0 else 1
    after = (root_solution, *after)
    for k in range(kids):
        _, rounded = row_end(*begun[k], after, forward[k], False, pieces_of(k == 0))
        pair = halves(rounded)
        for at in range(chunks):
            out = held_nt(*pair, inverses[k], core, at, chunks)
            after = (out,)
            terms = [out, to_col(out)]
            for bit in bits(cols)[1:]:
                out = add(*terms).astype(BF16)
                terms = [out, to_col(out, bit)]
            solved = finish(solved, kids, k, at, chunks, terms)
    return (solved, root_solution)


def solution(mesh):
    sizes = tuple(mesh.shape[a] for a in ("leaf", "row", "col"))
    in_specs = (
        P("leaf", None, "row"),
        P("leaf", "row", "col"),
        P("leaf", "row", "col"),
        P("leaf", None),
        P(None, "row"),
        P("row", "col"),
    )
    out_specs = (P("leaf", None, "row"), P(None, "row"))
    return jax.shard_map(
        functools.partial(on_device, sizes),
        mesh=mesh,
        in_specs=in_specs,
        out_specs=out_specs,
        check_vma=False,
    )
```

time: 197 us -> 170 us (0.86)
  waiting for transfers between devices: 70.5 us -> 33.6 us
  starting transfers between devices: 32.8 us -> 40.3 us
  local copies, waits for them, and re-layouts: 2.31 us -> 6.33 us
    ppermute x37 -> x53, waiting for transfers between devices: 70.5 us -> 33.6 us  [swap(): return lax.ppermute(x, axis, [(i, i ^ bit) for i in range(size)])]
    ppermute x37 -> x53, starting transfers between devices: 32.8 us -> 40.3 us  [swap(): return lax.ppermute(x, axis, [(i, i ^ bit) for i in range(size)])]
    unnamed x13 -> x18, local copies, waits for them, and re-layouts: 2.19 us -> 5.5 us
    pallas_call x24 -> x44, Pallas kernels: 66.1 us -> 64 us  [the longest x7 25.8 us: preload(): pl.pallas_call(functools.partial(preload_kernel, child), in_specs=[pl.Blo...]
  transfers between devices with their start and end apart: 37 -> 53, of which waited for: 24 -> 25; matrix products, arithmetic and copies ran while one was open for 0% -> 1% of each run, Pallas kernels for 22% -> 40%
where the time goes in v3:
time: 170 us; the launch traced here: 169 us
  Pallas kernels  86.2 us (51%)
  starting transfers between devices  40.3 us (24%)
  waiting for transfers between devices  33.6 us (20%)
  local copies, waits for them, and re-layouts  6.33 us (4%)
    ppermute x53, starting transfers between devices, swap(): return lax.ppermute(x, axis, [(i, i ^ bit) for i in range(size)])  40.3 us
    ppermute x53, waiting for transfers between devices, swap(): return lax.ppermute(x, axis, [(i, i ^ bit) for i in range(size)])  33.6 us
    pallas_call x7, Pallas kernels, preload(): pl.pallas_call(functools.partial(preload_kernel, child), in_specs=[pl.Blo...  25.8 us
    pallas_call x7, Pallas kernels, held_nt(): pl.pallas_call(kernel, in_specs=[SCALARS] + [WHOLE] * (len(mine) + len(ot...  15.3 us
    pallas_call x4, Pallas kernels, nn(): pl.pallas_call(kernel, grid_spec=pltpu.PrefetchScalarGridSpec(num_scalar_...  12.2 us
    pallas_call x4, Pallas kernels, scatter(): pl.pallas_call(functools.partial(scatter_kernel, block_rows, tile, odd, c...  11.7 us
    pallas_call x4, Pallas kernels, gather(): pl.pallas_call(functools.partial(gather_kernel, block_rows, tile, which,...  9.88 us
    unnamed x18, local copies, waits for them, and re-layouts  5.5 us
  transfers between devices with their start and end apart: 53, of which 25 were waited for; matrix products, arithmetic and copies ran while one was open for 1% of the time, Pallas kernels for 40%

profile of v3, /device:TPU:0, one launch (start us, length us, event | category | flops | bytes accessed | tf_op | source)
XLA Modules:
  0.0 169.4 jit_solution(3663278723574322199)
XLA Ops:
  0.7 3.1 %shard_map.78.rest_0_ = bf16[128,1536]{1,0:T(8,128)(2,1)S(1)} custom-call(s32[1]{0:T(128)} %bitcast.half_ref, bf16[2,128,1536]{2,1,0:T(8,128)(2,1)} %x_ref.7, bf16[2,1536,3072]{2,1,0:T(8,128)(2,1)} %w_ref.19), custom_call_target="tpu_custom_call" | custom-call | flops 9437184 | bytes 73728 | tf_op jit(solution)/shard_map/pallas_call | solution.py:93
  4.3 3.0 %shard_map.79.refs_0_ = f32[128,1536]{1,0:T(8,128)S(1)} custom-call(s32[1]{0:T(128)} %bitcast.half_ref, bf16[2,128,1536]{2,1,0:T(8,128)(2,1)} %x_ref.7, bf16[2,1536,3072]{2,1,0:T(8,128)(2,1)} %w_ref.19, bf16[128,1536]{1,0:T(8,128)(2,1)S(1)} %shard_map.78.rest_0_), custom_call_target="tpu_custom_call" | custom-call | flops 9437184 | bytes 73728 | tf_op jit(solution)/shard_map/pallas_call | solution.py:93
  7.4 2.6 %collective-permute-start.6 = (bf16[128,1536]{1,0:T(8,128)(2,1)S(1)}, bf16[128,1536]{1,0:T(8,128)(2,1)S(1)}, u32[]{:S(2)}, u32[]{:S(2)}) collective-permute-start(bf16[128,1536]{1,0:T(8,128)(2,1)S(1)} %get-tuple-element.36.rest_1_), channel_id=1, source_target_pairs={{0,4},{2,6},{4,0},{6,2},{1,5},{3,7},{5,1},{7,3},{8,12},{10,14},{12... | collective-permute-start | bytes 1179656 | tf_op jit(solution)/shard_map/ppermute | solution.py:391
  10.0 3.0 %shard_map.77 = (bf16[32,1536]{1,0:T(8,128)(2,1)S(1)}, bf16[32,1536]{1,0:T(8,128)(2,1)S(1)}, bf16[32,1536]{1,0:T(8,128)(2,1)S(1)}, bf16[32,1536]{1,0:T(8,128)(2,1)S(1)}) custom-call(s32[1]{0:T(128)} %bitcast.half_ref, bf16[2,128,1536]{2,1,0:T(8,128)(2,1)} %x_ref.7, bf16[2,1536,3072]{2,1,0:T(8,128)(2,1)} %w_ref.19), custom_call_target="tpu_custom_call" | custom-call | flops 9437184 | bytes 73728 | tf_op jit(solution)/shard_map/pallas_call | solution.py:93
  14.2 3.0 %shard_map.81.refs_0_ = f32[128,1536]{1,0:T(8,128)S(1)} custom-call(s32[1]{0:T(128)} %bitcast.half_ref, bf16[2,128,1536]{2,1,0:T(8,128)(2,1)} %x_ref.7, bf16[2,1536,3072]{2,1,0:T(8,128)(2,1)} %w_ref.19, bf16[32,1536]{1,0:T(8,128)(2,1)S(1)} %get-tuple-element.35.rest_0_, bf16[128,1536]{1,0:T(8,128)(2,1)S(1)} %get-tuple-element.36.rest_1_), custom_call_target="tpu_custom_call" | custom-call | flops 9437184 | bytes 73728 | tf_op jit(solution)/shard_map/pallas_call | solution.py:93
  19.6 3.7 %shard_map.84.rest_0_.refs_8_ = bf16[1536,3072]{1,0:T(8,128)(2,1)S(1)} custom-call(bf16[2,1536,3072]{2,1,0:T(8,128)(2,1)} %w_ref.17, bf16[128,1536]{1,0:T(8,128)(2,1)S(1)} %get-tuple-element.41.rest_0_), custom_call_target="tpu_custom_call" | custom-call | bytes 147456 | tf_op jit(solution)/shard_map/pallas_call | solution.py:52
  23.3 3.7 %shard_map.85.refs_2_ = bf16[1536,3072]{1,0:T(8,128)(2,1)S(1)} custom-call(bf16[2,1536,3072]{2,1,0:T(8,128)(2,1)} %w_ref.17, bf16[1536,3072]{1,0:T(8,128)(2,1)S(1)} %shard_map.84.rest_0_.refs_8_), custom_call_target="tpu_custom_call" | custom-call | bytes 147456 | tf_op jit(solution)/shard_map/pallas_call | solution.py:52
  30.9 3.2 %shard_map.87.refs_3_ = bf16[128,1536]{1,0:T(8,128)(2,1)S(1)} custom-call(s32[1]{0:T(128)} %bitcast.half_ref, bf16[32,1536]{1,0:T(8,128)(2,1)S(1)} %get-tuple-element.43.refs_0_, bf16[32,1536]{1,0:T(8,128)(2,1)S(1)} %get-tuple-element.44.refs_1_, bf16[32,1536]{1,0:T(8,128)(2,1)S(1)} %get-tuple-element.45.refs_2_, ...), custom_call_target="tpu_custom_call" | custom-call | flops 18874368 | bytes 147456 | tf_op jit(solution)/shard_map/pallas_call | solution.py:158
  34.1 2.7 %shard_map.88.refs_2_.refs_4_ = bf16[2,128,1536]{2,1,0:T(8,128)(2,1)S(1)} custom-call(s32[1]{0:T(128)} %bitcast.1.refs_0_.row_ref, s32[8]{0:T(128)S(1)} %iota_xor_fusion.refs_1_.order_ref, s16[2,1536,128]{2,1,0:T(8,128)(2,1)S(1)} %shard_map.83.refs_2_, bf16[128,1536]{1,0:T(8,128)(2,1)S(1)} %shard_map.87.refs_3_), custom_call_target="tpu_custom_call" | custom-call | flops 18874368 | bytes 24576 | tf_op jit(solution)/shard_map/pallas_call | solution.py:242
  40.5 3.2 %shard_map.90.refs_3_ = bf16[128,1536]{1,0:T(8,128)(2,1)S(1)} custom-call(s32[1]{0:T(128)} %bitcast.half_ref, bf16[128,1536]{1,0:T(8,128)(2,1)S(1)} %get-tuple-element.48.refs_0_, bf16[128,1536]{1,0:T(8,128)(2,1)S(1)} %collective-permute-done.11.refs_1_, bf16[1536,3072]{1,0:T(8,128)(2,1)S(1)} %shard_map.85.refs_2_), custom_call_target="tpu_custom_call" | custom-call | flops 18874368 | bytes 147456 | tf_op jit(solution)/shard_map/pallas_call | solution.py:158
  43.7 3.5 %shard_map.93 = bf16[2,128,1536]{2,1,0:T(8,128)(2,1)} custom-call(s32[1]{0:T(128)} %bitcast.1.refs_0_.row_ref, s32[8]{0:T(128)S(1)} %iota_xor_fusion.refs_1_.order_ref, s16[2,1536,128]{2,1,0:T(8,128)(2,1)S(1)} %shard_map.83.refs_2_, bf16[128,1536]{1,0:T(8,128)(2,1)S(1)} %shard_map.90.refs_3_, bf16[2,128,1536]{2,1,0:T(8,128)(2,1)S(1)} %shard_map.88.refs_2_.refs_4_), custom_call_target="tpu_custom_call" | custom-call | flops 18874368 | bytes 24576 | tf_op jit(solution)/shard_map/pallas_call | solution.py:242
  47.5 2.7 %shard_map.91.refs_4_ = bf16[2,128,1536]{2,1,0:T(8,128)(2,1)S(1)} custom-call(s32[1]{0:T(128)} %bitcast.1.refs_0_.row_ref, s32[8]{0:T(128)S(1)} %iota_xor_fusion.refs_1_.order_ref, s16[2,1536,128]{2,1,0:T(8,128)(2,1)S(1)} %shard_map.83.refs_2_, bf16[128,1536]{1,0:T(8,128)(2,1)S(1)} %shard_map.87.refs_3_), custom_call_target="tpu_custom_call" | custom-call | flops 18874368 | bytes 24576 | tf_op jit(solution)/shard_map/pallas_call | solution.py:242
  50.2 2.9 %shard_map.92 = bf16[2,128,1536]{2,1,0:T(8,128)(2,1)S(1)} custom-call(s32[1]{0:T(128)} %bitcast.1.refs_0_.row_ref, s32[8]{0:T(128)S(1)} %iota_xor_fusion.refs_1_.order_ref, s16[2,1536,128]{2,1,0:T(8,128)(2,1)S(1)} %shard_map.83.refs_2_, bf16[128,1536]{1,0:T(8,128)(2,1)S(1)} %shard_map.90.refs_3_, bf16[2,128,1536]{2,1,0:T(8,128)(2,1)S(1)} %shard_map.91.refs_4_), custom_call_target="tpu_custom_call" | custom-call | flops 18874368 | bytes 24576 | tf_op jit(solution)/shard_map/pallas_call | solution.py:242
  54.6 2.0 %collective-permute-start.13 = (bf16[2,64,768]{2,1,0:T(8,128)(2,1)S(1)}, bf16[2,64,768]{2,1,0:T(8,128)(2,1)S(1)}, u32[]{:S(2)}, u32[]{:S(2)}) collective-permute-start(bf16[2,64,768]{2,1,0:T(8,128)(2,1)S(1)} %slice.69), channel_id=1, source_target_pairs={{0,1},{1,0},{2,3},{3,2},{4,5},{5,4},{6,7},{7,6},{8,9},{9,8},{10,11... | collective-permute-start | bytes 589832 | tf_op jit(solution)/shard_map/ppermute | solution.py:391
  56.6 1.6 collective-permute-start.15
  58.2 3.6 %collective-permute-done.13 = bf16[2,64,768]{2,1,0:T(8,128)(2,1)S(1)} collective-permute-done((bf16[2,64,768]{2,1,0:T(8,128)(2,1)S(1)}, bf16[2,64,768]{2,1,0:T(8,128)(2,1)S(1)}, u32[]{:S(2)}, u32[]{:S(2)}) %collective-permute-start.13) | collective-permute-done | bytes 196640 | tf_op jit(solution)/shard_map/ppermute | solution.py:391
  61.9 1.8 %collective-permute-start.14 = (bf16[64,768]{1,0:T(8,128)(2,1)S(1)}, bf16[64,768]{1,0:T(8,128)(2,1)S(1)}, u32[]{:S(2)}, u32[]{:S(2)}) collective-permute-start(bf16[64,768]{1,0:T(8,128)(2,1)S(1)} %fusion.3), channel_id=1, source_target_pairs={{0,4},{2,6},{4,0},{6,2},{1,5},{3,7},{5,1},{7,3},{8,12},{10,14},{12... | collective-permute-start | bytes 294920 | tf_op jit(solution)/shard_map/ppermute | solution.py:391
  63.8 1.6 collective-permute-start.16
  66.6 1.9 %collective-permute-done.16 = bf16[64,768]{1,0:T(8,128)(2,1)S(1)} collective-permute-done((bf16[64,768]{1,0:T(8,128)(2,1)S(1)}, bf16[64,768]{1,0:T(8,128)(2,1)S(1)}, u32[]{:S(2)}, u32[]{:S(2)}) %collective-permute-start.16) | collective-permute-done | bytes 98336 | tf_op jit(solution)/shard_map/ppermute | solution.py:391
  68.5 1.6 collective-permute-start.17
  70.2 2.6 %collective-permute-start.18 = (bf16[16,1536]{1,0:T(8,128)(2,1)S(1)}, bf16[16,1536]{1,0:T(8,128)(2,1)S(1)}, u32[]{:S(2)}, u32[]{:S(2)}) collective-permute-start(bf16[16,1536]{1,0:T(8,128)(2,1)S(1)} %get-tuple-element.71.rest_1_), channel_id=1, source_target_pairs={{0,16},{8,24},{16,0},{24,8},{1,17},{9,25},{17,1},{25,9},{2,18},{10... | collective-permute-start | bytes 147464 | tf_op jit(solution)/shard_map/ppermute | solution.py:391
  73.0 3.7 %shard_map.94.refs_5_.w_ref.refs_2_ = bf16[1536,3072]{1,0:T(8,128)(2,1)S(1)} custom-call(bf16[1,1536,3072]{2,1,0:T(8,128)(2,1)} %bitcast.15, bf16[16,1536]{1,0:T(8,128)(2,1)S(1)} %get-tuple-element.72.rest_0_, bf16[16,1536]{1,0:T(8,128)(2,1)S(1)} %get-tuple-element.71.rest_1_, bf16[16,1536]{1,0:T(8,128)(2,1)S(1)} %get-tuple-element.70.rest_2_), custom_call_target="tpu_custom_call" | custom-call | bytes 147456 | tf_op jit(solution)/shard_map/pallas_call | solution.py:52
  76.7 2.0 %collective-permute-done.19.refs_4_ = bf16[16,1536]{1,0:T(8,128)(2,1)S(1)} collective-permute-done((bf16[16,1536]{1,0:T(8,128)(2,1)S(1)}, bf16[16,1536]{1,0:T(8,128)(2,1)S(1)}, u32[]{:S(2)}, u32[]{:S(2)}) %collective-permute-start.19) | collective-permute-done | bytes 49184 | tf_op jit(solution)/shard_map/ppermute | solution.py:391
  78.7 1.6 collective-permute-start.20
  80.3 2.6 %collective-permute-done.20 = bf16[16,1536]{1,0:T(8,128)(2,1)S(1)} collective-permute-done((bf16[16,1536]{1,0:T(8,128)(2,1)S(1)}, bf16[16,1536]{1,0:T(8,128)(2,1)S(1)}, u32[]{:S(2)}, u32[]{:S(2)}) %collective-permute-start.20) | collective-permute-done | bytes 49184 | tf_op jit(solution)/shard_map/ppermute | solution.py:391
  86.4 3.7 %shard_map.99.refs_2_.w_ref = bf16[1536,3072]{1,0:T(8,128)(2,1)S(1)} custom-call(bf16[2,1536,3072]{2,1,0:T(8,128)(2,1)} %w_ref.17, bf16[32,1536]{1,0:T(8,128)(2,1)S(1)} %get-tuple-element.50.rest_0_), custom_call_target="tpu_custom_call" | custom-call | bytes 147456 | tf_op jit(solution)/shard_map/pallas_call | solution.py:52
  91.5 2.8 %shard_map.101.rest_0_ = bf16[32,1536]{1,0:T(8,128)(2,1)S(1)} custom-call(s32[1]{0:T(128)} %bitcast.half_ref, bf16[32,1536]{1,0:T(8,128)(2,1)S(1)} %shard_map.100.refs_0_, bf16[32,1536]{1,0:T(8,128)(2,1)S(1)} %collective-permute-done.23.refs_1_, bf16[1536,3072]{1,0:T(8,128)(2,1)S(1)} %shard_map.94.refs_5_.w_ref.refs_2_), custom_call_target="tpu_custom_call" | custom-call | flops 4718592 | bytes 147456 | tf_op jit(solution)/shard_map/pallas_call | solution.py:158
  94.3 1.5 collective-permute-start.24
  95.9 3.7 %shard_map.102.refs_2_.w_ref = bf16[1536,3072]{1,0:T(8,128)(2,1)S(1)} custom-call(bf16[2,1536,3072]{2,1,0:T(8,128)(2,1)} %w_ref.17, bf16[32,1536]{1,0:T(8,128)(2,1)S(1)} %shard_map.101.rest_0_), custom_call_target="tpu_custom_call" | custom-call | bytes 147456 | tf_op jit(solution)/shard_map/pallas_call | solution.py:52
  99.7 2.2 %collective-permute-start.26 = (bf16[16,1536]{1,0:T(8,128)(2,1)S(1)}, bf16[16,1536]{1,0:T(8,128)(2,1)S(1)}, u32[]{:S(2)}, u32[]{:S(2)}) collective-permute-start(bf16[16,1536]{1,0:T(8,128)(2,1)S(1)} %shard_map.103.rest_0_.refs_0_), channel_id=1, source_target_pairs={{0,16},{8,24},{16,0},{24,8},{1,17},{9,25},{17,1},{25,9},{2,18},{10... | collective-permute-start | bytes 147464 | tf_op jit(solution)/shard_map/ppermute | solution.py:391
  101.9 2.1 %collective-permute-start.27 = (bf16[16,1536]{1,0:T(8,128)(2,1)S(1)}, bf16[16,1536]{1,0:T(8,128)(2,1)S(1)}, u32[]{:S(2)}, u32[]{:S(2)}) collective-permute-start(bf16[16,1536]{1,0:T(8,128)(2,1)S(1)} %shard_map.103.rest_0_.refs_0_), channel_id=1, source_target_pairs={{0,24},{8,16},{16,8},{24,0},{1,25},{9,17},{17,9},{25,1},{2,26},{10... | collective-permute-start | bytes 147464 | tf_op jit(solution)/shard_map/ppermute | solution.py:391
  104.1 3.7 %shard_map.104.refs_4_.refs_8_ = bf16[1536,3072]{1,0:T(8,128)(2,1)S(1)} custom-call(bf16[2,1536,3072]{2,1,0:T(8,128)(2,1)} %w_ref.19, bf16[16,1536]{1,0:T(8,128)(2,1)S(1)} %shard_map.103.rest_0_.refs_0_), custom_call_target="tpu_custom_call" | custom-call | bytes 147456 | tf_op jit(solution)/shard_map/pallas_call | solution.py:52
  109.6 3.7 %shard_map.106.refs_2_ = bf16[1536,3072]{1,0:T(8,128)(2,1)S(1)} custom-call(bf16[2,1536,3072]{2,1,0:T(8,128)(2,1)} %w_ref.19, bf16[64,1536]{1,0:T(8,128)(2,1)S(1)} %shard_map.105.rest_0_.refs_0_), custom_call_target="tpu_custom_call" | custom-call | bytes 147456 | tf_op jit(solution)/shard_map/pallas_call | solution.py:52
  116.9 2.4 %shard_map.108.refs_3_.rest_2_ = bf16[128,1536]{1,0:T(8,128)(2,1)S(1)} custom-call(s32[1]{0:T(128)} %bitcast.1.refs_0_.row_ref, s32[8]{0:T(128)S(1)} %iota_xor_fusion.refs_1_.order_ref, s32[2,1,1536]{2,1,0:T(1,128)S(1)} %reshape.9.map_ref, bf16[32,1536]{1,0:T(8,128)(2,1)S(1)} %get-tuple-element.51.rest_0_.refs_0_, ...), custom_call_target="tpu_custom_call" | custom-call | flops 18874368 | bytes 12288 | tf_op jit(solution)/shard_map/pallas_call | solution.py:299
  119.3 2.4 %shard_map.109.refs_4_.rest_2_ = bf16[128,1536]{1,0:T(8,128)(2,1)S(1)} custom-call(s32[1]{0:T(128)} %bitcast.1.refs_0_.row_ref, s32[8]{0:T(128)S(1)} %iota_xor_fusion.refs_1_.order_ref, s32[2,1,1536]{2,1,0:T(1,128)S(1)} %reshape.9.map_ref, bf16[32,1536]{1,0:T(8,128)(2,1)S(1)} %get-tuple-element.51.rest_0_.refs_0_, ...), custom_call_target="tpu_custom_call" | custom-call | flops 18874368 | bytes 12288 | tf_op jit(solution)/shard_map/pallas_call | solution.py:299
  121.9 1.7 %collective-permute-done.36.rest_1_ = bf16[128,1536]{1,0:T(8,128)(2,1)S(1)} collective-permute-done((bf16[128,1536]{1,0:T(8,128)(2,1)S(1)}, bf16[128,1536]{1,0:T(8,128)(2,1)S(1)}, u32[]{:S(2)}, u32[]{:S(2)}) %collective-permute-start.36) | collective-permute-done | bytes 393248 | tf_op jit(solution)/shard_map/ppermute | solution.py:391
  123.6 2.4 %shard_map.111.x_ref = bf16[128,1536]{1,0:T(8,128)(2,1)S(1)} custom-call(s32[1]{0:T(128)} %bitcast.1.refs_0_.row_ref, s32[8]{0:T(128)S(1)} %iota_xor_fusion.refs_1_.order_ref, s32[2,1,1536]{2,1,0:T(1,128)S(1)} %reshape.9.map_ref, bf16[128,1536]{1,0:T(8,128)(2,1)S(1)} %shard_map.110.rest_0_, bf16[128,1536]{1,0:T(8,128)(2,1)S(1)} %collective-permute-done.36.rest_1_, ...), custom_call_target="tpu_custom_call" | custom-call | flops 18874368 | bytes 12288 | tf_op jit(solution)/shard_map/pallas_call | solution.py:299
  129.7 2.7 %shard_map.115.x_ref = bf16[128,1536]{1,0:T(8,128)(2,1)S(1)} custom-call(s32[1]{0:T(128)} %bitcast.1.refs_0_.row_ref, s32[8]{0:T(128)S(1)} %iota_xor_fusion.refs_1_.order_ref, s32[2,1,1536]{2,1,0:T(1,128)S(1)} %reshape.9.map_ref, bf16[128,1536]{1,0:T(8,128)(2,1)S(1)} %shard_map.110.rest_0_, bf16[128,1536]{1,0:T(8,128)(2,1)S(1)} %collective-permute-done.36.rest_1_, ...), custom_call_target="tpu_custom_call" | custom-call | flops 18874368 | bytes 12288 | tf_op jit(solution)/shard_map/pallas_call | solution.py:299
  136.5 1.5 shard_map.119.refs_3_
  138.0 2.8 %collective-permute-done.43.refs_2_ = bf16[128,1536]{1,0:T(8,128)(2,1)S(1)} collective-permute-done((bf16[128,1536]{1,0:T(8,128)(2,1)S(1)}, bf16[128,1536]{1,0:T(8,128)(2,1)S(1)}, u32[]{:S(2)}, u32[]{:S(2)}) %collective-permute-start.43) | collective-permute-done | bytes 393248 | tf_op jit(solution)/shard_map/ppermute | solution.py:391
  144.1 1.5 shard_map.121.refs_3_.refs_0_
  145.6 2.8 %collective-permute-done.42.refs_2_ = bf16[128,1536]{1,0:T(8,128)(2,1)S(1)} collective-permute-done((bf16[128,1536]{1,0:T(8,128)(2,1)S(1)}, bf16[128,1536]{1,0:T(8,128)(2,1)S(1)}, u32[]{:S(2)}, u32[]{:S(2)}) %collective-permute-start.42) | collective-permute-done | bytes 393248 | tf_op jit(solution)/shard_map/ppermute | solution.py:391
  149.7 1.5 shard_map.125.refs_0_
  152.3 1.5 shard_map.124.refs_0_
  154.9 1.5 shard_map.123.refs_0_
  157.5 3.1 %collective-permute-done.52.refs_1_ = bf16[128,768]{1,0:T(8,128)(2,1)S(1)} collective-permute-done((bf16[128,768]{1,0:T(8,128)(2,1)S(1)}, bf16[128,768]{1,0:T(8,128)(2,1)S(1)}, u32[]{:S(2)}, u32[]{:S(2)}) %collective-permute-start.52) | collective-permute-done | bytes 196640 | tf_op jit(solution)/shard_map/ppermute | solution.py:391
  162.2 2.6 %collective-permute-done.50.refs_1_ = bf16[128,768]{1,0:T(8,128)(2,1)S(1)} collective-permute-done((bf16[128,768]{1,0:T(8,128)(2,1)S(1)}, bf16[128,768]{1,0:T(8,128)(2,1)S(1)}, u32[]{:S(2)}, u32[]{:S(2)}) %collective-permute-start.50) | collective-permute-done | bytes 196640 | tf_op jit(solution)/shard_map/ppermute | solution.py:391
  165.6 3.0 %collective-permute-done.49.refs_1_ = bf16[128,768]{1,0:T(8,128)(2,1)S(1)} collective-permute-done((bf16[128,768]{1,0:T(8,128)(2,1)S(1)}, bf16[128,768]{1,0:T(8,128)(2,1)S(1)}, u32[]{:S(2)}, u32[]{:S(2)}) %collective-permute-start.49) | collective-permute-done | bytes 196640 | tf_op jit(solution)/shard_map/ppermute | solution.py:391
  (149 shorter events, 44.3 us)
Async XLA Ops:
  3.7 3.6 %collective-permute-start = (bf16[128,1536]{1,0:T(8,128)(2,1)S(1)}, bf16[128,1536]{1,0:T(8,128)(2,1)S(1)}, u32[]{:S(2)}, u32[]{:S(2)}) collective-permute-start(bf16[128,1536]{1,0:T(8,128)(2,1)S(1)} %shard_map.78.rest_0_), channel_id=1, source_target_pairs={{0,2},{2,0},{4,6},{6,4},{1,3},{3,1},{5,7},{7,5},{8,10},{10,8},{12,... | collective-permute-start | bytes 1179656 | tf_op jit(solution)/shard_map/ppermute | solution.py:391
  7.4 19.6 %collective-permute-start.6 = (bf16[128,1536]{1,0:T(8,128)(2,1)S(1)}, bf16[128,1536]{1,0:T(8,128)(2,1)S(1)}, u32[]{:S(2)}, u32[]{:S(2)}) collective-permute-start(bf16[128,1536]{1,0:T(8,128)(2,1)S(1)} %get-tuple-element.36.rest_1_), channel_id=1, source_target_pairs={{0,4},{2,6},{4,0},{6,2},{1,5},{3,7},{5,1},{7,3},{8,12},{10,14},{12... | collective-permute-start | bytes 1179656 | tf_op jit(solution)/shard_map/ppermute | solution.py:391
  13.1 4.1 %collective-permute-start.1 = (bf16[32,1536]{1,0:T(8,128)(2,1)S(1)}, bf16[32,1536]{1,0:T(8,128)(2,1)S(1)}, u32[]{:S(2)}, u32[]{:S(2)}) collective-permute-start(bf16[32,1536]{1,0:T(8,128)(2,1)S(1)} %get-tuple-element.35.rest_0_), channel_id=1, source_target_pairs={{0,2},{2,0},{4,6},{6,4},{1,3},{3,1},{5,7},{7,5},{8,10},{10,8},{12,... | collective-permute-start | bytes 294920 | tf_op jit(solution)/shard_map/ppermute | solution.py:391
  13.3 3.9 %collective-permute-start.2 = (bf16[32,1536]{1,0:T(8,128)(2,1)S(1)}, bf16[32,1536]{1,0:T(8,128)(2,1)S(1)}, u32[]{:S(2)}, u32[]{:S(2)}) collective-permute-start(bf16[32,1536]{1,0:T(8,128)(2,1)S(1)} %get-tuple-element.37), channel_id=1, source_target_pairs={{0,2},{2,0},{4,6},{6,4},{1,3},{3,1},{5,7},{7,5},{8,10},{10,8},{12,... | collective-permute-start | bytes 294920 | tf_op jit(solution)/shard_map/ppermute | solution.py:391
  13.7 3.6 %collective-permute-start.3 = (bf16[32,1536]{1,0:T(8,128)(2,1)S(1)}, bf16[32,1536]{1,0:T(8,128)(2,1)S(1)}, u32[]{:S(2)}, u32[]{:S(2)}) collective-permute-start(bf16[32,1536]{1,0:T(8,128)(2,1)S(1)} %get-tuple-element.38), channel_id=1, source_target_pairs={{0,2},{2,0},{4,6},{6,4},{1,3},{3,1},{5,7},{7,5},{8,10},{10,8},{12,... | collective-permute-start | bytes 294920 | tf_op jit(solution)/shard_map/ppermute | solution.py:391
  13.8 3.4 %collective-permute-start.4 = (bf16[32,1536]{1,0:T(8,128)(2,1)S(1)}, bf16[32,1536]{1,0:T(8,128)(2,1)S(1)}, u32[]{:S(2)}, u32[]{:S(2)}) collective-permute-start(bf16[32,1536]{1,0:T(8,128)(2,1)S(1)} %get-tuple-element.39), channel_id=1, source_target_pairs={{0,2},{2,0},{4,6},{6,4},{1,3},{3,1},{5,7},{7,5},{8,10},{10,8},{12,... | collective-permute-start | bytes 294920 | tf_op jit(solution)/shard_map/ppermute | solution.py:391
  18.2 18.6 %collective-permute-start.5 = (bf16[128,1536]{1,0:T(8,128)(2,1)S(1)}, bf16[128,1536]{1,0:T(8,128)(2,1)S(1)}, u32[]{:S(2)}, u32[]{:S(2)}) collective-permute-start(bf16[128,1536]{1,0:T(8,128)(2,1)S(1)} %get-tuple-element.41.rest_0_), channel_id=1, source_target_pairs={{0,4},{2,6},{4,0},{6,2},{1,5},{3,7},{5,1},{7,3},{8,12},{10,14},{12... | collective-permute-start | bytes 1179656 | tf_op jit(solution)/shard_map/ppermute | solution.py:391
  28.9 1.4 collective-permute-start.7
  38.7 1.8 %collective-permute-start.11 = (bf16[128,1536]{1,0:T(8,128)(2,1)S(1)}, bf16[128,1536]{1,0:T(8,128)(2,1)S(1)}, u32[]{:S(2)}, u32[]{:S(2)}) collective-permute-start(bf16[128,1536]{1,0:T(8,128)(2,1)S(1)} %get-tuple-element.48.refs_0_), channel_id=1, source_target_pairs={{0,2},{2,0},{4,6},{6,4},{1,3},{3,1},{5,7},{7,5},{8,10},{10,8},{12,... | collective-permute-start | bytes 1179656 | tf_op jit(solution)/shard_map/ppermute | solution.py:391
  47.2 6.0 %collective-permute-start.12 = (bf16[2,128,1536]{2,1,0:T(8,128)(2,1)}, bf16[2,128,1536]{2,1,0:T(8,128)(2,1)}, u32[]{:S(2)}, u32[]{:S(2)}) collective-permute-start(bf16[2,128,1536]{2,1,0:T(8,128)(2,1)} %shard_map.93), channel_id=1, source_target_pairs={{0,2},{2,0},{4,6},{6,4},{1,3},{3,1},{5,7},{7,5},{8,10},{10,8},{12,... | collective-permute-start | bytes 2359304 | tf_op jit(solution)/shard_map/ppermute | solution.py:391
  54.6 7.2 %collective-permute-start.13 = (bf16[2,64,768]{2,1,0:T(8,128)(2,1)S(1)}, bf16[2,64,768]{2,1,0:T(8,128)(2,1)S(1)}, u32[]{:S(2)}, u32[]{:S(2)}) collective-permute-start(bf16[2,64,768]{2,1,0:T(8,128)(2,1)S(1)} %slice.69), channel_id=1, source_target_pairs={{0,1},{1,0},{2,3},{3,2},{4,5},{5,4},{6,7},{7,6},{8,9},{9,8},{10,11... | collective-permute-start | bytes 589832 | tf_op jit(solution)/shard_map/ppermute | solution.py:391
  56.6 7.1 %collective-permute-start.15 = (bf16[128,768]{1,0:T(8,128)(2,1)S(1)}, bf16[128,768]{1,0:T(8,128)(2,1)S(1)}, u32[]{:S(2)}, u32[]{:S(2)}) collective-permute-start(bf16[128,768]{1,0:T(8,128)(2,1)S(1)} %slice_bitcast_fusion.1), channel_id=1, source_target_pairs={{0,4},{2,6},{4,0},{6,2},{1,5},{3,7},{5,1},{7,3},{8,12},{10,14},{12... | collective-permute-start | bytes 589832 | tf_op jit(solution)/shard_map/ppermute | solution.py:391
  61.9 4.7 %collective-permute-start.14 = (bf16[64,768]{1,0:T(8,128)(2,1)S(1)}, bf16[64,768]{1,0:T(8,128)(2,1)S(1)}, u32[]{:S(2)}, u32[]{:S(2)}) collective-permute-start(bf16[64,768]{1,0:T(8,128)(2,1)S(1)} %fusion.3), channel_id=1, source_target_pairs={{0,4},{2,6},{4,0},{6,2},{1,5},{3,7},{5,1},{7,3},{8,12},{10,14},{12... | collective-permute-start | bytes 294920 | tf_op jit(solution)/shard_map/ppermute | solution.py:391
  63.8 4.7 %collective-permute-start.16 = (bf16[64,768]{1,0:T(8,128)(2,1)S(1)}, bf16[64,768]{1,0:T(8,128)(2,1)S(1)}, u32[]{:S(2)}, u32[]{:S(2)}) collective-permute-start(bf16[64,768]{1,0:T(8,128)(2,1)S(1)} %slice.104), channel_id=1, source_target_pairs={{0,1},{1,0},{2,3},{3,2},{4,5},{5,4},{6,7},{7,6},{8,9},{9,8},{10,11... | collective-permute-start | bytes 294920 | tf_op jit(solution)/shard_map/ppermute | solution.py:391
  68.5 8.2 %collective-permute-start.17 = (bf16[16,1536]{1,0:T(8,128)(2,1)S(1)}, bf16[16,1536]{1,0:T(8,128)(2,1)S(1)}, u32[]{:S(2)}, u32[]{:S(2)}) collective-permute-start(bf16[16,1536]{1,0:T(8,128)(2,1)S(1)} %get-tuple-element.72.rest_0_), channel_id=1, source_target_pairs={{0,8},{8,0},{16,24},{24,16},{1,9},{9,1},{17,25},{25,17},{2,10},{10... | collective-permute-start | bytes 147464 | tf_op jit(solution)/shard_map/ppermute | solution.py:391
  70.2 6.5 %collective-permute-start.18 = (bf16[16,1536]{1,0:T(8,128)(2,1)S(1)}, bf16[16,1536]{1,0:T(8,128)(2,1)S(1)}, u32[]{:S(2)}, u32[]{:S(2)}) collective-permute-start(bf16[16,1536]{1,0:T(8,128)(2,1)S(1)} %get-tuple-element.71.rest_1_), channel_id=1, source_target_pairs={{0,16},{8,24},{16,0},{24,8},{1,17},{9,25},{17,1},{25,9},{2,18},{10... | collective-permute-start | bytes 147464 | tf_op jit(solution)/shard_map/ppermute | solution.py:391
  72.8 5.9 %collective-permute-start.19 = (bf16[16,1536]{1,0:T(8,128)(2,1)S(1)}, bf16[16,1536]{1,0:T(8,128)(2,1)S(1)}, u32[]{:S(2)}, u32[]{:S(2)}) collective-permute-start(bf16[16,1536]{1,0:T(8,128)(2,1)S(1)} %get-tuple-element.70.rest_2_), channel_id=1, source_target_pairs={{0,24},{8,16},{16,8},{24,0},{1,25},{9,17},{17,9},{25,1},{2,26},{10... | collective-permute-start | bytes 147464 | tf_op jit(solution)/shard_map/ppermute | solution.py:391
  78.7 4.2 %collective-permute-start.20 = (bf16[16,1536]{1,0:T(8,128)(2,1)S(1)}, bf16[16,1536]{1,0:T(8,128)(2,1)S(1)}, u32[]{:S(2)}, u32[]{:S(2)}) collective-permute-start(bf16[16,1536]{1,0:T(8,128)(2,1)S(1)} %shard_map.95), channel_id=1, source_target_pairs={{0,1},{1,0},{2,3},{3,2},{4,5},{5,4},{6,7},{7,6},{8,9},{9,8},{10,11... | collective-permute-start | bytes 147464 | tf_op jit(solution)/shard_map/ppermute | solution.py:391
  85.1 4.9 %collective-permute-start.22 = (bf16[32,1536]{1,0:T(8,128)(2,1)S(1)}, bf16[32,1536]{1,0:T(8,128)(2,1)S(1)}, u32[]{:S(2)}, u32[]{:S(2)}) collective-permute-start(bf16[32,1536]{1,0:T(8,128)(2,1)S(1)} %get-tuple-element.50.rest_0_), channel_id=1, source_target_pairs={{0,4},{2,6},{4,0},{6,2},{1,5},{3,7},{5,1},{7,3},{8,12},{10,14},{12... | collective-permute-start | bytes 294920 | tf_op jit(solution)/shard_map/ppermute | solution.py:391
  90.1 1.4 collective-permute-start.23
  94.3 5.2 %collective-permute-start.24 = (bf16[16,1536]{1,0:T(8,128)(2,1)S(1)}, bf16[16,1536]{1,0:T(8,128)(2,1)S(1)}, u32[]{:S(2)}, u32[]{:S(2)}) collective-permute-start(bf16[16,1536]{1,0:T(8,128)(2,1)S(1)} %get-tuple-element.73), channel_id=1, source_target_pairs={{0,1},{1,0},{2,3},{3,2},{4,5},{5,4},{6,7},{7,6},{8,9},{9,8},{10,11... | collective-permute-start | bytes 147464 | tf_op jit(solution)/shard_map/ppermute | solution.py:391
  99.6 8.2 %collective-permute-start.25 = (bf16[16,1536]{1,0:T(8,128)(2,1)S(1)}, bf16[16,1536]{1,0:T(8,128)(2,1)S(1)}, u32[]{:S(2)}, u32[]{:S(2)}) collective-permute-start(bf16[16,1536]{1,0:T(8,128)(2,1)S(1)} %shard_map.103.rest_0_.refs_0_), channel_id=1, source_target_pairs={{0,8},{8,0},{16,24},{24,16},{1,9},{9,1},{17,25},{25,17},{2,10},{10... | collective-permute-start | bytes 147464 | tf_op jit(solution)/shard_map/ppermute | solution.py:391
  99.7 8.1 %collective-permute-start.26 = (bf16[16,1536]{1,0:T(8,128)(2,1)S(1)}, bf16[16,1536]{1,0:T(8,128)(2,1)S(1)}, u32[]{:S(2)}, u32[]{:S(2)}) collective-permute-start(bf16[16,1536]{1,0:T(8,128)(2,1)S(1)} %shard_map.103.rest_0_.refs_0_), channel_id=1, source_target_pairs={{0,16},{8,24},{16,0},{24,8},{1,17},{9,25},{17,1},{25,9},{2,18},{10... | collective-permute-start | bytes 147464 | tf_op jit(solution)/shard_map/ppermute | solution.py:391
  101.9 5.9 %collective-permute-start.27 = (bf16[16,1536]{1,0:T(8,128)(2,1)S(1)}, bf16[16,1536]{1,0:T(8,128)(2,1)S(1)}, u32[]{:S(2)}, u32[]{:S(2)}) collective-permute-start(bf16[16,1536]{1,0:T(8,128)(2,1)S(1)} %shard_map.103.rest_0_.refs_0_), channel_id=1, source_target_pairs={{0,24},{8,16},{16,8},{24,0},{1,25},{9,17},{17,9},{25,1},{2,26},{10... | collective-permute-start | bytes 147464 | tf_op jit(solution)/shard_map/ppermute | solution.py:391
  107.8 5.9 %collective-permute-start.30 = (bf16[64,1536]{1,0:T(8,128)(2,1)S(1)}, bf16[64,1536]{1,0:T(8,128)(2,1)S(1)}, u32[]{:S(2)}, u32[]{:S(2)}) collective-permute-start(bf16[64,1536]{1,0:T(8,128)(2,1)S(1)} %shard_map.105.rest_0_.refs_0_), channel_id=1, source_target_pairs={{0,1},{1,0},{2,3},{3,2},{4,5},{5,4},{6,7},{7,6},{8,9},{9,8},{10,11... | collective-permute-start | bytes 589832 | tf_op jit(solution)/shard_map/ppermute | solution.py:391
  108.4 6.4 %collective-permute-start.28 = (bf16[64,1536]{1,0:T(8,128)(2,1)S(1)}, bf16[64,1536]{1,0:T(8,128)(2,1)S(1)}, u32[]{:S(2)}, u32[]{:S(2)}) collective-permute-start(bf16[64,1536]{1,0:T(8,128)(2,1)S(1)} %shard_map.105.rest_0_.refs_0_), channel_id=1, source_target_pairs={{0,4},{2,6},{4,0},{6,2},{1,5},{3,7},{5,1},{7,3},{8,12},{10,14},{12... | collective-permute-start | bytes 589832 | tf_op jit(solution)/shard_map/ppermute | solution.py:391
  113.7 2.0 %collective-permute-start.32 = (bf16[32,1536]{1,0:T(8,128)(2,1)S(1)}, bf16[32,1536]{1,0:T(8,128)(2,1)S(1)}, u32[]{:S(2)}, u32[]{:S(2)}) collective-permute-start(bf16[32,1536]{1,0:T(8,128)(2,1)S(1)} %get-tuple-element.51.rest_0_.refs_0_), channel_id=1, source_target_pairs={{0,2},{2,0},{4,6},{6,4},{1,3},{3,1},{5,7},{7,5},{8,10},{10,8},{12,... | collective-permute-start | bytes 294920 | tf_op jit(solution)/shard_map/ppermute | solution.py:391
  113.8 3.1 %collective-permute-start.33 = (bf16[32,1536]{1,0:T(8,128)(2,1)S(1)}, bf16[32,1536]{1,0:T(8,128)(2,1)S(1)}, u32[]{:S(2)}, u32[]{:S(2)}) collective-permute-start(bf16[32,1536]{1,0:T(8,128)(2,1)S(1)} %get-tuple-element.52.rest_1_.refs_1_), channel_id=1, source_target_pairs={{0,2},{2,0},{4,6},{6,4},{1,3},{3,1},{5,7},{7,5},{8,10},{10,8},{12,... | collective-permute-start | bytes 294920 | tf_op jit(solution)/shard_map/ppermute | solution.py:391
  114.3 2.6 %collective-permute-start.34 = (bf16[32,1536]{1,0:T(8,128)(2,1)S(1)}, bf16[32,1536]{1,0:T(8,128)(2,1)S(1)}, u32[]{:S(2)}, u32[]{:S(2)}) collective-permute-start(bf16[32,1536]{1,0:T(8,128)(2,1)S(1)} %get-tuple-element.53.rest_2_.refs_2_), channel_id=1, source_target_pairs={{0,2},{2,0},{4,6},{6,4},{1,3},{3,1},{5,7},{7,5},{8,10},{10,8},{12,... | collective-permute-start | bytes 294920 | tf_op jit(solution)/shard_map/ppermute | solution.py:391
  114.4 2.5 %collective-permute-start.35 = (bf16[32,1536]{1,0:T(8,128)(2,1)S(1)}, bf16[32,1536]{1,0:T(8,128)(2,1)S(1)}, u32[]{:S(2)}, u32[]{:S(2)}) collective-permute-start(bf16[32,1536]{1,0:T(8,128)(2,1)S(1)} %get-tuple-element.54.rest_3_.refs_3_), channel_id=1, source_target_pairs={{0,2},{2,0},{4,6},{6,4},{1,3},{3,1},{5,7},{7,5},{8,10},{10,8},{12,... | collective-permute-start | bytes 294920 | tf_op jit(solution)/shard_map/ppermute | solution.py:391
  114.8 6.9 %collective-permute-start.29 = (bf16[32,1536]{1,0:T(8,128)(2,1)S(1)}, bf16[32,1536]{1,0:T(8,128)(2,1)S(1)}, u32[]{:S(2)}, u32[]{:S(2)}) collective-permute-start(bf16[32,1536]{1,0:T(8,128)(2,1)S(1)} %slice.83), channel_id=1, source_target_pairs={{0,1},{1,0},{2,3},{3,2},{4,5},{5,4},{6,7},{7,6},{8,9},{9,8},{10,11... | collective-permute-start | bytes 294920 | tf_op jit(solution)/shard_map/ppermute | solution.py:391
  115.7 6.0 %collective-permute-start.31 = (bf16[32,1536]{1,0:T(8,128)(2,1)S(1)}, bf16[32,1536]{1,0:T(8,128)(2,1)S(1)}, u32[]{:S(2)}, u32[]{:S(2)}) collective-permute-start(bf16[32,1536]{1,0:T(8,128)(2,1)S(1)} %slice.84), channel_id=1, source_target_pairs={{0,4},{2,6},{4,0},{6,2},{1,5},{3,7},{5,1},{7,3},{8,12},{10,14},{12... | collective-permute-start | bytes 294920 | tf_op jit(solution)/shard_map/ppermute | solution.py:391
  121.8 1.8 %collective-permute-start.36 = (bf16[128,1536]{1,0:T(8,128)(2,1)S(1)}, bf16[128,1536]{1,0:T(8,128)(2,1)S(1)}, u32[]{:S(2)}, u32[]{:S(2)}) collective-permute-start(bf16[128,1536]{1,0:T(8,128)(2,1)S(1)} %shard_map.110.rest_0_), channel_id=1, source_target_pairs={{0,2},{2,0},{4,6},{6,4},{1,3},{3,1},{5,7},{7,5},{8,10},{10,8},{12,... | collective-permute-start | bytes 1179656 | tf_op jit(solution)/shard_map/ppermute | solution.py:391
  126.8 1.8 %collective-permute-start.37 = (bf16[128,1536]{1,0:T(8,128)(2,1)S(1)}, bf16[128,1536]{1,0:T(8,128)(2,1)S(1)}, u32[]{:S(2)}, u32[]{:S(2)}) collective-permute-start(bf16[128,1536]{1,0:T(8,128)(2,1)S(1)} %shard_map.112.rest_0_), channel_id=1, source_target_pairs={{0,2},{2,0},{4,6},{6,4},{1,3},{3,1},{5,7},{7,5},{8,10},{10,8},{12,... | collective-permute-start | bytes 1179656 | tf_op jit(solution)/shard_map/ppermute | solution.py:391
  128.8 12.0 %collective-permute-start.43 = (bf16[128,1536]{1,0:T(8,128)(2,1)S(1)}, bf16[128,1536]{1,0:T(8,128)(2,1)S(1)}, u32[]{:S(2)}, u32[]{:S(2)}) collective-permute-start(bf16[128,1536]{1,0:T(8,128)(2,1)S(1)} %get-tuple-element.55.rest_3_), channel_id=1, source_target_pairs={{0,4},{2,6},{4,0},{6,2},{1,5},{3,7},{5,1},{7,3},{8,12},{10,14},{12... | collective-permute-start | bytes 1179656 | tf_op jit(solution)/shard_map/ppermute | solution.py:391
  133.2 1.9 %collective-permute-start.38 = (bf16[32,1536]{1,0:T(8,128)(2,1)S(1)}, bf16[32,1536]{1,0:T(8,128)(2,1)S(1)}, u32[]{:S(2)}, u32[]{:S(2)}) collective-permute-start(bf16[32,1536]{1,0:T(8,128)(2,1)S(1)} %get-tuple-element.56.rest_0_), channel_id=1, source_target_pairs={{0,2},{2,0},{4,6},{6,4},{1,3},{3,1},{5,7},{7,5},{8,10},{10,8},{12,... | collective-permute-start | bytes 294920 | tf_op jit(solution)/shard_map/ppermute | solution.py:391
  133.3 1.8 %collective-permute-start.39 = (bf16[32,1536]{1,0:T(8,128)(2,1)S(1)}, bf16[32,1536]{1,0:T(8,128)(2,1)S(1)}, u32[]{:S(2)}, u32[]{:S(2)}) collective-permute-start(bf16[32,1536]{1,0:T(8,128)(2,1)S(1)} %get-tuple-element.57), channel_id=1, source_target_pairs={{0,2},{2,0},{4,6},{6,4},{1,3},{3,1},{5,7},{7,5},{8,10},{10,8},{12,... | collective-permute-start | bytes 294920 | tf_op jit(solution)/shard_map/ppermute | solution.py:391
  133.8 1.3 collective-permute-start.40
  133.8 1.4 collective-permute-start.41
  135.3 13.1 %collective-permute-start.42 = (bf16[128,1536]{1,0:T(8,128)(2,1)S(1)}, bf16[128,1536]{1,0:T(8,128)(2,1)S(1)}, u32[]{:S(2)}, u32[]{:S(2)}) collective-permute-start(bf16[128,1536]{1,0:T(8,128)(2,1)S(1)} %get-tuple-element.61.refs_4_), channel_id=1, source_target_pairs={{0,4},{2,6},{4,0},{6,2},{1,5},{3,7},{5,1},{7,3},{8,12},{10,14},{12... | collective-permute-start | bytes 1179656 | tf_op jit(solution)/shard_map/ppermute | solution.py:391
  142.1 1.4 collective-permute-start.44
  142.1 1.4 collective-permute-start.45
  142.7 1.4 collective-permute-start.47
  148.6 3.8 %collective-permute-start.48 = (bf16[128,1536]{1,0:T(8,128)(2,1)S(1)}, bf16[128,1536]{1,0:T(8,128)(2,1)S(1)}, u32[]{:S(2)}, u32[]{:S(2)}) collective-permute-start(bf16[128,1536]{1,0:T(8,128)(2,1)S(1)} %shard_map.122.refs_0_), channel_id=1, source_target_pairs={{0,2},{2,0},{4,6},{6,4},{1,3},{3,1},{5,7},{7,5},{8,10},{10,8},{12,... | collective-permute-start | bytes 1179656 | tf_op jit(solution)/shard_map/ppermute | solution.py:391
  148.6 12.8 %collective-permute-start.51 = (bf16[128,768]{1,0:T(8,128)(2,1)S(1)}, bf16[128,768]{1,0:T(8,128)(2,1)S(1)}, u32[]{:S(2)}, u32[]{:S(2)}) collective-permute-start(bf16[128,768]{1,0:T(8,128)(2,1)S(1)} %shard_map.121.refs_3_.refs_0_), channel_id=1, source_target_pairs={{0,1},{1,0},{2,3},{3,2},{4,5},{5,4},{6,7},{7,6},{8,9},{9,8},{10,11... | collective-permute-start | bytes 589832 | tf_op jit(solution)/shard_map/ppermute | solution.py:391
  151.2 9.4 %collective-permute-start.52 = (bf16[128,768]{1,0:T(8,128)(2,1)S(1)}, bf16[128,768]{1,0:T(8,128)(2,1)S(1)}, u32[]{:S(2)}, u32[]{:S(2)}) collective-permute-start(bf16[128,768]{1,0:T(8,128)(2,1)S(1)} %shard_map.125.refs_0_), channel_id=1, source_target_pairs={{0,1},{1,0},{2,3},{3,2},{4,5},{5,4},{6,7},{7,6},{8,9},{9,8},{10,11... | collective-permute-start | bytes 589832 | tf_op jit(solution)/shard_map/ppermute | solution.py:391
  153.9 11.0 %collective-permute-start.50 = (bf16[128,768]{1,0:T(8,128)(2,1)S(1)}, bf16[128,768]{1,0:T(8,128)(2,1)S(1)}, u32[]{:S(2)}, u32[]{:S(2)}) collective-permute-start(bf16[128,768]{1,0:T(8,128)(2,1)S(1)} %shard_map.124.refs_0_), channel_id=1, source_target_pairs={{0,1},{1,0},{2,3},{3,2},{4,5},{5,4},{6,7},{7,6},{8,9},{9,8},{10,11... | collective-permute-start | bytes 589832 | tf_op jit(solution)/shard_map/ppermute | solution.py:391
  156.4 12.2 %collective-permute-start.49 = (bf16[128,768]{1,0:T(8,128)(2,1)S(1)}, bf16[128,768]{1,0:T(8,128)(2,1)S(1)}, u32[]{:S(2)}, u32[]{:S(2)}) collective-permute-start(bf16[128,768]{1,0:T(8,128)(2,1)S(1)} %shard_map.123.refs_0_), channel_id=1, source_target_pairs={{0,1},{1,0},{2,3},{3,2},{4,5},{5,4},{6,7},{7,6},{8,9},{9,8},{10,11... | collective-permute-start | bytes 589832 | tf_op jit(solution)/shard_map/ppermute | solution.py:391
  (14 other events, 84.8 us)

commit v4 on v3

--- a/solution.py
+++ b/solution.py
@@ -16,6 +16,7 @@
 ANY = pl.BlockSpec(memory_space=pl.ANY)
 WHOLE = pl.BlockSpec(memory_space=pltpu.VMEM)
 SCALARS = pl.BlockSpec(memory_space=pltpu.SMEM)
+IN_HBM = pl.BlockSpec(memory_space=pltpu.HBM)
 
 
 def tile_of(extent, *sizes):
@@ -41,10 +42,14 @@
     return pltpu.with_memory_space_constraint(w, pltpu.VMEM)
 
 
+TOKEN = jax.ShapeDtypeStruct((8, LANES), F32)
+
+
 def preload_kernel(child, w_ref, *rest):
-    o_ref, sem = rest[-2:]
+    o_ref, token_ref, sem = rest[-3:]
     copy = pltpu.make_async_copy(w_ref.at[child], o_ref, sem)
     copy.start()
+    token_ref[...] = jnp.zeros_like(token_ref)
     copy.wait()
 
 
@@ -52,8 +57,8 @@
     return pl.pallas_call(
         functools.partial(preload_kernel, child),
         in_specs=[pl.BlockSpec(memory_space=pltpu.HBM)] + [ANY] * len(after),
-        out_specs=WHOLE,
-        out_shape=pltpu.VMEM(w.shape[1:], w.dtype),
+        out_specs=[WHOLE, WHOLE],
+        out_shape=[pltpu.VMEM(w.shape[1:], w.dtype), TOKEN],
         scratch_shapes=[pltpu.SemaphoreType.DMA],
         compiler_params=params(),
         cost_estimate=cost(0, w[0].size * 2),
@@ -111,61 +116,79 @@
 
 
 def held_nn(x, w, core, part, pieces=1, after=()):
-    m, k = x.shape
+    m, k = sum(p.shape[0] for p in x), x[0].shape[1]
     n_half = w.shape[1] // 2
     bn = tile_of(n_half, 512, 384, 256, 128)
 
-    def kernel(half_ref, x_ref, w_ref, *rest):
-        outs = rest[len(after) :]
+    def kernel(half_ref, *refs):
+        x_value, w_ref = take_pieces(refs[: len(x)]), refs[len(x)]
+        outs = refs[len(x) + 1 + len(after) :]
         base = lax.bitwise_xor(half_ref[0], part) * n_half
-        x = x_ref[...]
+        rows = m // pieces
         for start in range(0, n_half, bn):
             cols = pl.ds(pl.multiple_of(base + start, LANES), bn)
-            product = lax.dot_general(x, w_ref[:, cols], NN, preferred_element_type=F32)
+            product = lax.dot_general(x_value, w_ref[:, cols], NN, preferred_element_type=F32)
             for i, out in enumerate(outs):
-                rows = m // pieces
                 out[:, start : start + bn] = product[i * rows : (i + 1) * rows].astype(out.dtype)
 
     return pl.pallas_call(
         kernel,
-        in_specs=[SCALARS, WHOLE, WHOLE] + [ANY] * len(after),
+        in_specs=[SCALARS] + [WHOLE] * (len(x) + 1) + [ANY] * len(after),
         out_specs=[WHOLE] * pieces,
         out_shape=[jax.ShapeDtypeStruct((m // pieces, n_half), BF16 if part else F32)] * pieces,
         compiler_params=params(),
         cost_estimate=cost(2 * m * k * n_half, 2 * k * n_half),
-    )(core, x, in_vmem(w), *after)
-
-
-def held_nt(mine, other, w, core, chunk=0, chunks=1, after=()):
+    )(core, *x, in_vmem(w), *after)
+
+
+def held_nt(mine, other, w, core, chunk=0, chunks=1, pieces=1, bring=None, after=()):
     m = sum(x.shape[0] for x in mine)
     k_half = mine[0].shape[1]
     u = w.shape[0] // chunks
     bu = tile_of(u, 512, 384, 256, 128)
     first = chunk * u
+    extra = [] if bring is None else [in_hbm(bring[0])]
 
     def kernel(half_ref, *refs):
-        a = take_pieces(refs[: len(mine)])
-        b = take_pieces(refs[len(mine) : len(mine) + len(other)])
-        w_ref, o_ref = refs[len(mine) + len(other)], refs[-1]
+        at = len(mine) + len(other)
+        a, b, w_ref = take_pieces(refs[: len(mine)]), take_pieces(refs[len(mine) : at]), refs[at]
+        outs = refs[at + 1 + len(extra) + len(after) :]
+        outs, sem = outs[:-1], outs[-1]
+        if extra:
+            brought = pltpu.make_async_copy(refs[at + 1].at[bring[1]], outs[-1], sem)
+            brought.start()
+            outs = outs[:-1]
         low = half_ref[0] == 0
         left, right = jnp.where(low, a, b), jnp.where(low, b, a)
+        rows = m // pieces
         for start in range(0, u, bu):
             at = slice(first + start, first + start + bu)
             total = lax.dot_general(left, w_ref[at, :k_half], NT, preferred_element_type=F32)
             total += lax.dot_general(right, w_ref[at, k_half:], NT, preferred_element_type=F32)
-            o_ref[:, start : start + bu] = total.astype(o_ref.dtype)
-
+            for i, out in enumerate(outs):
+                out[:, start : start + bu] = total[i * rows : (i + 1) * rows].astype(out.dtype)
+        if extra:
+            brought.wait()
+
+    shapes = [jax.ShapeDtypeStruct((m // pieces, u), BF16)] * pieces
+    if extra:
+        shapes.append(pltpu.VMEM(bring[0].shape[1:], bring[0].dtype))
     return pl.pallas_call(
         kernel,
-        in_specs=[SCALARS] + [WHOLE] * (len(mine) + len(other) + 1) + [ANY] * len(after),
-        out_specs=WHOLE,
-        out_shape=jax.ShapeDtypeStruct((m, u), BF16),
+        in_specs=[SCALARS]
+        + [WHOLE] * (len(mine) + len(other) + 1)
+        + [IN_HBM] * len(extra)
+        + [ANY] * len(after),
+        out_specs=[WHOLE] * len(shapes),
+        out_shape=shapes,
+        scratch_shapes=[pltpu.SemaphoreType.DMA],
         compiler_params=params(),
         cost_estimate=cost(4 * m * k_half * u, 4 * k_half * u),
-    )(core, *mine, *other, in_vmem(w), *after)
-
-
-def spread_kernel(map_ref, o_ref):
+    )(core, *mine, *other, in_vmem(w), *extra, *after)
+
+
+def spread_kernel(row_ref, map_ref, *rest):
+    o_ref = rest[-1]
     u = map_ref.shape[2]
     step = tile_of(u, LANES)
     for start in range(0, u, step):
@@ -173,23 +196,26 @@
         o_ref[0, start : start + step, :] = jnp.broadcast_to(row, (LANES, step)).T.astype(I16)
 
 
-def spread(maps):
-    kids, _, u = maps.shape
+def spread(maps, row, u, after=()):
+    kids = maps.shape[0]
     return pl.pallas_call(
         spread_kernel,
-        grid=(kids,),
-        in_specs=[pl.BlockSpec((1, 1, u), lambda k: (k, 0, 0))],
-        out_specs=pl.BlockSpec((1, u, LANES), lambda k: (k, 0, 0)),
+        grid_spec=pltpu.PrefetchScalarGridSpec(
+            num_scalar_prefetch=1,
+            grid=(kids,),
+            in_specs=[pl.BlockSpec((1, 1, u), lambda k, r: (k, 0, r[0]))] + [ANY] * len(after),
+            out_specs=pl.BlockSpec((1, u, LANES), lambda k, r: (k, 0, 0)),
+        ),
         out_shape=jax.ShapeDtypeStruct((kids, u, LANES), I16),
         compiler_params=params(),
         cost_estimate=cost(kids * u * LANES, 2 * kids * u * LANES),
-    )(maps)
+    )(row, maps, *after)
 
 
 def store_in_order(order_ref, chunk, store, value):
     for i in range(value.shape[0] // chunk):
         store(
-            pl.ds(pl.multiple_of(order_ref[i] * chunk, chunk), chunk),
+            pl.ds(pl.multiple_of(lax.bitwise_xor(order_ref[0], i) * chunk, chunk), chunk),
             value[i * chunk : (i + 1) * chunk],
         )
 
@@ -229,7 +255,7 @@
     m, u = upd.shape
     tile = tile_of(block_rows, 768, 512, 384, 256, 128)
     count = rows_count // 2
-    chunk = m // order.shape[0]
+    chunk = m // order[1]
     block = pl.BlockSpec((1, m, tile), lambda j, t, r, o: (j, 0, t))
     in_specs = [
         pl.BlockSpec((1, u, LANES), lambda j, t, r, o: (child, 0, 0)),
@@ -250,10 +276,16 @@
         out_shape=jax.ShapeDtypeStruct((count, m, block_rows), BF16),
         compiler_params=params(),
         cost_estimate=cost(2 * m * u * count * block_rows, 4 * m * count * block_rows),
-    )(row, order, *args)
-
-
-def gather_kernel(block_rows, tile, which, counts, chunk, added, row_ref, order_ref, map_ref, *rest):
+    )(row, order[0], *args)
+
+
+def gather_kernel(block_rows, tile, which, counts, chunk, added, steps, bring, row_ref, order_ref, map_ref, *rest):
+    rest, sem = rest[:-1], rest[-1]
+    if bring is not None:
+        source, target = rest[-3 - bring[1]], rest[-1]
+        rest = rest[:-1]
+        brought = pltpu.make_async_copy(source.at[bring[0]], target, sem)
+        pl.when(pl.program_id(0) == 0)(brought.start)
     o_ref = rest[-1]
     slot_map = map_ref[0]
     total, at = None, 0
@@ -276,17 +308,19 @@
         o_ref[ds, :] = value.astype(o_ref.dtype)
 
     store_in_order(order_ref, chunk, store, total)
-
-
-def gather(blocks, which, maps, child, row, order, before, after=()):
+    if bring is not None:
+        pl.when(pl.program_id(0) == steps - 1)(brought.wait)
+
+
+def gather(blocks, which, maps, u, child, row, order, before, bring=None, after=()):
     m = sum(p.shape[0] for p in blocks[0])
     block_rows = blocks[0][0].shape[1]
-    u = maps.shape[2]
     tile = tile_of(block_rows, 512, 384, 256, 128)
     bu = tile_of(u, 512, 384, 256, 128)
-    chunk = m // order.shape[0]
+    chunk = m // order[1]
     counts = [len(b) for b in blocks]
-    in_specs = [pl.BlockSpec((1, 1, bu), lambda i, r, o: (child, 0, i))]
+    steps = u // bu
+    in_specs = [pl.BlockSpec((1, 1, bu), lambda i, r, o: (child, 0, r[0] * steps + i))]
     args = [maps]
     for p in (p for b in blocks for p in b):
         in_specs.append(pl.BlockSpec(p.shape, lambda i, r, o: (0, 0)))
@@ -295,20 +329,38 @@
     if before is not None:
         in_specs.append(out_block)
         args.append(before)
+    if bring is not None:
+        in_specs.append(IN_HBM)
+        args.append(in_hbm(bring[0]))
     in_specs += [ANY] * len(after)
+    shapes, out_specs = [jax.ShapeDtypeStruct((m, u), BF16)], [out_block]
+    if bring is not None:
+        shapes.append(pltpu.VMEM(bring[0].shape[1:], bring[0].dtype))
+        out_specs.append(WHOLE)
     return pl.pallas_call(
         functools.partial(
-            gather_kernel, block_rows, tile, which, counts, chunk, before is not None
+            gather_kernel, block_rows,
+            tile,
+            which,
+            counts,
+            chunk,
+            before is not None,
+            steps,
+            None if bring is None else (bring[1], len(after)),
         ),
         grid_spec=pltpu.PrefetchScalarGridSpec(
-            num_scalar_prefetch=2, grid=(u // bu,), in_specs=in_specs, out_specs=out_block
+            num_scalar_prefetch=2,
+            grid=(steps,),
+            in_specs=in_specs,
+            out_specs=out_specs,
+            scratch_shapes=[pltpu.SemaphoreType.DMA],
         ),
-        out_shape=jax.ShapeDtypeStruct((m, u), BF16),
+        out_shape=shapes,
         compiler_params=params(),
         cost_estimate=cost(
             2 * m * u * len(blocks) * block_rows, 2 * m * len(blocks) * block_rows
         ),
-    )(row, order, *args, *after)
+    )(row, order[0], *args, *after)
 
 
 def finish(held, kids, child, chunk, chunks, terms):
@@ -320,15 +372,16 @@
         total = refs[0][...].astype(F32)
         for ref in refs[1 : len(terms)]:
             total += ref[...].astype(F32)
-        refs[-1][0] = total
-
-    extra = () if held is None else (held,)
+        refs[-2][0] = total
+        refs[-1][...] = jnp.zeros_like(refs[-1])
+
+    extra = () if held is None else (in_hbm(held),)
     return pl.pallas_call(
         kernel,
         grid=(1,),
         in_specs=[whole] * len(terms) + [ANY] * len(extra),
-        out_specs=place,
-        out_shape=jax.ShapeDtypeStruct((kids, m, n * chunks), F32),
+        out_specs=[place, pl.BlockSpec(TOKEN.shape, lambda i: (0, 0))],
+        out_shape=[pltpu.HBM((kids, m, n * chunks), F32), TOKEN],
         input_output_aliases={len(terms): 0} if extra else {},
         compiler_params=params(),
         cost_estimate=cost(m * n, 8 * m * n),
@@ -337,22 +390,25 @@
 
 def reorder(pieces, order):
     m, n = sum(p.shape[0] for p in pieces), pieces[0].shape[1]
-    chunk = m // order.shape[0]
+    chunk = m // order[1]
 
     def kernel(order_ref, *refs):
+        *inputs, o_ref, token_ref = refs
+
         def store(ds, value):
-            refs[-1][ds, :] = value
-
-        store_in_order(order_ref, chunk, store, take_pieces(refs[:-1]).astype(F32))
+            o_ref[ds, :] = value
+
+        store_in_order(order_ref, chunk, store, take_pieces(inputs).astype(F32))
+        token_ref[...] = jnp.zeros_like(token_ref)
 
     return pl.pallas_call(
         kernel,
         in_specs=[SCALARS] + [WHOLE] * len(pieces),
-        out_specs=WHOLE,
-        out_shape=jax.ShapeDtypeStruct((m, n), F32),
+        out_specs=[WHOLE, WHOLE],
+        out_shape=[jax.ShapeDtypeStruct((m, n), F32), TOKEN],
         compiler_params=params(),
         cost_estimate=cost(m * n, 6 * m * n),
-    )(order, *pieces)
+    )(order[0], *pieces)
 
 
 def join(terms, signs, after=(), wide=True, narrow=1):
@@ -387,6 +443,81 @@
     return (outs[0] if wide else None), (outs[1:] if wide else outs)
 
 
+def call_whole(kernel, args, shapes, scalars=(), after=()):
+    def body(*refs):
+        count = len(scalars) + len(args)
+        kernel(*refs[:count], *refs[count + len(after) :])
+
+    return pl.pallas_call(
+        body,
+        in_specs=[SCALARS] * len(scalars) + [WHOLE] * len(args) + [ANY] * len(after),
+        out_specs=[WHOLE] * len(shapes),
+        out_shape=[jax.ShapeDtypeStruct(*s) for s in shapes],
+        compiler_params=params(),
+        cost_estimate=cost(args[0].size, 8 * args[0].size),
+    )(*scalars, *args, *after)
+
+
+def cut_core_sum(kept, got):
+    _, m, n = kept.shape
+    half, cut = m // 2, n // 2
+
+    def kernel(kept_ref, got_ref, left_ref, left_away, right_ref, right_away):
+        for j in range(2):
+            left = kept_ref[j, :, :cut].astype(F32) + got_ref[j, :, :cut].astype(F32)
+            left_ref[j * half : (j + 1) * half] = left[:half]
+            left_away[j * half : (j + 1) * half] = left[half:].astype(BF16)
+            right = kept_ref[j, :, cut:].astype(F32) + got_ref[j, :, cut:].astype(F32)
+            if j == 0:
+                right_ref[...] = right
+            else:
+                right_away[...] = right.astype(BF16)
+
+    shape = (m, cut)
+    return call_whole(
+        kernel, (kept, got), [(shape, F32), (shape, BF16), (shape, F32), (shape, BF16)]
+    )
+
+
+def cut_rows(kept, got):
+    m, n = kept.shape
+
+    def kernel(kept_ref, got_ref, first, second):
+        total = kept_ref[...] + got_ref[...].astype(F32)
+        first[...] = total[: m // 2]
+        second[...] = total[m // 2 :].astype(BF16)
+
+    return call_whole(kernel, (kept, got), [((m // 2, n), F32), ((m // 2, n), BF16)])
+
+
+def cut_cases(left, left_got, right, right_got, count):
+    m, n = left.shape
+    piece = m // count
+
+    def kernel(a, b, c, d, *outs):
+        sums = a[...] + b[...].astype(F32), c[...] + d[...].astype(F32)
+        for i, out in enumerate(outs):
+            for at, total in enumerate(sums):
+                rows = total[i * piece : (i + 1) * piece]
+                out[:, at * n : (at + 1) * n] = rows.astype(out.dtype)
+
+    shapes = [((piece, 2 * n), BF16 if i else F32) for i in range(count)]
+    return call_whole(kernel, (left, left_got, right, right_got), shapes)
+
+
+def residual_of(loads, first, terms, after):
+    piece, n = terms[0].shape
+
+    def kernel(first_ref, loads_ref, *refs):
+        rows = pl.ds(pl.multiple_of(first_ref[0] * piece, piece), piece)
+        total = refs[0][...].astype(F32)
+        for ref in refs[1:-1]:
+            total += ref[...].astype(F32)
+        refs[-1][...] = (loads_ref[rows, :].astype(F32) - total).astype(BF16)
+
+    return call_whole(kernel, (loads, *terms), [((piece, n), BF16)], (first,), after)[0]
+
+
 def swap(x, axis, bit, size):
     return lax.ppermute(x, axis, [(i, i ^ bit) for i in range(size)])
 
@@ -432,7 +563,7 @@
             last = at == len(steps) - 1
             terms, signs = [[total], [to_row(narrow, bit)]], (1, 1)
             if last and base is not None:
-                terms, signs = [[base], *terms], (1, -1, -1)
+                terms, signs = [base, *terms], (1, -1, -1)
             total, out = join(
                 terms, signs, after, wide or not last, pieces if last else 1
             )
@@ -443,54 +574,48 @@
         return rounded, [to_row(x, 1) for x in rounded]
 
     slot_rows = child_panel.shape[1]
-    own_map = lax.dynamic_slice_in_dim(child_map, row * slot_rows, slot_rows, 1)
-    maps = own_map.reshape(kids, 1, slot_rows)
-    spread_maps = spread(maps)
-
-    if wide:
-        ids = jnp.arange(cols * leafs, dtype=jnp.int32)
-        order = lax.bitwise_xor(ids, col * leafs + leaf)
-    else:
-        order = jnp.zeros((1,), jnp.int32)
+    maps = child_map.reshape(kids, 1, child_map.shape[1])
+
+    share = (col * leafs + leaf)[None]
+    order = (share, cols * leafs) if wide else (jnp.zeros((1,), jnp.int32), 1)
 
     begun = []
     after = ()
     for k in range(kids):
-        sent = nn(child_loads, child_inverse, k, core, 1, pieces_of(k))
-        kept = nn(child_loads, child_inverse, k, core, 0, 1, (sent[0], *after))
-        begun.append(core_sum(kept[0], sent))
+        sent = nn(child_loads, child_inverse, k, core, 1, pieces_of(k), after)
+        (kept,) = nn(child_loads, child_inverse, k, core, 0, 1, sent[:1])
+        begun.append(core_sum(kept, sent))
         after = begun[k][1:]
-    panels = []
-    for k in range(kids):
-        panels.append(preload(child_panel, k, after))
-        after = (panels[k],)
+    spread_maps = spread(maps, row_1, slot_rows, after)
+    after = (spread_maps,)
     forward = []
     sent = kept = None
     for k in range(kids):
         after = after if k == 0 else (sent,)
-        total, rounded = row_end(*begun[k], after, pieces=pieces_of(k == 0))
-        forward.append(total)
-        upd = held_nt(*halves(rounded), panels[k], core)
+        _, rounded = row_end(*begun[k], after, wide=False, pieces=pieces_of(k == 0))
+        forward.append(rounded)
+        if k == 0:
+            panel, _ = preload(child_panel, 0, rounded)
+        bring = (child_panel, k + 1) if k < kids - 1 else None
+        upd, *brought = held_nt(*halves(rounded), panel, core, bring=bring)
+        panel = brought[0] if brought else None
         sent = scatter(upd, spread_maps, k, row_1, order, rows, root_rows, 1, sent)
         kept = scatter(upd, spread_maps, k, row_1, order, rows, root_rows, 0, kept)
 
-    total = add(kept, to_row(sent, 1))
     if wide:
-        half, cut = case_count // 2, root_rows // 2
-        left = add(total[:, :half, :cut], to_col(total[:, half:, :cut].astype(BF16)))
-        right = add(total[0, :, cut:], to_row(total[1, :, cut:].astype(BF16), 2))
-        left = add(left[0], to_row(left[1].astype(BF16), 2))
-        right = add(right[:half], to_col(right[half:].astype(BF16)))
-        total = jnp.concatenate([left, right], axis=1)
-        narrow = total.astype(BF16)
-        shares = [narrow[j * piece : (j + 1) * piece] for j in range(1, leafs)]
-        root_held = preload(root_w, 0, shares)
-        first_case = (col * leafs + leaf) * piece
-        loads = lax.dynamic_slice_in_dim(root_loads, first_case, piece, 0)
-        terms = [loads, total[:piece]] + [to_leaf(x, j + 1) for j, x in enumerate(shares)]
-        _, (residual,) = join([[x] for x in terms], (1,) + (-1,) * leafs, (root_held,), False)
-        residual = jnp.concatenate([residual, to_col(residual)])
+        left, left_away, right, right_away = cut_core_sum(kept, to_row(sent, 1))
+        left_got, right_got = to_col(left_away), to_row(right_away, 2)
+        left, left_away = cut_rows(left, left_got)
+        right, right_away = cut_rows(right, right_got)
+        mine, *shares = cut_cases(
+            left, to_row(left_away, 2), right, to_col(right_away), leafs
+        )
+        root_held, token = preload(root_w, 0, shares)
+        terms = [mine] + [to_leaf(x, j + 1) for j, x in enumerate(shares)]
+        residual = residual_of(root_loads, share, terms, (token,))
+        residual = [residual, to_col(residual)]
     else:
+        total = add(kept, to_row(sent, 1))
         for bit in bits(rows)[1:]:
             total = add(total[0::2], to_row(total[1::2].astype(BF16), bit))
         total = total[0]
@@ -506,40 +631,48 @@
         for bit in bits(cols):
             narrow = mine_cases.astype(BF16)
             mine_cases = add(narrow, to_col(narrow, bit))
-        residual = (cases_of(root_loads, 0).astype(F32) - mine_cases).astype(BF16)
-
-    if not wide:
-        root_held = preload(root_w, 0, (kept,))
+        residual = [(cases_of(root_loads, 0).astype(F32) - mine_cases).astype(BF16)]
+        root_held, _ = preload(root_w, 0, (kept,))
+
     sent = held_nn(residual, root_held, core, 1)
     kept = held_nn(residual, root_held, core, 0, 1, sent)
     begun = core_sum(kept[0], sent)
-    panels = [preload(child_panel, 0, begun[1:])]
-    _, root_forward = row_end(*begun, (panels[0],), wide=False)
-    part = held_nt(*halves(root_forward), root_held, core)
-    panels += [preload(child_panel, k, (part,)) for k in range(1, kids)]
+    *panels, token = preload(child_panel, 0, begun[1:])
+    _, root_forward = row_end(*begun, (token,), wide=False)
+    *part, panel = held_nt(
+        *halves(root_forward),
+        root_held,
+        core,
+        pieces=2 if wide else 1,
+        bring=(child_panel, kids - 1),
+    )
+    panels += [preload(child_panel, k, part)[0] for k in range(1, kids - 1)] + [panel]
 
     picked = [None] * kids
+    inverses = []
     if wide:
-        _, (part,) = join(
-            [[part[:piece]], [to_col(part[piece:])]], (1, 1), tuple(panels[1:]), False
-        )
-        inverses = [preload(child_inverse, 0, (part,))]
+        _, (part,) = join([[part[0]], [to_col(part[1])]], (1, 1), (), False)
         shares = [part] + [to_leaf(part, j) for j in range(1, leafs)]
-        _, (held,) = join([shares], (1,), tuple(inverses), False)
-        inverses += [preload(child_inverse, k, (held,)) for k in range(1, kids)]
+        _, (held,) = join([shares], (1,), (), False)
+        brought = [preload(child_inverse, k, (held,)) for k in range(kids - 1)]
+        inverses = [b[0] for b in brought]
+        tokens = tuple(b[1] for b in brought)
         beside, across = to_col(held), to_row(held, 2)
         cut = held.shape[0] // 2
-        _, near = join([[held, beside]], (1,), tuple(inverses[1:]), False, 4)
+        _, near = join([[held, beside]], (1,), tokens, False, 4)
         near_other = [to_row(x, 1) for x in near]
         rest = [to_col(across[:cut]), to_row(beside[cut:], 2)]
         for k in range(kids):
-            picked[k] = gather([near, near_other], [0, 1], maps, k, row_1, order, None, (across,))
+            (picked[k],) = gather(
+                [near, near_other], [0, 1], maps, slot_rows, k, row_1, order, None, None, (across,)
+            )
         _, far = join([[across, *rest]], (1,), tuple(picked), False)
         far_other = [to_row(x, 1) for x in far]
-        root_solution = reorder(near, order)
+        root_solution, token = reorder(near, order)
         last_blocks, last_at = [far, far_other], [2, 3]
     else:
-        inverses = [preload(child_inverse, k, (part,)) for k in range(kids)]
+        (part,) = part
+        inverses = [preload(child_inverse, k, (part,))[0] for k in range(kids - 1)]
         for bit in bits(cols):
             part = add(part, to_col(part, bit)).astype(BF16)
         own = jnp.zeros((case_count, root_rows), BF16)
@@ -558,25 +691,32 @@
     begun = []
     after = ()
     for k in range(kids):
-        full = gather(last_blocks, last_at, maps, k, row_1, order, picked[k], after)
-        sent = held_nn(full, panels[k], core, 1, pieces_of(k))
-        kept = held_nn(full, panels[k], core, 0, 1, sent[:1])
+        bring = (child_inverse, k) if k == kids - 1 else None
+        full, *brought = gather(
+            last_blocks, last_at, maps, slot_rows, k, row_1, order, picked[k], bring, after
+        )
+        inverses += brought
+        sent = held_nn([full], panels[k], core, 1, pieces_of(k))
+        kept = held_nn([full], panels[k], core, 0, 1, sent[:1])
         begun.append(core_sum(kept[0], sent))
         after = begun[k][1:]
-    solved = None
+    solved = first = None
     chunks = 2 if slot_rows % 256 == 0 else 1
-    after = (root_solution, *after)
+    after = (token, *after)
     for k in range(kids):
-        _, rounded = row_end(*begun[k], after, forward[k], False, pieces_of(k == 0))
+        _, rounded = row_end(*begun[k], after, forward[k], False, pieces_of(1))
         pair = halves(rounded)
+        after = ()
         for at in range(chunks):
-            out = held_nt(*pair, inverses[k], core, at, chunks)
-            after = (out,)
+            ready = (first,) if k and at else ()
+            (out,) = held_nt(*pair, inverses[k], core, at, chunks, after=ready)
+            after += (out,)
             terms = [out, to_col(out)]
             for bit in bits(cols)[1:]:
                 out = add(*terms).astype(BF16)
                 terms = [out, to_col(out, bit)]
-            solved = finish(solved, kids, k, at, chunks, terms)
+            solved, done = finish(solved, kids, k, at, chunks, terms)
+            first = done if first is None else first
     return (solved, root_solution)
 
 

time: 170 us -> 156 us (0.918)
  Pallas kernels: 86.2 us -> 76 us
  local copies, waits for them, and re-layouts: 6.33 us -> 0.06 us
  starting transfers between devices: 40.3 us -> 42.7 us
  waiting for transfers between devices: 33.6 us -> 35.8 us
    pallas_call x7 -> x4, Pallas kernels: 25.8 us -> 15.3 us  [preload(): pl.pallas_call(functools.partial(preload_kernel, child), in_specs=[pl.Blo...]
    unnamed x18 -> x4, local copies, waits for them, and re-layouts: 5.5 us -> 0.01 us
    pallas_call x7, Pallas kernels: 15.3 us -> 18.7 us  [held_nt(): pl.pallas_call(kernel, in_specs=[SCALARS] + [WHOLE] * (len(mine) + len(ot...]
    pallas_call x4, Pallas kernels: 11.7 us -> 8.89 us  [scatter(): pl.pallas_call(functools.partial(scatter_kernel, block_rows, tile, odd, c...]
    ppermute x53 -> x56, starting transfers between devices: 40.3 us -> 42.7 us  [swap(): return lax.ppermute(x, axis, [(i, i ^ bit) for i in range(size)])]
    ppermute x53 -> x56, waiting for transfers between devices: 33.6 us -> 35.8 us  [swap(): return lax.ppermute(x, axis, [(i, i ^ bit) for i in range(size)])]
    pallas_call x7 -> x12, Pallas kernels: 5.56 us -> 6.02 us  [the longest x6 5.13 us: held_nn(): pl.pallas_call(kernel, in_specs=[SCALARS] + [WHOLE] * (len(x) + 1) + [ANY...]
  transfers between devices with their start and end apart: 53 -> 56, of which waited for: 25 -> 25; matrix products, arithmetic and copies ran while one was open for 1% -> 0% of each run, Pallas kernels for 40% -> 37%
where the time goes in v4:
time: 156 us
  Pallas kernels  76 us (49%)
  starting transfers between devices  42.7 us (27%)
  waiting for transfers between devices  35.8 us (23%)
    ppermute x56, starting transfers between devices, swap(): return lax.ppermute(x, axis, [(i, i ^ bit) for i in range(size)])  42.7 us
    ppermute x56, waiting for transfers between devices, swap(): return lax.ppermute(x, axis, [(i, i ^ bit) for i in range(size)])  35.8 us
    pallas_call x7, Pallas kernels, held_nt(): pl.pallas_call(kernel, in_specs=[SCALARS] + [WHOLE] * (len(mine) + len(ot...  18.7 us
    pallas_call x4, Pallas kernels, preload(): pl.pallas_call(functools.partial(preload_kernel, child), in_specs=[pl.Blo...  15.3 us
    pallas_call x4, Pallas kernels, nn(): pl.pallas_call(kernel, grid_spec=pltpu.PrefetchScalarGridSpec(num_scalar_...  12.1 us
    pallas_call x4, Pallas kernels, gather(): pl.pallas_call(functools.partial(gather_kernel, block_rows, tile, which,...  9.8 us
    pallas_call x4, Pallas kernels, scatter(): pl.pallas_call(functools.partial(scatter_kernel, block_rows, tile, odd, c...  8.89 us
    pallas_call x6, Pallas kernels, held_nn(): pl.pallas_call(kernel, in_specs=[SCALARS] + [WHOLE] * (len(x) + 1) + [ANY...  5.13 us
  transfers between devices with their start and end apart: 56, of which 25 were waited for; matrix products, arithmetic and copies ran while one was open for 0% of the time, Pallas kernels for 37%

profile of v4, /device:TPU:0, one launch (start us, length us, event | category | flops | bytes accessed | tf_op | source)
XLA Modules:
  0.0 155.8 jit_solution(4241190284151536950)
XLA Ops:
  0.6 3.0 %shard_map.77.rest_0_ = bf16[128,1536]{1,0:T(8,128)(2,1)S(1)} custom-call(s32[1]{0:T(128)} %bitcast.half_ref, bf16[2,128,1536]{2,1,0:T(8,128)(2,1)} %x_ref.7, bf16[2,1536,3072]{2,1,0:T(8,128)(2,1)} %rest_3_.1), custom_call_target="tpu_custom_call" | custom-call | flops 9437184 | bytes 73728 | tf_op jit(solution)/shard_map/pallas_call | solution.py:98
  4.2 3.0 %shard_map.78.refs_0_ = f32[128,1536]{1,0:T(8,128)S(1)} custom-call(s32[1]{0:T(128)} %bitcast.half_ref, bf16[2,128,1536]{2,1,0:T(8,128)(2,1)} %x_ref.7, bf16[2,1536,3072]{2,1,0:T(8,128)(2,1)} %rest_3_.1, bf16[128,1536]{1,0:T(8,128)(2,1)S(1)} %shard_map.77.rest_0_), custom_call_target="tpu_custom_call" | custom-call | flops 9437184 | bytes 73728 | tf_op jit(solution)/shard_map/pallas_call | solution.py:98
  7.4 2.6 %collective-permute-start.6 = (bf16[128,1536]{1,0:T(8,128)(2,1)S(1)}, bf16[128,1536]{1,0:T(8,128)(2,1)S(1)}, u32[]{:S(2)}, u32[]{:S(2)}) collective-permute-start(bf16[128,1536]{1,0:T(8,128)(2,1)S(1)} %get-tuple-element.69.rest_0_), channel_id=1, source_target_pairs={{0,4},{2,6},{4,0},{6,2},{1,5},{3,7},{5,1},{7,3},{8,12},{10,14},{12... | collective-permute-start | bytes 1179656 | tf_op jit(solution)/shard_map/ppermute | solution.py:522
  10.0 3.0 %shard_map.80 = (bf16[32,1536]{1,0:T(8,128)(2,1)S(1)}, bf16[32,1536]{1,0:T(8,128)(2,1)S(1)}, bf16[32,1536]{1,0:T(8,128)(2,1)S(1)}, bf16[32,1536]{1,0:T(8,128)(2,1)S(1)}) custom-call(s32[1]{0:T(128)} %bitcast.half_ref, bf16[2,128,1536]{2,1,0:T(8,128)(2,1)} %x_ref.7, bf16[2,1536,3072]{2,1,0:T(8,128)(2,1)} %rest_3_.1, ...), custom_call_target="tpu_custom_call" | custom-call | flops 9437184 | bytes 73728 | tf_op jit(solution)/shard_map/pallas_call | solution.py:98
  14.1 3.0 %shard_map.81.refs_0_ = f32[128,1536]{1,0:T(8,128)S(1)} custom-call(s32[1]{0:T(128)} %bitcast.half_ref, bf16[2,128,1536]{2,1,0:T(8,128)(2,1)} %x_ref.7, bf16[2,1536,3072]{2,1,0:T(8,128)(2,1)} %rest_3_.1, bf16[32,1536]{1,0:T(8,128)(2,1)S(1)} %get-tuple-element.70.rest_0_), custom_call_target="tpu_custom_call" | custom-call | flops 9437184 | bytes 73728 | tf_op jit(solution)/shard_map/pallas_call | solution.py:98
  18.1 1.7 %collective-permute-done.6.refs_1_ = bf16[128,1536]{1,0:T(8,128)(2,1)S(1)} collective-permute-done((bf16[128,1536]{1,0:T(8,128)(2,1)S(1)}, bf16[128,1536]{1,0:T(8,128)(2,1)S(1)}, u32[]{:S(2)}, u32[]{:S(2)}) %collective-permute-start.6) | collective-permute-done | bytes 393248 | tf_op jit(solution)/shard_map/ppermute | solution.py:522
  20.9 4.3 %shard_map.85 = (bf16[1536,3072]{1,0:T(8,128)(2,1)S(1)}, f32[8,128]{1,0:T(8,128)}) custom-call(bf16[2,1536,3072]{2,1,0:T(8,128)(2,1)} %refs_3_.1, bf16[32,1536]{1,0:T(8,128)(2,1)S(1)} %get-tuple-element.77.rest_0_.refs_0_, bf16[32,1536]{1,0:T(8,128)(2,1)S(1)} %get-tuple-element.78.rest_1_.refs_1_, bf16[32,1536]{1,0:T(8,128)(2,1)S(1)} %get-tuple-element.79.rest_2_.refs_2_, ...), custom_call_target="tpu_custom_call" | custom-call | bytes 147456 | tf_op jit(solution)/shard_map/pallas_call | solution.py:57
  25.2 4.8 %shard_map.86 = (bf16[128,1536]{1,0:T(8,128)(2,1)S(1)}, bf16[1536,3072]{1,0:T(8,128)(2,1)S(1)}) custom-call(s32[1]{0:T(128)} %bitcast.half_ref, bf16[32,1536]{1,0:T(8,128)(2,1)S(1)} %get-tuple-element.77.rest_0_.refs_0_, bf16[32,1536]{1,0:T(8,128)(2,1)S(1)} %get-tuple-element.78.rest_1_.refs_1_, bf16[32,1536]{1,0:T(8,128)(2,1)S(1)} %get-tuple-element.79.rest_2_.refs_2_, ...), custom_call_target="tpu_custom_call" | custom-call | flops 18874368 | bytes 147456 | tf_op jit(solution)/shard_map/pallas_call | solution.py:176
  30.0 2.1 %shard_map.87.refs_2_.refs_4_ = bf16[2,128,1536]{2,1,0:T(8,128)(2,1)S(1)} custom-call(s32[1]{0:T(128)} %bitcast.1.row_ref.refs_0_, s32[1]{0:T(128)} %bitcast.2.refs_1_.refs_0_.order_ref, s16[2,1536,128]{2,1,0:T(8,128)(2,1)S(1)} %shard_map.83.refs_2_, bf16[128,1536]{1,0:T(8,128)(2,1)S(1)} %get-tuple-element.82.refs_3_), custom_call_target="tpu_custom_call" | custom-call | flops 18874368 | bytes 24576 | tf_op jit(solution)/shard_map/pallas_call | solution.py:268
  32.4 1.6 %collective-permute-done.11.refs_1_ = bf16[128,1536]{1,0:T(8,128)(2,1)S(1)} collective-permute-done((bf16[128,1536]{1,0:T(8,128)(2,1)S(1)}, bf16[128,1536]{1,0:T(8,128)(2,1)S(1)}, u32[]{:S(2)}, u32[]{:S(2)}) %collective-permute-start.11) | collective-permute-done | bytes 393248 | tf_op jit(solution)/shard_map/ppermute | solution.py:522
  34.0 3.2 %shard_map.89.refs_3_ = bf16[128,1536]{1,0:T(8,128)(2,1)S(1)} custom-call(s32[1]{0:T(128)} %bitcast.half_ref, bf16[128,1536]{1,0:T(8,128)(2,1)S(1)} %shard_map.88.refs_0_, bf16[128,1536]{1,0:T(8,128)(2,1)S(1)} %collective-permute-done.11.refs_1_, bf16[1536,3072]{1,0:T(8,128)(2,1)S(1)} %get-tuple-element.83.refs_2_), custom_call_target="tpu_custom_call" | custom-call | flops 18874368 | bytes 147456 | tf_op jit(solution)/shard_map/pallas_call | solution.py:176
  37.2 2.2 %shard_map.92 = bf16[2,128,1536]{2,1,0:T(8,128)(2,1)S(1)} custom-call(s32[1]{0:T(128)} %bitcast.1.row_ref.refs_0_, s32[1]{0:T(128)} %bitcast.2.refs_1_.refs_0_.order_ref, s16[2,1536,128]{2,1,0:T(8,128)(2,1)S(1)} %shard_map.83.refs_2_, bf16[128,1536]{1,0:T(8,128)(2,1)S(1)} %shard_map.89.refs_3_, bf16[2,128,1536]{2,1,0:T(8,128)(2,1)S(1)} %shard_map.87.refs_2_.refs_4_), custom_call_target="tpu_custom_call" | custom-call | flops 18874368 | bytes 24576 | tf_op jit(solution)/shard_map/pallas_call | solution.py:268
  39.7 2.1 %shard_map.90.refs_4_ = bf16[2,128,1536]{2,1,0:T(8,128)(2,1)S(1)} custom-call(s32[1]{0:T(128)} %bitcast.1.row_ref.refs_0_, s32[1]{0:T(128)} %bitcast.2.refs_1_.refs_0_.order_ref, s16[2,1536,128]{2,1,0:T(8,128)(2,1)S(1)} %shard_map.83.refs_2_, bf16[128,1536]{1,0:T(8,128)(2,1)S(1)} %get-tuple-element.82.refs_3_), custom_call_target="tpu_custom_call" | custom-call | flops 18874368 | bytes 24576 | tf_op jit(solution)/shard_map/pallas_call | solution.py:268
  41.8 2.4 %shard_map.91.refs_0_ = bf16[2,128,1536]{2,1,0:T(8,128)(2,1)S(1)} custom-call(s32[1]{0:T(128)} %bitcast.1.row_ref.refs_0_, s32[1]{0:T(128)} %bitcast.2.refs_1_.refs_0_.order_ref, s16[2,1536,128]{2,1,0:T(8,128)(2,1)S(1)} %shard_map.83.refs_2_, bf16[128,1536]{1,0:T(8,128)(2,1)S(1)} %shard_map.89.refs_3_, bf16[2,128,1536]{2,1,0:T(8,128)(2,1)S(1)} %shard_map.90.refs_4_), custom_call_target="tpu_custom_call" | custom-call | flops 18874368 | bytes 24576 | tf_op jit(solution)/shard_map/pallas_call | solution.py:268
  44.4 1.8 %collective-permute-start.13 = (bf16[128,768]{1,0:T(8,128)(2,1)S(1)}, bf16[128,768]{1,0:T(8,128)(2,1)S(1)}, u32[]{:S(2)}, u32[]{:S(2)}) collective-permute-start(bf16[128,768]{1,0:T(8,128)(2,1)S(1)} %get-tuple-element.85), channel_id=1, source_target_pairs={{0,1},{1,0},{2,3},{3,2},{4,5},{5,4},{6,7},{7,6},{8,9},{9,8},{10,11... | collective-permute-start | bytes 589832 | tf_op jit(solution)/shard_map/ppermute | solution.py:522
  46.3 1.9 %collective-permute-start.15 = (bf16[128,768]{1,0:T(8,128)(2,1)S(1)}, bf16[128,768]{1,0:T(8,128)(2,1)S(1)}, u32[]{:S(2)}, u32[]{:S(2)}) collective-permute-start(bf16[128,768]{1,0:T(8,128)(2,1)S(1)} %get-tuple-element.89), channel_id=1, source_target_pairs={{0,4},{2,6},{4,0},{6,2},{1,5},{3,7},{5,1},{7,3},{8,12},{10,14},{12... | collective-permute-start | bytes 589832 | tf_op jit(solution)/shard_map/ppermute | solution.py:522
  48.2 3.5 %collective-permute-done.13.refs_1_ = bf16[128,768]{1,0:T(8,128)(2,1)S(1)} collective-permute-done((bf16[128,768]{1,0:T(8,128)(2,1)S(1)}, bf16[128,768]{1,0:T(8,128)(2,1)S(1)}, u32[]{:S(2)}, u32[]{:S(2)}) %collective-permute-start.13) | collective-permute-done | bytes 196640 | tf_op jit(solution)/shard_map/ppermute | solution.py:522
  51.7 2.2 %collective-permute-start.14 = (bf16[64,768]{1,0:T(8,128)(2,1)S(1)}, bf16[64,768]{1,0:T(8,128)(2,1)S(1)}, u32[]{:S(2)}, u32[]{:S(2)}) collective-permute-start(bf16[64,768]{1,0:T(8,128)(2,1)S(1)} %get-tuple-element.87), channel_id=1, source_target_pairs={{0,4},{2,6},{4,0},{6,2},{1,5},{3,7},{5,1},{7,3},{8,12},{10,14},{12... | collective-permute-start | bytes 294920 | tf_op jit(solution)/shard_map/ppermute | solution.py:522
  54.0 1.6 %collective-permute-start.16 = (bf16[64,768]{1,0:T(8,128)(2,1)S(1)}, bf16[64,768]{1,0:T(8,128)(2,1)S(1)}, u32[]{:S(2)}, u32[]{:S(2)}) collective-permute-start(bf16[64,768]{1,0:T(8,128)(2,1)S(1)} %get-tuple-element.91), channel_id=1, source_target_pairs={{0,1},{1,0},{2,3},{3,2},{4,5},{5,4},{6,7},{7,6},{8,9},{9,8},{10,11... | collective-permute-start | bytes 294920 | tf_op jit(solution)/shard_map/ppermute | solution.py:522
  56.6 2.1 %collective-permute-done.16.refs_3_ = bf16[64,768]{1,0:T(8,128)(2,1)S(1)} collective-permute-done((bf16[64,768]{1,0:T(8,128)(2,1)S(1)}, bf16[64,768]{1,0:T(8,128)(2,1)S(1)}, u32[]{:S(2)}, u32[]{:S(2)}) %collective-permute-start.16) | collective-permute-done | bytes 98336 | tf_op jit(solution)/shard_map/ppermute | solution.py:522
  58.7 1.6 %collective-permute-start.17 = (bf16[16,1536]{1,0:T(8,128)(2,1)S(1)}, bf16[16,1536]{1,0:T(8,128)(2,1)S(1)}, u32[]{:S(2)}, u32[]{:S(2)}) collective-permute-start(bf16[16,1536]{1,0:T(8,128)(2,1)S(1)} %get-tuple-element.93.rest_0_), channel_id=1, source_target_pairs={{0,8},{8,0},{16,24},{24,16},{1,9},{9,1},{17,25},{25,17},{2,10},{10... | collective-permute-start | bytes 147464 | tf_op jit(solution)/shard_map/ppermute | solution.py:522
  60.4 2.6 %collective-permute-start.18 = (bf16[16,1536]{1,0:T(8,128)(2,1)S(1)}, bf16[16,1536]{1,0:T(8,128)(2,1)S(1)}, u32[]{:S(2)}, u32[]{:S(2)}) collective-permute-start(bf16[16,1536]{1,0:T(8,128)(2,1)S(1)} %get-tuple-element.94.rest_1_), channel_id=1, source_target_pairs={{0,16},{8,24},{16,0},{24,8},{1,17},{9,25},{17,1},{25,9},{2,18},{10... | collective-permute-start | bytes 147464 | tf_op jit(solution)/shard_map/ppermute | solution.py:522
  63.2 3.7 %shard_map.97 = (bf16[1536,3072]{1,0:T(8,128)(2,1)S(1)}, f32[8,128]{1,0:T(8,128)S(1)}) custom-call(bf16[1,1536,3072]{2,1,0:T(8,128)(2,1)} %bitcast.4, bf16[16,1536]{1,0:T(8,128)(2,1)S(1)} %get-tuple-element.93.rest_0_, bf16[16,1536]{1,0:T(8,128)(2,1)S(1)} %get-tuple-element.94.rest_1_, bf16[16,1536]{1,0:T(8,128)(2,1)S(1)} %get-tuple-element.95.rest_2_), custom_call_target="tpu_custom_call" | custom-call | bytes 147456 | tf_op jit(solution)/shard_map/pallas_call | solution.py:57
  66.9 2.0 %collective-permute-done.19.refs_5_ = bf16[16,1536]{1,0:T(8,128)(2,1)S(1)} collective-permute-done((bf16[16,1536]{1,0:T(8,128)(2,1)S(1)}, bf16[16,1536]{1,0:T(8,128)(2,1)S(1)}, u32[]{:S(2)}, u32[]{:S(2)}) %collective-permute-start.19) | collective-permute-done | bytes 49184 | tf_op jit(solution)/shard_map/ppermute | solution.py:522
  68.9 1.6 %collective-permute-start.20 = (bf16[16,1536]{1,0:T(8,128)(2,1)S(1)}, bf16[16,1536]{1,0:T(8,128)(2,1)S(1)}, u32[]{:S(2)}, u32[]{:S(2)}) collective-permute-start(bf16[16,1536]{1,0:T(8,128)(2,1)S(1)} %shard_map.98.refs_0_), channel_id=1, source_target_pairs={{0,1},{1,0},{2,3},{3,2},{4,5},{5,4},{6,7},{7,6},{8,9},{9,8},{10,11... | collective-permute-start | bytes 147464 | tf_op jit(solution)/shard_map/ppermute | solution.py:522
  70.5 2.5 %collective-permute-done.20.refs_1_ = bf16[16,1536]{1,0:T(8,128)(2,1)S(1)} collective-permute-done((bf16[16,1536]{1,0:T(8,128)(2,1)S(1)}, bf16[16,1536]{1,0:T(8,128)(2,1)S(1)}, u32[]{:S(2)}, u32[]{:S(2)}) %collective-permute-start.20) | collective-permute-done | bytes 49184 | tf_op jit(solution)/shard_map/ppermute | solution.py:522
  76.5 3.7 %shard_map.102 = (bf16[1536,3072]{1,0:T(8,128)(2,1)S(1)}, f32[8,128]{1,0:T(8,128)S(1)}) custom-call(bf16[2,1536,3072]{2,1,0:T(8,128)(2,1)} %refs_3_.1, bf16[32,1536]{1,0:T(8,128)(2,1)S(1)} %get-tuple-element.99.rest_0_), custom_call_target="tpu_custom_call" | custom-call | bytes 147456 | tf_op jit(solution)/shard_map/pallas_call | solution.py:57
  81.6 4.6 %shard_map.104 = (bf16[16,1536]{1,0:T(8,128)(2,1)S(1)}, bf16[16,1536]{1,0:T(8,128)(2,1)S(1)}, bf16[1536,3072]{1,0:T(8,128)(2,1)S(1)}) custom-call(s32[1]{0:T(128)} %bitcast.half_ref, bf16[32,1536]{1,0:T(8,128)(2,1)S(1)} %shard_map.103.refs_0_, bf16[32,1536]{1,0:T(8,128)(2,1)S(1)} %collective-permute-done.23.refs_1_, ...), custom_call_target="tpu_custom_call" | custom-call | flops 4718592 | bytes 147456 | tf_op jit(solution)/shard_map/pallas_call | solution.py:176
  86.2 1.6 %collective-permute-start.24 = (bf16[16,1536]{1,0:T(8,128)(2,1)S(1)}, bf16[16,1536]{1,0:T(8,128)(2,1)S(1)}, u32[]{:S(2)}, u32[]{:S(2)}) collective-permute-start(bf16[16,1536]{1,0:T(8,128)(2,1)S(1)} %get-tuple-element.102), channel_id=1, source_target_pairs={{0,1},{1,0},{2,3},{3,2},{4,5},{5,4},{6,7},{7,6},{8,9},{9,8},{10,11... | collective-permute-start | bytes 147464 | tf_op jit(solution)/shard_map/ppermute | solution.py:522
  87.8 2.6 %collective-permute-done.24.refs_1_ = bf16[16,1536]{1,0:T(8,128)(2,1)S(1)} collective-permute-done((bf16[16,1536]{1,0:T(8,128)(2,1)S(1)}, bf16[16,1536]{1,0:T(8,128)(2,1)S(1)}, u32[]{:S(2)}, u32[]{:S(2)}) %collective-permute-start.24) | collective-permute-done | bytes 49184 | tf_op jit(solution)/shard_map/ppermute | solution.py:522
  90.5 2.2 %collective-permute-start.26 = (bf16[16,1536]{1,0:T(8,128)(2,1)S(1)}, bf16[16,1536]{1,0:T(8,128)(2,1)S(1)}, u32[]{:S(2)}, u32[]{:S(2)}) collective-permute-start(bf16[16,1536]{1,0:T(8,128)(2,1)S(1)} %shard_map.105.refs_0_), channel_id=1, source_target_pairs={{0,16},{8,24},{16,0},{24,8},{1,17},{9,25},{17,1},{25,9},{2,18},{10... | collective-permute-start | bytes 147464 | tf_op jit(solution)/shard_map/ppermute | solution.py:522
  92.7 2.1 %collective-permute-start.27 = (bf16[16,1536]{1,0:T(8,128)(2,1)S(1)}, bf16[16,1536]{1,0:T(8,128)(2,1)S(1)}, u32[]{:S(2)}, u32[]{:S(2)}) collective-permute-start(bf16[16,1536]{1,0:T(8,128)(2,1)S(1)} %shard_map.105.refs_0_), channel_id=1, source_target_pairs={{0,24},{8,16},{16,8},{24,0},{1,25},{9,17},{17,9},{25,1},{2,26},{10... | collective-permute-start | bytes 147464 | tf_op jit(solution)/shard_map/ppermute | solution.py:522
  95.5 3.1 %collective-permute-done.27.refs_3_ = bf16[16,1536]{1,0:T(8,128)(2,1)S(1)} collective-permute-done((bf16[16,1536]{1,0:T(8,128)(2,1)S(1)}, bf16[16,1536]{1,0:T(8,128)(2,1)S(1)}, u32[]{:S(2)}, u32[]{:S(2)}) %collective-permute-start.27) | collective-permute-done | bytes 49184 | tf_op jit(solution)/shard_map/ppermute | solution.py:522
  98.6 1.6 %collective-permute-start.30 = (bf16[64,1536]{1,0:T(8,128)(2,1)S(1)}, bf16[64,1536]{1,0:T(8,128)(2,1)S(1)}, u32[]{:S(2)}, u32[]{:S(2)}) collective-permute-start(bf16[64,1536]{1,0:T(8,128)(2,1)S(1)} %shard_map.106.rest_0_.refs_0_), channel_id=1, source_target_pairs={{0,1},{1,0},{2,3},{3,2},{4,5},{5,4},{6,7},{7,6},{8,9},{9,8},{10,11... | collective-permute-start | bytes 589832 | tf_op jit(solution)/shard_map/ppermute | solution.py:522
  101.1 3.7 %shard_map.107 = (bf16[1536,3072]{1,0:T(8,128)(2,1)S(1)}, f32[8,128]{1,0:T(8,128)S(1)}) custom-call(bf16[2,1536,3072]{2,1,0:T(8,128)(2,1)} %rest_3_.1, bf16[64,1536]{1,0:T(8,128)(2,1)S(1)} %shard_map.106.rest_0_.refs_0_), custom_call_target="tpu_custom_call" | custom-call | bytes 147456 | tf_op jit(solution)/shard_map/pallas_call | solution.py:57
  108.1 1.9 %shard_map.109.refs_3_.rest_2_ = bf16[128,1536]{1,0:T(8,128)(2,1)S(1)} custom-call(s32[1]{0:T(128)} %bitcast.1.row_ref.refs_0_, s32[1]{0:T(128)} %bitcast.2.refs_1_.refs_0_.order_ref, s32[2,1,6144]{2,1,0:T(1,128)S(1)} %reshape.7.map_ref, bf16[32,1536]{1,0:T(8,128)(2,1)S(1)} %get-tuple-element.104.rest_0_.refs_0_, ...), custom_call_target="tpu_custom_call" | custom-call | flops 18874368 | bytes 12288 | tf_op jit(solution)/shard_map/pallas_call | solution.py:340
  109.9 1.9 %shard_map.110.refs_4_.rest_2_ = bf16[128,1536]{1,0:T(8,128)(2,1)S(1)} custom-call(s32[1]{0:T(128)} %bitcast.1.row_ref.refs_0_, s32[1]{0:T(128)} %bitcast.2.refs_1_.refs_0_.order_ref, s32[2,1,6144]{2,1,0:T(1,128)S(1)} %reshape.7.map_ref, bf16[32,1536]{1,0:T(8,128)(2,1)S(1)} %get-tuple-element.104.rest_0_.refs_0_, ...), custom_call_target="tpu_custom_call" | custom-call | flops 18874368 | bytes 12288 | tf_op jit(solution)/shard_map/pallas_call | solution.py:340
  111.9 1.7 %collective-permute-done.36.rest_1_ = bf16[128,1536]{1,0:T(8,128)(2,1)S(1)} collective-permute-done((bf16[128,1536]{1,0:T(8,128)(2,1)S(1)}, bf16[128,1536]{1,0:T(8,128)(2,1)S(1)}, u32[]{:S(2)}, u32[]{:S(2)}) %collective-permute-start.36) | collective-permute-done | bytes 393248 | tf_op jit(solution)/shard_map/ppermute | solution.py:522
  113.6 1.9 %shard_map.112.refs_0_ = bf16[128,1536]{1,0:T(8,128)(2,1)S(1)} custom-call(s32[1]{0:T(128)} %bitcast.1.row_ref.refs_0_, s32[1]{0:T(128)} %bitcast.2.refs_1_.refs_0_.order_ref, s32[2,1,6144]{2,1,0:T(1,128)S(1)} %reshape.7.map_ref, bf16[128,1536]{1,0:T(8,128)(2,1)S(1)} %shard_map.111.rest_0_, bf16[128,1536]{1,0:T(8,128)(2,1)S(1)} %collective-permute-done.36.rest_1_, ...), custom_call_target="tpu_custom_call" | custom-call | flops 18874368 | bytes 12288 | tf_op jit(solution)/shard_map/pallas_call | solution.py:340
  119.6 4.2 %shard_map.116 = (bf16[128,1536]{1,0:T(8,128)(2,1)S(1)}, bf16[1536,3072]{1,0:T(8,128)(2,1)S(1)}) custom-call(s32[1]{0:T(128)} %bitcast.1.row_ref.refs_0_, s32[1]{0:T(128)} %bitcast.2.refs_1_.refs_0_.order_ref, s32[2,1,6144]{2,1,0:T(1,128)S(1)} %reshape.7.map_ref, bf16[128,1536]{1,0:T(8,128)(2,1)S(1)} %shard_map.111.rest_0_, ...), custom_call_target="tpu_custom_call" | custom-call | flops 18874368 | bytes 12288 | tf_op jit(solution)/shard_map/pallas_call | solution.py:340
  131.8 1.5 shard_map.122.refs_3_.refs_0_
  133.3 1.4 collective-permute-start.52
  134.7 1.5 shard_map.123.refs_4_.refs_0_
  136.2 1.9 %collective-permute-done.42.refs_2_ = bf16[128,1536]{1,0:T(8,128)(2,1)S(1)} collective-permute-done((bf16[128,1536]{1,0:T(8,128)(2,1)S(1)}, bf16[128,1536]{1,0:T(8,128)(2,1)S(1)}, u32[]{:S(2)}, u32[]{:S(2)}) %collective-permute-start.42) | collective-permute-done | bytes 393248 | tf_op jit(solution)/shard_map/ppermute | solution.py:522
  140.8 1.5 shard_map.127.refs_0_
  144.1 1.5 shard_map.126.refs_0_
  148.2 3.4 %collective-permute-done.54.refs_1_ = bf16[128,768]{1,0:T(8,128)(2,1)S(1)} collective-permute-done((bf16[128,768]{1,0:T(8,128)(2,1)S(1)}, bf16[128,768]{1,0:T(8,128)(2,1)S(1)}, u32[]{:S(2)}, u32[]{:S(2)}) %collective-permute-start.54) | collective-permute-done | bytes 196640 | tf_op jit(solution)/shard_map/ppermute | solution.py:522
  152.4 2.6 %collective-permute-done.53.refs_1_ = bf16[128,768]{1,0:T(8,128)(2,1)S(1)} collective-permute-done((bf16[128,768]{1,0:T(8,128)(2,1)S(1)}, bf16[128,768]{1,0:T(8,128)(2,1)S(1)}, u32[]{:S(2)}, u32[]{:S(2)}) %collective-permute-start.53) | collective-permute-done | bytes 196640 | tf_op jit(solution)/shard_map/ppermute | solution.py:522
  (125 shorter events, 36.0 us)
Async XLA Ops:
  3.7 3.6 %collective-permute-start = (bf16[128,1536]{1,0:T(8,128)(2,1)S(1)}, bf16[128,1536]{1,0:T(8,128)(2,1)S(1)}, u32[]{:S(2)}, u32[]{:S(2)}) collective-permute-start(bf16[128,1536]{1,0:T(8,128)(2,1)S(1)} %shard_map.77.rest_0_), channel_id=1, source_target_pairs={{0,2},{2,0},{4,6},{6,4},{1,3},{3,1},{5,7},{7,5},{8,10},{10,8},{12,... | collective-permute-start | bytes 1179656 | tf_op jit(solution)/shard_map/ppermute | solution.py:522
  7.4 12.4 %collective-permute-start.6 = (bf16[128,1536]{1,0:T(8,128)(2,1)S(1)}, bf16[128,1536]{1,0:T(8,128)(2,1)S(1)}, u32[]{:S(2)}, u32[]{:S(2)}) collective-permute-start(bf16[128,1536]{1,0:T(8,128)(2,1)S(1)} %get-tuple-element.69.rest_0_), channel_id=1, source_target_pairs={{0,4},{2,6},{4,0},{6,2},{1,5},{3,7},{5,1},{7,3},{8,12},{10,14},{12... | collective-permute-start | bytes 1179656 | tf_op jit(solution)/shard_map/ppermute | solution.py:522
  13.0 4.1 %collective-permute-start.1 = (bf16[32,1536]{1,0:T(8,128)(2,1)S(1)}, bf16[32,1536]{1,0:T(8,128)(2,1)S(1)}, u32[]{:S(2)}, u32[]{:S(2)}) collective-permute-start(bf16[32,1536]{1,0:T(8,128)(2,1)S(1)} %get-tuple-element.70.rest_0_), channel_id=1, source_target_pairs={{0,2},{2,0},{4,6},{6,4},{1,3},{3,1},{5,7},{7,5},{8,10},{10,8},{12,... | collective-permute-start | bytes 294920 | tf_op jit(solution)/shard_map/ppermute | solution.py:522
  13.3 3.9 %collective-permute-start.2 = (bf16[32,1536]{1,0:T(8,128)(2,1)S(1)}, bf16[32,1536]{1,0:T(8,128)(2,1)S(1)}, u32[]{:S(2)}, u32[]{:S(2)}) collective-permute-start(bf16[32,1536]{1,0:T(8,128)(2,1)S(1)} %get-tuple-element.71), channel_id=1, source_target_pairs={{0,2},{2,0},{4,6},{6,4},{1,3},{3,1},{5,7},{7,5},{8,10},{10,8},{12,... | collective-permute-start | bytes 294920 | tf_op jit(solution)/shard_map/ppermute | solution.py:522
  13.6 3.6 %collective-permute-start.3 = (bf16[32,1536]{1,0:T(8,128)(2,1)S(1)}, bf16[32,1536]{1,0:T(8,128)(2,1)S(1)}, u32[]{:S(2)}, u32[]{:S(2)}) collective-permute-start(bf16[32,1536]{1,0:T(8,128)(2,1)S(1)} %get-tuple-element.72), channel_id=1, source_target_pairs={{0,2},{2,0},{4,6},{6,4},{1,3},{3,1},{5,7},{7,5},{8,10},{10,8},{12,... | collective-permute-start | bytes 294920 | tf_op jit(solution)/shard_map/ppermute | solution.py:522
  13.8 3.4 %collective-permute-start.4 = (bf16[32,1536]{1,0:T(8,128)(2,1)S(1)}, bf16[32,1536]{1,0:T(8,128)(2,1)S(1)}, u32[]{:S(2)}, u32[]{:S(2)}) collective-permute-start(bf16[32,1536]{1,0:T(8,128)(2,1)S(1)} %get-tuple-element.73), channel_id=1, source_target_pairs={{0,2},{2,0},{4,6},{6,4},{1,3},{3,1},{5,7},{7,5},{8,10},{10,8},{12,... | collective-permute-start | bytes 294920 | tf_op jit(solution)/shard_map/ppermute | solution.py:522
  17.3 14.9 %collective-permute-start.5 = (bf16[128,1536]{1,0:T(8,128)(2,1)S(1)}, bf16[128,1536]{1,0:T(8,128)(2,1)S(1)}, u32[]{:S(2)}, u32[]{:S(2)}) collective-permute-start(bf16[128,1536]{1,0:T(8,128)(2,1)S(1)} %get-tuple-element.75.rest_0_), channel_id=1, source_target_pairs={{0,4},{2,6},{4,0},{6,2},{1,5},{3,7},{5,1},{7,3},{8,12},{10,14},{12... | collective-permute-start | bytes 1179656 | tf_op jit(solution)/shard_map/ppermute | solution.py:522
  19.8 5.4 %collective-permute-start.7 = (bf16[32,1536]{1,0:T(8,128)(2,1)S(1)}, bf16[32,1536]{1,0:T(8,128)(2,1)S(1)}, u32[]{:S(2)}, u32[]{:S(2)}) collective-permute-start(bf16[32,1536]{1,0:T(8,128)(2,1)S(1)} %get-tuple-element.77.rest_0_.refs_0_), channel_id=1, source_target_pairs={{0,2},{2,0},{4,6},{6,4},{1,3},{3,1},{5,7},{7,5},{8,10},{10,8},{12,... | collective-permute-start | bytes 294920 | tf_op jit(solution)/shard_map/ppermute | solution.py:522
  19.9 5.3 %collective-permute-start.8 = (bf16[32,1536]{1,0:T(8,128)(2,1)S(1)}, bf16[32,1536]{1,0:T(8,128)(2,1)S(1)}, u32[]{:S(2)}, u32[]{:S(2)}) collective-permute-start(bf16[32,1536]{1,0:T(8,128)(2,1)S(1)} %get-tuple-element.78.rest_1_.refs_1_), channel_id=1, source_target_pairs={{0,2},{2,0},{4,6},{6,4},{1,3},{3,1},{5,7},{7,5},{8,10},{10,8},{12,... | collective-permute-start | bytes 294920 | tf_op jit(solution)/shard_map/ppermute | solution.py:522
  20.4 4.8 %collective-permute-start.9 = (bf16[32,1536]{1,0:T(8,128)(2,1)S(1)}, bf16[32,1536]{1,0:T(8,128)(2,1)S(1)}, u32[]{:S(2)}, u32[]{:S(2)}) collective-permute-start(bf16[32,1536]{1,0:T(8,128)(2,1)S(1)} %get-tuple-element.79.rest_2_.refs_2_), channel_id=1, source_target_pairs={{0,2},{2,0},{4,6},{6,4},{1,3},{3,1},{5,7},{7,5},{8,10},{10,8},{12,... | collective-permute-start | bytes 294920 | tf_op jit(solution)/shard_map/ppermute | solution.py:522
  20.5 4.8 %collective-permute-start.10 = (bf16[32,1536]{1,0:T(8,128)(2,1)S(1)}, bf16[32,1536]{1,0:T(8,128)(2,1)S(1)}, u32[]{:S(2)}, u32[]{:S(2)}) collective-permute-start(bf16[32,1536]{1,0:T(8,128)(2,1)S(1)} %get-tuple-element.80.rest_3_.refs_3_), channel_id=1, source_target_pairs={{0,2},{2,0},{4,6},{6,4},{1,3},{3,1},{5,7},{7,5},{8,10},{10,8},{12,... | collective-permute-start | bytes 294920 | tf_op jit(solution)/shard_map/ppermute | solution.py:522
  32.2 1.8 %collective-permute-start.11 = (bf16[128,1536]{1,0:T(8,128)(2,1)S(1)}, bf16[128,1536]{1,0:T(8,128)(2,1)S(1)}, u32[]{:S(2)}, u32[]{:S(2)}) collective-permute-start(bf16[128,1536]{1,0:T(8,128)(2,1)S(1)} %shard_map.88.refs_0_), channel_id=1, source_target_pairs={{0,2},{2,0},{4,6},{6,4},{1,3},{3,1},{5,7},{7,5},{8,10},{10,8},{12,... | collective-permute-start | bytes 1179656 | tf_op jit(solution)/shard_map/ppermute | solution.py:522
  39.5 4.8 %collective-permute-start.12 = (bf16[2,128,1536]{2,1,0:T(8,128)(2,1)S(1)}, bf16[2,128,1536]{2,1,0:T(8,128)(2,1)S(1)}, u32[]{:S(2)}, u32[]{:S(2)}) collective-permute-start(bf16[2,128,1536]{2,1,0:T(8,128)(2,1)S(1)} %shard_map.92), channel_id=1, source_target_pairs={{0,2},{2,0},{4,6},{6,4},{1,3},{3,1},{5,7},{7,5},{8,10},{10,8},{12,... | collective-permute-start | bytes 2359304 | tf_op jit(solution)/shard_map/ppermute | solution.py:522
  44.4 7.3 %collective-permute-start.13 = (bf16[128,768]{1,0:T(8,128)(2,1)S(1)}, bf16[128,768]{1,0:T(8,128)(2,1)S(1)}, u32[]{:S(2)}, u32[]{:S(2)}) collective-permute-start(bf16[128,768]{1,0:T(8,128)(2,1)S(1)} %get-tuple-element.85), channel_id=1, source_target_pairs={{0,1},{1,0},{2,3},{3,2},{4,5},{5,4},{6,7},{7,6},{8,9},{9,8},{10,11... | collective-permute-start | bytes 589832 | tf_op jit(solution)/shard_map/ppermute | solution.py:522
  46.3 7.7 %collective-permute-start.15 = (bf16[128,768]{1,0:T(8,128)(2,1)S(1)}, bf16[128,768]{1,0:T(8,128)(2,1)S(1)}, u32[]{:S(2)}, u32[]{:S(2)}) collective-permute-start(bf16[128,768]{1,0:T(8,128)(2,1)S(1)} %get-tuple-element.89), channel_id=1, source_target_pairs={{0,4},{2,6},{4,0},{6,2},{1,5},{3,7},{5,1},{7,3},{8,12},{10,14},{12... | collective-permute-start | bytes 589832 | tf_op jit(solution)/shard_map/ppermute | solution.py:522
  51.7 4.8 %collective-permute-start.14 = (bf16[64,768]{1,0:T(8,128)(2,1)S(1)}, bf16[64,768]{1,0:T(8,128)(2,1)S(1)}, u32[]{:S(2)}, u32[]{:S(2)}) collective-permute-start(bf16[64,768]{1,0:T(8,128)(2,1)S(1)} %get-tuple-element.87), channel_id=1, source_target_pairs={{0,4},{2,6},{4,0},{6,2},{1,5},{3,7},{5,1},{7,3},{8,12},{10,14},{12... | collective-permute-start | bytes 294920 | tf_op jit(solution)/shard_map/ppermute | solution.py:522
  54.0 4.7 %collective-permute-start.16 = (bf16[64,768]{1,0:T(8,128)(2,1)S(1)}, bf16[64,768]{1,0:T(8,128)(2,1)S(1)}, u32[]{:S(2)}, u32[]{:S(2)}) collective-permute-start(bf16[64,768]{1,0:T(8,128)(2,1)S(1)} %get-tuple-element.91), channel_id=1, source_target_pairs={{0,1},{1,0},{2,3},{3,2},{4,5},{5,4},{6,7},{7,6},{8,9},{9,8},{10,11... | collective-permute-start | bytes 294920 | tf_op jit(solution)/shard_map/ppermute | solution.py:522
  58.7 8.2 %collective-permute-start.17 = (bf16[16,1536]{1,0:T(8,128)(2,1)S(1)}, bf16[16,1536]{1,0:T(8,128)(2,1)S(1)}, u32[]{:S(2)}, u32[]{:S(2)}) collective-permute-start(bf16[16,1536]{1,0:T(8,128)(2,1)S(1)} %get-tuple-element.93.rest_0_), channel_id=1, source_target_pairs={{0,8},{8,0},{16,24},{24,16},{1,9},{9,1},{17,25},{25,17},{2,10},{10... | collective-permute-start | bytes 147464 | tf_op jit(solution)/shard_map/ppermute | solution.py:522
  60.4 6.5 %collective-permute-start.18 = (bf16[16,1536]{1,0:T(8,128)(2,1)S(1)}, bf16[16,1536]{1,0:T(8,128)(2,1)S(1)}, u32[]{:S(2)}, u32[]{:S(2)}) collective-permute-start(bf16[16,1536]{1,0:T(8,128)(2,1)S(1)} %get-tuple-element.94.rest_1_), channel_id=1, source_target_pairs={{0,16},{8,24},{16,0},{24,8},{1,17},{9,25},{17,1},{25,9},{2,18},{10... | collective-permute-start | bytes 147464 | tf_op jit(solution)/shard_map/ppermute | solution.py:522
  63.0 5.9 %collective-permute-start.19 = (bf16[16,1536]{1,0:T(8,128)(2,1)S(1)}, bf16[16,1536]{1,0:T(8,128)(2,1)S(1)}, u32[]{:S(2)}, u32[]{:S(2)}) collective-permute-start(bf16[16,1536]{1,0:T(8,128)(2,1)S(1)} %get-tuple-element.95.rest_2_), channel_id=1, source_target_pairs={{0,24},{8,16},{16,8},{24,0},{1,25},{9,17},{17,9},{25,1},{2,26},{10... | collective-permute-start | bytes 147464 | tf_op jit(solution)/shard_map/ppermute | solution.py:522
  68.9 4.2 %collective-permute-start.20 = (bf16[16,1536]{1,0:T(8,128)(2,1)S(1)}, bf16[16,1536]{1,0:T(8,128)(2,1)S(1)}, u32[]{:S(2)}, u32[]{:S(2)}) collective-permute-start(bf16[16,1536]{1,0:T(8,128)(2,1)S(1)} %shard_map.98.refs_0_), channel_id=1, source_target_pairs={{0,1},{1,0},{2,3},{3,2},{4,5},{5,4},{6,7},{7,6},{8,9},{9,8},{10,11... | collective-permute-start | bytes 147464 | tf_op jit(solution)/shard_map/ppermute | solution.py:522
  75.3 4.9 %collective-permute-start.22 = (bf16[32,1536]{1,0:T(8,128)(2,1)S(1)}, bf16[32,1536]{1,0:T(8,128)(2,1)S(1)}, u32[]{:S(2)}, u32[]{:S(2)}) collective-permute-start(bf16[32,1536]{1,0:T(8,128)(2,1)S(1)} %get-tuple-element.99.rest_0_), channel_id=1, source_target_pairs={{0,4},{2,6},{4,0},{6,2},{1,5},{3,7},{5,1},{7,3},{8,12},{10,14},{12... | collective-permute-start | bytes 294920 | tf_op jit(solution)/shard_map/ppermute | solution.py:522
  86.2 4.2 %collective-permute-start.24 = (bf16[16,1536]{1,0:T(8,128)(2,1)S(1)}, bf16[16,1536]{1,0:T(8,128)(2,1)S(1)}, u32[]{:S(2)}, u32[]{:S(2)}) collective-permute-start(bf16[16,1536]{1,0:T(8,128)(2,1)S(1)} %get-tuple-element.102), channel_id=1, source_target_pairs={{0,1},{1,0},{2,3},{3,2},{4,5},{5,4},{6,7},{7,6},{8,9},{9,8},{10,11... | collective-permute-start | bytes 147464 | tf_op jit(solution)/shard_map/ppermute | solution.py:522
  90.4 4.5 %collective-permute-start.25 = (bf16[16,1536]{1,0:T(8,128)(2,1)S(1)}, bf16[16,1536]{1,0:T(8,128)(2,1)S(1)}, u32[]{:S(2)}, u32[]{:S(2)}) collective-permute-start(bf16[16,1536]{1,0:T(8,128)(2,1)S(1)} %shard_map.105.refs_0_), channel_id=1, source_target_pairs={{0,8},{8,0},{16,24},{24,16},{1,9},{9,1},{17,25},{25,17},{2,10},{10... | collective-permute-start | bytes 147464 | tf_op jit(solution)/shard_map/ppermute | solution.py:522
  90.5 5.1 %collective-permute-start.26 = (bf16[16,1536]{1,0:T(8,128)(2,1)S(1)}, bf16[16,1536]{1,0:T(8,128)(2,1)S(1)}, u32[]{:S(2)}, u32[]{:S(2)}) collective-permute-start(bf16[16,1536]{1,0:T(8,128)(2,1)S(1)} %shard_map.105.refs_0_), channel_id=1, source_target_pairs={{0,16},{8,24},{16,0},{24,8},{1,17},{9,25},{17,1},{25,9},{2,18},{10... | collective-permute-start | bytes 147464 | tf_op jit(solution)/shard_map/ppermute | solution.py:522
  92.7 5.9 %collective-permute-start.27 = (bf16[16,1536]{1,0:T(8,128)(2,1)S(1)}, bf16[16,1536]{1,0:T(8,128)(2,1)S(1)}, u32[]{:S(2)}, u32[]{:S(2)}) collective-permute-start(bf16[16,1536]{1,0:T(8,128)(2,1)S(1)} %shard_map.105.refs_0_), channel_id=1, source_target_pairs={{0,24},{8,16},{16,8},{24,0},{1,25},{9,17},{17,9},{25,1},{2,26},{10... | collective-permute-start | bytes 147464 | tf_op jit(solution)/shard_map/ppermute | solution.py:522
  98.6 6.2 %collective-permute-start.30 = (bf16[64,1536]{1,0:T(8,128)(2,1)S(1)}, bf16[64,1536]{1,0:T(8,128)(2,1)S(1)}, u32[]{:S(2)}, u32[]{:S(2)}) collective-permute-start(bf16[64,1536]{1,0:T(8,128)(2,1)S(1)} %shard_map.106.rest_0_.refs_0_), channel_id=1, source_target_pairs={{0,1},{1,0},{2,3},{3,2},{4,5},{5,4},{6,7},{7,6},{8,9},{9,8},{10,11... | collective-permute-start | bytes 589832 | tf_op jit(solution)/shard_map/ppermute | solution.py:522
  100.2 5.7 %collective-permute-start.28 = (bf16[64,1536]{1,0:T(8,128)(2,1)S(1)}, bf16[64,1536]{1,0:T(8,128)(2,1)S(1)}, u32[]{:S(2)}, u32[]{:S(2)}) collective-permute-start(bf16[64,1536]{1,0:T(8,128)(2,1)S(1)} %shard_map.106.rest_0_.refs_0_), channel_id=1, source_target_pairs={{0,4},{2,6},{4,0},{6,2},{1,5},{3,7},{5,1},{7,3},{8,12},{10,14},{12... | collective-permute-start | bytes 589832 | tf_op jit(solution)/shard_map/ppermute | solution.py:522
  104.9 2.3 %collective-permute-start.32 = (bf16[32,1536]{1,0:T(8,128)(2,1)S(1)}, bf16[32,1536]{1,0:T(8,128)(2,1)S(1)}, u32[]{:S(2)}, u32[]{:S(2)}) collective-permute-start(bf16[32,1536]{1,0:T(8,128)(2,1)S(1)} %get-tuple-element.104.rest_0_.refs_0_), channel_id=1, source_target_pairs={{0,2},{2,0},{4,6},{6,4},{1,3},{3,1},{5,7},{7,5},{8,10},{10,8},{12,... | collective-permute-start | bytes 294920 | tf_op jit(solution)/shard_map/ppermute | solution.py:522
  104.9 3.1 %collective-permute-start.33 = (bf16[32,1536]{1,0:T(8,128)(2,1)S(1)}, bf16[32,1536]{1,0:T(8,128)(2,1)S(1)}, u32[]{:S(2)}, u32[]{:S(2)}) collective-permute-start(bf16[32,1536]{1,0:T(8,128)(2,1)S(1)} %get-tuple-element.105.rest_1_.refs_1_), channel_id=1, source_target_pairs={{0,2},{2,0},{4,6},{6,4},{1,3},{3,1},{5,7},{7,5},{8,10},{10,8},{12,... | collective-permute-start | bytes 294920 | tf_op jit(solution)/shard_map/ppermute | solution.py:522
  105.4 2.6 %collective-permute-start.34 = (bf16[32,1536]{1,0:T(8,128)(2,1)S(1)}, bf16[32,1536]{1,0:T(8,128)(2,1)S(1)}, u32[]{:S(2)}, u32[]{:S(2)}) collective-permute-start(bf16[32,1536]{1,0:T(8,128)(2,1)S(1)} %get-tuple-element.106.rest_2_.refs_2_), channel_id=1, source_target_pairs={{0,2},{2,0},{4,6},{6,4},{1,3},{3,1},{5,7},{7,5},{8,10},{10,8},{12,... | collective-permute-start | bytes 294920 | tf_op jit(solution)/shard_map/ppermute | solution.py:522
  105.5 2.6 %collective-permute-start.35 = (bf16[32,1536]{1,0:T(8,128)(2,1)S(1)}, bf16[32,1536]{1,0:T(8,128)(2,1)S(1)}, u32[]{:S(2)}, u32[]{:S(2)}) collective-permute-start(bf16[32,1536]{1,0:T(8,128)(2,1)S(1)} %get-tuple-element.107.rest_3_.refs_3_), channel_id=1, source_target_pairs={{0,2},{2,0},{4,6},{6,4},{1,3},{3,1},{5,7},{7,5},{8,10},{10,8},{12,... | collective-permute-start | bytes 294920 | tf_op jit(solution)/shard_map/ppermute | solution.py:522
  106.0 5.9 %collective-permute-start.29 = (bf16[32,1536]{1,0:T(8,128)(2,1)S(1)}, bf16[32,1536]{1,0:T(8,128)(2,1)S(1)}, u32[]{:S(2)}, u32[]{:S(2)}) collective-permute-start(bf16[32,1536]{1,0:T(8,128)(2,1)S(1)} %slice.8), channel_id=1, source_target_pairs={{0,1},{1,0},{2,3},{3,2},{4,5},{5,4},{6,7},{7,6},{8,9},{9,8},{10,11... | collective-permute-start | bytes 294920 | tf_op jit(solution)/shard_map/ppermute | solution.py:522
  107.1 4.7 %collective-permute-start.31 = (bf16[32,1536]{1,0:T(8,128)(2,1)S(1)}, bf16[32,1536]{1,0:T(8,128)(2,1)S(1)}, u32[]{:S(2)}, u32[]{:S(2)}) collective-permute-start(bf16[32,1536]{1,0:T(8,128)(2,1)S(1)} %slice.9), channel_id=1, source_target_pairs={{0,4},{2,6},{4,0},{6,2},{1,5},{3,7},{5,1},{7,3},{8,12},{10,14},{12... | collective-permute-start | bytes 294920 | tf_op jit(solution)/shard_map/ppermute | solution.py:522
  111.9 1.8 %collective-permute-start.36 = (bf16[128,1536]{1,0:T(8,128)(2,1)S(1)}, bf16[128,1536]{1,0:T(8,128)(2,1)S(1)}, u32[]{:S(2)}, u32[]{:S(2)}) collective-permute-start(bf16[128,1536]{1,0:T(8,128)(2,1)S(1)} %shard_map.111.rest_0_), channel_id=1, source_target_pairs={{0,2},{2,0},{4,6},{6,4},{1,3},{3,1},{5,7},{7,5},{8,10},{10,8},{12,... | collective-permute-start | bytes 1179656 | tf_op jit(solution)/shard_map/ppermute | solution.py:522
  116.4 1.8 %collective-permute-start.37 = (bf16[128,1536]{1,0:T(8,128)(2,1)S(1)}, bf16[128,1536]{1,0:T(8,128)(2,1)S(1)}, u32[]{:S(2)}, u32[]{:S(2)}) collective-permute-start(bf16[128,1536]{1,0:T(8,128)(2,1)S(1)} %shard_map.113.refs_2_), channel_id=1, source_target_pairs={{0,2},{2,0},{4,6},{6,4},{1,3},{3,1},{5,7},{7,5},{8,10},{10,8},{12,... | collective-permute-start | bytes 1179656 | tf_op jit(solution)/shard_map/ppermute | solution.py:522
  118.3 11.2 %collective-permute-start.43 = (bf16[128,1536]{1,0:T(8,128)(2,1)S(1)}, bf16[128,1536]{1,0:T(8,128)(2,1)S(1)}, u32[]{:S(2)}, u32[]{:S(2)}) collective-permute-start(bf16[128,1536]{1,0:T(8,128)(2,1)S(1)} %get-tuple-element.109.rest_4_), channel_id=1, source_target_pairs={{0,4},{2,6},{4,0},{6,2},{1,5},{3,7},{5,1},{7,3},{8,12},{10,14},{12... | collective-permute-start | bytes 1179656 | tf_op jit(solution)/shard_map/ppermute | solution.py:522
  124.6 1.9 %collective-permute-start.38 = (bf16[32,1536]{1,0:T(8,128)(2,1)S(1)}, bf16[32,1536]{1,0:T(8,128)(2,1)S(1)}, u32[]{:S(2)}, u32[]{:S(2)}) collective-permute-start(bf16[32,1536]{1,0:T(8,128)(2,1)S(1)} %get-tuple-element.112.refs_2_), channel_id=1, source_target_pairs={{0,2},{2,0},{4,6},{6,4},{1,3},{3,1},{5,7},{7,5},{8,10},{10,8},{12,... | collective-permute-start | bytes 294920 | tf_op jit(solution)/shard_map/ppermute | solution.py:522
  124.6 1.8 %collective-permute-start.39 = (bf16[32,1536]{1,0:T(8,128)(2,1)S(1)}, bf16[32,1536]{1,0:T(8,128)(2,1)S(1)}, u32[]{:S(2)}, u32[]{:S(2)}) collective-permute-start(bf16[32,1536]{1,0:T(8,128)(2,1)S(1)} %get-tuple-element.113), channel_id=1, source_target_pairs={{0,2},{2,0},{4,6},{6,4},{1,3},{3,1},{5,7},{7,5},{8,10},{10,8},{12,... | collective-permute-start | bytes 294920 | tf_op jit(solution)/shard_map/ppermute | solution.py:522
  126.7 11.4 %collective-permute-start.42 = (bf16[128,1536]{1,0:T(8,128)(2,1)S(1)}, bf16[128,1536]{1,0:T(8,128)(2,1)S(1)}, u32[]{:S(2)}, u32[]{:S(2)}) collective-permute-start(bf16[128,1536]{1,0:T(8,128)(2,1)S(1)} %get-tuple-element.117.refs_7_), channel_id=1, source_target_pairs={{0,4},{2,6},{4,0},{6,2},{1,5},{3,7},{5,1},{7,3},{8,12},{10,14},{12... | collective-permute-start | bytes 1179656 | tf_op jit(solution)/shard_map/ppermute | solution.py:522
  129.8 1.4 collective-permute-start.45
  133.3 10.0 %collective-permute-start.52 = (bf16[128,768]{1,0:T(8,128)(2,1)S(1)}, bf16[128,768]{1,0:T(8,128)(2,1)S(1)}, u32[]{:S(2)}, u32[]{:S(2)}) collective-permute-start(bf16[128,768]{1,0:T(8,128)(2,1)S(1)} %shard_map.122.refs_3_.refs_0_), channel_id=1, source_target_pairs={{0,1},{1,0},{2,3},{3,2},{4,5},{5,4},{6,7},{7,6},{8,9},{9,8},{10,11... | collective-permute-start | bytes 589832 | tf_op jit(solution)/shard_map/ppermute | solution.py:522
  138.4 2.4 %collective-permute-start.49 = (bf16[32,1536]{1,0:T(8,128)(2,1)S(1)}, bf16[32,1536]{1,0:T(8,128)(2,1)S(1)}, u32[]{:S(2)}, u32[]{:S(2)}) collective-permute-start(bf16[32,1536]{1,0:T(8,128)(2,1)S(1)} %get-tuple-element.126.refs_1_), channel_id=1, source_target_pairs={{0,2},{2,0},{4,6},{6,4},{1,3},{3,1},{5,7},{7,5},{8,10},{10,8},{12,... | collective-permute-start | bytes 294920 | tf_op jit(solution)/shard_map/ppermute | solution.py:522
  138.9 1.9 %collective-permute-start.50 = (bf16[32,1536]{1,0:T(8,128)(2,1)S(1)}, bf16[32,1536]{1,0:T(8,128)(2,1)S(1)}, u32[]{:S(2)}, u32[]{:S(2)}) collective-permute-start(bf16[32,1536]{1,0:T(8,128)(2,1)S(1)} %get-tuple-element.127.refs_2_), channel_id=1, source_target_pairs={{0,2},{2,0},{4,6},{6,4},{1,3},{3,1},{5,7},{7,5},{8,10},{10,8},{12,... | collective-permute-start | bytes 294920 | tf_op jit(solution)/shard_map/ppermute | solution.py:522
  139.0 1.8 %collective-permute-start.51 = (bf16[32,1536]{1,0:T(8,128)(2,1)S(1)}, bf16[32,1536]{1,0:T(8,128)(2,1)S(1)}, u32[]{:S(2)}, u32[]{:S(2)}) collective-permute-start(bf16[32,1536]{1,0:T(8,128)(2,1)S(1)} %get-tuple-element.128.refs_3_), channel_id=1, source_target_pairs={{0,2},{2,0},{4,6},{6,4},{1,3},{3,1},{5,7},{7,5},{8,10},{10,8},{12,... | collective-permute-start | bytes 294920 | tf_op jit(solution)/shard_map/ppermute | solution.py:522
  139.7 7.7 %collective-permute-start.55 = (bf16[128,768]{1,0:T(8,128)(2,1)S(1)}, bf16[128,768]{1,0:T(8,128)(2,1)S(1)}, u32[]{:S(2)}, u32[]{:S(2)}) collective-permute-start(bf16[128,768]{1,0:T(8,128)(2,1)S(1)} %shard_map.123.refs_4_.refs_0_), channel_id=1, source_target_pairs={{0,1},{1,0},{2,3},{3,2},{4,5},{5,4},{6,7},{7,6},{8,9},{9,8},{10,11... | collective-permute-start | bytes 589832 | tf_op jit(solution)/shard_map/ppermute | solution.py:522
  142.3 9.3 %collective-permute-start.54 = (bf16[128,768]{1,0:T(8,128)(2,1)S(1)}, bf16[128,768]{1,0:T(8,128)(2,1)S(1)}, u32[]{:S(2)}, u32[]{:S(2)}) collective-permute-start(bf16[128,768]{1,0:T(8,128)(2,1)S(1)} %shard_map.127.refs_0_), channel_id=1, source_target_pairs={{0,1},{1,0},{2,3},{3,2},{4,5},{5,4},{6,7},{7,6},{8,9},{9,8},{10,11... | collective-permute-start | bytes 589832 | tf_op jit(solution)/shard_map/ppermute | solution.py:522
  145.6 9.4 %collective-permute-start.53 = (bf16[128,768]{1,0:T(8,128)(2,1)S(1)}, bf16[128,768]{1,0:T(8,128)(2,1)S(1)}, u32[]{:S(2)}, u32[]{:S(2)}) collective-permute-start(bf16[128,768]{1,0:T(8,128)(2,1)S(1)} %shard_map.126.refs_0_), channel_id=1, source_target_pairs={{0,1},{1,0},{2,3},{3,2},{4,5},{5,4},{6,7},{7,6},{8,9},{9,8},{10,11... | collective-permute-start | bytes 589832 | tf_op jit(solution)/shard_map/ppermute | solution.py:522
  (10 other events, 43.8 us)

commit v5 on v4

--- a/solution.py
+++ b/solution.py
@@ -597,7 +597,8 @@
         if k == 0:
             panel, _ = preload(child_panel, 0, rounded)
         bring = (child_panel, k + 1) if k < kids - 1 else None
-        upd, *brought = held_nt(*halves(rounded), panel, core, bring=bring)
+        ready = () if kept is None else (kept,)
+        upd, *brought = held_nt(*halves(rounded), panel, core, bring=bring, after=ready)
         panel = brought[0] if brought else None
         sent = scatter(upd, spread_maps, k, row_1, order, rows, root_rows, 1, sent)
         kept = scatter(upd, spread_maps, k, row_1, order, rows, root_rows, 0, kept)
@@ -639,27 +640,22 @@
     begun = core_sum(kept[0], sent)
     *panels, token = preload(child_panel, 0, begun[1:])
     _, root_forward = row_end(*begun, (token,), wide=False)
-    *part, panel = held_nt(
-        *halves(root_forward),
-        root_held,
-        core,
-        pieces=2 if wide else 1,
-        bring=(child_panel, kids - 1),
-    )
-    panels += [preload(child_panel, k, part)[0] for k in range(1, kids - 1)] + [panel]
+    part = held_nt(*halves(root_forward), root_held, core, pieces=2 if wide else 1)
 
     picked = [None] * kids
     inverses = []
     if wide:
         _, (part,) = join([[part[0]], [to_col(part[1])]], (1, 1), (), False)
         shares = [part] + [to_leaf(part, j) for j in range(1, leafs)]
-        _, (held,) = join([shares], (1,), (), False)
+        brought = [preload(child_panel, k, (part,)) for k in range(1, kids)]
+        panels += [b[0] for b in brought]
+        _, (held,) = join([shares], (1,), tuple(b[1] for b in brought), False)
         brought = [preload(child_inverse, k, (held,)) for k in range(kids - 1)]
         inverses = [b[0] for b in brought]
         tokens = tuple(b[1] for b in brought)
         beside, across = to_col(held), to_row(held, 2)
         cut = held.shape[0] // 2
-        _, near = join([[held, beside]], (1,), tokens, False, 4)
+        _, near = join([[held, beside]], (1,), tokens, False, 2)
         near_other = [to_row(x, 1) for x in near]
         rest = [to_col(across[:cut]), to_row(beside[cut:], 2)]
         for k in range(kids):
@@ -672,6 +668,7 @@
         last_blocks, last_at = [far, far_other], [2, 3]
     else:
         (part,) = part
+        panels += [preload(child_panel, k, (part,))[0] for k in range(1, kids)]
         inverses = [preload(child_inverse, k, (part,))[0] for k in range(kids - 1)]
         for bit in bits(cols):
             part = add(part, to_col(part, bit)).astype(BF16)

time: 156 us -> 152 us (0.974)
  waiting for transfers between devices: 35.8 us -> 30.2 us
  Pallas kernels: 76 us -> 78.1 us
    ppermute x56 -> x54, waiting for transfers between devices: 35.8 us -> 30.2 us  [swap(): return lax.ppermute(x, axis, [(i, i ^ bit) for i in range(size)])]
    pallas_call x4 -> x5, Pallas kernels: 15.3 us -> 19 us  [preload(): pl.pallas_call(functools.partial(preload_kernel, child), in_specs=[pl.Blo...]
    pallas_call x7, Pallas kernels: 18.7 us -> 17 us  [held_nt(): pl.pallas_call(kernel, in_specs=[SCALARS] + [WHOLE] * (len(mine) + len(ot...]
    ppermute x56 -> x54, starting transfers between devices: 42.7 us -> 42.4 us  [swap(): return lax.ppermute(x, axis, [(i, i ^ bit) for i in range(size)])]
  transfers between devices with their start and end apart: 56 -> 54, of which waited for: 25 -> 23; matrix products, arithmetic and copies ran while one was open for 0% -> 0% of each run, Pallas kernels for 37% -> 41%
where the time goes in v5:
time: 152 us
  Pallas kernels  78.1 us (51%)
  starting transfers between devices  42.4 us (28%)
  waiting for transfers between devices  30.2 us (20%)
    ppermute x54, starting transfers between devices, swap(): return lax.ppermute(x, axis, [(i, i ^ bit) for i in range(size)])  42.4 us
    ppermute x54, waiting for transfers between devices, swap(): return lax.ppermute(x, axis, [(i, i ^ bit) for i in range(size)])  30.2 us
    pallas_call x5, Pallas kernels, preload(): pl.pallas_call(functools.partial(preload_kernel, child), in_specs=[pl.Blo...  19 us
    pallas_call x7, Pallas kernels, held_nt(): pl.pallas_call(kernel, in_specs=[SCALARS] + [WHOLE] * (len(mine) + len(ot...  17 us
    pallas_call x4, Pallas kernels, nn(): pl.pallas_call(kernel, grid_spec=pltpu.PrefetchScalarGridSpec(num_scalar_...  12.1 us
    pallas_call x4, Pallas kernels, gather(): pl.pallas_call(functools.partial(gather_kernel, block_rows, tile, which,...  9.78 us
    pallas_call x4, Pallas kernels, scatter(): pl.pallas_call(functools.partial(scatter_kernel, block_rows, tile, odd, c...  8.92 us
    pallas_call x6, Pallas kernels, held_nn(): pl.pallas_call(kernel, in_specs=[SCALARS] + [WHOLE] * (len(x) + 1) + [ANY...  5.11 us
  transfers between devices with their start and end apart: 54, of which 23 were waited for; matrix products, arithmetic and copies ran while one was open for 0% of the time, Pallas kernels for 41%

profile of v5, /device:TPU:0, one launch (start us, length us, event | category | flops | bytes accessed | tf_op | source)
XLA Modules:
  0.0 152.0 jit_solution(5687059202669154059)
XLA Ops:
  0.6 3.0 %shard_map.77.rest_0_ = bf16[128,1536]{1,0:T(8,128)(2,1)S(1)} custom-call(s32[1]{0:T(128)} %bitcast.half_ref, bf16[2,128,1536]{2,1,0:T(8,128)(2,1)} %x_ref.7, bf16[2,1536,3072]{2,1,0:T(8,128)(2,1)} %rest_3_.1), custom_call_target="tpu_custom_call" | custom-call | flops 9437184 | bytes 73728 | tf_op jit(solution)/shard_map/pallas_call | solution.py:98
  4.2 3.0 %shard_map.78.refs_0_ = f32[128,1536]{1,0:T(8,128)S(1)} custom-call(s32[1]{0:T(128)} %bitcast.half_ref, bf16[2,128,1536]{2,1,0:T(8,128)(2,1)} %x_ref.7, bf16[2,1536,3072]{2,1,0:T(8,128)(2,1)} %rest_3_.1, bf16[128,1536]{1,0:T(8,128)(2,1)S(1)} %shard_map.77.rest_0_), custom_call_target="tpu_custom_call" | custom-call | flops 9437184 | bytes 73728 | tf_op jit(solution)/shard_map/pallas_call | solution.py:98
  7.4 2.6 %collective-permute-start.6 = (bf16[128,1536]{1,0:T(8,128)(2,1)S(1)}, bf16[128,1536]{1,0:T(8,128)(2,1)S(1)}, u32[]{:S(2)}, u32[]{:S(2)}) collective-permute-start(bf16[128,1536]{1,0:T(8,128)(2,1)S(1)} %get-tuple-element.68.rest_0_), channel_id=1, source_target_pairs={{0,4},{2,6},{4,0},{6,2},{1,5},{3,7},{5,1},{7,3},{8,12},{10,14},{12... | collective-permute-start | bytes 1179656 | tf_op jit(solution)/shard_map/ppermute | solution.py:522
  10.0 3.0 %shard_map.80 = (bf16[32,1536]{1,0:T(8,128)(2,1)S(1)}, bf16[32,1536]{1,0:T(8,128)(2,1)S(1)}, bf16[32,1536]{1,0:T(8,128)(2,1)S(1)}, bf16[32,1536]{1,0:T(8,128)(2,1)S(1)}) custom-call(s32[1]{0:T(128)} %bitcast.half_ref, bf16[2,128,1536]{2,1,0:T(8,128)(2,1)} %x_ref.7, bf16[2,1536,3072]{2,1,0:T(8,128)(2,1)} %rest_3_.1, ...), custom_call_target="tpu_custom_call" | custom-call | flops 9437184 | bytes 73728 | tf_op jit(solution)/shard_map/pallas_call | solution.py:98
  14.1 3.0 %shard_map.81.refs_0_ = f32[128,1536]{1,0:T(8,128)S(1)} custom-call(s32[1]{0:T(128)} %bitcast.half_ref, bf16[2,128,1536]{2,1,0:T(8,128)(2,1)} %x_ref.7, bf16[2,1536,3072]{2,1,0:T(8,128)(2,1)} %rest_3_.1, bf16[32,1536]{1,0:T(8,128)(2,1)S(1)} %get-tuple-element.69.rest_0_), custom_call_target="tpu_custom_call" | custom-call | flops 9437184 | bytes 73728 | tf_op jit(solution)/shard_map/pallas_call | solution.py:98
  18.1 1.7 %collective-permute-done.6.refs_1_ = bf16[128,1536]{1,0:T(8,128)(2,1)S(1)} collective-permute-done((bf16[128,1536]{1,0:T(8,128)(2,1)S(1)}, bf16[128,1536]{1,0:T(8,128)(2,1)S(1)}, u32[]{:S(2)}, u32[]{:S(2)}) %collective-permute-start.6) | collective-permute-done | bytes 393248 | tf_op jit(solution)/shard_map/ppermute | solution.py:522
  20.9 4.3 %shard_map.85 = (bf16[1536,3072]{1,0:T(8,128)(2,1)S(1)}, f32[8,128]{1,0:T(8,128)}) custom-call(bf16[2,1536,3072]{2,1,0:T(8,128)(2,1)} %w_ref.14, bf16[32,1536]{1,0:T(8,128)(2,1)S(1)} %get-tuple-element.76.rest_0_.refs_0_, bf16[32,1536]{1,0:T(8,128)(2,1)S(1)} %get-tuple-element.77.rest_1_.refs_1_, bf16[32,1536]{1,0:T(8,128)(2,1)S(1)} %get-tuple-element.78.rest_2_.refs_2_, ...), custom_call_target="tpu_custom_call" | custom-call | bytes 147456 | tf_op jit(solution)/shard_map/pallas_call | solution.py:57
  25.2 4.8 %shard_map.86 = (bf16[128,1536]{1,0:T(8,128)(2,1)S(1)}, bf16[1536,3072]{1,0:T(8,128)(2,1)S(1)}) custom-call(s32[1]{0:T(128)} %bitcast.half_ref, bf16[32,1536]{1,0:T(8,128)(2,1)S(1)} %get-tuple-element.76.rest_0_.refs_0_, bf16[32,1536]{1,0:T(8,128)(2,1)S(1)} %get-tuple-element.77.rest_1_.refs_1_, bf16[32,1536]{1,0:T(8,128)(2,1)S(1)} %get-tuple-element.78.rest_2_.refs_2_, ...), custom_call_target="tpu_custom_call" | custom-call | flops 18874368 | bytes 147456 | tf_op jit(solution)/shard_map/pallas_call | solution.py:176
  30.0 2.1 %shard_map.87.refs_2_.refs_4_ = bf16[2,128,1536]{2,1,0:T(8,128)(2,1)S(1)} custom-call(s32[1]{0:T(128)} %bitcast.1.row_ref.refs_0_, s32[1]{0:T(128)} %bitcast.2.refs_1_.refs_0_.order_ref, s16[2,1536,128]{2,1,0:T(8,128)(2,1)S(1)} %shard_map.83.refs_2_, bf16[128,1536]{1,0:T(8,128)(2,1)S(1)} %get-tuple-element.81.refs_3_), custom_call_target="tpu_custom_call" | custom-call | flops 18874368 | bytes 24576 | tf_op jit(solution)/shard_map/pallas_call | solution.py:268
  32.4 2.1 %shard_map.89.refs_3_.refs_4_ = bf16[2,128,1536]{2,1,0:T(8,128)(2,1)S(1)} custom-call(s32[1]{0:T(128)} %bitcast.1.row_ref.refs_0_, s32[1]{0:T(128)} %bitcast.2.refs_1_.refs_0_.order_ref, s16[2,1536,128]{2,1,0:T(8,128)(2,1)S(1)} %shard_map.83.refs_2_, bf16[128,1536]{1,0:T(8,128)(2,1)S(1)} %get-tuple-element.81.refs_3_), custom_call_target="tpu_custom_call" | custom-call | flops 18874368 | bytes 24576 | tf_op jit(solution)/shard_map/pallas_call | solution.py:268
  34.5 3.2 %shard_map.90.refs_3_ = bf16[128,1536]{1,0:T(8,128)(2,1)S(1)} custom-call(s32[1]{0:T(128)} %bitcast.half_ref, bf16[128,1536]{1,0:T(8,128)(2,1)S(1)} %shard_map.88.refs_0_, bf16[128,1536]{1,0:T(8,128)(2,1)S(1)} %collective-permute-done.11.refs_1_, bf16[1536,3072]{1,0:T(8,128)(2,1)S(1)} %get-tuple-element.82.refs_2_, ...), custom_call_target="tpu_custom_call" | custom-call | flops 18874368 | bytes 147456 | tf_op jit(solution)/shard_map/pallas_call | solution.py:176
  37.8 2.2 %shard_map.92 = bf16[2,128,1536]{2,1,0:T(8,128)(2,1)S(1)} custom-call(s32[1]{0:T(128)} %bitcast.1.row_ref.refs_0_, s32[1]{0:T(128)} %bitcast.2.refs_1_.refs_0_.order_ref, s16[2,1536,128]{2,1,0:T(8,128)(2,1)S(1)} %shard_map.83.refs_2_, bf16[128,1536]{1,0:T(8,128)(2,1)S(1)} %shard_map.90.refs_3_, bf16[2,128,1536]{2,1,0:T(8,128)(2,1)S(1)} %shard_map.87.refs_2_.refs_4_), custom_call_target="tpu_custom_call" | custom-call | flops 18874368 | bytes 24576 | tf_op jit(solution)/shard_map/pallas_call | solution.py:268
  40.5 2.4 %shard_map.91.refs_0_ = bf16[2,128,1536]{2,1,0:T(8,128)(2,1)S(1)} custom-call(s32[1]{0:T(128)} %bitcast.1.row_ref.refs_0_, s32[1]{0:T(128)} %bitcast.2.refs_1_.refs_0_.order_ref, s16[2,1536,128]{2,1,0:T(8,128)(2,1)S(1)} %shard_map.83.refs_2_, bf16[128,1536]{1,0:T(8,128)(2,1)S(1)} %shard_map.90.refs_3_, bf16[2,128,1536]{2,1,0:T(8,128)(2,1)S(1)} %shard_map.89.refs_3_.refs_4_), custom_call_target="tpu_custom_call" | custom-call | flops 18874368 | bytes 24576 | tf_op jit(solution)/shard_map/pallas_call | solution.py:268
  43.1 1.8 %collective-permute-start.13 = (bf16[128,768]{1,0:T(8,128)(2,1)S(1)}, bf16[128,768]{1,0:T(8,128)(2,1)S(1)}, u32[]{:S(2)}, u32[]{:S(2)}) collective-permute-start(bf16[128,768]{1,0:T(8,128)(2,1)S(1)} %get-tuple-element.84), channel_id=1, source_target_pairs={{0,1},{1,0},{2,3},{3,2},{4,5},{5,4},{6,7},{7,6},{8,9},{9,8},{10,11... | collective-permute-start | bytes 589832 | tf_op jit(solution)/shard_map/ppermute | solution.py:522
  45.0 1.9 %collective-permute-start.15 = (bf16[128,768]{1,0:T(8,128)(2,1)S(1)}, bf16[128,768]{1,0:T(8,128)(2,1)S(1)}, u32[]{:S(2)}, u32[]{:S(2)}) collective-permute-start(bf16[128,768]{1,0:T(8,128)(2,1)S(1)} %get-tuple-element.88), channel_id=1, source_target_pairs={{0,4},{2,6},{4,0},{6,2},{1,5},{3,7},{5,1},{7,3},{8,12},{10,14},{12... | collective-permute-start | bytes 589832 | tf_op jit(solution)/shard_map/ppermute | solution.py:522
  46.9 3.2 %collective-permute-done.13.refs_1_ = bf16[128,768]{1,0:T(8,128)(2,1)S(1)} collective-permute-done((bf16[128,768]{1,0:T(8,128)(2,1)S(1)}, bf16[128,768]{1,0:T(8,128)(2,1)S(1)}, u32[]{:S(2)}, u32[]{:S(2)}) %collective-permute-start.13) | collective-permute-done | bytes 196640 | tf_op jit(solution)/shard_map/ppermute | solution.py:522
  50.1 2.2 %collective-permute-start.14 = (bf16[64,768]{1,0:T(8,128)(2,1)S(1)}, bf16[64,768]{1,0:T(8,128)(2,1)S(1)}, u32[]{:S(2)}, u32[]{:S(2)}) collective-permute-start(bf16[64,768]{1,0:T(8,128)(2,1)S(1)} %get-tuple-element.86), channel_id=1, source_target_pairs={{0,4},{2,6},{4,0},{6,2},{1,5},{3,7},{5,1},{7,3},{8,12},{10,14},{12... | collective-permute-start | bytes 294920 | tf_op jit(solution)/shard_map/ppermute | solution.py:522
  52.4 1.6 %collective-permute-start.16 = (bf16[64,768]{1,0:T(8,128)(2,1)S(1)}, bf16[64,768]{1,0:T(8,128)(2,1)S(1)}, u32[]{:S(2)}, u32[]{:S(2)}) collective-permute-start(bf16[64,768]{1,0:T(8,128)(2,1)S(1)} %get-tuple-element.90), channel_id=1, source_target_pairs={{0,1},{1,0},{2,3},{3,2},{4,5},{5,4},{6,7},{7,6},{8,9},{9,8},{10,11... | collective-permute-start | bytes 294920 | tf_op jit(solution)/shard_map/ppermute | solution.py:522
  55.0 2.1 %collective-permute-done.16.refs_3_ = bf16[64,768]{1,0:T(8,128)(2,1)S(1)} collective-permute-done((bf16[64,768]{1,0:T(8,128)(2,1)S(1)}, bf16[64,768]{1,0:T(8,128)(2,1)S(1)}, u32[]{:S(2)}, u32[]{:S(2)}) %collective-permute-start.16) | collective-permute-done | bytes 98336 | tf_op jit(solution)/shard_map/ppermute | solution.py:522
  57.1 1.7 %collective-permute-start.17 = (bf16[16,1536]{1,0:T(8,128)(2,1)S(1)}, bf16[16,1536]{1,0:T(8,128)(2,1)S(1)}, u32[]{:S(2)}, u32[]{:S(2)}) collective-permute-start(bf16[16,1536]{1,0:T(8,128)(2,1)S(1)} %get-tuple-element.92.rest_0_), channel_id=1, source_target_pairs={{0,8},{8,0},{16,24},{24,16},{1,9},{9,1},{17,25},{25,17},{2,10},{10... | collective-permute-start | bytes 147464 | tf_op jit(solution)/shard_map/ppermute | solution.py:522
  58.8 2.6 %collective-permute-start.18 = (bf16[16,1536]{1,0:T(8,128)(2,1)S(1)}, bf16[16,1536]{1,0:T(8,128)(2,1)S(1)}, u32[]{:S(2)}, u32[]{:S(2)}) collective-permute-start(bf16[16,1536]{1,0:T(8,128)(2,1)S(1)} %get-tuple-element.93.rest_1_), channel_id=1, source_target_pairs={{0,16},{8,24},{16,0},{24,8},{1,17},{9,25},{17,1},{25,9},{2,18},{10... | collective-permute-start | bytes 147464 | tf_op jit(solution)/shard_map/ppermute | solution.py:522
  61.6 3.7 %shard_map.97 = (bf16[1536,3072]{1,0:T(8,128)(2,1)S(1)}, f32[8,128]{1,0:T(8,128)S(1)}) custom-call(bf16[1,1536,3072]{2,1,0:T(8,128)(2,1)} %bitcast.4, bf16[16,1536]{1,0:T(8,128)(2,1)S(1)} %get-tuple-element.92.rest_0_, bf16[16,1536]{1,0:T(8,128)(2,1)S(1)} %get-tuple-element.93.rest_1_, bf16[16,1536]{1,0:T(8,128)(2,1)S(1)} %get-tuple-element.94.rest_2_), custom_call_target="tpu_custom_call" | custom-call | bytes 147456 | tf_op jit(solution)/shard_map/pallas_call | solution.py:57
  65.3 2.0 %collective-permute-done.19.refs_5_ = bf16[16,1536]{1,0:T(8,128)(2,1)S(1)} collective-permute-done((bf16[16,1536]{1,0:T(8,128)(2,1)S(1)}, bf16[16,1536]{1,0:T(8,128)(2,1)S(1)}, u32[]{:S(2)}, u32[]{:S(2)}) %collective-permute-start.19) | collective-permute-done | bytes 49184 | tf_op jit(solution)/shard_map/ppermute | solution.py:522
  67.3 1.6 %collective-permute-start.20 = (bf16[16,1536]{1,0:T(8,128)(2,1)S(1)}, bf16[16,1536]{1,0:T(8,128)(2,1)S(1)}, u32[]{:S(2)}, u32[]{:S(2)}) collective-permute-start(bf16[16,1536]{1,0:T(8,128)(2,1)S(1)} %shard_map.98.refs_0_), channel_id=1, source_target_pairs={{0,1},{1,0},{2,3},{3,2},{4,5},{5,4},{6,7},{7,6},{8,9},{9,8},{10,11... | collective-permute-start | bytes 147464 | tf_op jit(solution)/shard_map/ppermute | solution.py:522
  68.9 2.6 %collective-permute-done.20.refs_1_ = bf16[16,1536]{1,0:T(8,128)(2,1)S(1)} collective-permute-done((bf16[16,1536]{1,0:T(8,128)(2,1)S(1)}, bf16[16,1536]{1,0:T(8,128)(2,1)S(1)}, u32[]{:S(2)}, u32[]{:S(2)}) %collective-permute-start.20) | collective-permute-done | bytes 49184 | tf_op jit(solution)/shard_map/ppermute | solution.py:522
  74.9 3.7 %shard_map.102 = (bf16[1536,3072]{1,0:T(8,128)(2,1)S(1)}, f32[8,128]{1,0:T(8,128)S(1)}) custom-call(bf16[2,1536,3072]{2,1,0:T(8,128)(2,1)} %w_ref.14, bf16[32,1536]{1,0:T(8,128)(2,1)S(1)} %get-tuple-element.98.rest_0_), custom_call_target="tpu_custom_call" | custom-call | bytes 147456 | tf_op jit(solution)/shard_map/pallas_call | solution.py:57
  80.1 2.9 %shard_map.104 = (bf16[16,1536]{1,0:T(8,128)(2,1)S(1)}, bf16[16,1536]{1,0:T(8,128)(2,1)S(1)}) custom-call(s32[1]{0:T(128)} %bitcast.half_ref, bf16[32,1536]{1,0:T(8,128)(2,1)S(1)} %shard_map.103.refs_0_, bf16[32,1536]{1,0:T(8,128)(2,1)S(1)} %collective-permute-done.23.refs_1_, bf16[1536,3072]{1,0:T(8,128)(2,1)S(1)} %get-tuple-element.96.refs_2_), custom_call_target="tpu_custom_call" | custom-call | flops 4718592 | bytes 147456 | tf_op jit(solution)/shard_map/pallas_call | solution.py:176
  82.9 1.6 %collective-permute-start.24 = (bf16[16,1536]{1,0:T(8,128)(2,1)S(1)}, bf16[16,1536]{1,0:T(8,128)(2,1)S(1)}, u32[]{:S(2)}, u32[]{:S(2)}) collective-permute-start(bf16[16,1536]{1,0:T(8,128)(2,1)S(1)} %get-tuple-element.101), channel_id=1, source_target_pairs={{0,1},{1,0},{2,3},{3,2},{4,5},{5,4},{6,7},{7,6},{8,9},{9,8},{10,11... | collective-permute-start | bytes 147464 | tf_op jit(solution)/shard_map/ppermute | solution.py:522
  84.5 2.6 %collective-permute-done.24.refs_1_ = bf16[16,1536]{1,0:T(8,128)(2,1)S(1)} collective-permute-done((bf16[16,1536]{1,0:T(8,128)(2,1)S(1)}, bf16[16,1536]{1,0:T(8,128)(2,1)S(1)}, u32[]{:S(2)}, u32[]{:S(2)}) %collective-permute-start.24) | collective-permute-done | bytes 49184 | tf_op jit(solution)/shard_map/ppermute | solution.py:522
  87.2 2.2 %collective-permute-start.26 = (bf16[16,1536]{1,0:T(8,128)(2,1)S(1)}, bf16[16,1536]{1,0:T(8,128)(2,1)S(1)}, u32[]{:S(2)}, u32[]{:S(2)}) collective-permute-start(bf16[16,1536]{1,0:T(8,128)(2,1)S(1)} %shard_map.105.rest_0_.refs_0_), channel_id=1, source_target_pairs={{0,16},{8,24},{16,0},{24,8},{1,17},{9,25},{17,1},{25,9},{2,18},{10... | collective-permute-start | bytes 147464 | tf_op jit(solution)/shard_map/ppermute | solution.py:522
  89.4 2.1 %collective-permute-start.27 = (bf16[16,1536]{1,0:T(8,128)(2,1)S(1)}, bf16[16,1536]{1,0:T(8,128)(2,1)S(1)}, u32[]{:S(2)}, u32[]{:S(2)}) collective-permute-start(bf16[16,1536]{1,0:T(8,128)(2,1)S(1)} %shard_map.105.rest_0_.refs_0_), channel_id=1, source_target_pairs={{0,24},{8,16},{16,8},{24,0},{1,25},{9,17},{17,9},{25,1},{2,26},{10... | collective-permute-start | bytes 147464 | tf_op jit(solution)/shard_map/ppermute | solution.py:522
  91.6 3.7 %shard_map.106 = (bf16[1536,3072]{1,0:T(8,128)(2,1)S(1)}, f32[8,128]{1,0:T(8,128)S(1)}) custom-call(bf16[2,1536,3072]{2,1,0:T(8,128)(2,1)} %w_ref.14, bf16[16,1536]{1,0:T(8,128)(2,1)S(1)} %shard_map.105.rest_0_.refs_0_), custom_call_target="tpu_custom_call" | custom-call | bytes 147456 | tf_op jit(solution)/shard_map/pallas_call | solution.py:57
  95.3 1.6 %collective-permute-start.30 = (bf16[64,1536]{1,0:T(8,128)(2,1)S(1)}, bf16[64,1536]{1,0:T(8,128)(2,1)S(1)}, u32[]{:S(2)}, u32[]{:S(2)}) collective-permute-start(bf16[64,1536]{1,0:T(8,128)(2,1)S(1)} %shard_map.107.rest_0_.refs_0_), channel_id=1, source_target_pairs={{0,1},{1,0},{2,3},{3,2},{4,5},{5,4},{6,7},{7,6},{8,9},{9,8},{10,11... | collective-permute-start | bytes 589832 | tf_op jit(solution)/shard_map/ppermute | solution.py:522
  97.8 3.7 %shard_map.108 = (bf16[1536,3072]{1,0:T(8,128)(2,1)S(1)}, f32[8,128]{1,0:T(8,128)S(1)}) custom-call(bf16[2,1536,3072]{2,1,0:T(8,128)(2,1)} %rest_3_.1, bf16[64,1536]{1,0:T(8,128)(2,1)S(1)} %shard_map.107.rest_0_.refs_0_), custom_call_target="tpu_custom_call" | custom-call | bytes 147456 | tf_op jit(solution)/shard_map/pallas_call | solution.py:57
  104.4 1.8 %shard_map.110.refs_3_.rest_2_ = bf16[128,1536]{1,0:T(8,128)(2,1)S(1)} custom-call(s32[1]{0:T(128)} %bitcast.1.row_ref.refs_0_, s32[1]{0:T(128)} %bitcast.2.refs_1_.refs_0_.order_ref, s32[2,1,6144]{2,1,0:T(1,128)S(1)} %reshape.7.map_ref, bf16[64,1536]{1,0:T(8,128)(2,1)S(1)} %get-tuple-element.104.rest_0_.refs_0_, ...), custom_call_target="tpu_custom_call" | custom-call | flops 18874368 | bytes 12288 | tf_op jit(solution)/shard_map/pallas_call | solution.py:340
  106.2 1.9 %shard_map.111.refs_4_.rest_2_ = bf16[128,1536]{1,0:T(8,128)(2,1)S(1)} custom-call(s32[1]{0:T(128)} %bitcast.1.row_ref.refs_0_, s32[1]{0:T(128)} %bitcast.2.refs_1_.refs_0_.order_ref, s32[2,1,6144]{2,1,0:T(1,128)S(1)} %reshape.7.map_ref, bf16[64,1536]{1,0:T(8,128)(2,1)S(1)} %get-tuple-element.104.rest_0_.refs_0_, ...), custom_call_target="tpu_custom_call" | custom-call | flops 18874368 | bytes 12288 | tf_op jit(solution)/shard_map/pallas_call | solution.py:340
  108.2 1.7 %collective-permute-done.34.rest_1_ = bf16[128,1536]{1,0:T(8,128)(2,1)S(1)} collective-permute-done((bf16[128,1536]{1,0:T(8,128)(2,1)S(1)}, bf16[128,1536]{1,0:T(8,128)(2,1)S(1)}, u32[]{:S(2)}, u32[]{:S(2)}) %collective-permute-start.34) | collective-permute-done | bytes 393248 | tf_op jit(solution)/shard_map/ppermute | solution.py:522
  109.9 1.9 %shard_map.113.refs_0_ = bf16[128,1536]{1,0:T(8,128)(2,1)S(1)} custom-call(s32[1]{0:T(128)} %bitcast.1.row_ref.refs_0_, s32[1]{0:T(128)} %bitcast.2.refs_1_.refs_0_.order_ref, s32[2,1,6144]{2,1,0:T(1,128)S(1)} %reshape.7.map_ref, bf16[128,1536]{1,0:T(8,128)(2,1)S(1)} %shard_map.112.rest_0_, bf16[128,1536]{1,0:T(8,128)(2,1)S(1)} %collective-permute-done.34.rest_1_, ...), custom_call_target="tpu_custom_call" | custom-call | flops 18874368 | bytes 12288 | tf_op jit(solution)/shard_map/pallas_call | solution.py:340
  115.7 4.2 %shard_map.117 = (bf16[128,1536]{1,0:T(8,128)(2,1)S(1)}, bf16[1536,3072]{1,0:T(8,128)(2,1)S(1)}) custom-call(s32[1]{0:T(128)} %bitcast.1.row_ref.refs_0_, s32[1]{0:T(128)} %bitcast.2.refs_1_.refs_0_.order_ref, s32[2,1,6144]{2,1,0:T(1,128)S(1)} %reshape.7.map_ref, bf16[128,1536]{1,0:T(8,128)(2,1)S(1)} %shard_map.112.rest_0_, ...), custom_call_target="tpu_custom_call" | custom-call | flops 18874368 | bytes 12288 | tf_op jit(solution)/shard_map/pallas_call | solution.py:340
  128.1 1.6 %shard_map.123.refs_3_.refs_0_ = bf16[128,768]{1,0:T(8,128)(2,1)S(1)} custom-call(s32[1]{0:T(128)} %bitcast.half_ref, bf16[32,1536]{1,0:T(8,128)(2,1)S(1)} %get-tuple-element.118.refs_0_, bf16[32,1536]{1,0:T(8,128)(2,1)S(1)} %get-tuple-element.119.refs_1_, bf16[32,1536]{1,0:T(8,128)(2,1)S(1)} %get-tuple-element.120.refs_2_, ...), custom_call_target="tpu_custom_call" | custom-call | flops 9437184 | bytes 73728 | tf_op jit(solution)/shard_map/pallas_call | solution.py:176
  131.0 1.5 %shard_map.124.refs_4_.refs_0_ = bf16[128,768]{1,0:T(8,128)(2,1)S(1)} custom-call(s32[1]{0:T(128)} %bitcast.half_ref, bf16[32,1536]{1,0:T(8,128)(2,1)S(1)} %get-tuple-element.118.refs_0_, bf16[32,1536]{1,0:T(8,128)(2,1)S(1)} %get-tuple-element.119.refs_1_, bf16[32,1536]{1,0:T(8,128)(2,1)S(1)} %get-tuple-element.120.refs_2_, ...), custom_call_target="tpu_custom_call" | custom-call | flops 9437184 | bytes 73728 | tf_op jit(solution)/shard_map/pallas_call | solution.py:176
  132.6 1.7 %collective-permute-done.40.refs_2_ = bf16[128,1536]{1,0:T(8,128)(2,1)S(1)} collective-permute-done((bf16[128,1536]{1,0:T(8,128)(2,1)S(1)}, bf16[128,1536]{1,0:T(8,128)(2,1)S(1)}, u32[]{:S(2)}, u32[]{:S(2)}) %collective-permute-start.40) | collective-permute-done | bytes 393248 | tf_op jit(solution)/shard_map/ppermute | solution.py:522
  135.8 1.4 collective-permute-start.53
  137.2 1.5 %shard_map.128.refs_0_ = bf16[128,768]{1,0:T(8,128)(2,1)S(1)} custom-call(s32[1]{0:T(128)} %bitcast.half_ref, bf16[32,1536]{1,0:T(8,128)(2,1)S(1)} %get-tuple-element.123.refs_0_, bf16[32,1536]{1,0:T(8,128)(2,1)S(1)} %get-tuple-element.124.refs_1_, bf16[32,1536]{1,0:T(8,128)(2,1)S(1)} %get-tuple-element.125.refs_2_, ...), custom_call_target="tpu_custom_call" | custom-call | flops 9437184 | bytes 73728 | tf_op jit(solution)/shard_map/pallas_call | solution.py:176
  140.3 1.5 %shard_map.127.refs_0_ = bf16[128,768]{1,0:T(8,128)(2,1)S(1)} custom-call(s32[1]{0:T(128)} %bitcast.half_ref, bf16[32,1536]{1,0:T(8,128)(2,1)S(1)} %get-tuple-element.123.refs_0_, bf16[32,1536]{1,0:T(8,128)(2,1)S(1)} %get-tuple-element.124.refs_1_, bf16[32,1536]{1,0:T(8,128)(2,1)S(1)} %get-tuple-element.125.refs_2_, ...), custom_call_target="tpu_custom_call" | custom-call | flops 9437184 | bytes 73728 | tf_op jit(solution)/shard_map/pallas_call | solution.py:176
  141.8 1.4 collective-permute-start.51
  144.4 3.4 %collective-permute-done.52.refs_1_ = bf16[128,768]{1,0:T(8,128)(2,1)S(1)} collective-permute-done((bf16[128,768]{1,0:T(8,128)(2,1)S(1)}, bf16[128,768]{1,0:T(8,128)(2,1)S(1)}, u32[]{:S(2)}, u32[]{:S(2)}) %collective-permute-start.52) | collective-permute-done | bytes 196640 | tf_op jit(solution)/shard_map/ppermute | solution.py:522
  148.6 2.6 %collective-permute-done.51.refs_1_ = bf16[128,768]{1,0:T(8,128)(2,1)S(1)} collective-permute-done((bf16[128,768]{1,0:T(8,128)(2,1)S(1)}, bf16[128,768]{1,0:T(8,128)(2,1)S(1)}, u32[]{:S(2)}, u32[]{:S(2)}) %collective-permute-start.51) | collective-permute-done | bytes 196640 | tf_op jit(solution)/shard_map/ppermute | solution.py:522
  (122 shorter events, 33.8 us)
Async XLA Ops:
  3.7 3.6 %collective-permute-start = (bf16[128,1536]{1,0:T(8,128)(2,1)S(1)}, bf16[128,1536]{1,0:T(8,128)(2,1)S(1)}, u32[]{:S(2)}, u32[]{:S(2)}) collective-permute-start(bf16[128,1536]{1,0:T(8,128)(2,1)S(1)} %shard_map.77.rest_0_), channel_id=1, source_target_pairs={{0,2},{2,0},{4,6},{6,4},{1,3},{3,1},{5,7},{7,5},{8,10},{10,8},{12,... | collective-permute-start | bytes 1179656 | tf_op jit(solution)/shard_map/ppermute | solution.py:522
  7.4 12.4 %collective-permute-start.6 = (bf16[128,1536]{1,0:T(8,128)(2,1)S(1)}, bf16[128,1536]{1,0:T(8,128)(2,1)S(1)}, u32[]{:S(2)}, u32[]{:S(2)}) collective-permute-start(bf16[128,1536]{1,0:T(8,128)(2,1)S(1)} %get-tuple-element.68.rest_0_), channel_id=1, source_target_pairs={{0,4},{2,6},{4,0},{6,2},{1,5},{3,7},{5,1},{7,3},{8,12},{10,14},{12... | collective-permute-start | bytes 1179656 | tf_op jit(solution)/shard_map/ppermute | solution.py:522
  13.0 4.1 %collective-permute-start.1 = (bf16[32,1536]{1,0:T(8,128)(2,1)S(1)}, bf16[32,1536]{1,0:T(8,128)(2,1)S(1)}, u32[]{:S(2)}, u32[]{:S(2)}) collective-permute-start(bf16[32,1536]{1,0:T(8,128)(2,1)S(1)} %get-tuple-element.69.rest_0_), channel_id=1, source_target_pairs={{0,2},{2,0},{4,6},{6,4},{1,3},{3,1},{5,7},{7,5},{8,10},{10,8},{12,... | collective-permute-start | bytes 294920 | tf_op jit(solution)/shard_map/ppermute | solution.py:522
  13.3 3.9 %collective-permute-start.2 = (bf16[32,1536]{1,0:T(8,128)(2,1)S(1)}, bf16[32,1536]{1,0:T(8,128)(2,1)S(1)}, u32[]{:S(2)}, u32[]{:S(2)}) collective-permute-start(bf16[32,1536]{1,0:T(8,128)(2,1)S(1)} %get-tuple-element.70), channel_id=1, source_target_pairs={{0,2},{2,0},{4,6},{6,4},{1,3},{3,1},{5,7},{7,5},{8,10},{10,8},{12,... | collective-permute-start | bytes 294920 | tf_op jit(solution)/shard_map/ppermute | solution.py:522
  13.6 3.6 %collective-permute-start.3 = (bf16[32,1536]{1,0:T(8,128)(2,1)S(1)}, bf16[32,1536]{1,0:T(8,128)(2,1)S(1)}, u32[]{:S(2)}, u32[]{:S(2)}) collective-permute-start(bf16[32,1536]{1,0:T(8,128)(2,1)S(1)} %get-tuple-element.71), channel_id=1, source_target_pairs={{0,2},{2,0},{4,6},{6,4},{1,3},{3,1},{5,7},{7,5},{8,10},{10,8},{12,... | collective-permute-start | bytes 294920 | tf_op jit(solution)/shard_map/ppermute | solution.py:522
  13.8 3.4 %collective-permute-start.4 = (bf16[32,1536]{1,0:T(8,128)(2,1)S(1)}, bf16[32,1536]{1,0:T(8,128)(2,1)S(1)}, u32[]{:S(2)}, u32[]{:S(2)}) collective-permute-start(bf16[32,1536]{1,0:T(8,128)(2,1)S(1)} %get-tuple-element.72), channel_id=1, source_target_pairs={{0,2},{2,0},{4,6},{6,4},{1,3},{3,1},{5,7},{7,5},{8,10},{10,8},{12,... | collective-permute-start | bytes 294920 | tf_op jit(solution)/shard_map/ppermute | solution.py:522
  17.3 14.9 %collective-permute-start.5 = (bf16[128,1536]{1,0:T(8,128)(2,1)S(1)}, bf16[128,1536]{1,0:T(8,128)(2,1)S(1)}, u32[]{:S(2)}, u32[]{:S(2)}) collective-permute-start(bf16[128,1536]{1,0:T(8,128)(2,1)S(1)} %get-tuple-element.74.rest_0_), channel_id=1, source_target_pairs={{0,4},{2,6},{4,0},{6,2},{1,5},{3,7},{5,1},{7,3},{8,12},{10,14},{12... | collective-permute-start | bytes 1179656 | tf_op jit(solution)/shard_map/ppermute | solution.py:522
  19.8 5.4 %collective-permute-start.7 = (bf16[32,1536]{1,0:T(8,128)(2,1)S(1)}, bf16[32,1536]{1,0:T(8,128)(2,1)S(1)}, u32[]{:S(2)}, u32[]{:S(2)}) collective-permute-start(bf16[32,1536]{1,0:T(8,128)(2,1)S(1)} %get-tuple-element.76.rest_0_.refs_0_), channel_id=1, source_target_pairs={{0,2},{2,0},{4,6},{6,4},{1,3},{3,1},{5,7},{7,5},{8,10},{10,8},{12,... | collective-permute-start | bytes 294920 | tf_op jit(solution)/shard_map/ppermute | solution.py:522
  19.9 5.3 %collective-permute-start.8 = (bf16[32,1536]{1,0:T(8,128)(2,1)S(1)}, bf16[32,1536]{1,0:T(8,128)(2,1)S(1)}, u32[]{:S(2)}, u32[]{:S(2)}) collective-permute-start(bf16[32,1536]{1,0:T(8,128)(2,1)S(1)} %get-tuple-element.77.rest_1_.refs_1_), channel_id=1, source_target_pairs={{0,2},{2,0},{4,6},{6,4},{1,3},{3,1},{5,7},{7,5},{8,10},{10,8},{12,... | collective-permute-start | bytes 294920 | tf_op jit(solution)/shard_map/ppermute | solution.py:522
  20.4 4.8 %collective-permute-start.9 = (bf16[32,1536]{1,0:T(8,128)(2,1)S(1)}, bf16[32,1536]{1,0:T(8,128)(2,1)S(1)}, u32[]{:S(2)}, u32[]{:S(2)}) collective-permute-start(bf16[32,1536]{1,0:T(8,128)(2,1)S(1)} %get-tuple-element.78.rest_2_.refs_2_), channel_id=1, source_target_pairs={{0,2},{2,0},{4,6},{6,4},{1,3},{3,1},{5,7},{7,5},{8,10},{10,8},{12,... | collective-permute-start | bytes 294920 | tf_op jit(solution)/shard_map/ppermute | solution.py:522
  20.5 4.8 %collective-permute-start.10 = (bf16[32,1536]{1,0:T(8,128)(2,1)S(1)}, bf16[32,1536]{1,0:T(8,128)(2,1)S(1)}, u32[]{:S(2)}, u32[]{:S(2)}) collective-permute-start(bf16[32,1536]{1,0:T(8,128)(2,1)S(1)} %get-tuple-element.79.rest_3_.refs_3_), channel_id=1, source_target_pairs={{0,2},{2,0},{4,6},{6,4},{1,3},{3,1},{5,7},{7,5},{8,10},{10,8},{12,... | collective-permute-start | bytes 294920 | tf_op jit(solution)/shard_map/ppermute | solution.py:522
  32.2 2.3 %collective-permute-start.11 = (bf16[128,1536]{1,0:T(8,128)(2,1)S(1)}, bf16[128,1536]{1,0:T(8,128)(2,1)S(1)}, u32[]{:S(2)}, u32[]{:S(2)}) collective-permute-start(bf16[128,1536]{1,0:T(8,128)(2,1)S(1)} %shard_map.88.refs_0_), channel_id=1, source_target_pairs={{0,2},{2,0},{4,6},{6,4},{1,3},{3,1},{5,7},{7,5},{8,10},{10,8},{12,... | collective-permute-start | bytes 1179656 | tf_op jit(solution)/shard_map/ppermute | solution.py:522
  40.0 2.9 %collective-permute-start.12 = (bf16[2,128,1536]{2,1,0:T(8,128)(2,1)S(1)}, bf16[2,128,1536]{2,1,0:T(8,128)(2,1)S(1)}, u32[]{:S(2)}, u32[]{:S(2)}) collective-permute-start(bf16[2,128,1536]{2,1,0:T(8,128)(2,1)S(1)} %shard_map.92), channel_id=1, source_target_pairs={{0,2},{2,0},{4,6},{6,4},{1,3},{3,1},{5,7},{7,5},{8,10},{10,8},{12,... | collective-permute-start | bytes 2359304 | tf_op jit(solution)/shard_map/ppermute | solution.py:522
  43.1 7.0 %collective-permute-start.13 = (bf16[128,768]{1,0:T(8,128)(2,1)S(1)}, bf16[128,768]{1,0:T(8,128)(2,1)S(1)}, u32[]{:S(2)}, u32[]{:S(2)}) collective-permute-start(bf16[128,768]{1,0:T(8,128)(2,1)S(1)} %get-tuple-element.84), channel_id=1, source_target_pairs={{0,1},{1,0},{2,3},{3,2},{4,5},{5,4},{6,7},{7,6},{8,9},{9,8},{10,11... | collective-permute-start | bytes 589832 | tf_op jit(solution)/shard_map/ppermute | solution.py:522
  45.0 7.4 %collective-permute-start.15 = (bf16[128,768]{1,0:T(8,128)(2,1)S(1)}, bf16[128,768]{1,0:T(8,128)(2,1)S(1)}, u32[]{:S(2)}, u32[]{:S(2)}) collective-permute-start(bf16[128,768]{1,0:T(8,128)(2,1)S(1)} %get-tuple-element.88), channel_id=1, source_target_pairs={{0,4},{2,6},{4,0},{6,2},{1,5},{3,7},{5,1},{7,3},{8,12},{10,14},{12... | collective-permute-start | bytes 589832 | tf_op jit(solution)/shard_map/ppermute | solution.py:522
  50.1 4.8 %collective-permute-start.14 = (bf16[64,768]{1,0:T(8,128)(2,1)S(1)}, bf16[64,768]{1,0:T(8,128)(2,1)S(1)}, u32[]{:S(2)}, u32[]{:S(2)}) collective-permute-start(bf16[64,768]{1,0:T(8,128)(2,1)S(1)} %get-tuple-element.86), channel_id=1, source_target_pairs={{0,4},{2,6},{4,0},{6,2},{1,5},{3,7},{5,1},{7,3},{8,12},{10,14},{12... | collective-permute-start | bytes 294920 | tf_op jit(solution)/shard_map/ppermute | solution.py:522
  52.4 4.7 %collective-permute-start.16 = (bf16[64,768]{1,0:T(8,128)(2,1)S(1)}, bf16[64,768]{1,0:T(8,128)(2,1)S(1)}, u32[]{:S(2)}, u32[]{:S(2)}) collective-permute-start(bf16[64,768]{1,0:T(8,128)(2,1)S(1)} %get-tuple-element.90), channel_id=1, source_target_pairs={{0,1},{1,0},{2,3},{3,2},{4,5},{5,4},{6,7},{7,6},{8,9},{9,8},{10,11... | collective-permute-start | bytes 294920 | tf_op jit(solution)/shard_map/ppermute | solution.py:522
  57.1 8.2 %collective-permute-start.17 = (bf16[16,1536]{1,0:T(8,128)(2,1)S(1)}, bf16[16,1536]{1,0:T(8,128)(2,1)S(1)}, u32[]{:S(2)}, u32[]{:S(2)}) collective-permute-start(bf16[16,1536]{1,0:T(8,128)(2,1)S(1)} %get-tuple-element.92.rest_0_), channel_id=1, source_target_pairs={{0,8},{8,0},{16,24},{24,16},{1,9},{9,1},{17,25},{25,17},{2,10},{10... | collective-permute-start | bytes 147464 | tf_op jit(solution)/shard_map/ppermute | solution.py:522
  58.8 6.5 %collective-permute-start.18 = (bf16[16,1536]{1,0:T(8,128)(2,1)S(1)}, bf16[16,1536]{1,0:T(8,128)(2,1)S(1)}, u32[]{:S(2)}, u32[]{:S(2)}) collective-permute-start(bf16[16,1536]{1,0:T(8,128)(2,1)S(1)} %get-tuple-element.93.rest_1_), channel_id=1, source_target_pairs={{0,16},{8,24},{16,0},{24,8},{1,17},{9,25},{17,1},{25,9},{2,18},{10... | collective-permute-start | bytes 147464 | tf_op jit(solution)/shard_map/ppermute | solution.py:522
  61.4 5.9 %collective-permute-start.19 = (bf16[16,1536]{1,0:T(8,128)(2,1)S(1)}, bf16[16,1536]{1,0:T(8,128)(2,1)S(1)}, u32[]{:S(2)}, u32[]{:S(2)}) collective-permute-start(bf16[16,1536]{1,0:T(8,128)(2,1)S(1)} %get-tuple-element.94.rest_2_), channel_id=1, source_target_pairs={{0,24},{8,16},{16,8},{24,0},{1,25},{9,17},{17,9},{25,1},{2,26},{10... | collective-permute-start | bytes 147464 | tf_op jit(solution)/shard_map/ppermute | solution.py:522
  67.3 4.2 %collective-permute-start.20 = (bf16[16,1536]{1,0:T(8,128)(2,1)S(1)}, bf16[16,1536]{1,0:T(8,128)(2,1)S(1)}, u32[]{:S(2)}, u32[]{:S(2)}) collective-permute-start(bf16[16,1536]{1,0:T(8,128)(2,1)S(1)} %shard_map.98.refs_0_), channel_id=1, source_target_pairs={{0,1},{1,0},{2,3},{3,2},{4,5},{5,4},{6,7},{7,6},{8,9},{9,8},{10,11... | collective-permute-start | bytes 147464 | tf_op jit(solution)/shard_map/ppermute | solution.py:522
  73.7 4.9 %collective-permute-start.22 = (bf16[32,1536]{1,0:T(8,128)(2,1)S(1)}, bf16[32,1536]{1,0:T(8,128)(2,1)S(1)}, u32[]{:S(2)}, u32[]{:S(2)}) collective-permute-start(bf16[32,1536]{1,0:T(8,128)(2,1)S(1)} %get-tuple-element.98.rest_0_), channel_id=1, source_target_pairs={{0,4},{2,6},{4,0},{6,2},{1,5},{3,7},{5,1},{7,3},{8,12},{10,14},{12... | collective-permute-start | bytes 294920 | tf_op jit(solution)/shard_map/ppermute | solution.py:522
  82.9 4.2 %collective-permute-start.24 = (bf16[16,1536]{1,0:T(8,128)(2,1)S(1)}, bf16[16,1536]{1,0:T(8,128)(2,1)S(1)}, u32[]{:S(2)}, u32[]{:S(2)}) collective-permute-start(bf16[16,1536]{1,0:T(8,128)(2,1)S(1)} %get-tuple-element.101), channel_id=1, source_target_pairs={{0,1},{1,0},{2,3},{3,2},{4,5},{5,4},{6,7},{7,6},{8,9},{9,8},{10,11... | collective-permute-start | bytes 147464 | tf_op jit(solution)/shard_map/ppermute | solution.py:522
  87.1 8.2 %collective-permute-start.25 = (bf16[16,1536]{1,0:T(8,128)(2,1)S(1)}, bf16[16,1536]{1,0:T(8,128)(2,1)S(1)}, u32[]{:S(2)}, u32[]{:S(2)}) collective-permute-start(bf16[16,1536]{1,0:T(8,128)(2,1)S(1)} %shard_map.105.rest_0_.refs_0_), channel_id=1, source_target_pairs={{0,8},{8,0},{16,24},{24,16},{1,9},{9,1},{17,25},{25,17},{2,10},{10... | collective-permute-start | bytes 147464 | tf_op jit(solution)/shard_map/ppermute | solution.py:522
  87.2 8.1 %collective-permute-start.26 = (bf16[16,1536]{1,0:T(8,128)(2,1)S(1)}, bf16[16,1536]{1,0:T(8,128)(2,1)S(1)}, u32[]{:S(2)}, u32[]{:S(2)}) collective-permute-start(bf16[16,1536]{1,0:T(8,128)(2,1)S(1)} %shard_map.105.rest_0_.refs_0_), channel_id=1, source_target_pairs={{0,16},{8,24},{16,0},{24,8},{1,17},{9,25},{17,1},{25,9},{2,18},{10... | collective-permute-start | bytes 147464 | tf_op jit(solution)/shard_map/ppermute | solution.py:522
  89.4 5.9 %collective-permute-start.27 = (bf16[16,1536]{1,0:T(8,128)(2,1)S(1)}, bf16[16,1536]{1,0:T(8,128)(2,1)S(1)}, u32[]{:S(2)}, u32[]{:S(2)}) collective-permute-start(bf16[16,1536]{1,0:T(8,128)(2,1)S(1)} %shard_map.105.rest_0_.refs_0_), channel_id=1, source_target_pairs={{0,24},{8,16},{16,8},{24,0},{1,25},{9,17},{17,9},{25,1},{2,26},{10... | collective-permute-start | bytes 147464 | tf_op jit(solution)/shard_map/ppermute | solution.py:522
  95.3 6.2 %collective-permute-start.30 = (bf16[64,1536]{1,0:T(8,128)(2,1)S(1)}, bf16[64,1536]{1,0:T(8,128)(2,1)S(1)}, u32[]{:S(2)}, u32[]{:S(2)}) collective-permute-start(bf16[64,1536]{1,0:T(8,128)(2,1)S(1)} %shard_map.107.rest_0_.refs_0_), channel_id=1, source_target_pairs={{0,1},{1,0},{2,3},{3,2},{4,5},{5,4},{6,7},{7,6},{8,9},{9,8},{10,11... | collective-permute-start | bytes 589832 | tf_op jit(solution)/shard_map/ppermute | solution.py:522
  96.9 5.7 %collective-permute-start.28 = (bf16[64,1536]{1,0:T(8,128)(2,1)S(1)}, bf16[64,1536]{1,0:T(8,128)(2,1)S(1)}, u32[]{:S(2)}, u32[]{:S(2)}) collective-permute-start(bf16[64,1536]{1,0:T(8,128)(2,1)S(1)} %shard_map.107.rest_0_.refs_0_), channel_id=1, source_target_pairs={{0,4},{2,6},{4,0},{6,2},{1,5},{3,7},{5,1},{7,3},{8,12},{10,14},{12... | collective-permute-start | bytes 589832 | tf_op jit(solution)/shard_map/ppermute | solution.py:522
  101.5 2.8 %collective-permute-start.32 = (bf16[64,1536]{1,0:T(8,128)(2,1)S(1)}, bf16[64,1536]{1,0:T(8,128)(2,1)S(1)}, u32[]{:S(2)}, u32[]{:S(2)}) collective-permute-start(bf16[64,1536]{1,0:T(8,128)(2,1)S(1)} %get-tuple-element.104.rest_0_.refs_0_), channel_id=1, source_target_pairs={{0,2},{2,0},{4,6},{6,4},{1,3},{3,1},{5,7},{7,5},{8,10},{10,8},{12,... | collective-permute-start | bytes 589832 | tf_op jit(solution)/shard_map/ppermute | solution.py:522
  101.6 2.8 %collective-permute-start.33 = (bf16[64,1536]{1,0:T(8,128)(2,1)S(1)}, bf16[64,1536]{1,0:T(8,128)(2,1)S(1)}, u32[]{:S(2)}, u32[]{:S(2)}) collective-permute-start(bf16[64,1536]{1,0:T(8,128)(2,1)S(1)} %get-tuple-element.105.rest_1_.refs_1_), channel_id=1, source_target_pairs={{0,2},{2,0},{4,6},{6,4},{1,3},{3,1},{5,7},{7,5},{8,10},{10,8},{12,... | collective-permute-start | bytes 589832 | tf_op jit(solution)/shard_map/ppermute | solution.py:522
  102.6 5.5 %collective-permute-start.29 = (bf16[32,1536]{1,0:T(8,128)(2,1)S(1)}, bf16[32,1536]{1,0:T(8,128)(2,1)S(1)}, u32[]{:S(2)}, u32[]{:S(2)}) collective-permute-start(bf16[32,1536]{1,0:T(8,128)(2,1)S(1)} %slice.8), channel_id=1, source_target_pairs={{0,1},{1,0},{2,3},{3,2},{4,5},{5,4},{6,7},{7,6},{8,9},{9,8},{10,11... | collective-permute-start | bytes 294920 | tf_op jit(solution)/shard_map/ppermute | solution.py:522
  103.3 4.8 %collective-permute-start.31 = (bf16[32,1536]{1,0:T(8,128)(2,1)S(1)}, bf16[32,1536]{1,0:T(8,128)(2,1)S(1)}, u32[]{:S(2)}, u32[]{:S(2)}) collective-permute-start(bf16[32,1536]{1,0:T(8,128)(2,1)S(1)} %slice.9), channel_id=1, source_target_pairs={{0,4},{2,6},{4,0},{6,2},{1,5},{3,7},{5,1},{7,3},{8,12},{10,14},{12... | collective-permute-start | bytes 294920 | tf_op jit(solution)/shard_map/ppermute | solution.py:522
  108.1 1.8 %collective-permute-start.34 = (bf16[128,1536]{1,0:T(8,128)(2,1)S(1)}, bf16[128,1536]{1,0:T(8,128)(2,1)S(1)}, u32[]{:S(2)}, u32[]{:S(2)}) collective-permute-start(bf16[128,1536]{1,0:T(8,128)(2,1)S(1)} %shard_map.112.rest_0_), channel_id=1, source_target_pairs={{0,2},{2,0},{4,6},{6,4},{1,3},{3,1},{5,7},{7,5},{8,10},{10,8},{12,... | collective-permute-start | bytes 1179656 | tf_op jit(solution)/shard_map/ppermute | solution.py:522
  112.7 1.8 %collective-permute-start.35 = (bf16[128,1536]{1,0:T(8,128)(2,1)S(1)}, bf16[128,1536]{1,0:T(8,128)(2,1)S(1)}, u32[]{:S(2)}, u32[]{:S(2)}) collective-permute-start(bf16[128,1536]{1,0:T(8,128)(2,1)S(1)} %shard_map.114.refs_2_), channel_id=1, source_target_pairs={{0,2},{2,0},{4,6},{6,4},{1,3},{3,1},{5,7},{7,5},{8,10},{10,8},{12,... | collective-permute-start | bytes 1179656 | tf_op jit(solution)/shard_map/ppermute | solution.py:522
  114.6 11.2 %collective-permute-start.41 = (bf16[128,1536]{1,0:T(8,128)(2,1)S(1)}, bf16[128,1536]{1,0:T(8,128)(2,1)S(1)}, u32[]{:S(2)}, u32[]{:S(2)}) collective-permute-start(bf16[128,1536]{1,0:T(8,128)(2,1)S(1)} %get-tuple-element.107.rest_4_), channel_id=1, source_target_pairs={{0,4},{2,6},{4,0},{6,2},{1,5},{3,7},{5,1},{7,3},{8,12},{10,14},{12... | collective-permute-start | bytes 1179656 | tf_op jit(solution)/shard_map/ppermute | solution.py:522
  120.7 1.9 %collective-permute-start.36 = (bf16[32,1536]{1,0:T(8,128)(2,1)S(1)}, bf16[32,1536]{1,0:T(8,128)(2,1)S(1)}, u32[]{:S(2)}, u32[]{:S(2)}) collective-permute-start(bf16[32,1536]{1,0:T(8,128)(2,1)S(1)} %get-tuple-element.110.refs_2_), channel_id=1, source_target_pairs={{0,2},{2,0},{4,6},{6,4},{1,3},{3,1},{5,7},{7,5},{8,10},{10,8},{12,... | collective-permute-start | bytes 294920 | tf_op jit(solution)/shard_map/ppermute | solution.py:522
  120.8 1.8 %collective-permute-start.37 = (bf16[32,1536]{1,0:T(8,128)(2,1)S(1)}, bf16[32,1536]{1,0:T(8,128)(2,1)S(1)}, u32[]{:S(2)}, u32[]{:S(2)}) collective-permute-start(bf16[32,1536]{1,0:T(8,128)(2,1)S(1)} %get-tuple-element.111), channel_id=1, source_target_pairs={{0,2},{2,0},{4,6},{6,4},{1,3},{3,1},{5,7},{7,5},{8,10},{10,8},{12,... | collective-permute-start | bytes 294920 | tf_op jit(solution)/shard_map/ppermute | solution.py:522
  121.3 1.4 collective-permute-start.39
  122.8 11.5 %collective-permute-start.40 = (bf16[128,1536]{1,0:T(8,128)(2,1)S(1)}, bf16[128,1536]{1,0:T(8,128)(2,1)S(1)}, u32[]{:S(2)}, u32[]{:S(2)}) collective-permute-start(bf16[128,1536]{1,0:T(8,128)(2,1)S(1)} %get-tuple-element.115.refs_7_), channel_id=1, source_target_pairs={{0,4},{2,6},{4,0},{6,2},{1,5},{3,7},{5,1},{7,3},{8,12},{10,14},{12... | collective-permute-start | bytes 1179656 | tf_op jit(solution)/shard_map/ppermute | solution.py:522
  126.1 1.4 collective-permute-start.43
  126.7 1.4 collective-permute-start.45
  129.6 9.8 %collective-permute-start.50 = (bf16[128,768]{1,0:T(8,128)(2,1)S(1)}, bf16[128,768]{1,0:T(8,128)(2,1)S(1)}, u32[]{:S(2)}, u32[]{:S(2)}) collective-permute-start(bf16[128,768]{1,0:T(8,128)(2,1)S(1)} %shard_map.123.refs_3_.refs_0_), channel_id=1, source_target_pairs={{0,1},{1,0},{2,3},{3,2},{4,5},{5,4},{6,7},{7,6},{8,9},{9,8},{10,11... | collective-permute-start | bytes 589832 | tf_op jit(solution)/shard_map/ppermute | solution.py:522
  134.5 2.7 %collective-permute-start.47 = (bf16[32,1536]{1,0:T(8,128)(2,1)S(1)}, bf16[32,1536]{1,0:T(8,128)(2,1)S(1)}, u32[]{:S(2)}, u32[]{:S(2)}) collective-permute-start(bf16[32,1536]{1,0:T(8,128)(2,1)S(1)} %get-tuple-element.124.refs_1_), channel_id=1, source_target_pairs={{0,2},{2,0},{4,6},{6,4},{1,3},{3,1},{5,7},{7,5},{8,10},{10,8},{12,... | collective-permute-start | bytes 294920 | tf_op jit(solution)/shard_map/ppermute | solution.py:522
  135.0 2.2 %collective-permute-start.48 = (bf16[32,1536]{1,0:T(8,128)(2,1)S(1)}, bf16[32,1536]{1,0:T(8,128)(2,1)S(1)}, u32[]{:S(2)}, u32[]{:S(2)}) collective-permute-start(bf16[32,1536]{1,0:T(8,128)(2,1)S(1)} %get-tuple-element.125.refs_2_), channel_id=1, source_target_pairs={{0,2},{2,0},{4,6},{6,4},{1,3},{3,1},{5,7},{7,5},{8,10},{10,8},{12,... | collective-permute-start | bytes 294920 | tf_op jit(solution)/shard_map/ppermute | solution.py:522
  135.1 2.1 %collective-permute-start.49 = (bf16[32,1536]{1,0:T(8,128)(2,1)S(1)}, bf16[32,1536]{1,0:T(8,128)(2,1)S(1)}, u32[]{:S(2)}, u32[]{:S(2)}) collective-permute-start(bf16[32,1536]{1,0:T(8,128)(2,1)S(1)} %get-tuple-element.126.refs_3_), channel_id=1, source_target_pairs={{0,2},{2,0},{4,6},{6,4},{1,3},{3,1},{5,7},{7,5},{8,10},{10,8},{12,... | collective-permute-start | bytes 294920 | tf_op jit(solution)/shard_map/ppermute | solution.py:522
  135.8 7.7 %collective-permute-start.53 = (bf16[128,768]{1,0:T(8,128)(2,1)S(1)}, bf16[128,768]{1,0:T(8,128)(2,1)S(1)}, u32[]{:S(2)}, u32[]{:S(2)}) collective-permute-start(bf16[128,768]{1,0:T(8,128)(2,1)S(1)} %shard_map.124.refs_4_.refs_0_), channel_id=1, source_target_pairs={{0,1},{1,0},{2,3},{3,2},{4,5},{5,4},{6,7},{7,6},{8,9},{9,8},{10,11... | collective-permute-start | bytes 589832 | tf_op jit(solution)/shard_map/ppermute | solution.py:522
  138.8 9.0 %collective-permute-start.52 = (bf16[128,768]{1,0:T(8,128)(2,1)S(1)}, bf16[128,768]{1,0:T(8,128)(2,1)S(1)}, u32[]{:S(2)}, u32[]{:S(2)}) collective-permute-start(bf16[128,768]{1,0:T(8,128)(2,1)S(1)} %shard_map.128.refs_0_), channel_id=1, source_target_pairs={{0,1},{1,0},{2,3},{3,2},{4,5},{5,4},{6,7},{7,6},{8,9},{9,8},{10,11... | collective-permute-start | bytes 589832 | tf_op jit(solution)/shard_map/ppermute | solution.py:522
  141.8 9.4 %collective-permute-start.51 = (bf16[128,768]{1,0:T(8,128)(2,1)S(1)}, bf16[128,768]{1,0:T(8,128)(2,1)S(1)}, u32[]{:S(2)}, u32[]{:S(2)}) collective-permute-start(bf16[128,768]{1,0:T(8,128)(2,1)S(1)} %shard_map.127.refs_0_), channel_id=1, source_target_pairs={{0,1},{1,0},{2,3},{3,2},{4,5},{5,4},{6,7},{7,6},{8,9},{9,8},{10,11... | collective-permute-start | bytes 589832 | tf_op jit(solution)/shard_map/ppermute | solution.py:522
  (8 other events, 41.2 us)

commit v6 on v5

--- a/solution.py
+++ b/solution.py
@@ -582,7 +582,7 @@
     begun = []
     after = ()
     for k in range(kids):
-        sent = nn(child_loads, child_inverse, k, core, 1, pieces_of(k), after)
+        sent = nn(child_loads, child_inverse, k, core, 1, pieces_of(k) // 2 or 1, after)
         (kept,) = nn(child_loads, child_inverse, k, core, 0, 1, sent[:1])
         begun.append(core_sum(kept, sent))
         after = begun[k][1:]
@@ -592,7 +592,7 @@
     sent = kept = None
     for k in range(kids):
         after = after if k == 0 else (sent,)
-        _, rounded = row_end(*begun[k], after, wide=False, pieces=pieces_of(k == 0))
+        _, rounded = row_end(*begun[k], after, wide=False, pieces=pieces_of(k == 0) // 2 or 1)
         forward.append(rounded)
         if k == 0:
             panel, _ = preload(child_panel, 0, rounded)

time: 152 us -> 152 us (level)
    ppermute x54 -> x50, starting transfers between devices: 42.4 us -> 40.9 us  [swap(): return lax.ppermute(x, axis, [(i, i ^ bit) for i in range(size)])]
    ppermute x54 -> x50, waiting for transfers between devices: 30.2 us -> 31.2 us  [swap(): return lax.ppermute(x, axis, [(i, i ^ bit) for i in range(size)])]
  transfers between devices with their start and end apart: 54 -> 50, of which waited for: 23 -> 23; matrix products, arithmetic and copies ran while one was open for 0% -> 0% of each run, Pallas kernels for 41% -> 41%
where the time goes in v6:
time: 152 us; the launch traced here: 151 us
  Pallas kernels  78.1 us (51%)
  starting transfers between devices  40.9 us (27%)
  waiting for transfers between devices  31.2 us (21%)
    ppermute x50, starting transfers between devices, swap(): return lax.ppermute(x, axis, [(i, i ^ bit) for i in range(size)])  40.9 us
    ppermute x50, waiting for transfers between devices, swap(): return lax.ppermute(x, axis, [(i, i ^ bit) for i in range(size)])  31.2 us
    pallas_call x5, Pallas kernels, preload(): pl.pallas_call(functools.partial(preload_kernel, child), in_specs=[pl.Blo...  19 us
    pallas_call x7, Pallas kernels, held_nt(): pl.pallas_call(kernel, in_specs=[SCALARS] + [WHOLE] * (len(mine) + len(ot...  17 us
    pallas_call x4, Pallas kernels, nn(): pl.pallas_call(kernel, grid_spec=pltpu.PrefetchScalarGridSpec(num_scalar_...  12.1 us
    pallas_call x4, Pallas kernels, gather(): pl.pallas_call(functools.partial(gather_kernel, block_rows, tile, which,...  9.78 us
    pallas_call x4, Pallas kernels, scatter(): pl.pallas_call(functools.partial(scatter_kernel, block_rows, tile, odd, c...  8.92 us
    pallas_call x6, Pallas kernels, held_nn(): pl.pallas_call(kernel, in_specs=[SCALARS] + [WHOLE] * (len(x) + 1) + [ANY...  5.11 us
  transfers between devices with their start and end apart: 50, of which 23 were waited for; matrix products, arithmetic and copies ran while one was open for 0% of the time, Pallas kernels for 41%

profile of v6, /device:TPU:0, one launch (start us, length us, event | category | flops | bytes accessed | tf_op | source)
XLA Modules:
  0.0 151.4 jit_solution(18385522589163977369)
XLA Ops:
  0.6 3.0 %shard_map.77.rest_0_ = bf16[128,1536]{1,0:T(8,128)(2,1)S(1)} custom-call(s32[1]{0:T(128)} %bitcast.half_ref, bf16[2,128,1536]{2,1,0:T(8,128)(2,1)} %x_ref.7, bf16[2,1536,3072]{2,1,0:T(8,128)(2,1)} %rest_3_.1), custom_call_target="tpu_custom_call" | custom-call | flops 9437184 | bytes 73728 | tf_op jit(solution)/shard_map/pallas_call | solution.py:98
  4.2 3.0 %shard_map.78.refs_0_ = f32[128,1536]{1,0:T(8,128)S(1)} custom-call(s32[1]{0:T(128)} %bitcast.half_ref, bf16[2,128,1536]{2,1,0:T(8,128)(2,1)} %x_ref.7, bf16[2,1536,3072]{2,1,0:T(8,128)(2,1)} %rest_3_.1, bf16[128,1536]{1,0:T(8,128)(2,1)S(1)} %shard_map.77.rest_0_), custom_call_target="tpu_custom_call" | custom-call | flops 9437184 | bytes 73728 | tf_op jit(solution)/shard_map/pallas_call | solution.py:98
  7.4 2.6 %collective-permute-start.4 = (bf16[128,1536]{1,0:T(8,128)(2,1)S(1)}, bf16[128,1536]{1,0:T(8,128)(2,1)S(1)}, u32[]{:S(2)}, u32[]{:S(2)}) collective-permute-start(bf16[128,1536]{1,0:T(8,128)(2,1)S(1)} %get-tuple-element.64.rest_0_), channel_id=1, source_target_pairs={{0,4},{2,6},{4,0},{6,2},{1,5},{3,7},{5,1},{7,3},{8,12},{10,14},{12... | collective-permute-start | bytes 1179656 | tf_op jit(solution)/shard_map/ppermute | solution.py:522
  10.0 3.0 %shard_map.80 = (bf16[64,1536]{1,0:T(8,128)(2,1)S(1)}, bf16[64,1536]{1,0:T(8,128)(2,1)S(1)}) custom-call(s32[1]{0:T(128)} %bitcast.half_ref, bf16[2,128,1536]{2,1,0:T(8,128)(2,1)} %x_ref.7, bf16[2,1536,3072]{2,1,0:T(8,128)(2,1)} %rest_3_.1, bf16[128,1536]{1,0:T(8,128)(2,1)S(1)} %get-tuple-element.64.rest_0_), custom_call_target="tpu_custom_call" | custom-call | flops 9437184 | bytes 73728 | tf_op jit(solution)/shard_map/pallas_call | solution.py:98
  13.6 3.0 %shard_map.81.refs_0_ = f32[128,1536]{1,0:T(8,128)S(1)} custom-call(s32[1]{0:T(128)} %bitcast.half_ref, bf16[2,128,1536]{2,1,0:T(8,128)(2,1)} %x_ref.7, bf16[2,1536,3072]{2,1,0:T(8,128)(2,1)} %rest_3_.1, bf16[64,1536]{1,0:T(8,128)(2,1)S(1)} %get-tuple-element.65.rest_0_), custom_call_target="tpu_custom_call" | custom-call | flops 9437184 | bytes 73728 | tf_op jit(solution)/shard_map/pallas_call | solution.py:98
  17.5 2.3 %collective-permute-done.4.refs_1_ = bf16[128,1536]{1,0:T(8,128)(2,1)S(1)} collective-permute-done((bf16[128,1536]{1,0:T(8,128)(2,1)S(1)}, bf16[128,1536]{1,0:T(8,128)(2,1)S(1)}, u32[]{:S(2)}, u32[]{:S(2)}) %collective-permute-start.4) | collective-permute-done | bytes 393248 | tf_op jit(solution)/shard_map/ppermute | solution.py:522
  20.5 4.3 %shard_map.85 = (bf16[1536,3072]{1,0:T(8,128)(2,1)S(1)}, f32[8,128]{1,0:T(8,128)}) custom-call(bf16[2,1536,3072]{2,1,0:T(8,128)(2,1)} %w_ref.14, bf16[64,1536]{1,0:T(8,128)(2,1)S(1)} %get-tuple-element.70.rest_0_.refs_0_, bf16[64,1536]{1,0:T(8,128)(2,1)S(1)} %get-tuple-element.71.rest_1_.refs_1_), custom_call_target="tpu_custom_call" | custom-call | bytes 147456 | tf_op jit(solution)/shard_map/pallas_call | solution.py:57
  24.8 4.8 %shard_map.86 = (bf16[128,1536]{1,0:T(8,128)(2,1)S(1)}, bf16[1536,3072]{1,0:T(8,128)(2,1)S(1)}) custom-call(s32[1]{0:T(128)} %bitcast.half_ref, bf16[64,1536]{1,0:T(8,128)(2,1)S(1)} %get-tuple-element.70.rest_0_.refs_0_, bf16[64,1536]{1,0:T(8,128)(2,1)S(1)} %get-tuple-element.71.rest_1_.refs_1_, bf16[64,1536]{1,0:T(8,128)(2,1)S(1)} %collective-permute-done.5.refs_2_, ...), custom_call_target="tpu_custom_call" | custom-call | flops 18874368 | bytes 147456 | tf_op jit(solution)/shard_map/pallas_call | solution.py:176
  29.5 2.1 %shard_map.87.refs_2_.refs_4_ = bf16[2,128,1536]{2,1,0:T(8,128)(2,1)S(1)} custom-call(s32[1]{0:T(128)} %bitcast.1.row_ref.refs_0_, s32[1]{0:T(128)} %bitcast.2.refs_1_.refs_0_.order_ref, s16[2,1536,128]{2,1,0:T(8,128)(2,1)S(1)} %shard_map.83.refs_2_, bf16[128,1536]{1,0:T(8,128)(2,1)S(1)} %get-tuple-element.73.refs_3_), custom_call_target="tpu_custom_call" | custom-call | flops 18874368 | bytes 24576 | tf_op jit(solution)/shard_map/pallas_call | solution.py:268
  31.9 2.1 %shard_map.89.refs_3_.refs_4_ = bf16[2,128,1536]{2,1,0:T(8,128)(2,1)S(1)} custom-call(s32[1]{0:T(128)} %bitcast.1.row_ref.refs_0_, s32[1]{0:T(128)} %bitcast.2.refs_1_.refs_0_.order_ref, s16[2,1536,128]{2,1,0:T(8,128)(2,1)S(1)} %shard_map.83.refs_2_, bf16[128,1536]{1,0:T(8,128)(2,1)S(1)} %get-tuple-element.73.refs_3_), custom_call_target="tpu_custom_call" | custom-call | flops 18874368 | bytes 24576 | tf_op jit(solution)/shard_map/pallas_call | solution.py:268
  34.1 3.2 %shard_map.90.refs_3_ = bf16[128,1536]{1,0:T(8,128)(2,1)S(1)} custom-call(s32[1]{0:T(128)} %bitcast.half_ref, bf16[128,1536]{1,0:T(8,128)(2,1)S(1)} %shard_map.88.refs_0_, bf16[128,1536]{1,0:T(8,128)(2,1)S(1)} %collective-permute-done.7.refs_1_, bf16[1536,3072]{1,0:T(8,128)(2,1)S(1)} %get-tuple-element.74.refs_2_, ...), custom_call_target="tpu_custom_call" | custom-call | flops 18874368 | bytes 147456 | tf_op jit(solution)/shard_map/pallas_call | solution.py:176
  37.3 2.2 %shard_map.92 = bf16[2,128,1536]{2,1,0:T(8,128)(2,1)S(1)} custom-call(s32[1]{0:T(128)} %bitcast.1.row_ref.refs_0_, s32[1]{0:T(128)} %bitcast.2.refs_1_.refs_0_.order_ref, s16[2,1536,128]{2,1,0:T(8,128)(2,1)S(1)} %shard_map.83.refs_2_, bf16[128,1536]{1,0:T(8,128)(2,1)S(1)} %shard_map.90.refs_3_, bf16[2,128,1536]{2,1,0:T(8,128)(2,1)S(1)} %shard_map.87.refs_2_.refs_4_), custom_call_target="tpu_custom_call" | custom-call | flops 18874368 | bytes 24576 | tf_op jit(solution)/shard_map/pallas_call | solution.py:268
  40.1 2.4 %shard_map.91.refs_0_ = bf16[2,128,1536]{2,1,0:T(8,128)(2,1)S(1)} custom-call(s32[1]{0:T(128)} %bitcast.1.row_ref.refs_0_, s32[1]{0:T(128)} %bitcast.2.refs_1_.refs_0_.order_ref, s16[2,1536,128]{2,1,0:T(8,128)(2,1)S(1)} %shard_map.83.refs_2_, bf16[128,1536]{1,0:T(8,128)(2,1)S(1)} %shard_map.90.refs_3_, bf16[2,128,1536]{2,1,0:T(8,128)(2,1)S(1)} %shard_map.89.refs_3_.refs_4_), custom_call_target="tpu_custom_call" | custom-call | flops 18874368 | bytes 24576 | tf_op jit(solution)/shard_map/pallas_call | solution.py:268
  42.7 2.0 %collective-permute-start.9 = (bf16[128,768]{1,0:T(8,128)(2,1)S(1)}, bf16[128,768]{1,0:T(8,128)(2,1)S(1)}, u32[]{:S(2)}, u32[]{:S(2)}) collective-permute-start(bf16[128,768]{1,0:T(8,128)(2,1)S(1)} %get-tuple-element.76), channel_id=1, source_target_pairs={{0,1},{1,0},{2,3},{3,2},{4,5},{5,4},{6,7},{7,6},{8,9},{9,8},{10,11... | collective-permute-start | bytes 589832 | tf_op jit(solution)/shard_map/ppermute | solution.py:522
  44.7 1.7 %collective-permute-start.11 = (bf16[128,768]{1,0:T(8,128)(2,1)S(1)}, bf16[128,768]{1,0:T(8,128)(2,1)S(1)}, u32[]{:S(2)}, u32[]{:S(2)}) collective-permute-start(bf16[128,768]{1,0:T(8,128)(2,1)S(1)} %get-tuple-element.80), channel_id=1, source_target_pairs={{0,4},{2,6},{4,0},{6,2},{1,5},{3,7},{5,1},{7,3},{8,12},{10,14},{12... | collective-permute-start | bytes 589832 | tf_op jit(solution)/shard_map/ppermute | solution.py:522
  46.4 3.5 %collective-permute-done.9.refs_1_ = bf16[128,768]{1,0:T(8,128)(2,1)S(1)} collective-permute-done((bf16[128,768]{1,0:T(8,128)(2,1)S(1)}, bf16[128,768]{1,0:T(8,128)(2,1)S(1)}, u32[]{:S(2)}, u32[]{:S(2)}) %collective-permute-start.9) | collective-permute-done | bytes 196640 | tf_op jit(solution)/shard_map/ppermute | solution.py:522
  49.9 1.9 %collective-permute-start.10 = (bf16[64,768]{1,0:T(8,128)(2,1)S(1)}, bf16[64,768]{1,0:T(8,128)(2,1)S(1)}, u32[]{:S(2)}, u32[]{:S(2)}) collective-permute-start(bf16[64,768]{1,0:T(8,128)(2,1)S(1)} %get-tuple-element.78), channel_id=1, source_target_pairs={{0,4},{2,6},{4,0},{6,2},{1,5},{3,7},{5,1},{7,3},{8,12},{10,14},{12... | collective-permute-start | bytes 294920 | tf_op jit(solution)/shard_map/ppermute | solution.py:522
  51.9 1.6 %collective-permute-start.12 = (bf16[64,768]{1,0:T(8,128)(2,1)S(1)}, bf16[64,768]{1,0:T(8,128)(2,1)S(1)}, u32[]{:S(2)}, u32[]{:S(2)}) collective-permute-start(bf16[64,768]{1,0:T(8,128)(2,1)S(1)} %get-tuple-element.82), channel_id=1, source_target_pairs={{0,1},{1,0},{2,3},{3,2},{4,5},{5,4},{6,7},{7,6},{8,9},{9,8},{10,11... | collective-permute-start | bytes 294920 | tf_op jit(solution)/shard_map/ppermute | solution.py:522
  54.6 2.0 %collective-permute-done.12.refs_3_ = bf16[64,768]{1,0:T(8,128)(2,1)S(1)} collective-permute-done((bf16[64,768]{1,0:T(8,128)(2,1)S(1)}, bf16[64,768]{1,0:T(8,128)(2,1)S(1)}, u32[]{:S(2)}, u32[]{:S(2)}) %collective-permute-start.12) | collective-permute-done | bytes 98336 | tf_op jit(solution)/shard_map/ppermute | solution.py:522
  56.6 1.6 %collective-permute-start.13 = (bf16[16,1536]{1,0:T(8,128)(2,1)S(1)}, bf16[16,1536]{1,0:T(8,128)(2,1)S(1)}, u32[]{:S(2)}, u32[]{:S(2)}) collective-permute-start(bf16[16,1536]{1,0:T(8,128)(2,1)S(1)} %get-tuple-element.84.rest_0_), channel_id=1, source_target_pairs={{0,8},{8,0},{16,24},{24,16},{1,9},{9,1},{17,25},{25,17},{2,10},{10... | collective-permute-start | bytes 147464 | tf_op jit(solution)/shard_map/ppermute | solution.py:522
  58.2 2.6 %collective-permute-start.14 = (bf16[16,1536]{1,0:T(8,128)(2,1)S(1)}, bf16[16,1536]{1,0:T(8,128)(2,1)S(1)}, u32[]{:S(2)}, u32[]{:S(2)}) collective-permute-start(bf16[16,1536]{1,0:T(8,128)(2,1)S(1)} %get-tuple-element.85.rest_1_), channel_id=1, source_target_pairs={{0,16},{8,24},{16,0},{24,8},{1,17},{9,25},{17,1},{25,9},{2,18},{10... | collective-permute-start | bytes 147464 | tf_op jit(solution)/shard_map/ppermute | solution.py:522
  61.0 3.7 %shard_map.97 = (bf16[1536,3072]{1,0:T(8,128)(2,1)S(1)}, f32[8,128]{1,0:T(8,128)S(1)}) custom-call(bf16[1,1536,3072]{2,1,0:T(8,128)(2,1)} %bitcast.4, bf16[16,1536]{1,0:T(8,128)(2,1)S(1)} %get-tuple-element.84.rest_0_, bf16[16,1536]{1,0:T(8,128)(2,1)S(1)} %get-tuple-element.85.rest_1_, bf16[16,1536]{1,0:T(8,128)(2,1)S(1)} %get-tuple-element.86.rest_2_), custom_call_target="tpu_custom_call" | custom-call | bytes 147456 | tf_op jit(solution)/shard_map/pallas_call | solution.py:57
  64.8 2.0 %collective-permute-done.15.refs_5_ = bf16[16,1536]{1,0:T(8,128)(2,1)S(1)} collective-permute-done((bf16[16,1536]{1,0:T(8,128)(2,1)S(1)}, bf16[16,1536]{1,0:T(8,128)(2,1)S(1)}, u32[]{:S(2)}, u32[]{:S(2)}) %collective-permute-start.15) | collective-permute-done | bytes 49184 | tf_op jit(solution)/shard_map/ppermute | solution.py:522
  66.8 1.6 %collective-permute-start.16 = (bf16[16,1536]{1,0:T(8,128)(2,1)S(1)}, bf16[16,1536]{1,0:T(8,128)(2,1)S(1)}, u32[]{:S(2)}, u32[]{:S(2)}) collective-permute-start(bf16[16,1536]{1,0:T(8,128)(2,1)S(1)} %shard_map.98.refs_0_), channel_id=1, source_target_pairs={{0,1},{1,0},{2,3},{3,2},{4,5},{5,4},{6,7},{7,6},{8,9},{9,8},{10,11... | collective-permute-start | bytes 147464 | tf_op jit(solution)/shard_map/ppermute | solution.py:522
  68.4 2.6 %collective-permute-done.16.refs_1_ = bf16[16,1536]{1,0:T(8,128)(2,1)S(1)} collective-permute-done((bf16[16,1536]{1,0:T(8,128)(2,1)S(1)}, bf16[16,1536]{1,0:T(8,128)(2,1)S(1)}, u32[]{:S(2)}, u32[]{:S(2)}) %collective-permute-start.16) | collective-permute-done | bytes 49184 | tf_op jit(solution)/shard_map/ppermute | solution.py:522
  74.4 3.7 %shard_map.102 = (bf16[1536,3072]{1,0:T(8,128)(2,1)S(1)}, f32[8,128]{1,0:T(8,128)S(1)}) custom-call(bf16[2,1536,3072]{2,1,0:T(8,128)(2,1)} %w_ref.14, bf16[32,1536]{1,0:T(8,128)(2,1)S(1)} %get-tuple-element.90.rest_0_), custom_call_target="tpu_custom_call" | custom-call | bytes 147456 | tf_op jit(solution)/shard_map/pallas_call | solution.py:57
  79.5 2.9 %shard_map.104 = (bf16[16,1536]{1,0:T(8,128)(2,1)S(1)}, bf16[16,1536]{1,0:T(8,128)(2,1)S(1)}) custom-call(s32[1]{0:T(128)} %bitcast.half_ref, bf16[32,1536]{1,0:T(8,128)(2,1)S(1)} %shard_map.103.refs_0_, bf16[32,1536]{1,0:T(8,128)(2,1)S(1)} %collective-permute-done.19.refs_1_, bf16[1536,3072]{1,0:T(8,128)(2,1)S(1)} %get-tuple-element.88.refs_2_), custom_call_target="tpu_custom_call" | custom-call | flops 4718592 | bytes 147456 | tf_op jit(solution)/shard_map/pallas_call | solution.py:176
  82.4 1.6 %collective-permute-start.20 = (bf16[16,1536]{1,0:T(8,128)(2,1)S(1)}, bf16[16,1536]{1,0:T(8,128)(2,1)S(1)}, u32[]{:S(2)}, u32[]{:S(2)}) collective-permute-start(bf16[16,1536]{1,0:T(8,128)(2,1)S(1)} %get-tuple-element.93), channel_id=1, source_target_pairs={{0,1},{1,0},{2,3},{3,2},{4,5},{5,4},{6,7},{7,6},{8,9},{9,8},{10,11... | collective-permute-start | bytes 147464 | tf_op jit(solution)/shard_map/ppermute | solution.py:522
  84.0 2.6 %collective-permute-done.20.refs_1_ = bf16[16,1536]{1,0:T(8,128)(2,1)S(1)} collective-permute-done((bf16[16,1536]{1,0:T(8,128)(2,1)S(1)}, bf16[16,1536]{1,0:T(8,128)(2,1)S(1)}, u32[]{:S(2)}, u32[]{:S(2)}) %collective-permute-start.20) | collective-permute-done | bytes 49184 | tf_op jit(solution)/shard_map/ppermute | solution.py:522
  86.7 2.2 %collective-permute-start.22 = (bf16[16,1536]{1,0:T(8,128)(2,1)S(1)}, bf16[16,1536]{1,0:T(8,128)(2,1)S(1)}, u32[]{:S(2)}, u32[]{:S(2)}) collective-permute-start(bf16[16,1536]{1,0:T(8,128)(2,1)S(1)} %shard_map.105.rest_0_.refs_0_), channel_id=1, source_target_pairs={{0,16},{8,24},{16,0},{24,8},{1,17},{9,25},{17,1},{25,9},{2,18},{10... | collective-permute-start | bytes 147464 | tf_op jit(solution)/shard_map/ppermute | solution.py:522
  88.9 2.1 %collective-permute-start.23 = (bf16[16,1536]{1,0:T(8,128)(2,1)S(1)}, bf16[16,1536]{1,0:T(8,128)(2,1)S(1)}, u32[]{:S(2)}, u32[]{:S(2)}) collective-permute-start(bf16[16,1536]{1,0:T(8,128)(2,1)S(1)} %shard_map.105.rest_0_.refs_0_), channel_id=1, source_target_pairs={{0,24},{8,16},{16,8},{24,0},{1,25},{9,17},{17,9},{25,1},{2,26},{10... | collective-permute-start | bytes 147464 | tf_op jit(solution)/shard_map/ppermute | solution.py:522
  91.0 3.7 %shard_map.106 = (bf16[1536,3072]{1,0:T(8,128)(2,1)S(1)}, f32[8,128]{1,0:T(8,128)S(1)}) custom-call(bf16[2,1536,3072]{2,1,0:T(8,128)(2,1)} %w_ref.14, bf16[16,1536]{1,0:T(8,128)(2,1)S(1)} %shard_map.105.rest_0_.refs_0_), custom_call_target="tpu_custom_call" | custom-call | bytes 147456 | tf_op jit(solution)/shard_map/pallas_call | solution.py:57
  94.8 1.6 %collective-permute-start.26 = (bf16[64,1536]{1,0:T(8,128)(2,1)S(1)}, bf16[64,1536]{1,0:T(8,128)(2,1)S(1)}, u32[]{:S(2)}, u32[]{:S(2)}) collective-permute-start(bf16[64,1536]{1,0:T(8,128)(2,1)S(1)} %shard_map.107.rest_0_.refs_0_), channel_id=1, source_target_pairs={{0,1},{1,0},{2,3},{3,2},{4,5},{5,4},{6,7},{7,6},{8,9},{9,8},{10,11... | collective-permute-start | bytes 589832 | tf_op jit(solution)/shard_map/ppermute | solution.py:522
  97.2 3.7 %shard_map.108 = (bf16[1536,3072]{1,0:T(8,128)(2,1)S(1)}, f32[8,128]{1,0:T(8,128)S(1)}) custom-call(bf16[2,1536,3072]{2,1,0:T(8,128)(2,1)} %rest_3_.1, bf16[64,1536]{1,0:T(8,128)(2,1)S(1)} %shard_map.107.rest_0_.refs_0_), custom_call_target="tpu_custom_call" | custom-call | bytes 147456 | tf_op jit(solution)/shard_map/pallas_call | solution.py:57
  103.8 1.8 %shard_map.110.refs_3_.rest_2_ = bf16[128,1536]{1,0:T(8,128)(2,1)S(1)} custom-call(s32[1]{0:T(128)} %bitcast.1.row_ref.refs_0_, s32[1]{0:T(128)} %bitcast.2.refs_1_.refs_0_.order_ref, s32[2,1,6144]{2,1,0:T(1,128)S(1)} %reshape.7.map_ref, bf16[64,1536]{1,0:T(8,128)(2,1)S(1)} %get-tuple-element.96.rest_0_.refs_0_, ...), custom_call_target="tpu_custom_call" | custom-call | flops 18874368 | bytes 12288 | tf_op jit(solution)/shard_map/pallas_call | solution.py:340
  105.7 1.9 %shard_map.111.refs_4_.rest_2_ = bf16[128,1536]{1,0:T(8,128)(2,1)S(1)} custom-call(s32[1]{0:T(128)} %bitcast.1.row_ref.refs_0_, s32[1]{0:T(128)} %bitcast.2.refs_1_.refs_0_.order_ref, s32[2,1,6144]{2,1,0:T(1,128)S(1)} %reshape.7.map_ref, bf16[64,1536]{1,0:T(8,128)(2,1)S(1)} %get-tuple-element.96.rest_0_.refs_0_, ...), custom_call_target="tpu_custom_call" | custom-call | flops 18874368 | bytes 12288 | tf_op jit(solution)/shard_map/pallas_call | solution.py:340
  107.7 1.7 %collective-permute-done.30.rest_1_ = bf16[128,1536]{1,0:T(8,128)(2,1)S(1)} collective-permute-done((bf16[128,1536]{1,0:T(8,128)(2,1)S(1)}, bf16[128,1536]{1,0:T(8,128)(2,1)S(1)}, u32[]{:S(2)}, u32[]{:S(2)}) %collective-permute-start.30) | collective-permute-done | bytes 393248 | tf_op jit(solution)/shard_map/ppermute | solution.py:522
  109.4 1.9 %shard_map.113.refs_0_ = bf16[128,1536]{1,0:T(8,128)(2,1)S(1)} custom-call(s32[1]{0:T(128)} %bitcast.1.row_ref.refs_0_, s32[1]{0:T(128)} %bitcast.2.refs_1_.refs_0_.order_ref, s32[2,1,6144]{2,1,0:T(1,128)S(1)} %reshape.7.map_ref, bf16[128,1536]{1,0:T(8,128)(2,1)S(1)} %shard_map.112.rest_0_, bf16[128,1536]{1,0:T(8,128)(2,1)S(1)} %collective-permute-done.30.rest_1_, ...), custom_call_target="tpu_custom_call" | custom-call | flops 18874368 | bytes 12288 | tf_op jit(solution)/shard_map/pallas_call | solution.py:340
  115.1 4.2 %shard_map.117 = (bf16[128,1536]{1,0:T(8,128)(2,1)S(1)}, bf16[1536,3072]{1,0:T(8,128)(2,1)S(1)}) custom-call(s32[1]{0:T(128)} %bitcast.1.row_ref.refs_0_, s32[1]{0:T(128)} %bitcast.2.refs_1_.refs_0_.order_ref, s32[2,1,6144]{2,1,0:T(1,128)S(1)} %reshape.7.map_ref, bf16[128,1536]{1,0:T(8,128)(2,1)S(1)} %shard_map.112.rest_0_, ...), custom_call_target="tpu_custom_call" | custom-call | flops 18874368 | bytes 12288 | tf_op jit(solution)/shard_map/pallas_call | solution.py:340
  127.5 1.6 %shard_map.123.refs_3_.refs_0_ = bf16[128,768]{1,0:T(8,128)(2,1)S(1)} custom-call(s32[1]{0:T(128)} %bitcast.half_ref, bf16[32,1536]{1,0:T(8,128)(2,1)S(1)} %get-tuple-element.110.refs_0_, bf16[32,1536]{1,0:T(8,128)(2,1)S(1)} %get-tuple-element.111.refs_1_, bf16[32,1536]{1,0:T(8,128)(2,1)S(1)} %get-tuple-element.112.refs_2_, ...), custom_call_target="tpu_custom_call" | custom-call | flops 9437184 | bytes 73728 | tf_op jit(solution)/shard_map/pallas_call | solution.py:176
  130.4 1.5 %shard_map.124.refs_4_.refs_0_ = bf16[128,768]{1,0:T(8,128)(2,1)S(1)} custom-call(s32[1]{0:T(128)} %bitcast.half_ref, bf16[32,1536]{1,0:T(8,128)(2,1)S(1)} %get-tuple-element.110.refs_0_, bf16[32,1536]{1,0:T(8,128)(2,1)S(1)} %get-tuple-element.111.refs_1_, bf16[32,1536]{1,0:T(8,128)(2,1)S(1)} %get-tuple-element.112.refs_2_, ...), custom_call_target="tpu_custom_call" | custom-call | flops 9437184 | bytes 73728 | tf_op jit(solution)/shard_map/pallas_call | solution.py:176
  132.0 1.7 %collective-permute-done.36.refs_2_ = bf16[128,1536]{1,0:T(8,128)(2,1)S(1)} collective-permute-done((bf16[128,1536]{1,0:T(8,128)(2,1)S(1)}, bf16[128,1536]{1,0:T(8,128)(2,1)S(1)}, u32[]{:S(2)}, u32[]{:S(2)}) %collective-permute-start.36) | collective-permute-done | bytes 393248 | tf_op jit(solution)/shard_map/ppermute | solution.py:522
  135.3 1.4 collective-permute-start.49
  136.7 1.5 %shard_map.128.refs_0_ = bf16[128,768]{1,0:T(8,128)(2,1)S(1)} custom-call(s32[1]{0:T(128)} %bitcast.half_ref, bf16[32,1536]{1,0:T(8,128)(2,1)S(1)} %get-tuple-element.115.refs_0_, bf16[32,1536]{1,0:T(8,128)(2,1)S(1)} %get-tuple-element.116.refs_1_, bf16[32,1536]{1,0:T(8,128)(2,1)S(1)} %get-tuple-element.117.refs_2_, ...), custom_call_target="tpu_custom_call" | custom-call | flops 9437184 | bytes 73728 | tf_op jit(solution)/shard_map/pallas_call | solution.py:176
  139.7 1.5 %shard_map.127.refs_0_ = bf16[128,768]{1,0:T(8,128)(2,1)S(1)} custom-call(s32[1]{0:T(128)} %bitcast.half_ref, bf16[32,1536]{1,0:T(8,128)(2,1)S(1)} %get-tuple-element.115.refs_0_, bf16[32,1536]{1,0:T(8,128)(2,1)S(1)} %get-tuple-element.116.refs_1_, bf16[32,1536]{1,0:T(8,128)(2,1)S(1)} %get-tuple-element.117.refs_2_, ...), custom_call_target="tpu_custom_call" | custom-call | flops 9437184 | bytes 73728 | tf_op jit(solution)/shard_map/pallas_call | solution.py:176
  141.3 1.4 collective-permute-start.47
  143.8 3.4 %collective-permute-done.48.refs_1_ = bf16[128,768]{1,0:T(8,128)(2,1)S(1)} collective-permute-done((bf16[128,768]{1,0:T(8,128)(2,1)S(1)}, bf16[128,768]{1,0:T(8,128)(2,1)S(1)}, u32[]{:S(2)}, u32[]{:S(2)}) %collective-permute-start.48) | collective-permute-done | bytes 196640 | tf_op jit(solution)/shard_map/ppermute | solution.py:522
  148.0 2.6 %collective-permute-done.47.refs_1_ = bf16[128,768]{1,0:T(8,128)(2,1)S(1)} collective-permute-done((bf16[128,768]{1,0:T(8,128)(2,1)S(1)}, bf16[128,768]{1,0:T(8,128)(2,1)S(1)}, u32[]{:S(2)}, u32[]{:S(2)}) %collective-permute-start.47) | collective-permute-done | bytes 196640 | tf_op jit(solution)/shard_map/ppermute | solution.py:522
  (114 shorter events, 32.9 us)
Async XLA Ops:
  3.7 3.6 %collective-permute-start = (bf16[128,1536]{1,0:T(8,128)(2,1)S(1)}, bf16[128,1536]{1,0:T(8,128)(2,1)S(1)}, u32[]{:S(2)}, u32[]{:S(2)}) collective-permute-start(bf16[128,1536]{1,0:T(8,128)(2,1)S(1)} %shard_map.77.rest_0_), channel_id=1, source_target_pairs={{0,2},{2,0},{4,6},{6,4},{1,3},{3,1},{5,7},{7,5},{8,10},{10,8},{12,... | collective-permute-start | bytes 1179656 | tf_op jit(solution)/shard_map/ppermute | solution.py:522
  7.4 12.4 %collective-permute-start.4 = (bf16[128,1536]{1,0:T(8,128)(2,1)S(1)}, bf16[128,1536]{1,0:T(8,128)(2,1)S(1)}, u32[]{:S(2)}, u32[]{:S(2)}) collective-permute-start(bf16[128,1536]{1,0:T(8,128)(2,1)S(1)} %get-tuple-element.64.rest_0_), channel_id=1, source_target_pairs={{0,4},{2,6},{4,0},{6,2},{1,5},{3,7},{5,1},{7,3},{8,12},{10,14},{12... | collective-permute-start | bytes 1179656 | tf_op jit(solution)/shard_map/ppermute | solution.py:522
  13.0 3.6 %collective-permute-start.1 = (bf16[64,1536]{1,0:T(8,128)(2,1)S(1)}, bf16[64,1536]{1,0:T(8,128)(2,1)S(1)}, u32[]{:S(2)}, u32[]{:S(2)}) collective-permute-start(bf16[64,1536]{1,0:T(8,128)(2,1)S(1)} %get-tuple-element.65.rest_0_), channel_id=1, source_target_pairs={{0,2},{2,0},{4,6},{6,4},{1,3},{3,1},{5,7},{7,5},{8,10},{10,8},{12,... | collective-permute-start | bytes 589832 | tf_op jit(solution)/shard_map/ppermute | solution.py:522
  13.3 3.4 %collective-permute-start.2 = (bf16[64,1536]{1,0:T(8,128)(2,1)S(1)}, bf16[64,1536]{1,0:T(8,128)(2,1)S(1)}, u32[]{:S(2)}, u32[]{:S(2)}) collective-permute-start(bf16[64,1536]{1,0:T(8,128)(2,1)S(1)} %get-tuple-element.66), channel_id=1, source_target_pairs={{0,2},{2,0},{4,6},{6,4},{1,3},{3,1},{5,7},{7,5},{8,10},{10,8},{12,... | collective-permute-start | bytes 589832 | tf_op jit(solution)/shard_map/ppermute | solution.py:522
  16.7 15.0 %collective-permute-start.3 = (bf16[128,1536]{1,0:T(8,128)(2,1)S(1)}, bf16[128,1536]{1,0:T(8,128)(2,1)S(1)}, u32[]{:S(2)}, u32[]{:S(2)}) collective-permute-start(bf16[128,1536]{1,0:T(8,128)(2,1)S(1)} %get-tuple-element.68.rest_0_), channel_id=1, source_target_pairs={{0,4},{2,6},{4,0},{6,2},{1,5},{3,7},{5,1},{7,3},{8,12},{10,14},{12... | collective-permute-start | bytes 1179656 | tf_op jit(solution)/shard_map/ppermute | solution.py:522
  19.9 4.9 %collective-permute-start.5 = (bf16[64,1536]{1,0:T(8,128)(2,1)S(1)}, bf16[64,1536]{1,0:T(8,128)(2,1)S(1)}, u32[]{:S(2)}, u32[]{:S(2)}) collective-permute-start(bf16[64,1536]{1,0:T(8,128)(2,1)S(1)} %get-tuple-element.70.rest_0_.refs_0_), channel_id=1, source_target_pairs={{0,2},{2,0},{4,6},{6,4},{1,3},{3,1},{5,7},{7,5},{8,10},{10,8},{12,... | collective-permute-start | bytes 589832 | tf_op jit(solution)/shard_map/ppermute | solution.py:522
  20.0 4.8 %collective-permute-start.6 = (bf16[64,1536]{1,0:T(8,128)(2,1)S(1)}, bf16[64,1536]{1,0:T(8,128)(2,1)S(1)}, u32[]{:S(2)}, u32[]{:S(2)}) collective-permute-start(bf16[64,1536]{1,0:T(8,128)(2,1)S(1)} %get-tuple-element.71.rest_1_.refs_1_), channel_id=1, source_target_pairs={{0,2},{2,0},{4,6},{6,4},{1,3},{3,1},{5,7},{7,5},{8,10},{10,8},{12,... | collective-permute-start | bytes 589832 | tf_op jit(solution)/shard_map/ppermute | solution.py:522
  31.8 2.3 %collective-permute-start.7 = (bf16[128,1536]{1,0:T(8,128)(2,1)S(1)}, bf16[128,1536]{1,0:T(8,128)(2,1)S(1)}, u32[]{:S(2)}, u32[]{:S(2)}) collective-permute-start(bf16[128,1536]{1,0:T(8,128)(2,1)S(1)} %shard_map.88.refs_0_), channel_id=1, source_target_pairs={{0,2},{2,0},{4,6},{6,4},{1,3},{3,1},{5,7},{7,5},{8,10},{10,8},{12,... | collective-permute-start | bytes 1179656 | tf_op jit(solution)/shard_map/ppermute | solution.py:522
  39.6 2.9 %collective-permute-start.8 = (bf16[2,128,1536]{2,1,0:T(8,128)(2,1)S(1)}, bf16[2,128,1536]{2,1,0:T(8,128)(2,1)S(1)}, u32[]{:S(2)}, u32[]{:S(2)}) collective-permute-start(bf16[2,128,1536]{2,1,0:T(8,128)(2,1)S(1)} %shard_map.92), channel_id=1, source_target_pairs={{0,2},{2,0},{4,6},{6,4},{1,3},{3,1},{5,7},{7,5},{8,10},{10,8},{12,... | collective-permute-start | bytes 2359304 | tf_op jit(solution)/shard_map/ppermute | solution.py:522
  42.7 7.2 %collective-permute-start.9 = (bf16[128,768]{1,0:T(8,128)(2,1)S(1)}, bf16[128,768]{1,0:T(8,128)(2,1)S(1)}, u32[]{:S(2)}, u32[]{:S(2)}) collective-permute-start(bf16[128,768]{1,0:T(8,128)(2,1)S(1)} %get-tuple-element.76), channel_id=1, source_target_pairs={{0,1},{1,0},{2,3},{3,2},{4,5},{5,4},{6,7},{7,6},{8,9},{9,8},{10,11... | collective-permute-start | bytes 589832 | tf_op jit(solution)/shard_map/ppermute | solution.py:522
  44.7 7.1 %collective-permute-start.11 = (bf16[128,768]{1,0:T(8,128)(2,1)S(1)}, bf16[128,768]{1,0:T(8,128)(2,1)S(1)}, u32[]{:S(2)}, u32[]{:S(2)}) collective-permute-start(bf16[128,768]{1,0:T(8,128)(2,1)S(1)} %get-tuple-element.80), channel_id=1, source_target_pairs={{0,4},{2,6},{4,0},{6,2},{1,5},{3,7},{5,1},{7,3},{8,12},{10,14},{12... | collective-permute-start | bytes 589832 | tf_op jit(solution)/shard_map/ppermute | solution.py:522
  49.9 4.7 %collective-permute-start.10 = (bf16[64,768]{1,0:T(8,128)(2,1)S(1)}, bf16[64,768]{1,0:T(8,128)(2,1)S(1)}, u32[]{:S(2)}, u32[]{:S(2)}) collective-permute-start(bf16[64,768]{1,0:T(8,128)(2,1)S(1)} %get-tuple-element.78), channel_id=1, source_target_pairs={{0,4},{2,6},{4,0},{6,2},{1,5},{3,7},{5,1},{7,3},{8,12},{10,14},{12... | collective-permute-start | bytes 294920 | tf_op jit(solution)/shard_map/ppermute | solution.py:522
  51.9 4.7 %collective-permute-start.12 = (bf16[64,768]{1,0:T(8,128)(2,1)S(1)}, bf16[64,768]{1,0:T(8,128)(2,1)S(1)}, u32[]{:S(2)}, u32[]{:S(2)}) collective-permute-start(bf16[64,768]{1,0:T(8,128)(2,1)S(1)} %get-tuple-element.82), channel_id=1, source_target_pairs={{0,1},{1,0},{2,3},{3,2},{4,5},{5,4},{6,7},{7,6},{8,9},{9,8},{10,11... | collective-permute-start | bytes 294920 | tf_op jit(solution)/shard_map/ppermute | solution.py:522
  56.6 8.2 %collective-permute-start.13 = (bf16[16,1536]{1,0:T(8,128)(2,1)S(1)}, bf16[16,1536]{1,0:T(8,128)(2,1)S(1)}, u32[]{:S(2)}, u32[]{:S(2)}) collective-permute-start(bf16[16,1536]{1,0:T(8,128)(2,1)S(1)} %get-tuple-element.84.rest_0_), channel_id=1, source_target_pairs={{0,8},{8,0},{16,24},{24,16},{1,9},{9,1},{17,25},{25,17},{2,10},{10... | collective-permute-start | bytes 147464 | tf_op jit(solution)/shard_map/ppermute | solution.py:522
  58.2 6.5 %collective-permute-start.14 = (bf16[16,1536]{1,0:T(8,128)(2,1)S(1)}, bf16[16,1536]{1,0:T(8,128)(2,1)S(1)}, u32[]{:S(2)}, u32[]{:S(2)}) collective-permute-start(bf16[16,1536]{1,0:T(8,128)(2,1)S(1)} %get-tuple-element.85.rest_1_), channel_id=1, source_target_pairs={{0,16},{8,24},{16,0},{24,8},{1,17},{9,25},{17,1},{25,9},{2,18},{10... | collective-permute-start | bytes 147464 | tf_op jit(solution)/shard_map/ppermute | solution.py:522
  60.9 5.9 %collective-permute-start.15 = (bf16[16,1536]{1,0:T(8,128)(2,1)S(1)}, bf16[16,1536]{1,0:T(8,128)(2,1)S(1)}, u32[]{:S(2)}, u32[]{:S(2)}) collective-permute-start(bf16[16,1536]{1,0:T(8,128)(2,1)S(1)} %get-tuple-element.86.rest_2_), channel_id=1, source_target_pairs={{0,24},{8,16},{16,8},{24,0},{1,25},{9,17},{17,9},{25,1},{2,26},{10... | collective-permute-start | bytes 147464 | tf_op jit(solution)/shard_map/ppermute | solution.py:522
  66.8 4.2 %collective-permute-start.16 = (bf16[16,1536]{1,0:T(8,128)(2,1)S(1)}, bf16[16,1536]{1,0:T(8,128)(2,1)S(1)}, u32[]{:S(2)}, u32[]{:S(2)}) collective-permute-start(bf16[16,1536]{1,0:T(8,128)(2,1)S(1)} %shard_map.98.refs_0_), channel_id=1, source_target_pairs={{0,1},{1,0},{2,3},{3,2},{4,5},{5,4},{6,7},{7,6},{8,9},{9,8},{10,11... | collective-permute-start | bytes 147464 | tf_op jit(solution)/shard_map/ppermute | solution.py:522
  73.2 4.9 %collective-permute-start.18 = (bf16[32,1536]{1,0:T(8,128)(2,1)S(1)}, bf16[32,1536]{1,0:T(8,128)(2,1)S(1)}, u32[]{:S(2)}, u32[]{:S(2)}) collective-permute-start(bf16[32,1536]{1,0:T(8,128)(2,1)S(1)} %get-tuple-element.90.rest_0_), channel_id=1, source_target_pairs={{0,4},{2,6},{4,0},{6,2},{1,5},{3,7},{5,1},{7,3},{8,12},{10,14},{12... | collective-permute-start | bytes 294920 | tf_op jit(solution)/shard_map/ppermute | solution.py:522
  78.2 1.4 collective-permute-start.19
  82.4 4.2 %collective-permute-start.20 = (bf16[16,1536]{1,0:T(8,128)(2,1)S(1)}, bf16[16,1536]{1,0:T(8,128)(2,1)S(1)}, u32[]{:S(2)}, u32[]{:S(2)}) collective-permute-start(bf16[16,1536]{1,0:T(8,128)(2,1)S(1)} %get-tuple-element.93), channel_id=1, source_target_pairs={{0,1},{1,0},{2,3},{3,2},{4,5},{5,4},{6,7},{7,6},{8,9},{9,8},{10,11... | collective-permute-start | bytes 147464 | tf_op jit(solution)/shard_map/ppermute | solution.py:522
  86.6 8.2 %collective-permute-start.21 = (bf16[16,1536]{1,0:T(8,128)(2,1)S(1)}, bf16[16,1536]{1,0:T(8,128)(2,1)S(1)}, u32[]{:S(2)}, u32[]{:S(2)}) collective-permute-start(bf16[16,1536]{1,0:T(8,128)(2,1)S(1)} %shard_map.105.rest_0_.refs_0_), channel_id=1, source_target_pairs={{0,8},{8,0},{16,24},{24,16},{1,9},{9,1},{17,25},{25,17},{2,10},{10... | collective-permute-start | bytes 147464 | tf_op jit(solution)/shard_map/ppermute | solution.py:522
  86.7 8.1 %collective-permute-start.22 = (bf16[16,1536]{1,0:T(8,128)(2,1)S(1)}, bf16[16,1536]{1,0:T(8,128)(2,1)S(1)}, u32[]{:S(2)}, u32[]{:S(2)}) collective-permute-start(bf16[16,1536]{1,0:T(8,128)(2,1)S(1)} %shard_map.105.rest_0_.refs_0_), channel_id=1, source_target_pairs={{0,16},{8,24},{16,0},{24,8},{1,17},{9,25},{17,1},{25,9},{2,18},{10... | collective-permute-start | bytes 147464 | tf_op jit(solution)/shard_map/ppermute | solution.py:522
  88.9 5.9 %collective-permute-start.23 = (bf16[16,1536]{1,0:T(8,128)(2,1)S(1)}, bf16[16,1536]{1,0:T(8,128)(2,1)S(1)}, u32[]{:S(2)}, u32[]{:S(2)}) collective-permute-start(bf16[16,1536]{1,0:T(8,128)(2,1)S(1)} %shard_map.105.rest_0_.refs_0_), channel_id=1, source_target_pairs={{0,24},{8,16},{16,8},{24,0},{1,25},{9,17},{17,9},{25,1},{2,26},{10... | collective-permute-start | bytes 147464 | tf_op jit(solution)/shard_map/ppermute | solution.py:522
  94.8 6.1 %collective-permute-start.26 = (bf16[64,1536]{1,0:T(8,128)(2,1)S(1)}, bf16[64,1536]{1,0:T(8,128)(2,1)S(1)}, u32[]{:S(2)}, u32[]{:S(2)}) collective-permute-start(bf16[64,1536]{1,0:T(8,128)(2,1)S(1)} %shard_map.107.rest_0_.refs_0_), channel_id=1, source_target_pairs={{0,1},{1,0},{2,3},{3,2},{4,5},{5,4},{6,7},{7,6},{8,9},{9,8},{10,11... | collective-permute-start | bytes 589832 | tf_op jit(solution)/shard_map/ppermute | solution.py:522
  96.4 5.7 %collective-permute-start.24 = (bf16[64,1536]{1,0:T(8,128)(2,1)S(1)}, bf16[64,1536]{1,0:T(8,128)(2,1)S(1)}, u32[]{:S(2)}, u32[]{:S(2)}) collective-permute-start(bf16[64,1536]{1,0:T(8,128)(2,1)S(1)} %shard_map.107.rest_0_.refs_0_), channel_id=1, source_target_pairs={{0,4},{2,6},{4,0},{6,2},{1,5},{3,7},{5,1},{7,3},{8,12},{10,14},{12... | collective-permute-start | bytes 589832 | tf_op jit(solution)/shard_map/ppermute | solution.py:522
  101.0 2.8 %collective-permute-start.28 = (bf16[64,1536]{1,0:T(8,128)(2,1)S(1)}, bf16[64,1536]{1,0:T(8,128)(2,1)S(1)}, u32[]{:S(2)}, u32[]{:S(2)}) collective-permute-start(bf16[64,1536]{1,0:T(8,128)(2,1)S(1)} %get-tuple-element.96.rest_0_.refs_0_), channel_id=1, source_target_pairs={{0,2},{2,0},{4,6},{6,4},{1,3},{3,1},{5,7},{7,5},{8,10},{10,8},{12,... | collective-permute-start | bytes 589832 | tf_op jit(solution)/shard_map/ppermute | solution.py:522
  101.1 2.8 %collective-permute-start.29 = (bf16[64,1536]{1,0:T(8,128)(2,1)S(1)}, bf16[64,1536]{1,0:T(8,128)(2,1)S(1)}, u32[]{:S(2)}, u32[]{:S(2)}) collective-permute-start(bf16[64,1536]{1,0:T(8,128)(2,1)S(1)} %get-tuple-element.97.rest_1_.refs_1_), channel_id=1, source_target_pairs={{0,2},{2,0},{4,6},{6,4},{1,3},{3,1},{5,7},{7,5},{8,10},{10,8},{12,... | collective-permute-start | bytes 589832 | tf_op jit(solution)/shard_map/ppermute | solution.py:522
  102.0 5.5 %collective-permute-start.25 = (bf16[32,1536]{1,0:T(8,128)(2,1)S(1)}, bf16[32,1536]{1,0:T(8,128)(2,1)S(1)}, u32[]{:S(2)}, u32[]{:S(2)}) collective-permute-start(bf16[32,1536]{1,0:T(8,128)(2,1)S(1)} %slice.8), channel_id=1, source_target_pairs={{0,1},{1,0},{2,3},{3,2},{4,5},{5,4},{6,7},{7,6},{8,9},{9,8},{10,11... | collective-permute-start | bytes 294920 | tf_op jit(solution)/shard_map/ppermute | solution.py:522
  102.7 4.8 %collective-permute-start.27 = (bf16[32,1536]{1,0:T(8,128)(2,1)S(1)}, bf16[32,1536]{1,0:T(8,128)(2,1)S(1)}, u32[]{:S(2)}, u32[]{:S(2)}) collective-permute-start(bf16[32,1536]{1,0:T(8,128)(2,1)S(1)} %slice.9), channel_id=1, source_target_pairs={{0,4},{2,6},{4,0},{6,2},{1,5},{3,7},{5,1},{7,3},{8,12},{10,14},{12... | collective-permute-start | bytes 294920 | tf_op jit(solution)/shard_map/ppermute | solution.py:522
  107.6 1.8 %collective-permute-start.30 = (bf16[128,1536]{1,0:T(8,128)(2,1)S(1)}, bf16[128,1536]{1,0:T(8,128)(2,1)S(1)}, u32[]{:S(2)}, u32[]{:S(2)}) collective-permute-start(bf16[128,1536]{1,0:T(8,128)(2,1)S(1)} %shard_map.112.rest_0_), channel_id=1, source_target_pairs={{0,2},{2,0},{4,6},{6,4},{1,3},{3,1},{5,7},{7,5},{8,10},{10,8},{12,... | collective-permute-start | bytes 1179656 | tf_op jit(solution)/shard_map/ppermute | solution.py:522
  112.2 1.8 %collective-permute-start.31 = (bf16[128,1536]{1,0:T(8,128)(2,1)S(1)}, bf16[128,1536]{1,0:T(8,128)(2,1)S(1)}, u32[]{:S(2)}, u32[]{:S(2)}) collective-permute-start(bf16[128,1536]{1,0:T(8,128)(2,1)S(1)} %shard_map.114.refs_2_), channel_id=1, source_target_pairs={{0,2},{2,0},{4,6},{6,4},{1,3},{3,1},{5,7},{7,5},{8,10},{10,8},{12,... | collective-permute-start | bytes 1179656 | tf_op jit(solution)/shard_map/ppermute | solution.py:522
  114.1 11.2 %collective-permute-start.37 = (bf16[128,1536]{1,0:T(8,128)(2,1)S(1)}, bf16[128,1536]{1,0:T(8,128)(2,1)S(1)}, u32[]{:S(2)}, u32[]{:S(2)}) collective-permute-start(bf16[128,1536]{1,0:T(8,128)(2,1)S(1)} %get-tuple-element.99.rest_4_), channel_id=1, source_target_pairs={{0,4},{2,6},{4,0},{6,2},{1,5},{3,7},{5,1},{7,3},{8,12},{10,14},{12... | collective-permute-start | bytes 1179656 | tf_op jit(solution)/shard_map/ppermute | solution.py:522
  120.1 1.9 %collective-permute-start.32 = (bf16[32,1536]{1,0:T(8,128)(2,1)S(1)}, bf16[32,1536]{1,0:T(8,128)(2,1)S(1)}, u32[]{:S(2)}, u32[]{:S(2)}) collective-permute-start(bf16[32,1536]{1,0:T(8,128)(2,1)S(1)} %get-tuple-element.102.refs_2_), channel_id=1, source_target_pairs={{0,2},{2,0},{4,6},{6,4},{1,3},{3,1},{5,7},{7,5},{8,10},{10,8},{12,... | collective-permute-start | bytes 294920 | tf_op jit(solution)/shard_map/ppermute | solution.py:522
  120.2 1.8 %collective-permute-start.33 = (bf16[32,1536]{1,0:T(8,128)(2,1)S(1)}, bf16[32,1536]{1,0:T(8,128)(2,1)S(1)}, u32[]{:S(2)}, u32[]{:S(2)}) collective-permute-start(bf16[32,1536]{1,0:T(8,128)(2,1)S(1)} %get-tuple-element.103), channel_id=1, source_target_pairs={{0,2},{2,0},{4,6},{6,4},{1,3},{3,1},{5,7},{7,5},{8,10},{10,8},{12,... | collective-permute-start | bytes 294920 | tf_op jit(solution)/shard_map/ppermute | solution.py:522
  120.7 1.3 collective-permute-start.34
  120.8 1.4 collective-permute-start.35
  122.3 11.5 %collective-permute-start.36 = (bf16[128,1536]{1,0:T(8,128)(2,1)S(1)}, bf16[128,1536]{1,0:T(8,128)(2,1)S(1)}, u32[]{:S(2)}, u32[]{:S(2)}) collective-permute-start(bf16[128,1536]{1,0:T(8,128)(2,1)S(1)} %get-tuple-element.107.refs_5_), channel_id=1, source_target_pairs={{0,4},{2,6},{4,0},{6,2},{1,5},{3,7},{5,1},{7,3},{8,12},{10,14},{12... | collective-permute-start | bytes 1179656 | tf_op jit(solution)/shard_map/ppermute | solution.py:522
  125.5 1.4 collective-permute-start.38
  125.6 1.4 collective-permute-start.39
  126.2 1.4 collective-permute-start.41
  129.1 9.8 %collective-permute-start.46 = (bf16[128,768]{1,0:T(8,128)(2,1)S(1)}, bf16[128,768]{1,0:T(8,128)(2,1)S(1)}, u32[]{:S(2)}, u32[]{:S(2)}) collective-permute-start(bf16[128,768]{1,0:T(8,128)(2,1)S(1)} %shard_map.123.refs_3_.refs_0_), channel_id=1, source_target_pairs={{0,1},{1,0},{2,3},{3,2},{4,5},{5,4},{6,7},{7,6},{8,9},{9,8},{10,11... | collective-permute-start | bytes 589832 | tf_op jit(solution)/shard_map/ppermute | solution.py:522
  133.9 1.4 collective-permute-start.42
  134.0 2.7 %collective-permute-start.43 = (bf16[32,1536]{1,0:T(8,128)(2,1)S(1)}, bf16[32,1536]{1,0:T(8,128)(2,1)S(1)}, u32[]{:S(2)}, u32[]{:S(2)}) collective-permute-start(bf16[32,1536]{1,0:T(8,128)(2,1)S(1)} %get-tuple-element.116.refs_1_), channel_id=1, source_target_pairs={{0,2},{2,0},{4,6},{6,4},{1,3},{3,1},{5,7},{7,5},{8,10},{10,8},{12,... | collective-permute-start | bytes 294920 | tf_op jit(solution)/shard_map/ppermute | solution.py:522
  134.5 2.2 %collective-permute-start.44 = (bf16[32,1536]{1,0:T(8,128)(2,1)S(1)}, bf16[32,1536]{1,0:T(8,128)(2,1)S(1)}, u32[]{:S(2)}, u32[]{:S(2)}) collective-permute-start(bf16[32,1536]{1,0:T(8,128)(2,1)S(1)} %get-tuple-element.117.refs_2_), channel_id=1, source_target_pairs={{0,2},{2,0},{4,6},{6,4},{1,3},{3,1},{5,7},{7,5},{8,10},{10,8},{12,... | collective-permute-start | bytes 294920 | tf_op jit(solution)/shard_map/ppermute | solution.py:522
  134.6 2.1 %collective-permute-start.45 = (bf16[32,1536]{1,0:T(8,128)(2,1)S(1)}, bf16[32,1536]{1,0:T(8,128)(2,1)S(1)}, u32[]{:S(2)}, u32[]{:S(2)}) collective-permute-start(bf16[32,1536]{1,0:T(8,128)(2,1)S(1)} %get-tuple-element.118.refs_3_), channel_id=1, source_target_pairs={{0,2},{2,0},{4,6},{6,4},{1,3},{3,1},{5,7},{7,5},{8,10},{10,8},{12,... | collective-permute-start | bytes 294920 | tf_op jit(solution)/shard_map/ppermute | solution.py:522
  135.3 7.7 %collective-permute-start.49 = (bf16[128,768]{1,0:T(8,128)(2,1)S(1)}, bf16[128,768]{1,0:T(8,128)(2,1)S(1)}, u32[]{:S(2)}, u32[]{:S(2)}) collective-permute-start(bf16[128,768]{1,0:T(8,128)(2,1)S(1)} %shard_map.124.refs_4_.refs_0_), channel_id=1, source_target_pairs={{0,1},{1,0},{2,3},{3,2},{4,5},{5,4},{6,7},{7,6},{8,9},{9,8},{10,11... | collective-permute-start | bytes 589832 | tf_op jit(solution)/shard_map/ppermute | solution.py:522
  138.2 9.0 %collective-permute-start.48 = (bf16[128,768]{1,0:T(8,128)(2,1)S(1)}, bf16[128,768]{1,0:T(8,128)(2,1)S(1)}, u32[]{:S(2)}, u32[]{:S(2)}) collective-permute-start(bf16[128,768]{1,0:T(8,128)(2,1)S(1)} %shard_map.128.refs_0_), channel_id=1, source_target_pairs={{0,1},{1,0},{2,3},{3,2},{4,5},{5,4},{6,7},{7,6},{8,9},{9,8},{10,11... | collective-permute-start | bytes 589832 | tf_op jit(solution)/shard_map/ppermute | solution.py:522
  141.3 9.4 %collective-permute-start.47 = (bf16[128,768]{1,0:T(8,128)(2,1)S(1)}, bf16[128,768]{1,0:T(8,128)(2,1)S(1)}, u32[]{:S(2)}, u32[]{:S(2)}) collective-permute-start(bf16[128,768]{1,0:T(8,128)(2,1)S(1)} %shard_map.127.refs_0_), channel_id=1, source_target_pairs={{0,1},{1,0},{2,3},{3,2},{4,5},{5,4},{6,7},{7,6},{8,9},{9,8},{10,11... | collective-permute-start | bytes 589832 | tf_op jit(solution)/shard_map/ppermute | solution.py:522
  (4 other events, 35.7 us)
